TPU v7x, 32 devices: a whole 2x2x4 slice. The times are simulated.
32 devices in a mesh: dp: 4 (over y, x), fsdp: 8 (over z, core).
Axes of the slice: x: 2, y: 2, z: 4, core: 2. Of those that a mesh axis runs over, the one named last changes fastest.
Arguments:
- tokens: bfloat16 [96, 608, 768], P(('dp', 'fsdp')), may hold values from -6 to 6
- cotangent: bfloat16 [96, 608, 768], P(('dp', 'fsdp')), may hold values from -6 to 6
- group: int32 [96], P(('dp', 'fsdp')), may hold values from 0 to 1
- text_len: int32 [96], P(('dp', 'fsdp')), may hold values from 1 to 32
- qkv_w: bfloat16 [1769472], P(('dp', 'fsdp')), may hold values from -2 to 2
- out_w: bfloat16 [589824], P(('dp', 'fsdp')), may hold values from -0.21875 to 0.21875
- mlp_in: bfloat16 [2359296], P(('dp', 'fsdp')), may hold values from -0.21875 to 0.21875
- mlp_out: bfloat16 [2359296], P(('dp', 'fsdp')), may hold values from -0.21875 to 0.21875
- gains: bfloat16 [1536], P(('dp', 'fsdp')), may hold values from 0.5 to 1.5
- biases: bfloat16 [7680], P(('dp', 'fsdp')), may hold values from -0.59765625 to 0.59765625
Outputs:
- block_out: bfloat16 [96, 608, 768], P(('dp', 'fsdp'))
- input_grad: bfloat16 [96, 608, 768], P(('dp', 'fsdp'))
- qkv_grad: float32 [1769472], P(('dp', 'fsdp'))
- out_grad: float32 [589824], P(('dp', 'fsdp'))
- mlp_in_grad: float32 [2359296], P(('dp', 'fsdp'))
- mlp_out_grad: float32 [2359296], P(('dp', 'fsdp'))
- gains_grad: float32 [1536], P(('dp', 'fsdp'))
- biases_grad: float32 [7680], P(('dp', 'fsdp'))
All inputs are finite; a program needn't handle non-finite values.
Results may differ from a plain program's by a relative error of at most 0.014.
Values may be sent and summed in bfloat16 or wider, within the bound.
No kernel may reach another device: no remote copies, remote signals or barrier semaphores. Data moves between devices by JAX's collectives and lax.ppermute only.
A program may use at most 256 MiB of HBM per device.

v0:
```python
from functools import partial
import math

import jax
import jax.numpy as jnp
from jax import lax
from jax.sharding import PartitionSpec as P

HEADS = 12
FF = 3072
PATCH_SMALL = 196
PATCH_LARGE = 576


def layer_norm(values, gain, shift):
    center = values - jnp.mean(values, -1, keepdims=True)
    spread = jnp.mean(center * center, -1, keepdims=True)
    return center * lax.rsqrt(spread + 1e-05) * gain + shift


def split_small(gains, biases):
    width = gains.shape[0] // 2
    return (
        gains[:width],
        gains[width:],
        biases[:width],
        biases[width : 2 * width],
        biases[2 * width : 3 * width],
        biases[3 * width : 4 * width],
        biases[4 * width : 5 * width],
        biases[5 * width : 6 * width],
        biases[6 * width :],
    )


def to_blocks(tensor, item_count, seq_len):
    head_size = tensor.shape[1] // HEADS
    shaped = tensor.reshape(item_count, seq_len, HEADS, head_size).transpose(0, 2, 1, 3)
    return shaped.reshape(item_count * 2, HEADS // 2, seq_len, head_size)


def from_blocks(tensor, item_count, seq_len):
    head_size = tensor.shape[-1]
    shaped = tensor.reshape(item_count, HEADS, seq_len, head_size).transpose(0, 2, 1, 3)
    return shaped.reshape(item_count * seq_len, HEADS * head_size)


def masked_scores(query_block, key_block, key_keep):
    scaling = 1.0 / math.sqrt(query_block.shape[-1])
    scores = (
        jnp.einsum("hqe,hke->hqk", query_block, key_block, preferred_element_type=jnp.float32)
        * scaling
    )
    return jnp.where(key_keep[None, None, :], scores, -1e30)


def attend(block):
    query_block, key_block, value_block, key_keep = block
    scores = masked_scores(query_block, key_block, key_keep)
    maximum = jnp.max(scores, -1, keepdims=True)
    raised = jnp.exp(scores - maximum)
    row_total = jnp.sum(raised, -1, keepdims=True)
    weights = (raised / row_total).astype(jnp.bfloat16)
    mixture = jnp.einsum("hqk,hke->hqe", weights, value_block, preferred_element_type=jnp.float32)
    return (mixture.astype(jnp.bfloat16), (maximum + jnp.log(row_total))[..., 0])


def attend_back(block):
    query_block, key_block, value_block, mixture_grad, log_total, key_keep = block
    scaling = 1.0 / math.sqrt(query_block.shape[-1])
    scores = masked_scores(query_block, key_block, key_keep)
    probs = jnp.exp(scores - log_total[..., None])
    value_grad = jnp.einsum(
        "hqk,hqe->hke", probs.astype(jnp.bfloat16), mixture_grad, preferred_element_type=jnp.float32
    )
    prob_grad = jnp.einsum(
        "hqe,hke->hqk", mixture_grad, value_block, preferred_element_type=jnp.float32
    )
    centre = jnp.sum(probs * prob_grad, -1, keepdims=True)
    score_grad = (probs * (prob_grad - centre)).astype(jnp.bfloat16)
    query_grad = (
        jnp.einsum("hqk,hke->hqe", score_grad, key_block, preferred_element_type=jnp.float32)
        * scaling
    )
    key_grad = (
        jnp.einsum("hqk,hqe->hke", score_grad, query_block, preferred_element_type=jnp.float32)
        * scaling
    )
    return (query_grad, key_grad, value_grad)


def local(tokens, cotangent, group, text_len, qkv_w, out_w, mlp_in, mlp_out, gains, biases):
    item_count, seq_len, model_width = tokens.shape
    row_count = item_count * seq_len
    valid_len = PATCH_SMALL + (PATCH_LARGE - PATCH_SMALL) * group + text_len
    row_keep = jnp.arange(seq_len, dtype=jnp.int32)[None, :] < valid_len[:, None]
    row_scale = row_keep.astype(jnp.float32).reshape(row_count, 1)
    key_keep = jnp.repeat(row_keep, 2, axis=0)
    attn_parts = (
        lax.all_gather(qkv_w, ("dp", "fsdp"), axis=0, tiled=True),
        lax.all_gather(out_w, ("dp", "fsdp"), axis=0, tiled=True),
        lax.all_gather(gains, ("dp", "fsdp"), axis=0, tiled=True),
        lax.all_gather(biases, ("dp", "fsdp"), axis=0, tiled=True),
    )
    w_qkv = attn_parts[0].reshape(model_width, 3 * model_width)
    w_out = attn_parts[1].reshape(model_width, model_width)
    small_parts = split_small(attn_parts[2].astype(jnp.float32), attn_parts[3].astype(jnp.float32))
    (
        gain_one,
        gain_two,
        bias_query,
        bias_value,
        bias_output,
        shift_one,
        shift_two,
        bias_down,
        bias_up,
    ) = small_parts
    flat_in = tokens.reshape(row_count, model_width).astype(jnp.float32)
    normed, norm_one_back = jax.vjp(layer_norm, flat_in, gain_one, shift_one)
    normed_low = normed.astype(jnp.bfloat16)
    joined = jnp.dot(normed_low, w_qkv, preferred_element_type=jnp.float32)
    joined = joined + jnp.concatenate([bias_query, jnp.zeros_like(bias_query), bias_value])
    joined_low = joined.astype(jnp.bfloat16)
    query_blocks = to_blocks(joined_low[:, :model_width], item_count, seq_len)
    key_blocks = to_blocks(joined_low[:, model_width : 2 * model_width], item_count, seq_len)
    value_blocks = to_blocks(joined_low[:, 2 * model_width :], item_count, seq_len)
    mixed_blocks, log_totals = lax.map(attend, (query_blocks, key_blocks, value_blocks, key_keep))
    mixture = from_blocks(mixed_blocks, item_count, seq_len)
    mlp_parts = (
        lax.all_gather(mlp_in, ("dp", "fsdp"), axis=0, tiled=True),
        lax.all_gather(mlp_out, ("dp", "fsdp"), axis=0, tiled=True),
    )
    w_up = mlp_parts[0].reshape(model_width, FF)
    w_down = mlp_parts[1].reshape(FF, model_width)
    branch = jnp.dot(mixture, w_out, preferred_element_type=jnp.float32) + bias_output
    middle = flat_in + branch
    normed_two, norm_two_back = jax.vjp(layer_norm, middle, gain_two, shift_two)
    normed_two_low = normed_two.astype(jnp.bfloat16)
    hidden = jnp.dot(normed_two_low, w_up, preferred_element_type=jnp.float32) + bias_up
    active, gelu_back = jax.vjp(partial(jax.nn.gelu, approximate=False), hidden)
    active_low = active.astype(jnp.bfloat16)
    result = jnp.dot(active_low, w_down, preferred_element_type=jnp.float32) + bias_down
    block_out = ((middle + result) * row_scale).astype(jnp.bfloat16).reshape(tokens.shape)
    mlp_again = (
        lax.all_gather(mlp_in, ("dp", "fsdp"), axis=0, tiled=True),
        lax.all_gather(mlp_out, ("dp", "fsdp"), axis=0, tiled=True),
    )
    w_up = mlp_again[0].reshape(model_width, FF)
    w_down = mlp_again[1].reshape(FF, model_width)
    out_grad_full = cotangent.reshape(row_count, model_width).astype(jnp.float32) * row_scale
    result_grad = out_grad_full.astype(jnp.bfloat16)
    down_grad = jnp.einsum("rf,rd->fd", active_low, result_grad, preferred_element_type=jnp.float32)
    bias_down_grad = jnp.sum(result_grad.astype(jnp.float32), 0)
    active_grad = jnp.einsum("rd,fd->rf", result_grad, w_down, preferred_element_type=jnp.float32)
    hidden_grad = gelu_back(active_grad)[0]
    hidden_low = hidden_grad.astype(jnp.bfloat16)
    up_grad = jnp.einsum(
        "rd,rf->df", normed_two_low, hidden_low, preferred_element_type=jnp.float32
    )
    bias_up_grad = jnp.sum(hidden_low.astype(jnp.float32), 0)
    normed_two_grad = jnp.einsum("rf,df->rd", hidden_low, w_up, preferred_element_type=jnp.float32)
    middle_part, gain_two_grad, shift_two_grad = norm_two_back(normed_two_grad)
    middle_grad = out_grad_full + middle_part
    mlp_sums = (
        lax.psum_scatter(up_grad.reshape(-1), ("dp", "fsdp"), scatter_dimension=0, tiled=True),
        lax.psum_scatter(down_grad.reshape(-1), ("dp", "fsdp"), scatter_dimension=0, tiled=True),
    )
    attn_again = (
        lax.all_gather(qkv_w, ("dp", "fsdp"), axis=0, tiled=True),
        lax.all_gather(out_w, ("dp", "fsdp"), axis=0, tiled=True),
        lax.all_gather(gains, ("dp", "fsdp"), axis=0, tiled=True),
        lax.all_gather(biases, ("dp", "fsdp"), axis=0, tiled=True),
    )
    w_qkv = attn_again[0].reshape(model_width, 3 * model_width)
    w_out = attn_again[1].reshape(model_width, model_width)
    branch_grad = middle_grad.astype(jnp.bfloat16)
    out_w_grad = jnp.einsum("rd,re->de", mixture, branch_grad, preferred_element_type=jnp.float32)
    bias_output_grad = jnp.sum(branch_grad.astype(jnp.float32), 0)
    mixture_grad = jnp.einsum(
        "re,de->rd", branch_grad, w_out, preferred_element_type=jnp.float32
    ).astype(jnp.bfloat16)
    query_grads, key_grads, value_grads = lax.map(
        attend_back,
        (
            query_blocks,
            key_blocks,
            value_blocks,
            to_blocks(mixture_grad, item_count, seq_len),
            log_totals,
            key_keep,
        ),
    )
    joined_grad = jnp.concatenate(
        [
            from_blocks(query_grads, item_count, seq_len),
            from_blocks(key_grads, item_count, seq_len),
            from_blocks(value_grads, item_count, seq_len),
        ],
        1,
    ).astype(jnp.bfloat16)
    qkv_grad_local = jnp.einsum(
        "rd,rc->dc", normed_low, joined_grad, preferred_element_type=jnp.float32
    )
    joined_sums = jnp.sum(joined_grad.astype(jnp.float32), 0)
    bias_query_grad = joined_sums[:model_width]
    bias_value_grad = joined_sums[2 * model_width :]
    normed_grad = jnp.einsum("rc,dc->rd", joined_grad, w_qkv, preferred_element_type=jnp.float32)
    input_part, gain_one_grad, shift_one_grad = norm_one_back(normed_grad)
    input_grad = (middle_grad + input_part).astype(jnp.bfloat16).reshape(tokens.shape)
    gains_whole = jnp.concatenate([gain_one_grad, gain_two_grad])
    biases_whole = jnp.concatenate(
        [
            bias_query_grad,
            bias_value_grad,
            bias_output_grad,
            shift_one_grad,
            shift_two_grad,
            bias_down_grad,
            bias_up_grad,
        ]
    )
    attn_sums = (
        lax.psum_scatter(
            qkv_grad_local.reshape(-1), ("dp", "fsdp"), scatter_dimension=0, tiled=True
        ),
        lax.psum_scatter(out_w_grad.reshape(-1), ("dp", "fsdp"), scatter_dimension=0, tiled=True),
        lax.psum_scatter(gains_whole, ("dp", "fsdp"), scatter_dimension=0, tiled=True),
        lax.psum_scatter(biases_whole, ("dp", "fsdp"), scatter_dimension=0, tiled=True),
    )
    return (
        block_out,
        input_grad,
        attn_sums[0],
        attn_sums[1],
        mlp_sums[0],
        mlp_sums[1],
        attn_sums[2],
        attn_sums[3],
    )


def solution(mesh):
    return jax.shard_map(
        local,
        mesh=mesh,
        in_specs=(
            P(("dp", "fsdp"), None, None),
            P(("dp", "fsdp"), None, None),
            P(("dp", "fsdp")),
            P(("dp", "fsdp")),
            P(("dp", "fsdp")),
            P(("dp", "fsdp")),
            P(("dp", "fsdp")),
            P(("dp", "fsdp")),
            P(("dp", "fsdp")),
            P(("dp", "fsdp")),
        ),
        out_specs=(
            P(("dp", "fsdp"), None, None),
            P(("dp", "fsdp"), None, None),
            P(("dp", "fsdp")),
            P(("dp", "fsdp")),
            P(("dp", "fsdp")),
            P(("dp", "fsdp")),
            P(("dp", "fsdp")),
            P(("dp", "fsdp")),
        ),
        check_vma=False,
    )
```

profile of v0, /device:TPU:0, one launch (start us, length us, event | category | flops | bytes accessed | tf_op | source)
XLA Modules:
  0.0 1177.0 jit_solution(2737110019616233842)
XLA Ops:
  11.8 42.2 %all-reduce.10 = (bf16[7680]{0:T(1024)(128)(2,1)S(1)}, bf16[1536]{0:T(1024)(128)(2,1)S(1)}) all-reduce(bf16[7680]{0:T(1024)(128)(2,1)S(1)} %dynamic-update-slice.1, bf16[1536]{0:T(1024)(128)(2,1)S(1)} %dynamic-update-slice), channel_id=1, replica_groups=mesh['dp'=4,'fsdp'=8] {'dp','fsdp'}, use_global_device_ids=true, to_apply=%add.1 | all-reduce | flops 9216 | bytes 36864
  61.3 4.7 convert_reduce_fusion.2
  72.4 57.8 %all-gather.5.cloned.1.call-done = bf16[1769472]{0:T(1024)(128)(2,1)} async-done(((bf16[55296]{0:T(1024)(128)(2,1)}), bf16[1769472]{0:T(1024)(128)(2,1)}) %all-gather.5.cloned.1.call-update) | async-done | bytes 3538960 | tf_op jit(solution)/shard_map/all_gather | solution.py:100
  130.2 7.6 reshape.282
  137.8 9.4 add_convert_fusion.1
  150.6 4.6 copy.58
  155.2 9.2 reshape.283
  164.5 4.3 copy.59
  168.7 4.7 copy.60
  173.4 9.4 reshape.285
  182.8 4.3 copy.61
  187.1 4.7 copy.62
  191.8 9.5 reshape.287
  201.3 4.3 copy.63
  205.6 62.0 %while.26 = (s32[]{:T(128)}, bf16[6,6,608,64]{2,3,1,0:T(8,128)(2,1)}, f32[6,6,608]{2,1,0:T(8,128)}, pred[6,608]{1,0:T(8,128)(4,1)S(1)}, bf16[6,6,608,64]{2,3,1,0...) while((s32[]{:T(128)}, ...), condition=%wide.region_5.6_spmd, body=%wide.region_2.5_spmd.sunk | while | flops 594649536 | bytes 28710200 | solution.py:128
  211.5 4.4 fusion.124
  221.8 4.4 fusion.124
  232.2 4.4 fusion.124
  242.5 4.4 fusion.124
  252.8 4.4 fusion.124
  263.2 4.4 fusion.124
  267.6 6.2 copy.82
  273.8 18.2 %reshape.290 = bf16[1824,768]{0,1:T(8,128)(2,1)} reshape(bf16[3,608,12,64]{1,0,3,2:T(4,128)(2,1)} %bitcast.186) | data formatting | bytes 5603328 | tf_op jit(solution)/shard_map/reshape | solution.py:45
  292.1 4.8 fusion.77
  300.7 8.2 reshape.292
  308.9 63.1 %multiply_convert_fusion.1 = (bf16[1824,3072]{1,0:T(8,128)(2,1)}, f32[1824,3072]{1,0:T(8,128)}, f32[1824,3072]{1,0:T(8,128)}) fusion(f32[3072]{0:T(1024)S(1)} %slice.66, bf16[768,3072]{1,0:T(8,128)(2,1)} %reshape.292, f32[1824,768]{1,0:T(8,128)} %copy-done.5, f32[768]{0:T(1024)S(1)} %get-tuple-element.171, f32[768]{0:T(1024)S(1)} %get-tuple-element.178, ...), kind=kOutput, calls=%fused_computation.65 | convolution fusion | flops 8983535616 | bytes 66388224 | tf_op jit(solution)/shard_map/dot_general | solution.py:140
  372.1 9.4 reshape.293
  381.5 27.1 %convert_reduce_fusion = (f32[3072]{0:T(1024)}, bf16[1824,3072]{1,0:T(8,128)(2,1)}) fusion(f32[1824,3072]{1,0:T(8,128)} %get-tuple-element.160, bf16[1824,768]{1,0:T(8,128)(2,1)S(1)} %bitcast.196, bf16[3072,768]{1,0:T(8,128)(2,1)} %reshape.293, f32[1824,3072]{1,0:T(8,128)} %get-tuple-element.184, f32[3072]{0:T(1024)S(1)} %slice.66), kind=kOutput, calls=%fused_computation.63 | convolution fusion | flops 8701965312 | bytes 63578112 | tf_op jit(solution)/shard_map/rd,fd->rf/dot_general | solution.py:155
  408.6 16.0 %multiply_reduce_fusion.1 = (f32[768]{0:T(1024)}, f32[1824]{0:T(1024)S(1)}, f32[768]{0:T(1024)}, f32[1824,768]{1,0:T(8,128)S(1)}) fusion(f32[1824,768]{1,0:T(8,128)} %copy-done.5, f32[1824]{0:T(1024)S(1)} %fusion.67, f32[1824]{0:T(1024)S(1)} %broadcast_multiply_fusion.1, f32[768]{0:T(1024)S(1)} %get-tuple-element.178, ...), kind=kOutput, calls=%fused_computation.86 | convolution fusion | flops 8617914368 | bytes 27163008 | tf_op jit(solution)/shard_map/rf,df->rd/dot_general | solution.py:162
  424.6 16.4 %convolution_bitcast_fusion = f32[96,24,8,128]{3,2,1,0:T(8,128)} fusion(bf16[1824,3072]{1,0:T(8,128)(2,1)} %get-tuple-element.188, f32[1824,768]{1,0:T(8,128)S(1)} %copy-done.6, f32[768]{0:T(1024)S(1)} %get-tuple-element.171, f32[768]{0:T(1024)S(1)} %get-tuple-element.178, f32[1824]{0:T(1024)S(1)} %fusion.67, f32[1824]{0:T(1024)S(1)} %broadcast_multiply_fusion.1), kind=kOutput, calls=%fused_computation.106 | convolution fusion | flops 8613715968 | bytes 26267904 | tf_op jit(solution)/shard_map/rd,rf->df/dot_general | solution.py:158
  447.6 3.9 convolution_convert_fusion
  454.9 5.3 reshape.295
  460.2 4.3 copy.66
  464.5 129.9 %while.27 = (s32[]{:T(128)}, bf16[6,6,608,64]{2,3,1,0:T(8,128)(2,1)}, bf16[6,6,608,64]{2,3,1,0:T(8,128)(2,1)}, bf16[6,6,608,64]{2,3,1,0:T(8,128)(2,1)}, pred[6,6...) while((s32[]{:T(128)}, ...), condition=%wide.region_12.13_spmd, body=%wide.region_10.12_spmd.sunk | while | flops 1453242880 | bytes 95686536 | solution.py:183
  468.0 4.2 multiply_reduce_fusion.8
  482.1 4.1 fusion.136
  489.6 4.2 multiply_reduce_fusion.8
  503.7 4.1 fusion.136
  511.2 4.2 multiply_reduce_fusion.8
  525.3 4.1 fusion.136
  532.8 4.2 multiply_reduce_fusion.8
  546.9 4.1 fusion.136
  554.4 4.2 multiply_reduce_fusion.8
  568.5 4.1 fusion.136
  576.0 4.2 multiply_reduce_fusion.8
  590.1 4.1 fusion.136
  594.4 6.3 copy.81
  600.7 6.9 reshape.298
  610.4 4.5 copy.80
  615.0 6.9 reshape.300
  621.8 6.4 copy.79
  628.2 8.7 reshape.302
  643.1 13.6 %multiply_reduce_fusion.2 = (f32[768]{0:T(1024)S(1)}, f32[1824]{0:T(1024)S(1)}, f32[768]{0:T(1024)S(1)}, f32[1824,768]{1,0:T(8,128)S(1)}) fusion(f32[1824]{0:T(1024)S(1)} %copy-done.31, f32[1824]{0:T(1024)S(1)} %copy-done.32, bf16[3,608,768]{2,1,0:T(8,128)(2,1)S(1)} %copy-done.2, f32[768]{0:T(1024)S(1)} %copy-done.30, ...), kind=kOutput, calls=%fused_computation.87 | convolution fusion | flops 6470438912 | bytes 23181696 | tf_op jit(solution)/shard_map/rc,dc->rd/dot_general | solution.py:208
  656.7 11.3 fusion.62
  668.0 4.0 fusion.79
  679.1 7.0 fusion.60
  686.1 15.3 %fusion.80 = f32[3072,768]{1,0:T(8,128)} fusion(bf16[1824,3072]{1,0:T(8,128)(2,1)} %get-tuple-element.159, bf16[1824,768]{1,0:T(8,128)(2,1)S(1)} %get-tuple-element.168), kind=kOutput, calls=%fused_computation.147 | convolution fusion | flops 8606711808 | bytes 23445504 | tf_op jit(solution)/shard_map/rf,rd->fd/dot_general | solution.py:153
  701.4 10.8 reshape.307
  712.2 9.6 copy.74
  721.7 8.1 reshape.304
  731.5 4.8 convert_reduce_fusion.1
  736.4 41.3 %all-reduce.8 = (f32[1536]{0:T(1024)S(1)}, f32[7680]{0:T(1024)S(1)}) all-reduce(f32[1536]{0:T(1024)S(1)} %pad_maximum_fusion.1, f32[7680]{0:T(1024)S(1)} %constant_dynamic-update-slice_fusion.6), channel_id=6, replica_groups=mesh['dp'=4,'fsdp'=8] {'dp','fsdp'}, use_global_device_ids=true, to_apply=%region_21.22.clone | all-reduce | flops 9216 | bytes 73728
  778.9 15.9 %multiply_convert_fusion.3 = bf16[1824,768]{1,0:T(8,128)(2,1)} fusion(f32[1824,768]{1,0:T(8,128)} %copy-done.5, bf16[1824,3072]{1,0:T(8,128)(2,1)} %get-tuple-element.159, bf16[3072,768]{1,0:T(8,128)(2,1)} %reshape.293, f32[1824]{0:T(1024)S(1)} %copy-done.22, f32[768]{0:T(1024)S(1)} %copy-done.38), kind=kOutput, calls=%fused_computation.94 | convolution fusion | flops 8612315136 | bytes 24340608 | tf_op jit(solution)/shard_map/dot_general | solution.py:143
  794.9 368.8 %all-reduce.13.cloned.1.call-done = (f32[1769472]{0:T(1024)}, f32[589824]{0:T(1024)}, f32[2359296]{0:T(1024)}, f32[2359296]{0:T(1024)}) async-done(((f32[1769472]{0:T(1024)}, f32[589824]{0:T(1024)}, f32[2359296]{0:T(1024)}, f32[2359296]{0:T(1024)}), (f32[1769472]{0:T(1024)}, f32[589824]{0:T(1024)}, f32[2359296]{0:T(1024)}, f32[2359296]{0:T(1024)})) %all-reduce.13.cloned.1.call-update) | async-done | bytes 28311568
  (239 shorter events, 176.0 us)
Async XLA Ops:
  7.2 53.3 %copy-start.42 = (s32[3]{0:T(128)S(1)}, s32[3]{0:T(128)}, u32[]{:S(2)}) copy-start(s32[3]{0:T(128)} %param.16) | copy-start | bytes 40
  7.2 53.3 %copy-start.41 = (s32[3]{0:T(128)S(1)}, s32[3]{0:T(128)}, u32[]{:S(2)}) copy-start(s32[3]{0:T(128)} %param.17) | copy-start | bytes 40
  7.2 61.8 %all-gather.7.cloned.1.call-start = ((), (), s32[]{:S(2)}) async-start(), calls=%async_computation.1 | async-start | bytes 1216512 | tf_op jit(solution)/shard_map/all_gather | solution.py:101
  7.9 122.3 %all-gather.5.cloned.1.call-start = ((), (), s32[]{:S(2)}) async-start(), calls=%async_computation | async-start | bytes 3649536 | tf_op jit(solution)/shard_map/all_gather | solution.py:100
  8.7 292.0 %all-gather.9.cloned.1.call-start = ((), (), s32[]{:S(2)}) async-start(), calls=%async_computation.2 | async-start | bytes 4866048 | tf_op jit(solution)/shard_map/all_gather | solution.py:131
  9.4 362.6 %all-gather.11.cloned.1.call-start = ((), (), s32[]{:S(2)}) async-start(), calls=%async_computation.3 | async-start | bytes 4866048 | tf_op jit(solution)/shard_map/all_gather | solution.py:132
  10.0 1153.7 %all-reduce.13.cloned.1.call-start = ((), (), s32[]{:S(2)}) async-start(), calls=%async_computation.4 | async-start | bytes 56623104
  54.6 12.1 %copy-start.34 = (f32[768]{0:T(1024)}, f32[768]{0:T(1024)S(1)}, u32[]{:S(2)}) copy-start(f32[768]{0:T(1024)S(1)} %get-tuple-element.175) | copy-start | bytes 9220
  54.6 12.1 %copy-start.1 = (bf16[3,608,768]{2,1,0:T(8,128)(2,1)S(1)}, bf16[3,608,768]{2,1,0:T(8,128)(2,1)}, u32[]{:S(2)}) copy-start(bf16[3,608,768]{2,1,0:T(8,128)(2,1)} %param.14) | copy-start | bytes 8404996
  60.5 8.5 copy-start.29
  66.1 71.7 %copy-start.27 = (f32[1824]{0:T(1024)}, f32[1824]{0:T(1024)S(1)}, u32[]{:S(2)}) copy-start(f32[1824]{0:T(1024)S(1)} %add.147) | copy-start | bytes 21892
  267.6 24.5 %copy-start.19 = (pred[6,608]{1,0:T(8,128)(4,1)}, pred[6,608]{1,0:T(8,128)(4,1)S(1)}, u32[]{:S(2)}) copy-start(pred[6,608]{1,0:T(8,128)(4,1)S(1)} %get-tuple-element.382) | copy-start | bytes 10948
  296.9 2.4 copy-start.5
  300.1 0.6 copy-start.25
  372.1 9.4 copy-start.16
  408.6 16.0 %copy-start.6 = (f32[1824,768]{1,0:T(8,128)S(1)}, f32[1824,768]{1,0:T(8,128)}, u32[]{:S(2)}) copy-start(f32[1824,768]{1,0:T(8,128)} %copy-done.5) | copy-start | bytes 16809988
  424.6 16.4 %copy-start.26 = (f32[1824]{0:T(1024)S(1)}, f32[1824]{0:T(1024)}, u32[]{:S(2)}) copy-start(f32[1824]{0:T(1024)} %copy-done.25) | copy-start | bytes 21892
  441.0 2.6 copy-start.3
  441.0 2.6 copy-start.21
  443.6 2.4 copy-start
  443.6 2.4 copy-start.23
  443.6 3.9 copy-start.18
  446.0 1.6 copy-start.14
  454.9 9.5 copy-start.20
  475.0 3.5 copy-start.10
  480.5 1.6 copy-start.11
  496.6 3.5 copy-start.10
  502.1 1.6 copy-start.11
  518.2 3.5 copy-start.10
  523.6 1.6 copy-start.11
  539.8 3.5 copy-start.10
  545.3 1.6 copy-start.11
  561.3 3.6 copy-start.10
  566.9 1.6 copy-start.11
  583.0 3.5 copy-start.10
  588.5 1.6 copy-start.11
  607.5 2.9 copy-start.12
  636.9 2.9 copy-start.8
  636.9 4.8 copy-start.2
  636.9 4.8 copy-start.30
  636.9 4.7 copy-start.31
  636.9 4.7 copy-start.32
  639.8 3.3 copy-start.9
  643.1 13.6 %copy-start.7 = (bf16[1824,2304]{0,1:T(8,128)(2,1)S(1)}, bf16[1824,2304]{0,1:T(8,128)(2,1)}, u32[]{:S(2)}) copy-start(bf16[1824,2304]{0,1:T(8,128)(2,1)} %constant_dynamic-update-slice_fusion) | copy-start | bytes 25214980
  643.1 13.6 %copy-start.35 = (f32[768]{0:T(1024)S(1)}, f32[768]{0:T(1024)}, u32[]{:S(2)}) copy-start(f32[768]{0:T(1024)} %copy-done.34) | copy-start | bytes 9220
  656.7 11.3 copy-start.13
  656.7 11.3 copy-start.15
  668.0 4.0 copy-start.28
  675.7 3.4 copy-start.4
  675.7 3.4 copy-start.22
  675.7 3.4 copy-start.24
  721.7 8.1 copy-start.17
  731.4 4.9 copy-start.33
  731.4 4.9 copy-start.39
  731.4 4.9 copy-start.36
  731.5 4.9 copy-start.40
  731.5 4.9 copy-start.37
  731.5 47.5 %copy-start.38 = (f32[768]{0:T(1024)S(1)}, f32[768]{0:T(1024)}, u32[]{:S(2)}) copy-start(f32[768]{0:T(1024)} %get-tuple-element.170) | copy-start | bytes 9220
Sparse Core Ops, SparseCore 0:
  11.0 56.8 all-gather.6
  71.0 59.1 all-gather.4
  133.2 62.4 all-gather.8
  198.6 62.4 all-gather.10
  731.5 432.0 all-reduce.12
where the time goes:
time: 1190 us; the launch traced here: 1180 us
  waiting for transfers between devices  429 us (36%)
  matrix products  345 us (29%)
  local copies, waits for them, and re-layouts  235 us (20%)
  blocking collectives  83.5 us (7%)
  other arithmetic  68.7 us (6%)
  between operations  14.6 us (1%)
    unnamed x6, waiting for transfers between devices  371 us
    unnamed x2, blocking collectives  83.5 us
    dot_general x1, matrix products, local(): jnp.dot(normed_two_low, w_up, preferred_element_type=jnp.float32) + bias_up  63.1 us
    all_gather x1, waiting for transfers between devices, local(): lax.all_gather(qkv_w, ('dp', 'fsdp'), axis=0, tiled=True)  57.8 us
    reshape x4, local copies, waits for them, and re-layouts, from_blocks(): return shaped.reshape(item_count * seq_len, HEADS * head_size)  40.6 us
    dot_general x12, matrix products, masked_scores(): jnp.einsum('hqe,hke->hqk', query_block, key_block, preferred_element_type...  34.8 us
    reshape x4, local copies, waits for them, and re-layouts, to_blocks(): tensor.reshape(item_count, seq_len, HEADS, head_size).transpose(0, 2, 1, 3)  33.4 us
    unnamed x101, local copies, waits for them, and re-layouts  31.9 us
  transfers between devices with their start and end apart: 5, of which 2 were waited for; matrix products, arithmetic and copies ran while one was open for 24% of the time, Pallas kernels for 0%

commit v1 on v0

v1 whole, which is shorter than its diff:
```python
import functools
import math

import jax
import jax.numpy as jnp
from jax import lax
from jax.experimental import pallas as pl
from jax.experimental.pallas import tpu as pltpu
from jax.sharding import PartitionSpec as P

HEADS = 12
PATCH_SMALL = 196
PATCH_LARGE = 576
AXES = ("dp", "fsdp")
bf16 = jnp.bfloat16
f32 = jnp.float32
NN = (((1,), (0,)), ((), ()))
NT = (((1,), (1,)), ((), ()))
TN = (((0,), (0,)), ((), ()))
VMEM_LIMIT = 60 * 2**20
LOG2E = 1.4426950408889634


def dot(a, b, dims):
    return lax.dot_general(a, b, dims, preferred_element_type=f32)


def params(n):
    return pltpu.CompilerParams(
        vmem_limit_bytes=VMEM_LIMIT, dimension_semantics=("arbitrary",) * n
    )


def cost(*_):
    return pl.CostEstimate(flops=1, bytes_accessed=1, transcendentals=0)


def once(shape):
    return pl.BlockSpec(
        shape, lambda *_: (0,) * len(shape), pipeline_mode=pl.Buffered(buffer_count=1)
    )


def shape_of(shape, dtype):
    return jax.ShapeDtypeStruct(shape, dtype)


class Flights:
    def __init__(self):
        self.waiting = []
        self.flying = []

    def add(self, steps, lengths):
        job = {"steps": steps, "lengths": list(lengths), "result": None}
        self.advance(job, None)
        return job

    def advance(self, job, came):
        try:
            sends = job["steps"].send(came) if came is not None else next(job["steps"])
        except StopIteration as stop:
            job["result"] = stop.value
            return
        length = job["lengths"].pop(0) if job["lengths"] else 1
        self.waiting.append((job, sends, length))

    def depart(self):
        for job, sends, length in self.waiting:
            came = [lax.ppermute(array, AXES, pairs) for array, pairs in sends]
            self.flying.append([job, came, length])
        self.waiting = []

    def run(self, kernel, operand, *others):
        arrays = [array for _, sends, _ in self.waiting for array, _ in sends]
        if arrays:
            operand, arrays = lax.optimization_barrier((operand, arrays))
            left = iter(arrays)
            self.waiting = [
                (job, [(next(left), pairs) for _, pairs in sends], length)
                for job, sends, length in self.waiting
            ]
        self.depart()
        out = kernel(operand, *others)
        for flight in self.flying:
            flight[2] -= 1
        landed = [flight for flight in self.flying if flight[2] <= 0]
        self.flying = [flight for flight in self.flying if flight[2] > 0]
        if landed:
            out, came = lax.optimization_barrier((out, [flight[1] for flight in landed]))
            for flight, got in zip(landed, came):
                self.advance(flight[0], got)
        return out

    def behind(self, value):
        value, _ = lax.optimization_barrier((value, [array for _, sends, _ in self.waiting for array, _ in sends]))
        return value

    def finish(self, turns=1 << 30):
        while (self.waiting or self.flying) and turns > 0:
            turns -= 1
            self.depart()
            landed, self.flying = self.flying, []
            cames = lax.optimization_barrier([flight[1] for flight in landed])
            for flight, came in zip(landed, cames):
                self.advance(flight[0], came)


def bit_groups(mesh):
    inner = int(math.log2(mesh.shape["fsdp"]))
    outer = int(math.log2(mesh.shape["dp"]))
    rest = [list(range(b, min(b + 2, inner))) for b in range(1, inner, 2)]
    return [0], list(range(inner, inner + outer)), rest


def position(me, bits):
    spot = 0
    for place, bit in enumerate(bits):
        spot = spot + ((me >> bit) & 1) * (1 << place)
    return spot


def partners(count, bits):
    swaps = []
    for step in range(1, 1 << len(bits)):
        mask = 0
        for place, bit in enumerate(bits):
            if (step >> place) & 1:
                mask |= 1 << bit
        swaps.append((step, [(i, i ^ mask) for i in range(count)]))
    return swaps


def gather_steps(shard, mesh):
    count = mesh.size
    core, outer, rest = bit_groups(mesh)
    me = lax.axis_index(AXES)
    rows, columns = shard.shape
    held = shard
    rest_size = 1
    for bits in rest:
        size = 1 << len(bits)
        spot = position(me, bits)
        swaps = partners(count, bits)
        block = held.reshape(1, rest_size, rows, columns)
        came = yield [(block, pairs) for _, pairs in swaps]
        whole = jnp.zeros((size, rest_size, rows, columns), shard.dtype)
        for (step, _), got in zip([(0, None)] + swaps, [block] + came):
            whole = lax.dynamic_update_slice(whole, got, (spot ^ step, 0, 0, 0))
        rest_size *= size
        held = whole
    size = 1 << len(outer)
    spot = position(me, outer)
    swaps = partners(count, outer)
    block = held.reshape(1, rest_size, 1, rows, columns)
    came = yield [(block, pairs) for _, pairs in swaps]
    held = jnp.zeros((size, rest_size, 1, rows, columns), shard.dtype)
    for (step, _), got in zip([(0, None)] + swaps, [block] + came):
        held = lax.dynamic_update_slice(held, got, (spot ^ step, 0, 0, 0, 0))
    spot = position(me, core)
    (got,) = yield [(held, partners(count, core)[0][1])]
    whole = jnp.zeros((size, rest_size, 2, rows, columns), shard.dtype)
    whole = lax.dynamic_update_slice(whole, held, (0, 0, spot, 0, 0))
    whole = lax.dynamic_update_slice(whole, got, (0, 0, spot ^ 1, 0, 0))
    return whole.reshape(count * rows, columns)


def pick(array, axis, index):
    return lax.dynamic_slice_in_dim(array, index, 1, axis)


def total(terms, axis, index, kind):
    return sum(pick(term, axis, index).astype(f32) for term in terms).astype(kind)


def sum_steps(parts, mesh, kind):
    count = mesh.size
    core, outer, rest = bit_groups(mesh)
    me = lax.axis_index(AXES)
    rows, columns = parts.shape[0] // count, parts.shape[1]
    rest_size = mesh.shape["fsdp"] // 2
    held = parts.reshape(mesh.shape["dp"], rest_size, 2, rows, columns)
    spot = position(me, core)
    (got,) = yield [(pick(held, 2, spot ^ 1).astype(kind), partners(count, core)[0][1])]
    terms = [pick(held, 2, spot), got]
    split = 2 if len(outer) == 2 and columns % 256 == 0 else 1
    width = columns // split
    shape = (2,) * len(outer) + (rest_size, 1, rows, width)
    pieces = []
    for piece in range(split):
        own = [term[..., piece * width : (piece + 1) * width].reshape(shape) for term in terms]
        order = list(range(len(outer)))
        pieces.append((own, order if piece == 0 else order[::-1]))
    for turn in range(len(outer)):
        sends = []
        for own, order in pieces:
            axis = order[turn]
            bit = outer[len(outer) - 1 - axis]
            mine = position(me, [bit])
            sends.append((total(own, axis, mine ^ 1, kind), partners(count, [bit])[0][1]))
        came = yield sends
        pieces = [
            ([pick(term, order[turn], position(me, [outer[len(outer) - 1 - order[turn]]])) for term in own] + [got], order)
            for (own, order), got in zip(pieces, came)
        ]
    left = rest_size
    pieces = [[term.reshape(rest_size, rows, width) for term in own] for own, _ in pieces]
    for bits in reversed(rest):
        size = 1 << len(bits)
        left //= size
        pieces = [[term.reshape(size, left, rows, width) for term in own] for own in pieces]
        spot = position(me, bits)
        swaps = partners(count, bits)
        sends = [
            (jnp.concatenate([total(own, 0, spot ^ step, kind) for own in pieces], -1), pairs)
            for step, pairs in swaps
        ]
        came = yield sends
        pieces = [
            [pick(term, 0, spot) for term in own]
            + [got[..., place * width : (place + 1) * width] for got in came]
            for place, own in enumerate(pieces)
        ]
    sums = [sum(term.astype(f32) for term in own).reshape(rows, width) for own in pieces]
    return jnp.concatenate(sums, -1)


def plane_sum_kernel(where, *refs, parts):
    keeps, cames, outs = refs[:parts], refs[parts : 2 * parts], refs[2 * parts :]
    for step, out in enumerate(outs):
        place = where[1] ^ step
        start = 0
        for keep, came in zip(keeps, cames):
            lanes = slice(start, start + keep.shape[-1])
            start += keep.shape[-1]
            out[:, lanes] = (keep[place].astype(f32) + came[place].astype(f32)).astype(out.dtype)


def plane_sum(where, keeps, cames, size):
    blocks, rows, _ = keeps[0].shape
    left = blocks // size
    columns = sum(keep.shape[2] for keep in keeps)
    arrays = [array.reshape(size, left, rows, array.shape[2]) for array in (*keeps, *cames)]
    part = pl.BlockSpec((None, rows, columns), lambda j, where: (j, 0, 0))
    return pl.pallas_call(
        functools.partial(plane_sum_kernel, parts=len(keeps)),
        grid_spec=pltpu.PrefetchScalarGridSpec(
            num_scalar_prefetch=1,
            grid=(left,),
            in_specs=[
                pl.BlockSpec((size, None, rows, array.shape[3]), lambda j, where: (0, j, 0, 0))
                for array in arrays
            ],
            out_specs=[part] * size,
        ),
        out_shape=[shape_of((left, rows, columns), bf16)] * size,
        compiler_params=params(1),
        cost_estimate=cost(blocks * rows * columns, blocks * rows * columns * 6),
        name="plane_sum",
    )(where, *arrays)


def line_sum_kernel(where, *refs, size):
    terms, outs = refs[:size], refs[size:]
    for step, out in enumerate(outs):
        place = where[2] ^ step
        out[...] = sum(term[place].astype(f32) for term in terms).astype(out.dtype)


def line_sum(where, terms):
    size, rows, columns = terms[0].shape
    return pl.pallas_call(
        functools.partial(line_sum_kernel, size=len(terms)),
        grid_spec=pltpu.PrefetchScalarGridSpec(
            num_scalar_prefetch=1,
            grid=(1,),
            in_specs=[once((size, rows, columns))] * len(terms),
            out_specs=[once((rows, columns))] * size,
        ),
        out_shape=[shape_of((rows, columns), f32)] + [shape_of((rows, columns), bf16)] * (size - 1),
        compiler_params=params(1),
        cost_estimate=cost(size * size * rows * columns, size * rows * columns * 10),
        name="line_sum",
    )(where, *terms)


def fast_sum_steps(keeps, sends, where, mesh):
    count = mesh.size
    core, outer, rest = bit_groups(mesh)
    cames = yield [(send, partners(count, core)[0][1]) for send in sends]
    own, *sends = plane_sum(where, keeps, cames, 1 << len(outer))
    came = yield [(array, pairs) for array, (_, pairs) in zip(sends, partners(count, outer))]
    own, *sends = line_sum(where, [own, *came])
    came = yield [(array, pairs) for array, (_, pairs) in zip(sends, partners(count, rest[0]))]
    return own + sum(array.astype(f32) for array in came)


def small_sum_steps(parts, mesh):
    count = mesh.size
    core, outer, rest = bit_groups(mesh)
    groups = [core, outer, *reversed(rest)]
    order = [outer, *reversed(rest), core]
    me = lax.axis_index(AXES)
    columns = parts.shape[1]
    held = parts.reshape([1 << len(bits) for bits in order] + [columns])
    for bits in groups:
        axis = order.index(bits)
        spot = position(me, bits)
        swaps = partners(count, bits)
        came = yield [(pick(held, axis, spot ^ step), pairs) for step, pairs in swaps]
        held = pick(held, axis, spot) + sum(came)
    return held.reshape(columns)


def cut_by_core(mesh):
    _, outer, rest = bit_groups(mesh)
    return len(outer) == 2 and len(rest) == 1 and len(rest[0]) == 2


def store_cut(core, outs, lanes, value, rows):
    if len(outs) == 1:
        outs[0][:, lanes] = value.astype(bf16)
        return
    keep, send = outs
    for parity in range(2):
        @pl.when(core == parity)
        def _():
            for device in range(value.shape[0] // rows):
                out = keep if device % 2 == parity else send
                out[device // 2, :, lanes] = value[device * rows : (device + 1) * rows, :].astype(bf16)


def cut_shapes(width, columns, chunk, index, rows):
    if not rows:
        spec = pl.BlockSpec((width, chunk), lambda j, *_: (0, index(j)))
        return [spec], [shape_of((width, columns), bf16)]
    blocks = width // rows // 2
    spec = pl.BlockSpec((blocks, rows, chunk), lambda j, *_: (0, 0, index(j)))
    return [spec] * 2, [shape_of((blocks, rows, columns), bf16)] * 2


def normalize(values):
    center = values - jnp.mean(values, -1, keepdims=True)
    scale = lax.rsqrt(jnp.mean(center * center, -1, keepdims=True) + 1e-05)
    return center * scale, scale


def norm_back(grad, gain, unit, scale):
    inner = grad * gain
    return scale * (
        inner
        - jnp.mean(inner, -1, keepdims=True)
        - unit * jnp.mean(inner * unit, -1, keepdims=True)
    )


def gelu_parts(u):
    phi = 0.5 + 0.5 * lax.erf(u * 0.7071067811865476)
    slope = phi + u * (0.3989422804014327 * jnp.exp2((u * u) * (-0.5 * LOG2E)))
    return u * phi, slope


def column_sum(values):
    return jnp.sum(values, 0, keepdims=True)


def accumulate(ref, value, first):
    @pl.when(first)
    def _():
        ref[...] = value

    @pl.when(jnp.logical_not(first))
    def _():
        ref[...] += value


def first_qkv_kernel(tokens, gain, shift, weight, bias, normed, joined):
    unit, _ = normalize(tokens[...].astype(f32))
    low = (unit * gain[...] + shift[...]).astype(bf16)
    normed[...] = low
    joined[...] = (dot(low, weight[...], NN) + bias[...]).astype(bf16)


def first_qkv(tokens, gain, shift, weight, bias, seq):
    rows, width = tokens.shape
    span = bias.shape[1]
    row = lambda w: pl.BlockSpec((seq, w), lambda i: (i, 0))
    return pl.pallas_call(
        first_qkv_kernel,
        grid=(rows // seq,),
        in_specs=[row(width), once((1, width)), once((1, width)), once((width, span)), once((1, span))],
        out_specs=[row(width), row(span)],
        out_shape=[shape_of((rows, width), bf16), shape_of((rows, span), bf16)],
        compiler_params=params(1),
        cost_estimate=cost(2 * rows * width * span, rows * (2 * width + span) * 2),
        name="first_qkv",
    )(tokens, gain, shift, weight, bias)


def next_qkv_kernel(normed, weight, bias, joined):
    span = bias.shape[1]
    joined[...] = (dot(normed[...], weight[:, :span], NN) + bias[...]).astype(bf16)


def next_qkv(normed, weight, bias, seq):
    rows, width = normed.shape
    span = bias.shape[1]
    return pl.pallas_call(
        next_qkv_kernel,
        grid=(rows // seq,),
        in_specs=[
            pl.BlockSpec((seq, width), lambda i: (i, 0)),
            once(weight.shape),
            once((1, span)),
        ],
        out_specs=pl.BlockSpec((seq, span), lambda i: (i, 0)),
        out_shape=shape_of((rows, span), bf16),
        compiler_params=params(1),
        cost_estimate=cost(2 * rows * width * span, rows * (width + span) * 2),
        name="next_qkv",
    )(normed, weight, bias)


def two_heads(block, padded):
    seq = block.shape[0]
    first = lax.broadcasted_iota(jnp.int32, block.shape, 1) < 64
    zero = jnp.zeros_like(block)
    pad = jnp.zeros((padded - seq, 128), block.dtype)
    return jnp.concatenate(
        [jnp.where(first, block, zero), pad, jnp.where(first, zero, block), pad], 0
    )


def attend_kernel(valid, joined, mixed, raised_out, inverse, *, tile, padded):
    seq = joined.shape[0]
    length = valid[pl.program_id(0)]
    keys = two_heads(joined[:, 128:256], padded)
    values = two_heads(joined[:, 256:], padded)
    row = lax.broadcasted_iota(jnp.int32, (2 * padded, 128), 0)
    lane = lax.broadcasted_iota(jnp.int32, (2 * padded, 128), 1)
    ones = jnp.where((row < padded) == (lane < 64), 1.0, 0.0).astype(bf16)
    values = jnp.concatenate([values, ones], 1)
    column = lax.broadcasted_iota(jnp.int32, (1, padded), 1)
    mask = jnp.where(column < length, 0.0, -1e30).astype(f32)
    for start in range(0, seq, tile):
        scores = dot(joined[start : start + tile, :128], keys, NT)
        halves = []
        for head in range(2):
            part = scores[:, head * padded : (head + 1) * padded] * (0.125 * LOG2E) + mask
            halves.append(jnp.exp2(part - jnp.max(part, 1, keepdims=True)).astype(bf16))
        raised = jnp.concatenate(halves, 1)
        raised_out[start : start + tile, :] = raised
        both = dot(raised, values, NN)
        scale = 1.0 / both[:, 128:]
        inverse[start : start + tile, :] = scale
        mixed[start : start + tile, :] = (both[:, :128] * scale).astype(bf16)


def attend(joined, valid, seq):
    rows, span = joined.shape
    pairs = span // 384
    items = rows // seq
    padded = -(-seq // 128) * 128
    tile = seq // 2 if seq % 32 == 0 else seq
    block = lambda w: pl.BlockSpec((seq, w), lambda i, h, valid: (i, h))
    return pl.pallas_call(
        functools.partial(attend_kernel, tile=tile, padded=padded),
        grid_spec=pltpu.PrefetchScalarGridSpec(
            num_scalar_prefetch=1,
            grid=(items, pairs),
            in_specs=[block(384)],
            out_specs=[
                block(128),
                pl.BlockSpec((None, None, seq, 2 * padded), lambda i, h, valid: (i, h, 0, 0)),
                block(128),
            ],
        ),
        out_shape=[
            shape_of((rows, span // 3), bf16),
            shape_of((items, pairs, seq, 2 * padded), bf16),
            shape_of((rows, span // 3), f32),
        ],
        compiler_params=params(2),
        cost_estimate=cost(
            items * pairs * seq * padded * 2 * 2 * 3 * 128,
            items * pairs * seq * 2 * padded * 2,
            items * pairs * seq * 2 * padded,
        ),
        name="attend",
    )(valid, joined)


def attend_back_kernel(
    where, joined, mixed_grad, mixed, raised, normed, *rest, tile, extra, cut
):
    if extra:
        mixed_a, mixed_b, low_grad, joined_grad, column, *outs, held, total, total_out = rest
    else:
        joined_grad, column, *outs, held, total = rest
    item, pair = pl.program_id(0), pl.program_id(1)
    seq = joined.shape[0]
    span = total.shape[1]
    padded = raised.shape[1] // 2
    base = pl.multiple_of(pair * 384, 384)
    keys = two_heads(joined[:, 128:256], padded)
    values = two_heads(joined[:, 256:], padded)
    first = lax.broadcasted_iota(jnp.int32, (tile, 128), 1) < 64
    for start in range(0, seq, tile):
        rows = slice(start, start + tile)
        grad = mixed_grad[rows, :]
        prob_grad = dot(grad, values, NT)
        product = grad.astype(f32) * mixed[rows, :].astype(f32)
        zero = jnp.zeros_like(product)
        halves = []
        for head in range(2):
            own = jnp.where(first, product, zero) if head == 0 else jnp.where(first, zero, product)
            centre = jnp.sum(own, 1, keepdims=True)
            lanes = slice(head * padded, (head + 1) * padded)
            halves.append((raised[rows, lanes].astype(f32) * (prob_grad[:, lanes] - centre)).astype(bf16))
        score_grad = jnp.concatenate(halves, 1)
        held[rows, :] = score_grad
        joined_grad[rows, pl.ds(base, 128)] = (dot(score_grad, keys, NN) * 0.125).astype(bf16)

    def own_half(both):
        return jnp.concatenate([both[:64, :padded], both[64:, padded:]], 0).T[:seq]

    joined_grad[:, pl.ds(base + 128, 128)] = (
        own_half(dot(joined[:, :128].T, held[...], NN)) * 0.125
    ).astype(bf16)
    joined_grad[:, pl.ds(base + 256, 128)] = own_half(
        dot(mixed_grad[...].T, raised[...], NN)
    ).astype(bf16)

    @pl.when(pair == pl.num_programs(1) - 1)
    def _():
        value = joined_grad[...]
        accumulate(total, dot(normed[...], value, TN), item == 0)
        accumulate(column, column_sum(value.astype(f32)), item == 0)
        if extra:
            both = [dot(mixed_a[...], low_grad[...], TN), dot(mixed_b[...], low_grad[...], TN)]
            accumulate(total_out, jnp.concatenate(both, 0), item == 0)

        @pl.when(item == pl.num_programs(0) - 1)
        def _():
            store_cut(where[0], outs, slice(0, span), total[...], cut)
            if extra:
                store_cut(where[0], outs, slice(span, span + total_out.shape[1]), total_out[...], cut)


def attend_back(mixed_grad, where, joined, mixed, raised, normed, seq, part, cut, others=()):
    rows, span = joined.shape
    width = normed.shape[1]
    items, pairs, _, keys = raised.shape
    tile = seq // 2 if seq % 32 == 0 else seq
    block = lambda w, off=0: pl.BlockSpec((seq, w), lambda i, h, *_: (i, h + off))
    row = lambda w: pl.BlockSpec((seq, w), lambda i, h, *_: (i, 0))
    columns = span + (width if others else 0)
    specs, shapes = cut_shapes(width, columns, columns, lambda j: 0, cut)
    return pl.pallas_call(
        functools.partial(attend_back_kernel, tile=tile, extra=bool(others), cut=cut),
        grid_spec=pltpu.PrefetchScalarGridSpec(
            num_scalar_prefetch=1,
            grid=(items, pairs),
            in_specs=[
                block(384),
                block(128, part * pairs),
                block(128),
                pl.BlockSpec((None, None, seq, keys), lambda i, h, *_: (i, h, 0, 0)),
                row(width),
            ]
            + [row(array.shape[1]) for array in others],
            out_specs=[row(span), pl.BlockSpec((1, span), lambda i, h, *_: (0, 0))] + specs,
            scratch_shapes=[pltpu.VMEM((seq, keys), bf16), pltpu.VMEM((width, span), f32)]
            + ([pltpu.VMEM((width, width), f32)] if others else []),
        ),
        out_shape=[shape_of((rows, span), bf16), shape_of((1, span), f32)] + shapes,
        compiler_params=params(2),
        cost_estimate=cost(),
        name="attend_back",
    )(where, joined, mixed_grad, mixed, raised, normed, *others)


def middle_kernel(tokens, mixed_a, mixed_b, weight, bias, gain, shift, middle, normed):
    width = tokens.shape[1]
    half = width // 2
    value = tokens[...].astype(f32) + bias[...]
    value = value + (
        dot(mixed_a[...], weight[:half, -width:], NN) + dot(mixed_b[...], weight[half:, -width:], NN)
    )
    middle[...] = value
    unit, _ = normalize(value)
    normed[...] = (unit * gain[...] + shift[...]).astype(bf16)


def middle_of(tokens, mixed_a, mixed_b, weight, bias, gain, shift, seq):
    rows, width = tokens.shape
    row = lambda w: pl.BlockSpec((seq, w), lambda i: (i, 0))
    one = once((1, width))
    return pl.pallas_call(
        middle_kernel,
        grid=(rows // seq,),
        in_specs=[row(width), row(width // 2), row(width // 2), once(weight.shape), one, one, one],
        out_specs=[row(width), row(width)],
        out_shape=[shape_of((rows, width), f32), shape_of((rows, width), bf16)],
        compiler_params=params(1),
        cost_estimate=cost(2 * rows * width * width, rows * width * 10),
        name="middle",
    )(tokens, mixed_a, mixed_b, weight, bias, gain, shift)


def mlp_kernel(
    valid, where, normed, cotangent, total_in, back_in, up, down, bias_up, bias_down,
    total_out, back_out, up_sum, *rest, seq, tile, first, last, cut,
):
    *outs, normed_all, grad_all, active, hidden_grad = rest
    step = pl.program_id(0)
    tiles = pl.num_programs(0) - 1
    width = normed.shape[1]

    @pl.when(step < tiles)
    def _():
        span = pl.ds(pl.multiple_of(step * tile, tile), tile)
        each = seq // tile
        place = lax.broadcasted_iota(jnp.int32, (tile, 1), 0) + lax.rem(step, each) * tile
        kept = place < valid[step // each]
        low_in = normed[...]
        grad = jnp.where(kept, cotangent[...].astype(f32), 0.0).astype(bf16)
        hidden = dot(low_in, up[...], NN) + bias_up[...]
        wide = dot(grad, down[...], NT)
        value, slope = gelu_parts(hidden)
        value = value.astype(bf16)
        low = (slope * wide).astype(bf16)
        normed_all[span, :] = low_in
        grad_all[span, :] = grad
        active[span, :] = value
        hidden_grad[span, :] = low
        accumulate(up_sum, column_sum(low.astype(f32)), step == 0)
        total = total_in[...] + dot(value, down[...], NN)
        if first:
            total = total + bias_down[...]
        if last:
            total = jnp.where(kept, total, 0.0)
        total_out[...] = total.astype(total_out.dtype)
        back = dot(low, up[...], NT)
        back_out[...] = back if first else back_in[...] + back

    @pl.when(step == tiles)
    def _():
        store_cut(where[0], outs, slice(0, width), dot(normed_all[...], hidden_grad[...], TN), cut)
        store_cut(where[0], outs, slice(width, 2 * width), dot(active[...], grad_all[...], TN), cut)


def mlp(back, valid, where, normed, cotangent, total, both, bias_up, bias_down, seq, place, last, cut):
    rows, width = normed.shape
    tile = seq // 2 if seq % 32 == 0 else seq
    tiles = rows // tile
    first = back is None
    if first:
        back = total
    row = lambda: pl.BlockSpec((tile, width), lambda j, *_: (jnp.minimum(j, tiles - 1), 0))
    fixed = pl.BlockSpec((tile, width), lambda j, *_: (0, 0))
    square = lambda at: pl.BlockSpec(
        (width, width), lambda j, *_: (0, at), pipeline_mode=pl.Buffered(buffer_count=1)
    )
    specs, shapes = cut_shapes(width, 2 * width, 2 * width, lambda j: 0, cut)
    return pl.pallas_call(
        functools.partial(mlp_kernel, seq=seq, tile=tile, first=first, last=last, cut=cut),
        grid_spec=pltpu.PrefetchScalarGridSpec(
            num_scalar_prefetch=2,
            grid=(tiles + 1,),
            in_specs=[
                row(), row(), row(), fixed if first else row(),
                square(2 * place), square(2 * place + 1), once((1, width)), once((1, width)),
            ],
            out_specs=[row(), row(), pl.BlockSpec((1, width), lambda j, *_: (0, 0))] + specs,
            scratch_shapes=[pltpu.VMEM((rows, width), bf16)] * 4,
        ),
        out_shape=[
            shape_of((rows, width), bf16 if last else f32),
            shape_of((rows, width), f32),
            shape_of((1, width), f32),
        ]
        + shapes,
        compiler_params=params(1),
        cost_estimate=cost(),
        name="mlp",
    )(valid, where, normed, cotangent, total, back, both, both, bias_up, bias_down)


def middle_back_kernel(
    valid, hidden_back, middle, cotangent, gain, weight, inv_a, inv_b,
    middle_grad, low_grad, mixed_grad, gain_sum, shift_sum, bias_sum, down_sum,
):
    item = pl.program_id(0)
    first = item == 0
    seq, width = middle.shape
    half = width // 2
    grad = hidden_back[...]
    unit, scale = normalize(middle[...])
    place = lax.broadcasted_iota(jnp.int32, (seq, 1), 0)
    kept = jnp.where(place < valid[item], cotangent[...].astype(f32), 0.0)
    accumulate(gain_sum, column_sum(grad * unit), first)
    accumulate(shift_sum, column_sum(grad), first)
    accumulate(down_sum, column_sum(kept), first)
    full = kept + norm_back(grad, gain[...], unit, scale)
    middle_grad[...] = full
    low = full.astype(bf16)
    low_grad[...] = low
    accumulate(bias_sum, column_sum(low.astype(f32)), first)
    back = dot(low, weight[:, -width:], NT)
    mixed_grad[:, :half] = (back[:, :half] * inv_a[...]).astype(bf16)
    mixed_grad[:, half:] = (back[:, half:] * inv_b[...]).astype(bf16)


def middle_back(hidden_back, valid, middle, cotangent, gain, weight, inv_a, inv_b, seq):
    rows, width = middle.shape
    row = lambda w: pl.BlockSpec((seq, w), lambda i, valid: (i, 0))
    fixed = lambda s: pl.BlockSpec(s, lambda i, valid: (0, 0))
    return pl.pallas_call(
        middle_back_kernel,
        grid_spec=pltpu.PrefetchScalarGridSpec(
            num_scalar_prefetch=1,
            grid=(rows // seq,),
            in_specs=[
                row(width), row(width), row(width), once((1, width)),
                once(weight.shape), row(width // 2), row(width // 2),
            ],
            out_specs=[row(width), row(width), row(width)] + [fixed((1, width))] * 4,
        ),
        out_shape=[
            shape_of((rows, width), f32),
            shape_of((rows, width), bf16),
            shape_of((rows, width), bf16),
        ]
        + [shape_of((1, width), f32)] * 4,
        compiler_params=params(1),
        cost_estimate=cost(2 * rows * width * width, rows * width * 26),
        name="middle_back",
    )(valid, hidden_back, middle, cotangent, gain, weight, inv_a, inv_b)


def input_back_kernel(grad_a, grad_b, weight_a, weight_b, tokens, middle_grad, gain, input_grad, gain_sum, shift_sum):
    first = pl.program_id(0) == 0
    span = grad_a.shape[1]
    grad = dot(grad_a[...], weight_a[:, :span], NT) + dot(grad_b[...], weight_b[:, :span], NT)
    unit, scale = normalize(tokens[...].astype(f32))
    accumulate(gain_sum, column_sum(grad * unit), first)
    accumulate(shift_sum, column_sum(grad), first)
    full = middle_grad[...] + norm_back(grad, gain[...], unit, scale)
    input_grad[...] = full.astype(bf16)


def input_back(grad_a, grad_b, weight_a, weight_b, tokens, middle_grad, gain, seq):
    rows, width = tokens.shape
    row = lambda w: pl.BlockSpec((seq, w), lambda i: (i, 0))
    fixed = pl.BlockSpec((1, width), lambda i: (0, 0))
    return pl.pallas_call(
        input_back_kernel,
        grid=(rows // seq,),
        in_specs=[row(grad_a.shape[1]), row(grad_b.shape[1]), once(weight_a.shape), once(weight_b.shape)]
        + [row(width), row(width), once((1, width))],
        out_specs=[row(width), fixed, fixed],
        out_shape=[shape_of((rows, width), bf16)] + [shape_of((1, width), f32)] * 2,
        compiler_params=params(1),
        cost_estimate=cost(2 * rows * width * 3 * width, rows * width * 14),
        name="input_back",
    )(grad_a, grad_b, weight_a, weight_b, tokens, middle_grad, gain)


def local(mesh, tokens, cotangent, group, text_len, qkv_w, out_w, mlp_in, mlp_out, gains, biases):
    items, seq, width = tokens.shape
    rows = items * seq
    count = mesh.size
    share = width // count
    wide = mlp_in.shape[0] // share
    chunks = wide // width
    half = width // 2
    span = 3 * half
    valid = (PATCH_SMALL + (PATCH_LARGE - PATCH_SMALL) * group + text_len).astype(jnp.int32)
    flat = tokens.reshape(rows, width)
    cot = cotangent.reshape(rows, width)
    flights = Flights()
    me = lax.axis_index(AXES)
    core, outer, others = bit_groups(mesh)
    where = jnp.stack([position(me, core), position(me, outer), position(me, others[0])]).astype(jnp.int32)
    cut = share if cut_by_core(mesh) and share % 8 == 0 else 0

    def sums(arrays, lengths):
        if cut:
            keeps, sends = zip(*arrays)
            return flights.add(fast_sum_steps(keeps, sends, where, mesh), lengths)
        whole = jnp.concatenate([array for (array,) in arrays], 1)
        return flights.add(sum_steps(whole, mesh, bf16), lengths)


    def by_pairs(matrix, part):
        pieces = []
        for pair in range(part * 3, part * 3 + 3):
            for place in range(3):
                at = place * width + pair * 128
                pieces.append(matrix[:, at : at + 128])
        return jnp.concatenate(pieces, 1)

    own_up = mlp_in.reshape(share, count, chunks, share).transpose(0, 2, 1, 3).reshape(share, chunks, width)
    own_down = mlp_out.reshape(chunks, share, width).transpose(1, 0, 2)
    own_both = jnp.concatenate([own_up, own_down], 2).reshape(share, 2 * wide)

    own_qkv = qkv_w.reshape(share, 3 * width)
    small = jnp.concatenate([gains, biases])
    small_rows = -(-small.shape[0] // 128)
    padded = jnp.pad(small, (0, small_rows * 128 - small.shape[0])).reshape(small_rows, 128)
    padded = jnp.pad(padded, ((0, share - small_rows), (0, 0)))
    job = flights.add(gather_steps(jnp.concatenate([by_pairs(own_qkv, 0), padded], 1), mesh), [])
    flights.finish(len(others))
    own_both = flights.behind(own_both)
    early = chunks // 2 * 2 * width
    both = [
        lax.all_gather(part, AXES, axis=0, tiled=True)
        for part in (own_both[:, :early], own_both[:, early:])
    ]
    flights.finish()
    first = job["result"]
    own_second = jnp.concatenate([by_pairs(own_qkv, 1), out_w.reshape(share, width)], 1)
    second_job = flights.add(gather_steps(own_second, mesh), [1, 1, 1])

    small = first[:, span:].reshape(count, share, 128)[:, :small_rows]
    small = small.reshape(count, small_rows * 128).astype(f32)
    edge = gains.shape[0]
    gain = small[:, :edge].reshape(1, 2 * width)
    bias = small[:, edge : edge + biases.shape[0]].reshape(1, 6 * width + wide)
    gain_one, gain_two = gain[:, :width], gain[:, width:]
    bias_query, bias_value, bias_output, shift_one, shift_two, bias_down = (
        bias[:, p * width : (p + 1) * width] for p in range(6)
    )
    bias_up = bias[:, 6 * width :].reshape(count, chunks, share).transpose(1, 0, 2).reshape(1, wide)
    bias_joined = jnp.concatenate([bias_query, jnp.zeros_like(bias_query), bias_value], 1)
    bias_parts = [by_pairs(bias_joined, part) for part in range(2)]

    normed, joined_a = flights.run(
        lambda x: first_qkv(x, gain_one, shift_one, first, bias_parts[0], seq), flat
    )
    mixed_a, raised_a, inv_a = flights.run(lambda x: attend(x, valid, seq), joined_a)
    flights.finish()
    second = second_job["result"]
    joined_b = next_qkv(normed, second, bias_parts[1], seq)
    mixed_b, raised_b, inv_b = attend(joined_b, valid, seq)
    middle, normed_two = middle_of(
        flat, mixed_a, mixed_b, second, bias_output, gain_two, shift_two, seq
    )

    total, back, up_sums, mlp_jobs, grads = middle, None, [], [], []
    for chunk in range(chunks):
        place = chunk if chunk < chunks // 2 else chunk - chunks // 2
        lanes = slice(chunk * width, (chunk + 1) * width)
        total, back, up_sum, *outs = flights.run(
            lambda x: mlp(
                back, valid, where, x, cot, total, both[chunk >= chunks // 2], bias_up[:, lanes],
                bias_down, seq, place, chunk == chunks - 1, cut,
            ),
            normed_two,
        )
        up_sums.append(up_sum)
        grads.append(outs)
        if chunk in (chunks // 2 - 1, chunks - 1):
            mlp_jobs.append(sums(grads, [1, 1, 1]))
            grads = []
    block_out, hidden_back = total, back
    up_sum = jnp.concatenate(up_sums, 1)

    middle_grad, low_grad, mixed_grad, gain_two_sum, shift_two_sum, bias_out_sum, down_sum = flights.run(
        lambda x: middle_back(x, valid, middle, cot, gain_two, second, inv_a, inv_b, seq), hidden_back
    )
    joined_grad_a, qkv_sum_a, *grads_a = flights.run(
        lambda x: attend_back(
            x, where, joined_a, mixed_a, raised_a, normed, seq, 0, cut, (mixed_a, mixed_b, low_grad)
        ),
        mixed_grad,
    )
    sum_a = sums([grads_a], [1, 1, 1])
    joined_grad_b, qkv_sum_b, *grads_b = flights.run(
        lambda x: attend_back(x, where, joined_b, mixed_b, raised_b, normed, seq, 1, cut), mixed_grad
    )
    sum_b = sums([grads_b], [1, 1, 1])
    input_grad, gain_one_sum, shift_one_sum = flights.run(
        lambda x: input_back(joined_grad_a, x, first, second, flat, middle_grad, gain_one, seq),
        joined_grad_b,
    )

    def by_kind(part_a, part_b):
        return jnp.concatenate(
            [
                piece[:, (3 * pair + place) * 128 : (3 * pair + place + 1) * 128]
                for place in range(3)
                for piece in (part_a, part_b)
                for pair in range(3)
            ],
            1,
        )

    joined_sums = by_kind(qkv_sum_a, qkv_sum_b)
    up_sum = up_sum.reshape(chunks, count, share).transpose(1, 0, 2).reshape(1, wide)
    gain_sums = jnp.concatenate([gain_one_sum, gain_two_sum], 1).reshape(count, edge)
    bias_sums = jnp.concatenate(
        [
            joined_sums[:, :width],
            joined_sums[:, 2 * width :],
            bias_out_sum,
            shift_one_sum,
            shift_two_sum,
            down_sum,
            up_sum,
        ],
        1,
    ).reshape(count, biases.shape[0])
    small_job = flights.add(small_sum_steps(jnp.concatenate([gain_sums, bias_sums], 1), mesh), [])
    flights.finish()
    small_total = small_job["result"]
    mlp_total = jnp.concatenate([job["result"] for job in mlp_jobs], 1).reshape(share, chunks, 2, width)
    up_total = mlp_total[:, :, 0].reshape(share, chunks, count, share).transpose(0, 2, 1, 3)
    down_total = mlp_total[:, :, 1].transpose(1, 0, 2)
    total_a, total_b = sum_a["result"], sum_b["result"]
    return (
        block_out.reshape(tokens.shape),
        input_grad.reshape(tokens.shape),
        by_kind(total_a, total_b).reshape(-1),
        total_a[:, span:].reshape(-1),
        up_total.reshape(-1),
        down_total.reshape(-1),
        small_total[:edge],
        small_total[edge:],
    )


def solution(mesh):
    split = P(AXES)
    whole = P(AXES, None, None)
    return jax.shard_map(
        functools.partial(local, mesh),
        mesh=mesh,
        in_specs=(whole, whole) + (split,) * 8,
        out_specs=(whole, whole) + (split,) * 6,
        check_vma=False,
    )
```

time: 1190 us -> 421 us (0.35)
  waiting for transfers between devices: 429 us -> 23.5 us
  matrix products: 345 us -> 0 us
  Pallas kernels: 0 us -> 282 us
  local copies, waits for them, and re-layouts: 235 us -> 30.7 us
  blocking collectives: 83.5 us -> 0 us
  other arithmetic: 68.7 us -> 5.08 us
  starting transfers between devices: 0.19 us -> 58.6 us
    unnamed x6 -> x2, waiting for transfers between devices: 371 us -> 0.03 us
    dot_general x54 -> x0, matrix products: 345 us -> none  [the longest x1 63.1 us: local(): jnp.dot(normed_two_low, w_up, preferred_element_type=jnp.float32) + bias_up]
    pallas_call x0 -> x21, Pallas kernels: none -> 282 us  [the longest x4 102 us: mlp(): pl.pallas_call(functools.partial(mlp_kernel, seq=seq, tile=tile, first=fi...]
    reshape x20 -> x19, local copies, waits for them, and re-layouts: 146 us -> 10.3 us  [the longest x2 3.18 us: local(): mlp_in.reshape(share, count, chunks, share).transpose(0, 2, 1, 3)]
    unnamed x2 -> x0, blocking collectives: 83.5 us -> none
    ppermute x0 -> x51, starting transfers between devices: none -> 58.2 us  [depart(): came = [lax.ppermute(array, AXES, pairs) for array, pairs in sends]]
    all_gather x4 -> x2, waiting for transfers between devices: 57.8 us -> 0.01 us  [local(): lax.all_gather(part, AXES, axis=0, tiled=True)]
    reduce_sum x14 -> x0, other arithmetic: 35.1 us -> none  [the longest x6 12.4 us: attend(): row_total = jnp.sum(raised, -1, keepdims=True)]
  transfers between devices with their start and end apart: 5 -> 53, of which waited for: 2 -> 11; matrix products, arithmetic and copies ran while one was open for 24% -> 5% of each run, Pallas kernels for 0% -> 63%
where the time goes in v1:
time: 421 us; the launch traced here: 415 us
  Pallas kernels  282 us (67%)
  starting transfers between devices  58.6 us (14%)
  local copies, waits for them, and re-layouts  30.7 us (7%)
  waiting for transfers between devices  23.5 us (6%)
  between operations  15.6 us (4%)
  other arithmetic  5.08 us (1%)
    pallas_call x4, Pallas kernels, mlp(): pl.pallas_call(functools.partial(mlp_kernel, seq=seq, tile=tile, first=fi...  102 us
    pallas_call x2, Pallas kernels, attend_back(): pl.pallas_call(functools.partial(attend_back_kernel, tile=tile, extra=boo...  60.4 us
    ppermute x51, starting transfers between devices, depart(): came = [lax.ppermute(array, AXES, pairs) for array, pairs in sends]  58.2 us
    pallas_call x2, Pallas kernels, attend(): pl.pallas_call(functools.partial(attend_kernel, tile=tile, padded=padded)...  31.3 us
    ppermute x51, waiting for transfers between devices, depart(): came = [lax.ppermute(array, AXES, pairs) for array, pairs in sends]  23.4 us
    pallas_call x4, Pallas kernels, plane_sum(): pl.pallas_call(functools.partial(plane_sum_kernel, parts=len(keeps)), gri...  18.8 us
    pallas_call x1, Pallas kernels, input_back(): pl.pallas_call(input_back_kernel, grid=(rows // seq,), in_specs=[row(grad...  16.4 us
    pallas_call x1, Pallas kernels, middle_back(): pl.pallas_call(middle_back_kernel, grid_spec=pltpu.PrefetchScalarGridSpec...  15.9 us
  transfers between devices with their start and end apart: 53, of which 11 were waited for; matrix products, arithmetic and copies ran while one was open for 5% of the time, Pallas kernels for 63%

profile of v1, /device:TPU:0, one launch (start us, length us, event | category | flops | bytes accessed | tf_op | source)
XLA Modules:
  0.0 415.4 jit_solution(13287945420504811430)
XLA Ops:
  9.2 3.1 collective-permute-start
  12.3 2.6 collective-permute-start.1
  14.9 2.0 reshape.208
  17.0 1.2 reshape.209
  18.6 2.3 collective-permute-done.2
  22.1 1.6 collective-permute-start.3
  23.6 1.5 collective-permute-start.4
  25.7 5.1 %collective-permute-done.3 = bf16[1,4,1,24,1280]{4,3,2,1,0:T(8,128)(2,1)S(1)} collective-permute-done((bf16[1,4,1,24,1280]{4,3,2,1,0:T(8,128)(2,1)S(1)}, bf16[1,4,1,24,1280]{4,3,2,1,0:T(8,128)(2,1)S(1)}, u32[]{:S(2)}, u32[]{:S(2)}) %collective-permute-start.3) | collective-permute-done | bytes 245792 | tf_op jit(solution)/shard_map/ppermute | solution.py:69
  30.8 3.9 collective-permute-done.4
  35.9 2.1 collective-permute-start.8
  38.0 2.3 collective-permute-start.9
  40.6 1.3 constant_dynamic-update-slice_fusion.79
  44.5 8.6 %first_qkv.1 = (bf16[1824,768]{1,0:T(8,128)(2,1)}, bf16[1824,1152]{1,0:T(8,128)(2,1)}) custom-call(bf16[1824,768]{1,0:T(8,128)(2,1)} %bitcast.79, f32[1,768]{1,0:T(1,128)} %get-tuple-element.453.gain, f32[1,768]{1,0:T(1,128)} %get-tuple-element.429.shift, bf16[768,1280]{1,0:T(8,128)(2,1)} %bitcast.83, f32[1,1152]{1,0:T(1,128)} %copy-done.25), custom_call_target="tpu_custom_call" | custom-call | flops 1 | bytes 1 | tf_op jit(solution)/shard_map/first_qkv/pallas_call | solution.py:387
  54.9 1.5 collective-permute-start.10
  57.0 1.5 collective-permute-start.12
  59.0 15.7 %attend.2 = (bf16[1824,384]{1,0:T(8,128)(2,1)}, bf16[3,3,608,1280]{3,2,1,0:T(8,128)(2,1)}, f32[1824,384]{1,0:T(8,128)}) custom-call(s32[3]{0:T(128)} %add_add_fusion.4.valid, bf16[1824,1152]{1,0:T(8,128)(2,1)} %get-tuple-element.222.joined), custom_call_target="tpu_custom_call" | custom-call | flops 1 | bytes 1 | tf_op jit(solution)/shard_map/attend/pallas_call | solution.py:465
  74.8 2.2 collective-permute-done.12
  77.7 2.8 collective-permute-done.13
  80.7 1.6 copy-done
  82.3 7.8 %next_qkv.1.joined = bf16[1824,1152]{1,0:T(8,128)(2,1)} custom-call(bf16[1824,768]{1,0:T(8,128)(2,1)} %get-tuple-element.230.normed, bf16[768,1920]{1,0:T(8,128)(2,1)} %bitcast.70, f32[1,1152]{1,0:T(1,128)} %copy-done.24), custom_call_target="tpu_custom_call" | custom-call | flops 1 | bytes 1 | tf_op jit(solution)/shard_map/next_qkv/pallas_call | solution.py:407
  90.6 15.7 %attend.3 = (bf16[1824,384]{1,0:T(8,128)(2,1)}, bf16[3,3,608,1280]{3,2,1,0:T(8,128)(2,1)}, f32[1824,384]{1,0:T(8,128)}) custom-call(s32[3]{0:T(128)} %add_add_fusion.4.valid, bf16[1824,1152]{1,0:T(8,128)(2,1)} %next_qkv.1.joined), custom_call_target="tpu_custom_call" | custom-call | flops 1 | bytes 1 | tf_op jit(solution)/shard_map/attend/pallas_call | solution.py:465
  106.3 9.0 %middle.1 = (f32[1824,768]{1,0:T(8,128)}, bf16[1824,768]{1,0:T(8,128)(2,1)}) custom-call(bf16[1824,768]{1,0:T(8,128)(2,1)} %bitcast.80, bf16[1824,384]{1,0:T(8,128)(2,1)} %get-tuple-element.229.mixed_a.mixed.rest_0_, bf16[1824,384]{1,0:T(8,128)(2,1)} %get-tuple-element.234.mixed_b.rest_1_.mixed, bf16[768,1920]{1,0:T(8,128)(2,1)} %bitcast.71, ...), custom_call_target="tpu_custom_call" | custom-call | flops 1 | bytes 1 | tf_op jit(solution)/shard_map/middle/pallas_call | solution.py:598
  115.3 25.6 %mlp.4 = (f32[1824,768]{1,0:T(8,128)}, f32[1824,768]{1,0:T(8,128)}, f32[1,768]{1,0:T(1,128)}, bf16[16,24,1536]{2,1,0:T(8,128)(2,1)}, bf16[16,24,1536]{2,1,0:T(8,128)(2,1)}) custom-call(s32[3]{0:T(128)} %add_add_fusion.4.valid, s32[3]{0:T(128)} %pad_add_fusion.where, bf16[1824,768]{1,0:T(8,128)(2,1)} %get-tuple-element.259.normed, ...), custom_call_target="tpu_custom_call" | custom-call | flops 1 | bytes 1 | tf_op jit(solution)/shard_map/mlp/pallas_call | solution.py:665
  140.9 25.6 %mlp.5 = (f32[1824,768]{1,0:T(8,128)}, f32[1824,768]{1,0:T(8,128)}, f32[1,768]{1,0:T(1,128)}, bf16[16,24,1536]{2,1,0:T(8,128)(2,1)}, bf16[16,24,1536]{2,1,0:T(8,128)(2,1)}) custom-call(s32[3]{0:T(128)} %add_add_fusion.4.valid, s32[3]{0:T(128)} %pad_add_fusion.where, bf16[1824,768]{1,0:T(8,128)(2,1)} %get-tuple-element.259.normed, ...), custom_call_target="tpu_custom_call" | custom-call | flops 1 | bytes 1 | tf_op jit(solution)/shard_map/mlp/pallas_call | solution.py:665
  167.1 25.6 %mlp.6 = (f32[1824,768]{1,0:T(8,128)}, f32[1824,768]{1,0:T(8,128)}, f32[1,768]{1,0:T(1,128)}, bf16[16,24,1536]{2,1,0:T(8,128)(2,1)}, bf16[16,24,1536]{2,1,0:T(8,128)(2,1)}) custom-call(s32[3]{0:T(128)} %add_add_fusion.4.valid, s32[3]{0:T(128)} %pad_add_fusion.where, bf16[1824,768]{1,0:T(8,128)(2,1)} %get-tuple-element.259.normed, ...), custom_call_target="tpu_custom_call" | custom-call | flops 1 | bytes 1 | tf_op jit(solution)/shard_map/mlp/pallas_call | solution.py:665
  194.1 5.0 %plane_sum.4 = (bf16[4,24,3072]{2,1,0:T(8,128)(2,1)}, bf16[4,24,3072]{2,1,0:T(8,128)(2,1)}, bf16[4,24,3072]{2,1,0:T(8,128)(2,1)}, bf16[4,24,3072]{2,1,0:T(8,128)(2,1)}) custom-call(s32[3]{0:T(128)} %pad_add_fusion.where, bf16[4,4,24,1536]{3,2,1,0:T(8,128)(2,1)} %bitcast.93, bf16[4,4,24,1536]{3,2,1,0:T(8,128)(2,1)} %bitcast.94, ...), custom_call_target="tpu_custom_call" | custom-call | flops 1 | bytes 1 | tf_op jit(solution)/shard_map/plane_sum/pallas_call | solution.py:244
  199.1 2.8 collective-permute-start.17
  202.6 24.8 %mlp.7 = (bf16[1824,768]{1,0:T(8,128)(2,1)}, f32[1824,768]{1,0:T(8,128)}, f32[1,768]{1,0:T(1,128)}, bf16[16,24,1536]{2,1,0:T(8,128)(2,1)}, bf16[16,24,1536]{2,1,0:T(8,128)(2,1)}) custom-call(s32[3]{0:T(128)} %add_add_fusion.4.valid, s32[3]{0:T(128)} %pad_add_fusion.where, bf16[1824,768]{1,0:T(8,128)(2,1)} %get-tuple-element.259.normed, ...), custom_call_target="tpu_custom_call" | custom-call | flops 1 | bytes 1 | tf_op jit(solution)/shard_map/mlp/pallas_call | solution.py:665
  229.3 3.3 line_sum.4
  233.1 1.9 collective-permute-start.20
  235.0 2.5 collective-permute-start.21
  237.5 15.9 %middle_back.1 = (f32[1824,768]{1,0:T(8,128)}, bf16[1824,768]{1,0:T(8,128)(2,1)}, bf16[1824,768]{1,0:T(8,128)(2,1)}, f32[1,768]{1,0:T(1,128)}, f32[1,768]{1,0:T(...) custom-call(s32[3]{0:T(128)} %add_add_fusion.4.valid, f32[1824,768]{1,0:T(8,128)} %get-tuple-element.281.hidden_back, ...), custom_call_target="tpu_custom_call" | custom-call | flops 1 | bytes 1 | tf_op jit(solution)/shard_map/middle_back/pallas_call | solution.py:718
  254.9 5.0 %plane_sum.5 = (bf16[4,24,3072]{2,1,0:T(8,128)(2,1)}, bf16[4,24,3072]{2,1,0:T(8,128)(2,1)}, bf16[4,24,3072]{2,1,0:T(8,128)(2,1)}, bf16[4,24,3072]{2,1,0:T(8,128)(2,1)}) custom-call(s32[3]{0:T(128)} %pad_add_fusion.where, bf16[4,4,24,1536]{3,2,1,0:T(8,128)(2,1)} %bitcast.89, bf16[4,4,24,1536]{3,2,1,0:T(8,128)(2,1)} %bitcast.90, ...), custom_call_target="tpu_custom_call" | custom-call | flops 1 | bytes 1 | tf_op jit(solution)/shard_map/plane_sum/pallas_call | solution.py:244
  259.9 1.2 collective-permute-start.24
  262.2 1.2 collective-permute-start.26
  263.4 32.9 %attend_back.2 = (bf16[1824,1152]{1,0:T(8,128)(2,1)}, f32[1,1152]{1,0:T(1,128)}, bf16[16,24,1920]{2,1,0:T(8,128)(2,1)}, bf16[16,24,1920]{2,1,0:T(8,128)(2,1)}) custom-call(s32[3]{0:T(128)} %pad_add_fusion.where, bf16[1824,1152]{1,0:T(8,128)(2,1)} %get-tuple-element.222.joined, bf16[1824,768]{1,0:T(8,128)(2,1)} %get-tuple-element.323.mixed_grad, ...), custom_call_target="tpu_custom_call" | custom-call | flops 1 | bytes 1 | tf_op jit(solution)/shard_map/attend_back/pallas_call | solution.py:558
  297.5 3.3 line_sum.5
  301.3 1.9 collective-permute-start.28
  303.2 2.5 collective-permute-start.29
  305.7 27.6 %attend_back.3 = (bf16[1824,1152]{1,0:T(8,128)(2,1)}, f32[1,1152]{1,0:T(1,128)}, bf16[16,24,1152]{2,1,0:T(8,128)(2,1)}, bf16[16,24,1152]{2,1,0:T(8,128)(2,1)}) custom-call(s32[3]{0:T(128)} %pad_add_fusion.where, bf16[1824,1152]{1,0:T(8,128)(2,1)} %next_qkv.1.joined, bf16[1824,768]{1,0:T(8,128)(2,1)} %get-tuple-element.323.mixed_grad, ...), custom_call_target="tpu_custom_call" | custom-call | flops 1 | bytes 1 | tf_op jit(solution)/shard_map/attend_back/pallas_call | solution.py:558
  334.5 4.5 %plane_sum.6 = (bf16[4,24,1920]{2,1,0:T(8,128)(2,1)}, bf16[4,24,1920]{2,1,0:T(8,128)(2,1)}, bf16[4,24,1920]{2,1,0:T(8,128)(2,1)}, bf16[4,24,1920]{2,1,0:T(8,128)(2,1)}) custom-call(s32[3]{0:T(128)} %pad_add_fusion.where, bf16[4,4,24,1920]{3,2,1,0:T(8,128)(2,1)} %bitcast.87, bf16[4,4,24,1920]{3,2,1,0:T(8,128)(2,1)} %bitcast.88), custom_call_target="tpu_custom_call" | custom-call | flops 1 | bytes 1 | tf_op jit(solution)/shard_map/plane_sum/pallas_call | solution.py:244
  339.0 1.3 collective-permute-start.31
  341.4 1.2 collective-permute-start.33
  342.8 16.4 %input_back.1 = (bf16[1824,768]{1,0:T(8,128)(2,1)}, f32[1,768]{1,0:T(1,128)}, f32[1,768]{1,0:T(1,128)}) custom-call(bf16[1824,1152]{1,0:T(8,128)(2,1)} %get-tuple-element.314.grad_a, bf16[1824,1152]{1,0:T(8,128)(2,1)} %get-tuple-element.340.grad_b, bf16[768,1280]{1,0:T(8,128)(2,1)} %bitcast.84, bf16[768,1920]{1,0:T(8,128)(2,1)} %bitcast.73, ...), custom_call_target="tpu_custom_call" | custom-call | flops 1 | bytes 1 | tf_op jit(solution)/shard_map/input_back/pallas_call | solution.py:756
  361.3 2.8 line_sum.6
  364.7 4.2 %plane_sum.7 = (bf16[4,24,1152]{2,1,0:T(8,128)(2,1)}, bf16[4,24,1152]{2,1,0:T(8,128)(2,1)}, bf16[4,24,1152]{2,1,0:T(8,128)(2,1)}, bf16[4,24,1152]{2,1,0:T(8,128)(2,1)}) custom-call(s32[3]{0:T(128)} %pad_add_fusion.where, bf16[4,4,24,1152]{3,2,1,0:T(8,128)(2,1)} %bitcast.99, bf16[4,4,24,1152]{3,2,1,0:T(8,128)(2,1)} %bitcast.100), custom_call_target="tpu_custom_call" | custom-call | flops 1 | bytes 1 | tf_op jit(solution)/shard_map/plane_sum/pallas_call | solution.py:244
  368.9 1.2 collective-permute-start.38
  370.2 1.1 collective-permute-start.39
  371.3 1.1 collective-permute-start.40
  372.4 2.0 collective-permute-start.36
  374.4 2.4 collective-permute-start.37
  378.5 1.2 copy.24
  379.8 2.5 reshape.233
  383.3 1.3 collective-permute-start.45
  384.6 1.1 collective-permute-start.46
  385.7 1.1 collective-permute-start.47
  386.9 2.7 line_sum.7
  389.6 1.6 collective-permute-start.42
  392.6 2.5 collective-permute-start.44
  395.7 1.2 collective-permute-done.43
  396.9 1.9 collective-permute-done.44
  398.9 2.9 collective-permute-start.49
  401.9 1.4 collective-permute-start.50
  405.1 2.1 collective-permute-done.50
  (283 shorter events, 33.9 us)
Async XLA Ops:
  7.2 108.1 %all-gather.3.cloned.1.call-start = ((), (), s32[]{:S(2)}) async-start(), calls=%async_computation | async-start | bytes 4866048 | tf_op jit(solution)/shard_map/all_gather | solution.py:817
  9.2 9.3 %collective-permute-start = (bf16[1,1,24,1280]{3,2,1,0:T(8,128)(2,1)S(1)}, bf16[1,1,24,1280]{3,2,1,0:T(8,128)(2,1)S(1)}, u32[]{:S(2)}, u32[]{:S(2)}) collective-permute-start(bf16[1,1,24,1280]{3,2,1,0:T(8,128)(2,1)S(1)} %bitcast.111), channel_id=1, source_target_pairs={{0,2},{1,3},{2,0},{3,1},{4,6},{5,7},{6,4},{7,5},{8,10},{9,11},{10,... | collective-permute-start | bytes 184328 | tf_op jit(solution)/shard_map/ppermute | solution.py:69
  12.3 6.3 %collective-permute-start.1 = (bf16[1,1,24,1280]{3,2,1,0:T(8,128)(2,1)S(1)}, bf16[1,1,24,1280]{3,2,1,0:T(8,128)(2,1)S(1)}, u32[]{:S(2)}, u32[]{:S(2)}) collective-permute-start(bf16[1,1,24,1280]{3,2,1,0:T(8,128)(2,1)S(1)} %bitcast.112), channel_id=1, source_target_pairs={{0,4},{1,5},{2,6},{3,7},{4,0},{5,1},{6,2},{7,3},{8,12},{9,13},{10,... | collective-permute-start | bytes 184328 | tf_op jit(solution)/shard_map/ppermute | solution.py:69
  14.9 6.0 %collective-permute-start.2 = (bf16[1,1,24,1280]{3,2,1,0:T(8,128)(2,1)S(1)}, bf16[1,1,24,1280]{3,2,1,0:T(8,128)(2,1)S(1)}, u32[]{:S(2)}, u32[]{:S(2)}) collective-permute-start(bf16[1,1,24,1280]{3,2,1,0:T(8,128)(2,1)S(1)} %bitcast.113), channel_id=1, source_target_pairs={{0,6},{1,7},{2,4},{3,5},{4,2},{5,3},{6,0},{7,1},{8,14},{9,15},{10,... | collective-permute-start | bytes 184328 | tf_op jit(solution)/shard_map/ppermute | solution.py:69
  20.9 14.8 %copy-start.23 = (bf16[18432]{0:T(1024)(128)(2,1)S(1)}, bf16[18432]{0:T(1024)(128)(2,1)}, u32[]{:S(2)}) copy-start(bf16[18432]{0:T(1024)(128)(2,1)} %param.15) | copy-start | bytes 110596
  21.7 145.4 %all-gather.5.cloned.1.call-start = ((), (), s32[]{:S(2)}) async-start(), calls=%async_computation.1 | async-start | bytes 4866048 | tf_op jit(solution)/shard_map/all_gather | solution.py:817
  22.1 8.8 %collective-permute-start.3 = (bf16[1,4,1,24,1280]{4,3,2,1,0:T(8,128)(2,1)S(1)}, bf16[1,4,1,24,1280]{4,3,2,1,0:T(8,128)(2,1)S(1)}, u32[]{:S(2)}, u32[]{:S(2)}) collective-permute-start(bf16[1,4,1,24,1280]{4,3,2,1,0:T(8,128)(2,1)S(1)} %bitcast_dynamic-update-slice_fusion.4), channel_id=1, source_target_pairs={{0,8},{1,9},{2,10},{3,11},{4,12},{5,13},{6,14},{7,15},{8,0},{9,1},... | collective-permute-start | bytes 737288 | tf_op jit(solution)/shard_map/ppermute | solution.py:69
  23.6 11.2 %collective-permute-start.4 = (bf16[1,4,1,24,1280]{4,3,2,1,0:T(8,128)(2,1)S(1)}, bf16[1,4,1,24,1280]{4,3,2,1,0:T(8,128)(2,1)S(1)}, u32[]{:S(2)}, u32[]{:S(2)}) collective-permute-start(bf16[1,4,1,24,1280]{4,3,2,1,0:T(8,128)(2,1)S(1)} %bitcast_dynamic-update-slice_fusion.4), channel_id=1, source_target_pairs={{0,16},{1,17},{2,18},{3,19},{4,20},{5,21},{6,22},{7,23},{8,24},{9,... | collective-permute-start | bytes 737288 | tf_op jit(solution)/shard_map/ppermute | solution.py:69
  25.1 10.4 %collective-permute-start.5 = (bf16[1,4,1,24,1280]{4,3,2,1,0:T(8,128)(2,1)S(1)}, bf16[1,4,1,24,1280]{4,3,2,1,0:T(8,128)(2,1)S(1)}, u32[]{:S(2)}, u32[]{:S(2)}) collective-permute-start(bf16[1,4,1,24,1280]{4,3,2,1,0:T(8,128)(2,1)S(1)} %bitcast_dynamic-update-slice_fusion.4), channel_id=1, source_target_pairs={{0,24},{1,25},{2,26},{3,27},{4,28},{5,29},{6,30},{7,31},{8,16},{9,... | collective-permute-start | bytes 737288 | tf_op jit(solution)/shard_map/ppermute | solution.py:69
  35.6 5.0 %collective-permute-start.6 = (bf16[4,4,1,24,1280]{4,3,2,1,0:T(8,128)(2,1)S(1)}, bf16[4,4,1,24,1280]{4,3,2,1,0:T(8,128)(2,1)}, u32[]{:S(2)}, u32[]{:S(2)}) collective-permute-start(bf16[4,4,1,24,1280]{4,3,2,1,0:T(8,128)(2,1)S(1)} %constant_dynamic-update-slice_fusion.81), channel_id=1, source_target_pairs={{0,1},{1,0},{2,3},{3,2},{4,5},{5,4},{6,7},{7,6},{8,9},{9,8},{10,11... | collective-permute-start | bytes 2949128 | tf_op jit(solution)/shard_map/ppermute | solution.py:69
  35.8 17.2 %collective-permute-start.7 = (bf16[1,1,24,1920]{3,2,1,0:T(8,128)(2,1)S(1)}, bf16[1,1,24,1920]{3,2,1,0:T(8,128)(2,1)S(1)}, u32[]{:S(2)}, u32[]{:S(2)}) collective-permute-start(bf16[1,1,24,1920]{3,2,1,0:T(8,128)(2,1)S(1)} %bitcast.108), channel_id=1, source_target_pairs={{0,2},{1,3},{2,0},{3,1},{4,6},{5,7},{6,4},{7,5},{8,10},{9,11},{10,... | collective-permute-start | bytes 276488 | tf_op jit(solution)/shard_map/ppermute | solution.py:69
  35.9 17.2 %collective-permute-start.8 = (bf16[1,1,24,1920]{3,2,1,0:T(8,128)(2,1)S(1)}, bf16[1,1,24,1920]{3,2,1,0:T(8,128)(2,1)}, u32[]{:S(2)}, u32[]{:S(2)}) collective-permute-start(bf16[1,1,24,1920]{3,2,1,0:T(8,128)(2,1)S(1)} %bitcast.109), channel_id=1, source_target_pairs={{0,4},{1,5},{2,6},{3,7},{4,0},{5,1},{6,2},{7,3},{8,12},{9,13},{10,... | collective-permute-start | bytes 276488 | tf_op jit(solution)/shard_map/ppermute | solution.py:69
  38.0 15.1 %collective-permute-start.9 = (bf16[1,1,24,1920]{3,2,1,0:T(8,128)(2,1)S(1)}, bf16[1,1,24,1920]{3,2,1,0:T(8,128)(2,1)}, u32[]{:S(2)}, u32[]{:S(2)}) collective-permute-start(bf16[1,1,24,1920]{3,2,1,0:T(8,128)(2,1)S(1)} %bitcast.110), channel_id=1, source_target_pairs={{0,6},{1,7},{2,4},{3,5},{4,2},{5,3},{6,0},{7,1},{8,14},{9,15},{10,... | collective-permute-start | bytes 276488 | tf_op jit(solution)/shard_map/ppermute | solution.py:69
  44.5 14.0 %copy-start.37 = (s32[3]{0:T(128)S(1)}, s32[3]{0:T(128)}, u32[]{:S(2)}) copy-start(s32[3]{0:T(128)} %param.13) | copy-start | bytes 40
  44.5 14.0 %copy-start.38 = (s32[3]{0:T(128)S(1)}, s32[3]{0:T(128)}, u32[]{:S(2)}) copy-start(s32[3]{0:T(128)} %param.12) | copy-start | bytes 40
  54.9 19.9 %collective-permute-start.10 = (bf16[1,4,1,24,1920]{4,3,2,1,0:T(8,128)(2,1)S(1)}, bf16[1,4,1,24,1920]{4,3,2,1,0:T(8,128)(2,1)S(1)}, u32[]{:S(2)}, u32[]{:S(2)}) collective-permute-start(bf16[1,4,1,24,1920]{4,3,2,1,0:T(8,128)(2,1)S(1)} %bitcast_dynamic-update-slice_fusion), channel_id=1, source_target_pairs={{0,8},{1,9},{2,10},{3,11},{4,12},{5,13},{6,14},{7,15},{8,0},{9,1},... | collective-permute-start | bytes 1105928 | tf_op jit(solution)/shard_map/ppermute | solution.py:69
  56.4 18.4 %collective-permute-start.11 = (bf16[1,4,1,24,1920]{4,3,2,1,0:T(8,128)(2,1)S(1)}, bf16[1,4,1,24,1920]{4,3,2,1,0:T(8,128)(2,1)S(1)}, u32[]{:S(2)}, u32[]{:S(2)}) collective-permute-start(bf16[1,4,1,24,1920]{4,3,2,1,0:T(8,128)(2,1)S(1)} %bitcast_dynamic-update-slice_fusion), channel_id=1, source_target_pairs={{0,16},{1,17},{2,18},{3,19},{4,20},{5,21},{6,22},{7,23},{8,24},{9,... | collective-permute-start | bytes 1105928 | tf_op jit(solution)/shard_map/ppermute | solution.py:69
  57.0 20.1 %collective-permute-start.12 = (bf16[1,4,1,24,1920]{4,3,2,1,0:T(8,128)(2,1)S(1)}, bf16[1,4,1,24,1920]{4,3,2,1,0:T(8,128)(2,1)S(1)}, u32[]{:S(2)}, u32[]{:S(2)}) collective-permute-start(bf16[1,4,1,24,1920]{4,3,2,1,0:T(8,128)(2,1)S(1)} %bitcast_dynamic-update-slice_fusion), channel_id=1, source_target_pairs={{0,24},{1,25},{2,26},{3,27},{4,28},{5,29},{6,30},{7,31},{8,16},{9,... | collective-permute-start | bytes 1105928 | tf_op jit(solution)/shard_map/ppermute | solution.py:69
  77.2 3.3 collective-permute-start.13
  140.9 25.6 %copy-start.34 = (bf16[16,24,1536]{2,1,0:T(8,128)(2,1)S(1)}, bf16[16,24,1536]{2,1,0:T(8,128)(2,1)}, u32[]{:S(2)}) copy-start(bf16[16,24,1536]{2,1,0:T(8,128)(2,1)} %get-tuple-element.252) | copy-start | bytes 3538948
  166.5 26.2 %collective-permute-start.14 = (bf16[16,24,1536]{2,1,0:T(8,128)(2,1)S(1)}, bf16[16,24,1536]{2,1,0:T(8,128)(2,1)S(1)}, u32[]{:S(2)}, u32[]{:S(2)}) collective-permute-start(bf16[16,24,1536]{2,1,0:T(8,128)(2,1)S(1)} %copy-done.34), channel_id=1, source_target_pairs={{0,1},{1,0},{2,3},{3,2},{4,5},{5,4},{6,7},{7,6},{8,9},{9,8},{10,11... | collective-permute-start | bytes 3538952 | tf_op jit(solution)/shard_map/ppermute | solution.py:69
  166.8 26.0 %collective-permute-start.15 = (bf16[16,24,1536]{2,1,0:T(8,128)(2,1)}, bf16[16,24,1536]{2,1,0:T(8,128)(2,1)S(1)}, u32[]{:S(2)}, u32[]{:S(2)}) collective-permute-start(bf16[16,24,1536]{2,1,0:T(8,128)(2,1)} %get-tuple-element.253), channel_id=1, source_target_pairs={{0,1},{1,0},{2,3},{3,2},{4,5},{5,4},{6,7},{7,6},{8,9},{9,8},{10,11... | collective-permute-start | bytes 3538952 | tf_op jit(solution)/shard_map/ppermute | solution.py:69
  199.1 28.3 %collective-permute-start.16 = (bf16[4,24,3072]{2,1,0:T(8,128)(2,1)}, bf16[4,24,3072]{2,1,0:T(8,128)(2,1)S(1)}, u32[]{:S(2)}, u32[]{:S(2)}) collective-permute-start(bf16[4,24,3072]{2,1,0:T(8,128)(2,1)} %get-tuple-element.267), channel_id=1, source_target_pairs={{0,8},{1,9},{2,10},{3,11},{4,12},{5,13},{6,14},{7,15},{8,0},{9,1},... | collective-permute-start | bytes 1769480 | tf_op jit(solution)/shard_map/ppermute | solution.py:69
  199.1 29.1 %collective-permute-start.17 = (bf16[4,24,3072]{2,1,0:T(8,128)(2,1)}, bf16[4,24,3072]{2,1,0:T(8,128)(2,1)S(1)}, u32[]{:S(2)}, u32[]{:S(2)}) collective-permute-start(bf16[4,24,3072]{2,1,0:T(8,128)(2,1)} %get-tuple-element.268), channel_id=1, source_target_pairs={{0,16},{1,17},{2,18},{3,19},{4,20},{5,21},{6,22},{7,23},{8,24},{9,... | collective-permute-start | bytes 1769480 | tf_op jit(solution)/shard_map/ppermute | solution.py:69
  202.0 26.3 %collective-permute-start.18 = (bf16[4,24,3072]{2,1,0:T(8,128)(2,1)}, bf16[4,24,3072]{2,1,0:T(8,128)(2,1)S(1)}, u32[]{:S(2)}, u32[]{:S(2)}) collective-permute-start(bf16[4,24,3072]{2,1,0:T(8,128)(2,1)} %get-tuple-element.269), channel_id=1, source_target_pairs={{0,24},{1,25},{2,26},{3,27},{4,28},{5,29},{6,30},{7,31},{8,16},{9,... | collective-permute-start | bytes 1769480 | tf_op jit(solution)/shard_map/ppermute | solution.py:69
  232.6 20.9 %collective-permute-start.22 = (bf16[16,24,1536]{2,1,0:T(8,128)(2,1)}, bf16[16,24,1536]{2,1,0:T(8,128)(2,1)S(1)}, u32[]{:S(2)}, u32[]{:S(2)}) collective-permute-start(bf16[16,24,1536]{2,1,0:T(8,128)(2,1)} %get-tuple-element.294), channel_id=1, source_target_pairs={{0,1},{1,0},{2,3},{3,2},{4,5},{5,4},{6,7},{7,6},{8,9},{9,8},{10,11... | collective-permute-start | bytes 3538952 | tf_op jit(solution)/shard_map/ppermute | solution.py:69
  232.6 20.9 %collective-permute-start.23 = (bf16[16,24,1536]{2,1,0:T(8,128)(2,1)}, bf16[16,24,1536]{2,1,0:T(8,128)(2,1)S(1)}, u32[]{:S(2)}, u32[]{:S(2)}) collective-permute-start(bf16[16,24,1536]{2,1,0:T(8,128)(2,1)} %get-tuple-element.295), channel_id=1, source_target_pairs={{0,1},{1,0},{2,3},{3,2},{4,5},{5,4},{6,7},{7,6},{8,9},{9,8},{10,11... | collective-permute-start | bytes 3538952 | tf_op jit(solution)/shard_map/ppermute | solution.py:69
  233.1 20.3 %collective-permute-start.19 = (bf16[24,3072]{1,0:T(8,128)(2,1)}, bf16[24,3072]{1,0:T(8,128)(2,1)S(1)}, u32[]{:S(2)}, u32[]{:S(2)}) collective-permute-start(bf16[24,3072]{1,0:T(8,128)(2,1)} %get-tuple-element.291), channel_id=1, source_target_pairs={{0,2},{1,3},{2,0},{3,1},{4,6},{5,7},{6,4},{7,5},{8,10},{9,11},{10,... | collective-permute-start | bytes 442376 | tf_op jit(solution)/shard_map/ppermute | solution.py:69
  233.1 20.3 %collective-permute-start.20 = (bf16[24,3072]{1,0:T(8,128)(2,1)}, bf16[24,3072]{1,0:T(8,128)(2,1)S(1)}, u32[]{:S(2)}, u32[]{:S(2)}) collective-permute-start(bf16[24,3072]{1,0:T(8,128)(2,1)} %get-tuple-element.292), channel_id=1, source_target_pairs={{0,4},{1,5},{2,6},{3,7},{4,0},{5,1},{6,2},{7,3},{8,12},{9,13},{10,... | collective-permute-start | bytes 442376 | tf_op jit(solution)/shard_map/ppermute | solution.py:69
  235.0 18.4 %collective-permute-start.21 = (bf16[24,3072]{1,0:T(8,128)(2,1)}, bf16[24,3072]{1,0:T(8,128)(2,1)S(1)}, u32[]{:S(2)}, u32[]{:S(2)}) collective-permute-start(bf16[24,3072]{1,0:T(8,128)(2,1)} %get-tuple-element.293), channel_id=1, source_target_pairs={{0,6},{1,7},{2,4},{3,5},{4,2},{5,3},{6,0},{7,1},{8,14},{9,15},{10,... | collective-permute-start | bytes 442376 | tf_op jit(solution)/shard_map/ppermute | solution.py:69
  259.9 36.4 %collective-permute-start.24 = (bf16[4,24,3072]{2,1,0:T(8,128)(2,1)}, bf16[4,24,3072]{2,1,0:T(8,128)(2,1)S(1)}, u32[]{:S(2)}, u32[]{:S(2)}) collective-permute-start(bf16[4,24,3072]{2,1,0:T(8,128)(2,1)} %get-tuple-element.311), channel_id=1, source_target_pairs={{0,8},{1,9},{2,10},{3,11},{4,12},{5,13},{6,14},{7,15},{8,0},{9,1},... | collective-permute-start | bytes 1769480 | tf_op jit(solution)/shard_map/ppermute | solution.py:69
  261.1 35.2 %collective-permute-start.25 = (bf16[4,24,3072]{2,1,0:T(8,128)(2,1)}, bf16[4,24,3072]{2,1,0:T(8,128)(2,1)S(1)}, u32[]{:S(2)}, u32[]{:S(2)}) collective-permute-start(bf16[4,24,3072]{2,1,0:T(8,128)(2,1)} %get-tuple-element.312), channel_id=1, source_target_pairs={{0,16},{1,17},{2,18},{3,19},{4,20},{5,21},{6,22},{7,23},{8,24},{9,... | collective-permute-start | bytes 1769480 | tf_op jit(solution)/shard_map/ppermute | solution.py:69
  262.2 34.2 %collective-permute-start.26 = (bf16[4,24,3072]{2,1,0:T(8,128)(2,1)}, bf16[4,24,3072]{2,1,0:T(8,128)(2,1)S(1)}, u32[]{:S(2)}, u32[]{:S(2)}) collective-permute-start(bf16[4,24,3072]{2,1,0:T(8,128)(2,1)} %get-tuple-element.313), channel_id=1, source_target_pairs={{0,24},{1,25},{2,26},{3,27},{4,28},{5,29},{6,30},{7,31},{8,16},{9,... | collective-permute-start | bytes 1769480 | tf_op jit(solution)/shard_map/ppermute | solution.py:69
  300.8 32.5 %collective-permute-start.30 = (bf16[16,24,1920]{2,1,0:T(8,128)(2,1)}, bf16[16,24,1920]{2,1,0:T(8,128)(2,1)S(1)}, u32[]{:S(2)}, u32[]{:S(2)}) collective-permute-start(bf16[16,24,1920]{2,1,0:T(8,128)(2,1)} %get-tuple-element.332), channel_id=1, source_target_pairs={{0,1},{1,0},{2,3},{3,2},{4,5},{5,4},{6,7},{7,6},{8,9},{9,8},{10,11... | collective-permute-start | bytes 4423688 | tf_op jit(solution)/shard_map/ppermute | solution.py:69
  301.3 32.1 %collective-permute-start.27 = (bf16[24,3072]{1,0:T(8,128)(2,1)}, bf16[24,3072]{1,0:T(8,128)(2,1)S(1)}, u32[]{:S(2)}, u32[]{:S(2)}) collective-permute-start(bf16[24,3072]{1,0:T(8,128)(2,1)} %get-tuple-element.329), channel_id=1, source_target_pairs={{0,2},{1,3},{2,0},{3,1},{4,6},{5,7},{6,4},{7,5},{8,10},{9,11},{10,... | collective-permute-start | bytes 442376 | tf_op jit(solution)/shard_map/ppermute | solution.py:69
  301.3 32.0 %collective-permute-start.28 = (bf16[24,3072]{1,0:T(8,128)(2,1)}, bf16[24,3072]{1,0:T(8,128)(2,1)S(1)}, u32[]{:S(2)}, u32[]{:S(2)}) collective-permute-start(bf16[24,3072]{1,0:T(8,128)(2,1)} %get-tuple-element.330), channel_id=1, source_target_pairs={{0,4},{1,5},{2,6},{3,7},{4,0},{5,1},{6,2},{7,3},{8,12},{9,13},{10,... | collective-permute-start | bytes 442376 | tf_op jit(solution)/shard_map/ppermute | solution.py:69
  303.2 30.1 %collective-permute-start.29 = (bf16[24,3072]{1,0:T(8,128)(2,1)}, bf16[24,3072]{1,0:T(8,128)(2,1)S(1)}, u32[]{:S(2)}, u32[]{:S(2)}) collective-permute-start(bf16[24,3072]{1,0:T(8,128)(2,1)} %get-tuple-element.331), channel_id=1, source_target_pairs={{0,6},{1,7},{2,4},{3,5},{4,2},{5,3},{6,0},{7,1},{8,14},{9,15},{10,... | collective-permute-start | bytes 442376 | tf_op jit(solution)/shard_map/ppermute | solution.py:69
  305.7 27.6 %copy-start.35 = (f32[1,1152]{1,0:T(1,128)S(1)}, f32[1,1152]{1,0:T(1,128)}, u32[]{:S(2)}) copy-start(f32[1,1152]{1,0:T(1,128)} %get-tuple-element.365) | copy-start | bytes 13828
  339.0 20.3 %collective-permute-start.34 = (bf16[16,24,1152]{2,1,0:T(8,128)(2,1)}, bf16[16,24,1152]{2,1,0:T(8,128)(2,1)S(1)}, u32[]{:S(2)}, u32[]{:S(2)}) collective-permute-start(bf16[16,24,1152]{2,1,0:T(8,128)(2,1)} %get-tuple-element.348), channel_id=1, source_target_pairs={{0,1},{1,0},{2,3},{3,2},{4,5},{5,4},{6,7},{7,6},{8,9},{9,8},{10,11... | collective-permute-start | bytes 2654216 | tf_op jit(solution)/shard_map/ppermute | solution.py:69
  339.0 20.2 %collective-permute-start.31 = (bf16[4,24,1920]{2,1,0:T(8,128)(2,1)}, bf16[4,24,1920]{2,1,0:T(8,128)(2,1)S(1)}, u32[]{:S(2)}, u32[]{:S(2)}) collective-permute-start(bf16[4,24,1920]{2,1,0:T(8,128)(2,1)} %get-tuple-element.345), channel_id=1, source_target_pairs={{0,8},{1,9},{2,10},{3,11},{4,12},{5,13},{6,14},{7,15},{8,0},{9,1},... | collective-permute-start | bytes 1105928 | tf_op jit(solution)/shard_map/ppermute | solution.py:69
  340.3 19.0 %collective-permute-start.32 = (bf16[4,24,1920]{2,1,0:T(8,128)(2,1)}, bf16[4,24,1920]{2,1,0:T(8,128)(2,1)S(1)}, u32[]{:S(2)}, u32[]{:S(2)}) collective-permute-start(bf16[4,24,1920]{2,1,0:T(8,128)(2,1)} %get-tuple-element.346), channel_id=1, source_target_pairs={{0,16},{1,17},{2,18},{3,19},{4,20},{5,21},{6,22},{7,23},{8,24},{9,... | collective-permute-start | bytes 1105928 | tf_op jit(solution)/shard_map/ppermute | solution.py:69
  341.4 18.0 %collective-permute-start.33 = (bf16[4,24,1920]{2,1,0:T(8,128)(2,1)}, bf16[4,24,1920]{2,1,0:T(8,128)(2,1)S(1)}, u32[]{:S(2)}, u32[]{:S(2)}) collective-permute-start(bf16[4,24,1920]{2,1,0:T(8,128)(2,1)} %get-tuple-element.347), channel_id=1, source_target_pairs={{0,24},{1,25},{2,26},{3,27},{4,28},{5,29},{6,30},{7,31},{8,16},{9,... | collective-permute-start | bytes 1105928 | tf_op jit(solution)/shard_map/ppermute | solution.py:69
  342.7 16.5 %copy-start.33 = (f32[1,768]{1,0:T(1,128)S(1)}, f32[1,768]{1,0:T(1,128)}, u32[]{:S(2)}) copy-start(f32[1,768]{1,0:T(1,128)} %get-tuple-element.367) | copy-start | bytes 9220
  342.7 16.6 %copy-start.26 = (f32[1,768]{1,0:T(1,128)S(1)}, f32[1,768]{1,0:T(1,128)}, u32[]{:S(2)}) copy-start(f32[1,768]{1,0:T(1,128)} %get-tuple-element.364) | copy-start | bytes 9220
  342.7 18.1 %copy-start.32 = (f32[1,768]{1,0:T(1,128)S(1)}, f32[1,768]{1,0:T(1,128)}, u32[]{:S(2)}) copy-start(f32[1,768]{1,0:T(1,128)} %get-tuple-element.369) | copy-start | bytes 9220
  342.8 18.1 %copy-start.31 = (f32[1,768]{1,0:T(1,128)S(1)}, f32[1,768]{1,0:T(1,128)}, u32[]{:S(2)}) copy-start(f32[1,768]{1,0:T(1,128)} %get-tuple-element.370) | copy-start | bytes 9220
  361.2 11.2 %collective-permute-start.41 = (f32[4,4,1,288]{3,2,1,0:T(1,128)S(1)}, f32[4,4,1,288]{3,2,1,0:T(1,128)S(1)}, u32[]{:S(2)}, u32[]{:S(2)}) collective-permute-start(f32[4,4,1,288]{3,2,1,0:T(1,128)S(1)} %fusion.2), channel_id=1, source_target_pairs={{0,1},{1,0},{2,3},{3,2},{4,5},{5,4},{6,7},{7,6},{8,9},{9,8},{10,11... | collective-permute-start | bytes 55304 | tf_op jit(solution)/shard_map/ppermute | solution.py:69
  364.2 10.3 %collective-permute-start.35 = (bf16[24,1920]{1,0:T(8,128)(2,1)}, bf16[24,1920]{1,0:T(8,128)(2,1)S(1)}, u32[]{:S(2)}, u32[]{:S(2)}) collective-permute-start(bf16[24,1920]{1,0:T(8,128)(2,1)} %get-tuple-element.355), channel_id=1, source_target_pairs={{0,2},{1,3},{2,0},{3,1},{4,6},{5,7},{6,4},{7,5},{8,10},{9,11},{10,... | collective-permute-start | bytes 276488 | tf_op jit(solution)/shard_map/ppermute | solution.py:69
  368.9 14.2 %collective-permute-start.38 = (bf16[4,24,1152]{2,1,0:T(8,128)(2,1)}, bf16[4,24,1152]{2,1,0:T(8,128)(2,1)}, u32[]{:S(2)}, u32[]{:S(2)}) collective-permute-start(bf16[4,24,1152]{2,1,0:T(8,128)(2,1)} %get-tuple-element.360), channel_id=1, source_target_pairs={{0,8},{1,9},{2,10},{3,11},{4,12},{5,13},{6,14},{7,15},{8,0},{9,1},... | collective-permute-start | bytes 663560 | tf_op jit(solution)/shard_map/ppermute | solution.py:69
  370.2 13.0 %collective-permute-start.39 = (bf16[4,24,1152]{2,1,0:T(8,128)(2,1)}, bf16[4,24,1152]{2,1,0:T(8,128)(2,1)}, u32[]{:S(2)}, u32[]{:S(2)}) collective-permute-start(bf16[4,24,1152]{2,1,0:T(8,128)(2,1)} %get-tuple-element.361), channel_id=1, source_target_pairs={{0,16},{1,17},{2,18},{3,19},{4,20},{5,21},{6,22},{7,23},{8,24},{9,... | collective-permute-start | bytes 663560 | tf_op jit(solution)/shard_map/ppermute | solution.py:69
  371.3 11.9 %collective-permute-start.40 = (bf16[4,24,1152]{2,1,0:T(8,128)(2,1)}, bf16[4,24,1152]{2,1,0:T(8,128)(2,1)}, u32[]{:S(2)}, u32[]{:S(2)}) collective-permute-start(bf16[4,24,1152]{2,1,0:T(8,128)(2,1)} %get-tuple-element.362), channel_id=1, source_target_pairs={{0,24},{1,25},{2,26},{3,27},{4,28},{5,29},{6,30},{7,31},{8,16},{9,... | collective-permute-start | bytes 663560 | tf_op jit(solution)/shard_map/ppermute | solution.py:69
  372.4 10.7 %collective-permute-start.36 = (bf16[24,1920]{1,0:T(8,128)(2,1)}, bf16[24,1920]{1,0:T(8,128)(2,1)}, u32[]{:S(2)}, u32[]{:S(2)}) collective-permute-start(bf16[24,1920]{1,0:T(8,128)(2,1)} %get-tuple-element.356), channel_id=1, source_target_pairs={{0,4},{1,5},{2,6},{3,7},{4,0},{5,1},{6,2},{7,3},{8,12},{9,13},{10,... | collective-permute-start | bytes 276488 | tf_op jit(solution)/shard_map/ppermute | solution.py:69
  374.4 8.7 %collective-permute-start.37 = (bf16[24,1920]{1,0:T(8,128)(2,1)}, bf16[24,1920]{1,0:T(8,128)(2,1)}, u32[]{:S(2)}, u32[]{:S(2)}) collective-permute-start(bf16[24,1920]{1,0:T(8,128)(2,1)} %get-tuple-element.357), channel_id=1, source_target_pairs={{0,6},{1,7},{2,4},{3,5},{4,2},{5,3},{6,0},{7,1},{8,14},{9,15},{10,... | collective-permute-start | bytes 276488 | tf_op jit(solution)/shard_map/ppermute | solution.py:69
  379.8 11.8 %copy-start.19 = (f32[24,1920]{1,0:T(8,128)S(1)}, f32[24,1920]{1,0:T(8,128)}, u32[]{:S(2)}) copy-start(f32[24,1920]{1,0:T(8,128)} %get-tuple-element.354) | copy-start | bytes 552964
  379.8 11.8 %copy-start.22 = (bf16[24,1920]{1,0:T(8,128)(2,1)S(1)}, bf16[24,1920]{1,0:T(8,128)(2,1)}, u32[]{:S(2)}) copy-start(bf16[24,1920]{1,0:T(8,128)(2,1)} %copy-done.21) | copy-start | bytes 276484
  383.3 9.3 %collective-permute-start.45 = (f32[1,4,1,288]{3,2,1,0:T(1,128)S(1)}, f32[1,4,1,288]{3,2,1,0:T(1,128)S(1)}, u32[]{:S(2)}, u32[]{:S(2)}) collective-permute-start(f32[1,4,1,288]{3,2,1,0:T(1,128)S(1)} %get-tuple-element.444), channel_id=1, source_target_pairs={{0,8},{1,9},{2,10},{3,11},{4,12},{5,13},{6,14},{7,15},{8,0},{9,1},... | collective-permute-start | bytes 13832 | tf_op jit(solution)/shard_map/ppermute | solution.py:69
  384.6 11.1 %collective-permute-start.46 = (f32[1,4,1,288]{3,2,1,0:T(1,128)S(1)}, f32[1,4,1,288]{3,2,1,0:T(1,128)S(1)}, u32[]{:S(2)}, u32[]{:S(2)}) collective-permute-start(f32[1,4,1,288]{3,2,1,0:T(1,128)S(1)} %get-tuple-element.443), channel_id=1, source_target_pairs={{0,16},{1,17},{2,18},{3,19},{4,20},{5,21},{6,22},{7,23},{8,24},{9,... | collective-permute-start | bytes 13832 | tf_op jit(solution)/shard_map/ppermute | solution.py:69
  385.7 10.0 %collective-permute-start.47 = (f32[1,4,1,288]{3,2,1,0:T(1,128)S(1)}, f32[1,4,1,288]{3,2,1,0:T(1,128)S(1)}, u32[]{:S(2)}, u32[]{:S(2)}) collective-permute-start(f32[1,4,1,288]{3,2,1,0:T(1,128)S(1)} %get-tuple-element.442), channel_id=1, source_target_pairs={{0,24},{1,25},{2,26},{3,27},{4,28},{5,29},{6,30},{7,31},{8,16},{9,... | collective-permute-start | bytes 13832 | tf_op jit(solution)/shard_map/ppermute | solution.py:69
  389.6 6.1 %collective-permute-start.42 = (bf16[24,1152]{1,0:T(8,128)(2,1)}, bf16[24,1152]{1,0:T(8,128)(2,1)S(1)}, u32[]{:S(2)}, u32[]{:S(2)}) collective-permute-start(bf16[24,1152]{1,0:T(8,128)(2,1)} %get-tuple-element.383), channel_id=1, source_target_pairs={{0,2},{1,3},{2,0},{3,1},{4,6},{5,7},{6,4},{7,5},{8,10},{9,11},{10,... | collective-permute-start | bytes 165896 | tf_op jit(solution)/shard_map/ppermute | solution.py:69
  391.2 5.7 %collective-permute-start.43 = (bf16[24,1152]{1,0:T(8,128)(2,1)}, bf16[24,1152]{1,0:T(8,128)(2,1)S(1)}, u32[]{:S(2)}, u32[]{:S(2)}) collective-permute-start(bf16[24,1152]{1,0:T(8,128)(2,1)} %get-tuple-element.384), channel_id=1, source_target_pairs={{0,4},{1,5},{2,6},{3,7},{4,0},{5,1},{6,2},{7,3},{8,12},{9,13},{10,... | collective-permute-start | bytes 165896 | tf_op jit(solution)/shard_map/ppermute | solution.py:69
  392.6 6.2 %collective-permute-start.44 = (bf16[24,1152]{1,0:T(8,128)(2,1)}, bf16[24,1152]{1,0:T(8,128)(2,1)S(1)}, u32[]{:S(2)}, u32[]{:S(2)}) collective-permute-start(bf16[24,1152]{1,0:T(8,128)(2,1)} %get-tuple-element.385), channel_id=1, source_target_pairs={{0,6},{1,7},{2,4},{3,5},{4,2},{5,3},{6,0},{7,1},{8,14},{9,15},{10,... | collective-permute-start | bytes 165896 | tf_op jit(solution)/shard_map/ppermute | solution.py:69
  398.9 6.3 %collective-permute-start.48 = (f32[1,1,1,288]{3,2,1,0:T(1,128)S(1)}, f32[1,1,1,288]{3,2,1,0:T(1,128)S(1)}, u32[]{:S(2)}, u32[]{:S(2)}) collective-permute-start(f32[1,1,1,288]{3,2,1,0:T(1,128)S(1)} %get-tuple-element.451), channel_id=1, source_target_pairs={{0,2},{1,3},{2,0},{3,1},{4,6},{5,7},{6,4},{7,5},{8,10},{9,11},{10,... | collective-permute-start | bytes 3464 | tf_op jit(solution)/shard_map/ppermute | solution.py:69
  398.9 6.2 %collective-permute-start.49 = (f32[1,1,1,288]{3,2,1,0:T(1,128)S(1)}, f32[1,1,1,288]{3,2,1,0:T(1,128)S(1)}, u32[]{:S(2)}, u32[]{:S(2)}) collective-permute-start(f32[1,1,1,288]{3,2,1,0:T(1,128)S(1)} %get-tuple-element.450), channel_id=1, source_target_pairs={{0,4},{1,5},{2,6},{3,7},{4,0},{5,1},{6,2},{7,3},{8,12},{9,13},{10,... | collective-permute-start | bytes 3464 | tf_op jit(solution)/shard_map/ppermute | solution.py:69
  401.9 5.4 %collective-permute-start.50 = (f32[1,1,1,288]{3,2,1,0:T(1,128)S(1)}, f32[1,1,1,288]{3,2,1,0:T(1,128)S(1)}, u32[]{:S(2)}, u32[]{:S(2)}) collective-permute-start(f32[1,1,1,288]{3,2,1,0:T(1,128)S(1)} %get-tuple-element.449), channel_id=1, source_target_pairs={{0,6},{1,7},{2,4},{3,5},{4,2},{5,3},{6,0},{7,1},{8,14},{9,15},{10,... | collective-permute-start | bytes 3464 | tf_op jit(solution)/shard_map/ppermute | solution.py:69
  (28 other events, 93.3 us)
Sparse Core Ops, SparseCore 0:
  21.8 69.6 all-gather.2
  95.1 61.8 all-gather.4

commit v2 on v1

v2 whole, which is shorter than its diff:
```python
import functools
import math

import jax
import jax.numpy as jnp
from jax import lax
from jax.experimental import pallas as pl
from jax.experimental.pallas import tpu as pltpu
from jax.sharding import PartitionSpec as P

HEADS = 12
PATCH_SMALL = 196
PATCH_LARGE = 576
AXES = ("dp", "fsdp")
bf16 = jnp.bfloat16
f32 = jnp.float32
NN = (((1,), (0,)), ((), ()))
NT = (((1,), (1,)), ((), ()))
TN = (((0,), (0,)), ((), ()))
VMEM_LIMIT = 60 * 2**20
TILE = 304
ATILE = 304
AHEAD = 1
MTILE = 304
MAHEAD = 1
LTILE = 608
LSUB = 304
BOT = 304
BTILE = 304
BAHEAD = 1
LOG2E = 1.4426950408889634


def dot(a, b, dims):
    return lax.dot_general(a, b, dims, preferred_element_type=f32)


def params(n):
    return pltpu.CompilerParams(
        vmem_limit_bytes=VMEM_LIMIT, dimension_semantics=("arbitrary",) * n
    )


def cost(*_):
    return pl.CostEstimate(flops=1, bytes_accessed=1, transcendentals=0)


def tile_of(seq):
    return TILE if seq % TILE == 0 else seq


def once(shape):
    return pl.BlockSpec(
        shape, lambda *_: (0,) * len(shape), pipeline_mode=pl.Buffered(buffer_count=1)
    )


def shape_of(shape, dtype):
    return jax.ShapeDtypeStruct(shape, dtype)


class Flights:
    def __init__(self):
        self.waiting = []
        self.flying = []

    def add(self, steps, lengths):
        job = {"steps": steps, "lengths": list(lengths), "result": None}
        self.advance(job, None)
        return job

    def advance(self, job, came):
        try:
            sends = job["steps"].send(came) if came is not None else next(job["steps"])
        except StopIteration as stop:
            job["result"] = stop.value
            return
        length = job["lengths"].pop(0) if job["lengths"] else 1
        self.waiting.append((job, sends, length))

    def depart(self):
        for job, sends, length in self.waiting:
            came = [lax.ppermute(array, AXES, pairs) for array, pairs in sends]
            self.flying.append([job, came, length])
        self.waiting = []

    def run(self, kernel, operand, *others):
        arrays = [array for _, sends, _ in self.waiting for array, _ in sends]
        if arrays:
            operand, arrays = lax.optimization_barrier((operand, arrays))
            left = iter(arrays)
            self.waiting = [
                (job, [(next(left), pairs) for _, pairs in sends], length)
                for job, sends, length in self.waiting
            ]
        self.depart()
        out = kernel(operand, *others)
        for flight in self.flying:
            flight[2] -= 1
        landed = [flight for flight in self.flying if flight[2] <= 0]
        self.flying = [flight for flight in self.flying if flight[2] > 0]
        if landed:
            out, came = lax.optimization_barrier((out, [flight[1] for flight in landed]))
            for flight, got in zip(landed, came):
                self.advance(flight[0], got)
        return out

    def behind(self, value):
        value, _ = lax.optimization_barrier((value, [array for _, sends, _ in self.waiting for array, _ in sends]))
        return value

    def land(self):
        held, self.flying = self.flying, []
        self.finish(1)
        self.flying += held

    def finish(self, turns=1 << 30):
        while (self.waiting or self.flying) and turns > 0:
            turns -= 1
            self.depart()
            landed, self.flying = self.flying, []
            cames = lax.optimization_barrier([flight[1] for flight in landed])
            for flight, came in zip(landed, cames):
                self.advance(flight[0], came)


def bit_groups(mesh):
    inner = int(math.log2(mesh.shape["fsdp"]))
    outer = int(math.log2(mesh.shape["dp"]))
    rest = [list(range(b, min(b + 2, inner))) for b in range(1, inner, 2)]
    return [0], list(range(inner, inner + outer)), rest


def position(me, bits):
    spot = 0
    for place, bit in enumerate(bits):
        spot = spot + ((me >> bit) & 1) * (1 << place)
    return spot


def partners(count, bits):
    swaps = []
    for step in range(1, 1 << len(bits)):
        mask = 0
        for place, bit in enumerate(bits):
            if (step >> place) & 1:
                mask |= 1 << bit
        swaps.append((step, [(i, i ^ mask) for i in range(count)]))
    return swaps


def gather_steps(shard, mesh, groups):
    count = mesh.size
    me = lax.axis_index(AXES)
    bits = int(math.log2(count))
    rows, columns = shard.shape
    held = shard.reshape((1,) * bits + (rows, columns))
    for group in groups:
        swaps = partners(count, group)
        came = yield [(held, pairs) for _, pairs in swaps]
        shape = list(held.shape)
        for bit in group:
            shape[bits - 1 - bit] = 2
        whole = jnp.zeros(shape, shard.dtype)
        for (step, _), got in zip([(0, None)] + swaps, [held] + came):
            start = [0] * len(shape)
            for place, bit in enumerate(group):
                start[bits - 1 - bit] = ((me >> bit) & 1) ^ ((step >> place) & 1)
            whole = lax.dynamic_update_slice(whole, got, start)
        held = whole
    return held.reshape(count * rows, columns)


def pick(array, axis, index):
    return lax.dynamic_slice_in_dim(array, index, 1, axis)


def total(terms, axis, index, kind):
    return sum(pick(term, axis, index).astype(f32) for term in terms).astype(kind)


def sum_steps(parts, mesh, kind):
    count = mesh.size
    core, outer, rest = bit_groups(mesh)
    me = lax.axis_index(AXES)
    rows, columns = parts.shape[0] // count, parts.shape[1]
    rest_size = mesh.shape["fsdp"] // 2
    held = parts.reshape(mesh.shape["dp"], rest_size, 2, rows, columns)
    spot = position(me, core)
    (got,) = yield [(pick(held, 2, spot ^ 1).astype(kind), partners(count, core)[0][1])]
    terms = [pick(held, 2, spot), got]
    split = 2 if len(outer) == 2 and columns % 256 == 0 else 1
    width = columns // split
    shape = (2,) * len(outer) + (rest_size, 1, rows, width)
    pieces = []
    for piece in range(split):
        own = [term[..., piece * width : (piece + 1) * width].reshape(shape) for term in terms]
        order = list(range(len(outer)))
        pieces.append((own, order if piece == 0 else order[::-1]))
    for turn in range(len(outer)):
        sends = []
        for own, order in pieces:
            axis = order[turn]
            bit = outer[len(outer) - 1 - axis]
            mine = position(me, [bit])
            sends.append((total(own, axis, mine ^ 1, kind), partners(count, [bit])[0][1]))
        came = yield sends
        pieces = [
            ([pick(term, order[turn], position(me, [outer[len(outer) - 1 - order[turn]]])) for term in own] + [got], order)
            for (own, order), got in zip(pieces, came)
        ]
    left = rest_size
    pieces = [[term.reshape(rest_size, rows, width) for term in own] for own, _ in pieces]
    for bits in reversed(rest):
        size = 1 << len(bits)
        left //= size
        pieces = [[term.reshape(size, left, rows, width) for term in own] for own in pieces]
        spot = position(me, bits)
        swaps = partners(count, bits)
        sends = [
            (jnp.concatenate([total(own, 0, spot ^ step, kind) for own in pieces], -1), pairs)
            for step, pairs in swaps
        ]
        came = yield sends
        pieces = [
            [pick(term, 0, spot) for term in own]
            + [got[..., place * width : (place + 1) * width] for got in came]
            for place, own in enumerate(pieces)
        ]
    sums = [sum(term.astype(f32) for term in own).reshape(rows, width) for own in pieces]
    return jnp.concatenate(sums, -1)


def plane_sum_kernel(where, *refs, parts):
    keeps, cames, outs = refs[:parts], refs[parts : 2 * parts], refs[2 * parts :]
    for step, out in enumerate(outs):
        place = where[1] ^ step
        start = 0
        for keep, came in zip(keeps, cames):
            lanes = slice(start, start + keep.shape[-1])
            start += keep.shape[-1]
            out[:, lanes] = keep[place] + came[place]


def plane_sum(where, keeps, cames, size):
    blocks, rows, _ = keeps[0].shape
    left = blocks // size
    columns = sum(keep.shape[2] for keep in keeps)
    arrays = [array.reshape(size, left, rows, array.shape[2]) for array in (*keeps, *cames)]
    part = pl.BlockSpec((None, rows, columns), lambda j, where: (j, 0, 0))
    return pl.pallas_call(
        functools.partial(plane_sum_kernel, parts=len(keeps)),
        grid_spec=pltpu.PrefetchScalarGridSpec(
            num_scalar_prefetch=1,
            grid=(left,),
            in_specs=[
                pl.BlockSpec((size, None, rows, array.shape[3]), lambda j, where: (0, j, 0, 0))
                for array in arrays
            ],
            out_specs=[part] * size,
        ),
        out_shape=[shape_of((left, rows, columns), bf16)] * size,
        compiler_params=params(1),
        cost_estimate=cost(blocks * rows * columns, blocks * rows * columns * 6),
        name="plane_sum",
    )(where, *arrays)


def line_sum_kernel(where, *refs, sizes):
    outs = refs[sum(sizes) :]
    for step, out in enumerate(outs):
        place = where[2] ^ step
        at = start = 0
        for size in sizes:
            terms = refs[at : at + size]
            at += size
            lanes = slice(start, start + terms[0].shape[2])
            start += terms[0].shape[2]
            out[:, lanes] = sum(term[place].astype(f32) for term in terms).astype(out.dtype)


def line_sum(where, groups):
    size, rows, _ = groups[0][0].shape
    columns = sum(group[0].shape[2] for group in groups)
    arrays = [array for group in groups for array in group]
    return pl.pallas_call(
        functools.partial(line_sum_kernel, sizes=[len(group) for group in groups]),
        grid_spec=pltpu.PrefetchScalarGridSpec(
            num_scalar_prefetch=1,
            grid=(1,),
            in_specs=[once(array.shape) for array in arrays],
            out_specs=[once((rows, columns))] * size,
        ),
        out_shape=[shape_of((rows, columns), f32)] + [shape_of((rows, columns), bf16)] * (size - 1),
        compiler_params=params(1),
        cost_estimate=cost(),
        name="line_sum",
    )(where, *arrays)


def fold_first_kernel(where, keep, came, keep_a, send_a, keep_b, send_b):
    slow, fast = where[1] // 2, where[1] % 2
    cut = keep_a.shape[-1]
    for other in range(2):
        for place, out, lanes in (
            (slow * 2 + other, keep_a, slice(0, cut)),
            ((slow ^ 1) * 2 + other, send_a, slice(0, cut)),
            (other * 2 + fast, keep_b, slice(cut, None)),
            (other * 2 + (fast ^ 1), send_b, slice(cut, None)),
        ):
            out[other] = keep[place, :, lanes] + came[place, :, lanes]


def fold_first(where, keep, came):
    blocks, rows, columns = keep.shape
    left = blocks // 4
    cut = columns // 256 * 128
    whole = pl.BlockSpec((4, None, rows, columns), lambda j, where: (0, j, 0, 0))
    spec = lambda w: pl.BlockSpec((2, None, rows, w), lambda j, where: (0, j, 0, 0))
    widths = [cut, cut, columns - cut, columns - cut]
    return pl.pallas_call(
        fold_first_kernel,
        grid_spec=pltpu.PrefetchScalarGridSpec(
            num_scalar_prefetch=1,
            grid=(left,),
            in_specs=[whole, whole],
            out_specs=[spec(w) for w in widths],
        ),
        out_shape=[shape_of((2, left, rows, w), bf16) for w in widths],
        compiler_params=params(1),
        cost_estimate=cost(),
        name="fold_first",
    )(where, *(array.reshape(4, left, rows, columns) for array in (keep, came)))


def fold_second_kernel(where, keep_a, came_a, keep_b, came_b, own_a, send_a, own_b, send_b):
    slow, fast = where[1] // 2, where[1] % 2
    for keep, came, mine, own, send in (
        (keep_a, came_a, fast, own_a, send_a),
        (keep_b, came_b, slow, own_b, send_b),
    ):
        for place, out in ((mine, own), (mine ^ 1, send)):
            out[...] = keep[place] + came[place]


def fold_second(where, keep_a, came_a, keep_b, came_b):
    arrays = (keep_a, came_a, keep_b, came_b)
    _, left, rows, _ = keep_a.shape
    widths = [keep_a.shape[3], keep_a.shape[3], keep_b.shape[3], keep_b.shape[3]]
    return pl.pallas_call(
        fold_second_kernel,
        grid_spec=pltpu.PrefetchScalarGridSpec(
            num_scalar_prefetch=1,
            grid=(left,),
            in_specs=[pl.BlockSpec((2, None, rows, w), lambda j, where: (0, j, 0, 0)) for w in widths],
            out_specs=[pl.BlockSpec((None, rows, w), lambda j, where: (j, 0, 0)) for w in widths],
        ),
        out_shape=[shape_of((left, rows, w), bf16) for w in widths],
        compiler_params=params(1),
        cost_estimate=cost(),
        name="fold_second",
    )(where, *arrays)


def line_first_kernel(where, *refs, sizes):
    keep, send = refs[sum(sizes) :]
    fast = where[2] % 2
    for slow in range(2):
        for place, out in ((slow * 2 + fast, keep), (slow * 2 + (fast ^ 1), send)):
            at = start = 0
            for size in sizes:
                terms = refs[at : at + size]
                at += size
                lanes = slice(start, start + terms[0].shape[2])
                start += terms[0].shape[2]
                first, second = terms
                out[slow, :, lanes] = first[place] + second[place]


def line_first(where, groups):
    size, rows, _ = groups[0][0].shape
    columns = sum(group[0].shape[2] for group in groups)
    arrays = [array for group in groups for array in group]
    return pl.pallas_call(
        functools.partial(line_first_kernel, sizes=[len(group) for group in groups]),
        grid_spec=pltpu.PrefetchScalarGridSpec(
            num_scalar_prefetch=1,
            grid=(1,),
            in_specs=[once(array.shape) for array in arrays],
            out_specs=[once((size // 2, rows, columns))] * 2,
        ),
        out_shape=[shape_of((size // 2, rows, columns), bf16)] * 2,
        compiler_params=params(1),
        cost_estimate=cost(),
        name="line_first",
    )(where, *arrays)


def swap_steps(send, mesh):
    core, _, _ = bit_groups(mesh)
    (came,) = yield [(send, partners(mesh.size, core)[0][1])]
    return came


def fast_sum_steps(keeps, cames, where, mesh):
    count = mesh.size
    _, outer, rest = bit_groups(mesh)
    own, *sends = plane_sum(where, keeps, cames, 1 << len(outer))
    came = yield [(array, pairs) for array, (_, pairs) in zip(sends, partners(count, outer))]
    own, *sends = line_sum(where, [[own, *came]])
    came = yield [(array, pairs) for array, (_, pairs) in zip(sends, partners(count, rest[0]))]
    return own + sum(array.astype(f32) for array in came)


def fold_sum_steps(keep, send, where, mesh):
    count = mesh.size
    core, outer, rest = bit_groups(mesh)
    (came,) = yield [(send, partners(count, core)[0][1])]
    shape = (count // 2, keep.shape[0] * 2 // count, keep.shape[1])
    fast, slow = (partners(count, [bit])[0][1] for bit in outer)
    keep_a, send_a, keep_b, send_b = fold_first(where, keep.reshape(shape), came.reshape(shape))
    came_a, came_b = yield [(send_a, slow), (send_b, fast)]
    own_a, send_a, own_b, send_b = fold_second(where, keep_a, came_a, keep_b, came_b)
    came_a, came_b = yield [(send_a, fast), (send_b, slow)]
    keep, send = line_first(where, [[own_a, came_a], [own_b, came_b]])
    (came,) = yield [(send, partners(count, [rest[0][0]])[0][1])]
    me = lax.axis_index(AXES)
    spot = position(me, [rest[0][1]])
    both = [keep, came]
    (last,) = yield [(total(both, 0, spot ^ 1, bf16), partners(count, [rest[0][1]])[0][1])]
    done = (total(both, 0, spot, f32) + last.astype(f32)).reshape(2, shape[1] // 2, shape[2])
    spot = position(me, core)
    (came,) = yield [(pick(done, 0, spot ^ 1), partners(count, core)[0][1])]
    own, came = pick(done, 0, spot)[0], came[0]
    return jnp.where(spot == 0, own, came), jnp.where(spot == 0, came, own)


def small_sum_steps(parts, mesh):
    count = mesh.size
    core, outer, rest = bit_groups(mesh)
    groups = [core, outer, *reversed(rest)]
    order = [outer, *reversed(rest), core]
    me = lax.axis_index(AXES)
    columns = parts.shape[1]
    held = parts.reshape([1 << len(bits) for bits in order] + [columns])
    for bits in groups:
        axis = order.index(bits)
        spot = position(me, bits)
        swaps = partners(count, bits)
        came = yield [(pick(held, axis, spot ^ step), pairs) for step, pairs in swaps]
        held = pick(held, axis, spot) + sum(came)
    return held.reshape(columns)


def cut_by_core(mesh):
    _, outer, rest = bit_groups(mesh)
    return len(outer) == 2 and len(rest) == 1 and len(rest[0]) == 2


def store_cut(core, outs, lanes, value, rows):
    if len(outs) == 1:
        outs[0][:, lanes] = value.astype(bf16)
        return
    keep, send = outs
    for parity in range(2):
        @pl.when(core == parity)
        def _():
            for device in range(value.shape[0] // rows):
                out = keep if device % 2 == parity else send
                out[device // 2, :, lanes] = value[device * rows : (device + 1) * rows, :].astype(bf16)


def cut_shapes(width, columns, chunk, index, rows):
    if not rows:
        spec = pl.BlockSpec((width, chunk), lambda j, *_: (0, index(j)))
        return [spec], [shape_of((width, columns), bf16)]
    blocks = width // rows // 2
    spec = pl.BlockSpec((blocks, rows, chunk), lambda j, *_: (0, 0, index(j)))
    return [spec] * 2, [shape_of((blocks, rows, columns), bf16)] * 2


def normalize(values):
    center = values - jnp.mean(values, -1, keepdims=True)
    scale = lax.rsqrt(jnp.mean(center * center, -1, keepdims=True) + 1e-05)
    return center * scale, scale


def norm_back(grad, gain, unit, scale):
    inner = grad * gain
    return scale * (
        inner
        - jnp.mean(inner, -1, keepdims=True)
        - unit * jnp.mean(inner * unit, -1, keepdims=True)
    )


def gelu_parts(u):
    phi = 0.5 + 0.5 * lax.erf(u * 0.7071067811865476)
    slope = phi + u * (0.3989422804014327 * jnp.exp2((u * u) * (-0.5 * LOG2E)))
    return u * phi, slope


def column_sum(values):
    return jnp.sum(values, 0, keepdims=True)


def accumulate(ref, value, first):
    @pl.when(first)
    def _():
        ref[...] = value

    @pl.when(jnp.logical_not(first))
    def _():
        ref[...] += value


def two_heads(block, padded):
    seq = block.shape[0]
    first = lax.broadcasted_iota(jnp.int32, block.shape, 1) < 64
    zero = jnp.zeros_like(block)
    pad = jnp.zeros((padded - seq, 128), block.dtype)
    return jnp.concatenate(
        [jnp.where(first, block, zero), pad, jnp.where(first, zero, block), pad], 0
    )


def attend_kernel(valid, *refs, tile, padded, first, pairs):
    if first:
        tokens, gain, shift, weight, bias, normed, joined, mixed, raised_out, inverse = refs
    else:
        (
            normed, weight, bias, tokens, mixed_first, bias_out, gain, shift,
            joined, mixed, raised_out, inverse, middle, normed_two,
        ) = refs
    seq, span = joined.shape
    for start in range(0, seq, tile):
        rows = slice(start, start + tile)
        if first:
            unit, _ = normalize(tokens[rows, :].astype(f32))
            low = (unit * gain[...] + shift[...]).astype(bf16)
            normed[rows, :] = low
        else:
            low = normed[rows, :]
        joined[rows, :] = (dot(low, weight[:, :span], NN) + bias[...]).astype(bf16)

    column = lax.broadcasted_iota(jnp.int32, (1, padded), 1)
    mask = jnp.where(column < valid[pl.program_id(0)], 0.0, -1e30).astype(f32)
    places = [(pair, start) for pair in range(pairs) for start in range(0, seq, ATILE)]
    keys, values = {}, {}
    row = lax.broadcasted_iota(jnp.int32, (2 * padded, 128), 0)
    lane = lax.broadcasted_iota(jnp.int32, (2 * padded, 128), 1)
    ones = jnp.where((row < padded) == (lane < 64), 1.0, 0.0).astype(bf16)

    def scores_at(pair, start):
        if pair not in keys:
            at = pair * 384
            keys[pair] = two_heads(joined[:, at + 128 : at + 256], padded)
            values[pair] = jnp.concatenate([two_heads(joined[:, at + 256 : at + 384], padded), ones], 1)
        return dot(joined[start : start + ATILE, pair * 384 : pair * 384 + 128], keys[pair], NT)

    ahead = [scores_at(*place) for place in places[:AHEAD]]
    for index, (pair, start) in enumerate(places):
        rows = slice(start, start + ATILE)
        if index + AHEAD < len(places):
            ahead.append(scores_at(*places[index + AHEAD]))
        scores = ahead.pop(0)
        halves = []
        for head in range(2):
            part = scores[:, head * padded : (head + 1) * padded] * (0.125 * LOG2E) + mask
            halves.append(jnp.exp2(part - jnp.max(part, 1, keepdims=True)).astype(bf16))
        raised = jnp.concatenate(halves, 1)
        raised_out[pair, rows, :] = raised
        both = dot(raised, values[pair], NN)
        scale = 1.0 / both[:, 128:]
        inverse[rows, pair * 128 : (pair + 1) * 128] = scale
        mixed[rows, pair * 128 : (pair + 1) * 128] = (both[:, :128] * scale).astype(bf16)
    if first:
        return
    width = tokens.shape[1]
    for start in range(0, seq, tile):
        rows = slice(start, start + tile)
        value = tokens[rows, :].astype(f32) + bias_out[...]
        value = value + dot(mixed_first[rows, :], weight[: width // 2, -width:], NN)
        value = value + dot(mixed[rows, :], weight[width // 2 :, -width:], NN)
        middle[rows, :] = value
        unit, _ = normalize(value)
        normed_two[rows, :] = (unit * gain[...] + shift[...]).astype(bf16)


def attend(start, valid, weight, bias, seq, norm=None, after=None):
    rows, width = start.shape
    span = bias.shape[1]
    pairs = span // 384
    items = rows // seq
    padded = -(-seq // 128) * 128
    row = lambda w: pl.BlockSpec((seq, w), lambda i, *_: (i, 0))
    one = once((1, width))
    main = [once(weight.shape), once((1, span))]
    if norm:
        specs, arrays = [row(width), one, one, *main], [start, *norm, weight, bias]
    else:
        specs = [row(width), *main, row(width), row(width // 2), one, one, one]
        arrays = [start, weight, bias, *after]
    outs = [
        row(span),
        row(span // 3),
        pl.BlockSpec((None, pairs, seq, 2 * padded), lambda i, *_: (i, 0, 0, 0)),
        row(span // 3),
    ]
    shapes = [
        shape_of((rows, span), bf16),
        shape_of((rows, span // 3), bf16),
        shape_of((items, pairs, seq, 2 * padded), bf16),
        shape_of((rows, span // 3), f32),
    ]
    if norm:
        outs, shapes = [row(width)] + outs, [shape_of((rows, width), bf16)] + shapes
    else:
        outs += [row(width)] * 2
        shapes += [shape_of((rows, width), f32), shape_of((rows, width), bf16)]
    return pl.pallas_call(
        functools.partial(attend_kernel, tile=tile_of(seq), padded=padded, first=bool(norm), pairs=pairs),
        grid_spec=pltpu.PrefetchScalarGridSpec(
            num_scalar_prefetch=1, grid=(items,), in_specs=specs, out_specs=outs
        ),
        out_shape=shapes,
        compiler_params=params(1),
        cost_estimate=cost(),
        name="attend",
    )(valid, *arrays)


def attend_back_kernel(
    where, joined, mixed_grad, mixed, raised, inverse, normed, *rest, pairs, extra, cut
):
    if extra:
        mixed_a, mixed_b, low_grad, joined_grad, column, *outs, held, scaled, total, total_out = rest
    else:
        joined_grad, column, *outs, held, scaled, total = rest
    item = pl.program_id(0)
    seq, span = joined.shape
    padded = raised.shape[2] // 2
    first = lax.broadcasted_iota(jnp.int32, (BTILE, 128), 1) < 64
    places = [(pair, start) for pair in range(pairs) for start in range(0, seq, BTILE)]
    keys, values = {}, {}

    def prob_grad_at(pair, start):
        at = pair * 384
        if pair not in keys:
            keys[pair] = two_heads(joined[:, at + 128 : at + 256], padded)
            values[pair] = two_heads(joined[:, at + 256 : at + 384], padded)
        rows, lanes = slice(start, start + BTILE), slice(pair * 128, (pair + 1) * 128)
        grad = (mixed_grad[rows, lanes].astype(f32) * inverse[rows, lanes]).astype(bf16)
        scaled[rows, lanes] = grad
        return grad, dot(grad, values[pair], NT)

    def own_half(both):
        return jnp.concatenate([both[:64, :padded], both[64:, padded:]], 0).T[:seq]

    ahead = [prob_grad_at(*place) for place in places[:BAHEAD]]
    for index, (pair, start) in enumerate(places):
        rows, lanes = slice(start, start + BTILE), slice(pair * 128, (pair + 1) * 128)
        at = pair * 384
        if index + BAHEAD < len(places):
            ahead.append(prob_grad_at(*places[index + BAHEAD]))
        grad, prob_grad = ahead.pop(0)
        product = grad.astype(f32) * mixed[rows, lanes].astype(f32)
        zero = jnp.zeros_like(product)
        halves = []
        for head in range(2):
            own = jnp.where(first, product, zero) if head == 0 else jnp.where(first, zero, product)
            centre = jnp.sum(own, 1, keepdims=True)
            half = slice(head * padded, (head + 1) * padded)
            halves.append((raised[pair, rows, half].astype(f32) * (prob_grad[:, half] - centre)).astype(bf16))
        score_grad = jnp.concatenate(halves, 1)
        held[rows, :] = score_grad
        joined_grad[rows, at : at + 128] = (dot(score_grad, keys[pair], NN) * 0.125).astype(bf16)
        if start + BTILE == seq:
            joined_grad[:, at + 128 : at + 256] = (
                own_half(dot(joined[:, at : at + 128].T, held[...], NN)) * 0.125
            ).astype(bf16)
            joined_grad[:, at + 256 : at + 384] = own_half(
                dot(scaled[:, lanes].T, raised[pair], NN)
            ).astype(bf16)

    value = joined_grad[...]
    accumulate(total, dot(normed[...], value, TN), item == 0)
    accumulate(column, column_sum(value.astype(f32)), item == 0)
    if extra:
        both = [dot(mixed_a[...], low_grad[...], TN), dot(mixed_b[...], low_grad[...], TN)]
        accumulate(total_out, jnp.concatenate(both, 0), item == 0)

    @pl.when(item == pl.num_programs(0) - 1)
    def _():
        store_cut(where[0], outs, slice(0, span), total[...], cut)
        if extra:
            store_cut(where[0], outs, slice(span, span + total_out.shape[1]), total_out[...], cut)


def attend_back(mixed_grad, where, joined, mixed, raised, inverse, normed, seq, part, cut, others=()):
    rows, span = joined.shape
    width = normed.shape[1]
    items, pairs, _, keys = raised.shape
    row = lambda w, off=0: pl.BlockSpec((seq, w), lambda i, *_: (i, off))
    columns = span + (width if others else 0)
    specs, shapes = cut_shapes(width, columns, columns, lambda j: 0, cut)
    return pl.pallas_call(
        functools.partial(attend_back_kernel, pairs=pairs, extra=bool(others), cut=cut),
        grid_spec=pltpu.PrefetchScalarGridSpec(
            num_scalar_prefetch=1,
            grid=(items,),
            in_specs=[
                row(span),
                row(span // 3, part),
                row(span // 3),
                pl.BlockSpec((None, pairs, seq, keys), lambda i, *_: (i, 0, 0, 0)),
                row(span // 3),
                row(width),
            ]
            + [row(array.shape[1]) for array in others],
            out_specs=[row(span), pl.BlockSpec((1, span), lambda i, *_: (0, 0))] + specs,
            scratch_shapes=[
                pltpu.VMEM((seq, keys), bf16),
                pltpu.VMEM((seq, span // 3), bf16),
                pltpu.VMEM((width, span), f32),
            ]
            + ([pltpu.VMEM((width, width), f32)] if others else []),
        ),
        out_shape=[shape_of((rows, span), bf16), shape_of((1, span), f32)] + shapes,
        compiler_params=params(1),
        cost_estimate=cost(),
        name="attend_back",
    )(where, joined, mixed_grad, mixed, raised, inverse, normed, *others)


def mlp_kernel(
    valid, where, normed, cotangent, up, down, bias_up,
    active, hidden_grad, up_sum, *rest, seq, tile, cut,
):
    *outs, grad = rest
    rows, width = normed.shape

    @pl.when(pl.program_id(0) == 0)
    def _():
        place = lax.broadcasted_iota(jnp.int32, (seq, 1), 0)
        for item in range(rows // seq):
            span = slice(item * seq, (item + 1) * seq)
            grad[span, :] = jnp.where(place < valid[item], cotangent[span, :].astype(f32), 0.0).astype(bf16)

    def ahead_of(start):
        span = slice(start, start + MTILE)
        return dot(normed[span, :], up[...], NN), dot(grad[span, :], down[...], NT)

    column = jnp.zeros(up_sum.shape, f32)
    starts = list(range(0, rows, MTILE))
    ahead = [ahead_of(start) for start in starts[:MAHEAD]]
    for index, start in enumerate(starts):
        span = slice(start, start + MTILE)
        if index + MAHEAD < len(starts):
            ahead.append(ahead_of(starts[index + MAHEAD]))
        hidden, wide = ahead.pop(0)
        value, slope = gelu_parts(hidden + bias_up[...])
        low = (slope * wide).astype(bf16)
        active[span, :] = value.astype(bf16)
        hidden_grad[span, :] = low
        column = column + column_sum(low.astype(f32))
    up_sum[...] = column
    first = dot(normed[...], hidden_grad[...], TN).astype(bf16)
    second = dot(active[...], grad[...], TN).astype(bf16)
    if cut:
        keep, send = outs
        for core in range(2):
            @pl.when(where[0] == core)
            def _():
                (keep, send)[core][...] = first
                (send, keep)[core][...] = second
    else:
        outs[0][:, :width] = first
        outs[0][:, width:] = second


def mlp(normed, valid, where, cotangent, both, bias_up, seq, cut):
    rows, width = normed.shape
    wide = both.shape[1] // 2
    chunks = wide // width
    whole = once((rows, width))
    square = lambda off: pl.BlockSpec((width, width), lambda j, *_: (0, j + off))
    row = pl.BlockSpec((rows, width), lambda j, *_: (0, j))
    one = pl.BlockSpec((1, width), lambda j, *_: (0, j))
    if cut:
        specs = [pl.BlockSpec((width, width), lambda j, *_: (0, j))] * 2
        shapes = [shape_of((width, wide), bf16)] * 2
    else:
        specs, shapes = cut_shapes(width, 2 * wide, 2 * width, lambda j: j, 0)
    return pl.pallas_call(
        functools.partial(mlp_kernel, seq=seq, tile=tile_of(seq), cut=cut),
        grid_spec=pltpu.PrefetchScalarGridSpec(
            num_scalar_prefetch=2,
            grid=(chunks,),
            in_specs=[whole, whole, square(0), square(chunks), one],
            out_specs=[row, row, one] + specs,
            scratch_shapes=[pltpu.VMEM((rows, width), bf16)],
        ),
        out_shape=[
            shape_of((rows, width * chunks), bf16),
            shape_of((rows, width * chunks), bf16),
            shape_of((1, width * chunks), f32),
        ]
        + shapes,
        compiler_params=params(1),
        cost_estimate=cost(),
        name="mlp",
    )(valid, where, normed, cotangent, both, both, bias_up)


def block_out_kernel(valid, active, downs, middle, bias_down, *rest, seq, begin):
    block_out = rest[-1]
    tile, width = middle.shape
    step = pl.program_id(0) + begin // tile
    place = lax.broadcasted_iota(jnp.int32, (tile, 1), 0) + lax.rem(step, seq // tile) * tile
    value = middle[...] + bias_down[...]
    for at in range(0, downs.shape[1], width):
        value = value + dot(active[:, at : at + width], downs[:, at : at + width], NN)
    block_out[...] = jnp.where(place < valid[step // (seq // tile)], value, 0.0).astype(bf16)


def half_of(both, second):
    width, columns = both.shape
    return pl.BlockSpec(
        (width, columns // 2), lambda j, *_: (0, second), pipeline_mode=pl.Buffered(buffer_count=1)
    )


def block_out_of(middle, valid, active, both, bias_down, seq, begin, end, before=None):
    rows, width = middle.shape
    tile = BOT if seq % BOT == 0 else seq
    skip = begin // tile
    row = lambda w: pl.BlockSpec((tile, w), lambda j, *_: (j + skip, 0))
    specs = [row(active.shape[1]), half_of(both, 1), row(width), once((1, width))]
    arrays = [active, both, middle, bias_down]
    aliases = {}
    if before is not None:
        aliases = {len(arrays) + 1: 0}
        specs.append(pl.BlockSpec(memory_space=pl.ANY))
        arrays.append(before)
    return pl.pallas_call(
        functools.partial(block_out_kernel, seq=seq, begin=begin),
        grid_spec=pltpu.PrefetchScalarGridSpec(
            num_scalar_prefetch=1,
            grid=((end - begin) // tile,),
            in_specs=specs,
            out_specs=row(width),
        ),
        out_shape=shape_of((rows, width), bf16),
        input_output_aliases=aliases,
        compiler_params=params(1),
        cost_estimate=cost(),
        name="block_out",
    )(valid, *arrays)


def middle_back_kernel(
    valid, hidden_grad, ups, middle, cotangent, gain, weight,
    low_grad, mixed_grad, gain_sum, shift_sum, bias_sum, down_sum, *, seq, sub,
):
    step = pl.program_id(0)
    tile, width = middle.shape
    each = seq // tile
    starts = list(range(0, tile, sub))
    ahead = [dot(hidden_grad[:sub, :], ups[...], NT)]
    sums = [jnp.zeros((1, width), f32)] * 4
    for index, start in enumerate(starts):
        rows = slice(start, start + sub)
        if index + 1 < len(starts):
            ahead.append(dot(hidden_grad[start + sub : start + 2 * sub, :], ups[...], NT))
        grad = ahead.pop(0)
        unit, scale = normalize(middle[rows, :])
        place = lax.broadcasted_iota(jnp.int32, (sub, 1), 0) + (lax.rem(step, each) * tile + start)
        kept = jnp.where(place < valid[step // each], cotangent[rows, :].astype(f32), 0.0)
        low = (kept + norm_back(grad, gain[...], unit, scale)).astype(bf16)
        low_grad[rows, :] = low
        mixed_grad[rows, :] = dot(low, weight[:, -width:], NT).astype(bf16)
        terms = (grad * unit, grad, low.astype(f32), kept)
        sums = [before + column_sum(term) for before, term in zip(sums, terms)]
    for ref, value in zip((gain_sum, shift_sum, bias_sum, down_sum), sums):
        accumulate(ref, value, step == 0)


def middle_back(middle, valid, hidden_grad, both, cotangent, gain, weight, seq):
    rows, width = middle.shape
    tile = LTILE if seq % LTILE == 0 else seq
    sub = LSUB if tile % LSUB == 0 else tile
    row = lambda w: pl.BlockSpec((tile, w), lambda j, *_: (j, 0))
    one = pl.BlockSpec((1, width), lambda j, *_: (0, 0))
    return pl.pallas_call(
        functools.partial(middle_back_kernel, seq=seq, sub=sub),
        grid_spec=pltpu.PrefetchScalarGridSpec(
            num_scalar_prefetch=1,
            grid=(rows // tile,),
            in_specs=[
                row(hidden_grad.shape[1]), half_of(both, 0), row(width), row(width),
                once((1, width)), once(weight.shape),
            ],
            out_specs=[row(width), row(width)] + [one] * 4,
        ),
        out_shape=[shape_of((rows, width), bf16)] * 2 + [shape_of((1, width), f32)] * 4,
        compiler_params=params(1),
        cost_estimate=cost(),
        name="middle_back",
    )(valid, hidden_grad, both, middle, cotangent, gain, weight)


def input_back_kernel(
    grad_a, grad_b, weight_a, weight_b, tokens, low_grad, gain, input_grad, gain_sum, shift_sum, *, sub
):
    span = grad_a.shape[1]
    tile, width = tokens.shape

    def ahead_of(start):
        rows = slice(start, start + sub)
        return dot(grad_a[rows, :], weight_a[:, :span], NT) + dot(grad_b[rows, :], weight_b[:, :span], NT)

    starts = list(range(0, tile, sub))
    ahead = [ahead_of(0)]
    sums = [jnp.zeros((1, width), f32)] * 2
    for index, start in enumerate(starts):
        rows = slice(start, start + sub)
        if index + 1 < len(starts):
            ahead.append(ahead_of(start + sub))
        grad = ahead.pop(0)
        unit, scale = normalize(tokens[rows, :].astype(f32))
        sums = [before + column_sum(term) for before, term in zip(sums, (grad * unit, grad))]
        full = low_grad[rows, :].astype(f32) + norm_back(grad, gain[...], unit, scale)
        input_grad[rows, :] = full.astype(bf16)
    for ref, value in zip((gain_sum, shift_sum), sums):
        accumulate(ref, value, pl.program_id(0) == 0)


def input_back(grad_a, grad_b, weight_a, weight_b, tokens, low_grad, gain, seq):
    rows, width = tokens.shape
    tile = LTILE if seq % LTILE == 0 else seq
    sub = LSUB if tile % LSUB == 0 else tile
    row = lambda w: pl.BlockSpec((tile, w), lambda i: (i, 0))
    fixed = pl.BlockSpec((1, width), lambda i: (0, 0))
    return pl.pallas_call(
        functools.partial(input_back_kernel, sub=sub),
        grid=(rows // tile,),
        in_specs=[row(grad_a.shape[1]), row(grad_b.shape[1]), once(weight_a.shape), once(weight_b.shape)]
        + [row(width), row(width), once((1, width))],
        out_specs=[row(width), fixed, fixed],
        out_shape=[shape_of((rows, width), bf16)] + [shape_of((1, width), f32)] * 2,
        compiler_params=params(1),
        cost_estimate=cost(),
        name="input_back",
    )(grad_a, grad_b, weight_a, weight_b, tokens, low_grad, gain)


def local(mesh, tokens, cotangent, group, text_len, qkv_w, out_w, mlp_in, mlp_out, gains, biases):
    items, seq, width = tokens.shape
    rows = items * seq
    count = mesh.size
    share = width // count
    wide = mlp_in.shape[0] // share
    chunks = wide // width
    half = width // 2
    span = 3 * half
    valid = (PATCH_SMALL + (PATCH_LARGE - PATCH_SMALL) * group + text_len).astype(jnp.int32)
    flat = tokens.reshape(rows, width)
    cot = cotangent.reshape(rows, width)
    flights = Flights()
    me = lax.axis_index(AXES)
    core, outer, others = bit_groups(mesh)
    where = jnp.stack([position(me, core), position(me, outer), position(me, others[0])]).astype(jnp.int32)
    cut = share if cut_by_core(mesh) and share % 8 == 0 else 0

    def mlp_sums(arrays):
        if cut:
            return flights.add(fold_sum_steps(*arrays, where, mesh), [])
        return flights.add(sum_steps(arrays[0], mesh, bf16), [])

    def swap(arrays):
        return flights.add(swap_steps(arrays[1], mesh), []) if cut else None

    def sums_after(arrays, swaps):
        if cut:
            keeps, cames = [keep for keep, _ in arrays], [job["result"] for job in swaps]
            return flights.add(fast_sum_steps(keeps, cames, where, mesh), [])
        return flights.add(sum_steps(arrays[0][0], mesh, bf16), [])


    def by_pairs(matrix, part):
        pieces = []
        for pair in range(part * 3, part * 3 + 3):
            for place in range(3):
                at = place * width + pair * 128
                pieces.append(matrix[:, at : at + 128])
        return jnp.concatenate(pieces, 1)

    own_up = mlp_in.reshape(share, count, chunks, share).transpose(0, 2, 1, 3).reshape(share, wide)
    own_down = mlp_out.reshape(chunks, share, width).transpose(1, 0, 2).reshape(share, wide)
    own_both = jnp.concatenate([own_up, own_down], 1)

    own_qkv = qkv_w.reshape(share, 3 * width)
    small = jnp.concatenate([gains, biases])
    small_rows = -(-small.shape[0] // 128)
    padded = jnp.pad(small, (0, small_rows * 128 - small.shape[0])).reshape(small_rows, 128)
    padded = jnp.pad(padded, ((0, share - small_rows), (0, 0)))
    job = flights.add(
        gather_steps(jnp.concatenate([by_pairs(own_qkv, 0), padded], 1), mesh, [*others, outer, core]), []
    )
    flights.finish(len(others))
    own_both = flights.behind(own_both)
    both = lax.all_gather(own_both, AXES, axis=0, tiled=True)
    own_second = jnp.concatenate([by_pairs(own_qkv, 1), out_w.reshape(share, width)], 1)
    singles = [[bit] for group in reversed(others) for bit in reversed(group)]
    second_job = flights.add(gather_steps(own_second, mesh, [*singles, outer, core]), [])
    flights.finish(2)
    first = job["result"]

    small = first[:, span:].reshape(count, share, 128)[:, :small_rows]
    small = small.reshape(count, small_rows * 128).astype(f32)
    edge = gains.shape[0]
    gain = small[:, :edge].reshape(1, 2 * width)
    bias = small[:, edge : edge + biases.shape[0]].reshape(1, 6 * width + wide)
    gain_one, gain_two = gain[:, :width], gain[:, width:]
    bias_query, bias_value, bias_output, shift_one, shift_two, bias_down = (
        bias[:, p * width : (p + 1) * width] for p in range(6)
    )
    bias_up = bias[:, 6 * width :].reshape(count, chunks, share).transpose(1, 0, 2).reshape(1, wide)
    bias_joined = jnp.concatenate([bias_query, jnp.zeros_like(bias_query), bias_value], 1)
    bias_parts = [by_pairs(bias_joined, part) for part in range(2)]

    normed, joined_a, mixed_a, raised_a, inverse_a = flights.run(
        lambda x: attend(x, valid, first, bias_parts[0], seq, (gain_one, shift_one)), flat
    )
    flights.finish()
    second = second_job["result"]
    joined_b, mixed_b, raised_b, inverse_b, middle, normed_two = attend(
        normed, valid, second, bias_parts[1], seq,
        after=(flat, mixed_a, bias_output, gain_two, shift_two),
    )

    active, hidden_grad, up_sum, *mlp_grads = mlp(
        normed_two, valid, where, cot, both, bias_up, seq, cut
    )
    mlp_job = mlp_sums(mlp_grads)

    low_grad, mixed_grad, gain_two_sum, shift_two_sum, bias_out_sum, down_sum = flights.run(
        lambda x: middle_back(x, valid, hidden_grad, both, cot, gain_two, second, seq), middle
    )
    joined_grad_a, qkv_sum_a, *grads_a = flights.run(
        lambda x: attend_back(
            x, where, joined_a, mixed_a, raised_a, inverse_a, normed, seq, 0, cut, (mixed_a, mixed_b, low_grad)
        ),
        mixed_grad,
    )
    swap_a = swap(grads_a)
    joined_grad_b, qkv_sum_b, *grads_b = flights.run(
        lambda x: attend_back(x, where, joined_b, mixed_b, raised_b, inverse_b, normed, seq, 1, cut), mixed_grad
    )
    sum_a = sums_after([grads_a], [swap_a])
    swap_b = swap(grads_b)
    input_grad, gain_one_sum, shift_one_sum = flights.run(
        lambda x: input_back(joined_grad_a, x, first, second, flat, low_grad, gain_one, seq),
        joined_grad_b,
    )

    def by_kind(part_a, part_b):
        return jnp.concatenate(
            [
                piece[:, (3 * pair + place) * 128 : (3 * pair + place + 1) * 128]
                for place in range(3)
                for piece in (part_a, part_b)
                for pair in range(3)
            ],
            1,
        )

    joined_sums = by_kind(qkv_sum_a, qkv_sum_b)
    up_sum = up_sum.reshape(chunks, count, share).transpose(1, 0, 2).reshape(1, wide)
    gain_sums = jnp.concatenate([gain_one_sum, gain_two_sum], 1).reshape(count, edge)
    bias_sums = jnp.concatenate(
        [
            joined_sums[:, :width],
            joined_sums[:, 2 * width :],
            bias_out_sum,
            shift_one_sum,
            shift_two_sum,
            down_sum,
            up_sum,
        ],
        1,
    ).reshape(count, biases.shape[0])
    small = jnp.concatenate([gain_sums, bias_sums], 1)
    if cut:
        small = jnp.pad(small, ((0, 0), (0, small_rows * 128 - small.shape[1])))
        small = small.reshape(count // 2, 2, small_rows, 128)
        spot = position(me, core)
        small = [
            jnp.pad(pick(small, 1, place)[:, 0], ((0, 0), (0, share - small_rows), (0, 0))).astype(bf16)
            for place in (spot, spot ^ 1)
        ]
        swap_small = swap(small)
    else:
        small_job = flights.add(small_sum_steps(small, mesh), [])
        sum_b = sums_after([grads_b], [swap_b])
    cuts = [item * seq for item in range(items + 1)]
    block_out = None
    for begin, end in zip(cuts, cuts[1:]):
        if begin < end:
            block_out = flights.run(
                lambda x: block_out_of(
                    x, valid, active, both, bias_down, seq, begin, end, block_out
                ),
                middle,
            )
            if cut and begin == 0:
                sum_b = sums_after([grads_b, small], [swap_b, swap_small])
    flights.finish()
    total_a, total_b = sum_a["result"], sum_b["result"]
    if cut:
        small_total = total_b[:small_rows, span:].reshape(-1)
        small_total = small_total[: edge + biases.shape[0]]
    else:
        small_total = small_job["result"]
    if cut:
        up_total, down_total = mlp_job["result"]
    else:
        mlp_total = mlp_job["result"].reshape(share, chunks, 2, width)
        up_total, down_total = mlp_total[:, :, 0], mlp_total[:, :, 1]
    up_total = up_total.reshape(share, chunks, count, share).transpose(0, 2, 1, 3)
    down_total = down_total.reshape(share, chunks, width).transpose(1, 0, 2)
    return (
        block_out.reshape(tokens.shape),
        input_grad.reshape(tokens.shape),
        by_kind(total_a, total_b).reshape(-1),
        total_a[:, span:].reshape(-1),
        up_total.reshape(-1),
        down_total.reshape(-1),
        small_total[:edge],
        small_total[edge:],
    )


def solution(mesh):
    split = P(AXES)
    whole = P(AXES, None, None)
    return jax.shard_map(
        functools.partial(local, mesh),
        mesh=mesh,
        in_specs=(whole, whole) + (split,) * 8,
        out_specs=(whole, whole) + (split,) * 6,
        check_vma=False,
    )
```

time: 421 us -> 384 us (0.912)
  Pallas kernels: 282 us -> 245 us
  starting transfers between devices: 58.6 us -> 37.4 us
  waiting for transfers between devices: 23.5 us -> 34.5 us
  local copies, waits for them, and re-layouts: 30.7 us -> 40.5 us
    pallas_call x17 -> x15, Pallas kernels: 263 us -> 236 us  [the longest x2 58.8 us: attend_back(): pl.pallas_call(functools.partial(attend_back_kernel, pairs=pairs, extra=b...]
    ppermute x51 -> x36, starting transfers between devices: 58.2 us -> 37.3 us  [depart(): came = [lax.ppermute(array, AXES, pairs) for array, pairs in sends]]
    pallas_call x4 -> x2, Pallas kernels: 18.8 us -> 8.91 us  [plane_sum(): pl.pallas_call(functools.partial(plane_sum_kernel, parts=len(keeps)), gri...]
    ppermute x51 -> x36, waiting for transfers between devices: 23.4 us -> 30.5 us  [depart(): came = [lax.ppermute(array, AXES, pairs) for array, pairs in sends]]
    dynamic_update_slice x20, local copies, waits for them, and re-layouts: 3.94 us -> 9.05 us  [gather_steps(): whole = lax.dynamic_update_slice(whole, got, start)]
    unnamed x133 -> x123, local copies, waits for them, and re-layouts: 9.5 us -> 13.2 us
  transfers between devices with their start and end apart: 53 -> 37, of which waited for: 11 -> 10; matrix products, arithmetic and copies ran while one was open for 5% -> 7% of each run, Pallas kernels for 63% -> 43%
where the time goes in v2:
time: 384 us; the launch traced here: 379 us
  Pallas kernels  245 us (64%)
  local copies, waits for them, and re-layouts  40.5 us (11%)
  starting transfers between devices  37.4 us (10%)
  waiting for transfers between devices  34.5 us (9%)
  between operations  15.4 us (4%)
  other arithmetic  5.58 us (1%)
    pallas_call x2, Pallas kernels, attend_back(): pl.pallas_call(functools.partial(attend_back_kernel, pairs=pairs, extra=b...  58.8 us
    pallas_call x1, Pallas kernels, mlp(): pl.pallas_call(functools.partial(mlp_kernel, seq=seq, tile=tile_of(seq),...  52.5 us
    pallas_call x2, Pallas kernels, attend(): pl.pallas_call(functools.partial(attend_kernel, tile=tile_of(seq), padded...  44.6 us
    ppermute x36, starting transfers between devices, depart(): came = [lax.ppermute(array, AXES, pairs) for array, pairs in sends]  37.3 us
    ppermute x36, waiting for transfers between devices, depart(): came = [lax.ppermute(array, AXES, pairs) for array, pairs in sends]  30.5 us
    pallas_call x3, Pallas kernels, block_out_of(): pl.pallas_call(functools.partial(block_out_kernel, seq=seq, begin=begin),...  24 us
    pallas_call x1, Pallas kernels, middle_back(): pl.pallas_call(functools.partial(middle_back_kernel, seq=seq, sub=sub), g...  20.8 us
    pallas_call x1, Pallas kernels, input_back(): pl.pallas_call(functools.partial(input_back_kernel, sub=sub), grid=(rows...  14.7 us
  transfers between devices with their start and end apart: 37, of which 10 were waited for; matrix products, arithmetic and copies ran while one was open for 7% of the time, Pallas kernels for 43%

profile of v2, /device:TPU:0, one launch (start us, length us, event | category | flops | bytes accessed | tf_op | source)
XLA Modules:
  0.0 378.7 jit_solution(3521792397856180018)
XLA Ops:
  7.2 1.1 reshape.141
  9.2 3.1 collective-permute-start
  12.3 2.6 collective-permute-start.1
  14.9 2.0 reshape.152
  17.0 1.3 reshape.153
  19.3 1.6 collective-permute-done.2
  21.1 1.6 collective-permute-start.3
  22.6 1.5 collective-permute-start.4
  24.6 1.3 collective-permute-start.6
  26.0 4.3 %collective-permute-done.6 = bf16[1,1,1,1,1,24,1920]{6,5,4,3,2,1,0:T(8,128)(2,1)S(1)} collective-permute-done((bf16[1,1,1,1,1,24,1920]{6,5,4,3,2,1,0:T(8,128)(2,1)S(1)}, bf16[1,1,1,1,1,24,1920]{6,5,4,3,2,1,0:T(8,128)(2,1)S(1)}, u32[]{:S(2)}, u32[]{:S(2)}) %collective-permute-start.6) | collective-permute-done | bytes 92192 | tf_op jit(solution)/shard_map/ppermute | solution.py:83
  30.4 4.5 %collective-permute-done.4 = bf16[1,1,2,2,1,24,1280]{6,5,4,3,2,1,0:T(8,128)(2,1)S(1)} collective-permute-done((bf16[1,1,2,2,1,24,1280]{6,5,4,3,2,1,0:T(8,128)(2,1)S(1)}, bf16[1,1,2,2,1,24,1280]{6,5,4,3,2,1,0:T(8,128)(2,1)S(1)}, u32[]{:S(2)}, u32[]{:S(2)}) %collective-permute-start.4) | collective-permute-done | bytes 245792 | tf_op jit(solution)/shard_map/ppermute | solution.py:83
  36.1 9.1 %collective-permute-done.8 = bf16[1,1,2,1,1,24,1920]{6,5,4,3,2,1,0:T(8,128)(2,1)S(1)} collective-permute-done((bf16[1,1,2,1,1,24,1920]{6,5,4,3,2,1,0:T(8,128)(2,1)S(1)}, bf16[1,1,2,1,1,24,1920]{6,5,4,3,2,1,0:T(8,128)(2,1)S(1)}, u32[]{:S(2)}, u32[]{:S(2)}) %collective-permute-start.8) | collective-permute-done | bytes 184352 | tf_op jit(solution)/shard_map/ppermute | solution.py:83
  45.2 1.4 constant_dynamic-update-slice_fusion.79
  46.9 1.2 constant_dynamic-update-slice_fusion.81
  48.1 2.0 collective-permute-start.10
  50.1 1.3 collective-permute-start.11
  53.0 19.7 %attend.2 = (bf16[1824,768]{1,0:T(8,128)(2,1)}, bf16[1824,1152]{1,0:T(8,128)(2,1)}, bf16[1824,384]{1,0:T(8,128)(2,1)}, bf16[3,3,608,1280]{3,2,1,0:T(8,128)(2,1)}, f32[1824,384]{1,0:T(8,128)}) custom-call(s32[3]{0:T(128)} %get-tuple-element.361.valid, bf16[1824,768]{1,0:T(8,128)(2,1)} %bitcast.48, f32[1,768]{1,0:T(1,128)} %get-tuple-element.358.refs_1_.gain, ...), custom_call_target="tpu_custom_call" | custom-call | flops 1 | bytes 1 | tf_op jit(solution)/shard_map/attend/pallas_call | solution.py:621
  72.7 1.2 broadcast_in_dim.27
  73.9 0.8 constant_dynamic-update-slice_fusion.78
  74.7 1.0 collective-permute-done.9
  76.5 0.8 constant_dynamic-update-slice_fusion.76
  79.1 1.6 constant_dynamic-update-slice_fusion.74
  80.7 0.9 collective-permute-done.12
  81.6 1.6 constant_dynamic-update-slice_fusion.73
  83.2 1.6 copy-done
  84.8 24.9 %attend.3 = (bf16[1824,1152]{1,0:T(8,128)(2,1)}, bf16[1824,384]{1,0:T(8,128)(2,1)}, bf16[3,3,608,1280]{3,2,1,0:T(8,128)(2,1)}, f32[1824,384]{1,0:T(8,128)}, f32[...) custom-call(s32[3]{0:T(128)} %get-tuple-element.361.valid, bf16[1824,768]{1,0:T(8,128)(2,1)} %get-tuple-element.180.refs_0_.normed, ...), custom_call_target="tpu_custom_call" | custom-call | flops 1 | bytes 1 | tf_op jit(solution)/shard_map/attend/pallas_call | solution.py:621
  109.7 3.9 %all-gather.2.cloned.1.call-done.up.down.ups.downs = bf16[768,6144]{1,0:T(8,128)(2,1)} async-done(((bf16[24,6144]{1,0:T(8,128)(2,1)}), bf16[768,6144]{1,0:T(8,128)(2,1)}) %all-gather.2.cloned.1.call-update) | async-done | bytes 9437200 | tf_op jit(solution)/shard_map/all_gather | solution.py:1013
  113.6 52.5 %mlp.1 = (bf16[1824,3072]{1,0:T(8,128)(2,1)}, bf16[1824,3072]{1,0:T(8,128)(2,1)}, f32[1,3072]{1,0:T(1,128)}, bf16[768,3072]{1,0:T(8,128)(2,1)}, bf16[768,3072]{1,0:T(8,128)(2,1)}) custom-call(s32[3]{0:T(128)} %get-tuple-element.361.valid, s32[3]{0:T(128)} %get-tuple-element.360.where, bf16[1824,768]{1,0:T(8,128)(2,1)} %get-tuple-element.185.normed, ...), custom_call_target="tpu_custom_call" | custom-call | flops 1 | bytes 1 | tf_op jit(solution)/shard_map/mlp/pallas_call | solution.py:795
  166.4 20.8 %middle_back.1 = (bf16[1824,768]{1,0:T(8,128)(2,1)}, bf16[1824,768]{1,0:T(8,128)(2,1)}, f32[1,768]{1,0:T(1,128)}, f32[1,768]{1,0:T(1,128)}, f32[1,768]{1,0:T(1,128)}, /*index=5*/f32[1,768]{1,0:T(1,128)}) custom-call(s32[3]{0:T(128)} %get-tuple-element.361.valid, bf16[1824,3072]{1,0:T(8,128)(2,1)} %get-tuple-element.190.hidden_grad, ...), custom_call_target="tpu_custom_call" | custom-call | flops 1 | bytes 1 | tf_op jit(solution)/shard_map/middle_back/pallas_call | solution.py:895
  187.1 6.9 %fold_first.1 = (bf16[2,4,48,1536]{3,2,1,0:T(8,128)(2,1)}, bf16[2,4,48,1536]{3,2,1,0:T(8,128)(2,1)}, bf16[2,4,48,1536]{3,2,1,0:T(8,128)(2,1)}, bf16[2,4,48,1536]{3,2,1,0:T(8,128)(2,1)}) custom-call(s32[3]{0:T(128)} %get-tuple-element.360.where, bf16[4,4,48,3072]{3,2,1,0:T(8,128)(2,1)} %bitcast.58, bf16[4,4,48,3072]{3,2,1,0:T(8,128)(2,1)} %bitcast.15.came), custom_call_target="tpu_custom_call" | custom-call | flops 1 | bytes 1 | tf_op jit(solution)/shard_map/fold_first/pallas_call | solution.py:321
  194.0 1.5 collective-permute-start.14
  196.0 33.1 %attend_back.2 = (bf16[1824,1152]{1,0:T(8,128)(2,1)}, f32[1,1152]{1,0:T(1,128)}, bf16[16,24,1920]{2,1,0:T(8,128)(2,1)}, bf16[16,24,1920]{2,1,0:T(8,128)(2,1)}) custom-call(s32[3]{0:T(128)} %get-tuple-element.360.where, bf16[1824,1152]{1,0:T(8,128)(2,1)} %get-tuple-element.204.joined, bf16[1824,768]{1,0:T(8,128)(2,1)} %get-tuple-element.224.mixed_grad, ...), custom_call_target="tpu_custom_call" | custom-call | flops 1 | bytes 1 | tf_op jit(solution)/shard_map/attend_back/pallas_call | solution.py:707
  229.1 1.0 copy-done.3
  230.5 5.1 %fold_second.1 = (bf16[4,48,1536]{2,1,0:T(8,128)(2,1)}, bf16[4,48,1536]{2,1,0:T(8,128)(2,1)}, bf16[4,48,1536]{2,1,0:T(8,128)(2,1)}, bf16[4,48,1536]{2,1,0:T(8,128)(2,1)}) custom-call(s32[3]{0:T(128)} %get-tuple-element.360.where, bf16[2,4,48,1536]{3,2,1,0:T(8,128)(2,1)} %get-tuple-element.203.keep_a, bf16[2,4,48,1536]{3,2,1,0:T(8,128)(2,1)} %copy-done.3, ...), custom_call_target="tpu_custom_call" | custom-call | flops 1 | bytes 1 | tf_op jit(solution)/shard_map/fold_second/pallas_call | solution.py:350
  237.1 1.5 collective-permute-start.16
  239.2 25.7 %attend_back.3 = (bf16[1824,1152]{1,0:T(8,128)(2,1)}, f32[1,1152]{1,0:T(1,128)}, bf16[16,24,1152]{2,1,0:T(8,128)(2,1)}, bf16[16,24,1152]{2,1,0:T(8,128)(2,1)}) custom-call(s32[3]{0:T(128)} %get-tuple-element.360.where, bf16[1824,1152]{1,0:T(8,128)(2,1)} %get-tuple-element.189.joined, bf16[1824,768]{1,0:T(8,128)(2,1)} %get-tuple-element.224.mixed_grad, ...), custom_call_target="tpu_custom_call" | custom-call | flops 1 | bytes 1 | tf_op jit(solution)/shard_map/attend_back/pallas_call | solution.py:707
  265.1 1.2 copy-done.2
  266.2 4.7 %plane_sum.2 = (bf16[4,24,1920]{2,1,0:T(8,128)(2,1)}, bf16[4,24,1920]{2,1,0:T(8,128)(2,1)}, bf16[4,24,1920]{2,1,0:T(8,128)(2,1)}, bf16[4,24,1920]{2,1,0:T(8,128)(2,1)}) custom-call(s32[3]{0:T(128)} %get-tuple-element.360.where, bf16[4,4,24,1920]{3,2,1,0:T(8,128)(2,1)} %bitcast.62, bf16[4,4,24,1920]{3,2,1,0:T(8,128)(2,1)} %bitcast.63), custom_call_target="tpu_custom_call" | custom-call | flops 1 | bytes 1 | tf_op jit(solution)/shard_map/plane_sum/pallas_call | solution.py:251
  270.9 3.5 line_first.1
  274.4 1.5 collective-permute-start.19
  275.9 1.4 collective-permute-start.20
  277.9 1.5 collective-permute-start.22
  279.5 14.7 %input_back.1 = (bf16[1824,768]{1,0:T(8,128)(2,1)}, f32[1,768]{1,0:T(1,128)}, f32[1,768]{1,0:T(1,128)}) custom-call(bf16[1824,1152]{1,0:T(8,128)(2,1)} %get-tuple-element.235.grad_a, bf16[1824,1152]{1,0:T(8,128)(2,1)} %get-tuple-element.248.grad_b, bf16[768,1280]{1,0:T(8,128)(2,1)} %bitcast.54, bf16[768,1920]{1,0:T(8,128)(2,1)} %bitcast.47, ...), custom_call_target="tpu_custom_call" | custom-call | flops 1 | bytes 1 | tf_op jit(solution)/shard_map/input_back/pallas_call | solution.py:945
  294.2 1.6 collective-permute-done.21.refs_2_
  297.8 0.8 add_convert_fusion
  298.6 2.8 line_sum.2
  301.5 1.0 collective-permute-start.24
  302.5 1.5 collective-permute-start.25
  303.9 1.0 collective-permute-start.26
  305.0 1.9 collective-permute-start.27
  306.8 8.2 %block_out.3.rest_0_ = bf16[1824,768]{1,0:T(8,128)(2,1)} custom-call(s32[3]{0:T(128)} %get-tuple-element.361.valid, bf16[1824,3072]{1,0:T(8,128)(2,1)} %get-tuple-element.187.active, bf16[768,6144]{1,0:T(8,128)(2,1)} %all-gather.2.cloned.1.call-done.up.down.ups.downs, f32[1824,768]{1,0:T(8,128)} %get-tuple-element.300.middle, ...), custom_call_target="tpu_custom_call" | custom-call | flops 1 | bytes 1 | tf_op jit(solution)/shard_map/block_out/pallas_call | solution.py:846
  315.7 7.3 %collective-permute-done.26 = bf16[24,1920]{1,0:T(8,128)(2,1)S(1)} collective-permute-done((bf16[24,1920]{1,0:T(8,128)(2,1)}, bf16[24,1920]{1,0:T(8,128)(2,1)S(1)}, u32[]{:S(2)}, u32[]{:S(2)}) %collective-permute-start.26) | collective-permute-done | bytes 92192 | tf_op jit(solution)/shard_map/ppermute | solution.py:83
  323.7 4.3 %plane_sum.3 = (bf16[4,24,1280]{2,1,0:T(8,128)(2,1)}, bf16[4,24,1280]{2,1,0:T(8,128)(2,1)}, bf16[4,24,1280]{2,1,0:T(8,128)(2,1)}, bf16[4,24,1280]{2,1,0:T(8,128)(2,1)}) custom-call(s32[3]{0:T(128)} %get-tuple-element.360.where, bf16[4,4,24,1152]{3,2,1,0:T(8,128)(2,1)} %bitcast.65, bf16[4,4,24,128]{3,2,1,0:T(8,128)(2,1)} %bitcast.69, ...), custom_call_target="tpu_custom_call" | custom-call | flops 1 | bytes 1 | tf_op jit(solution)/shard_map/plane_sum/pallas_call | solution.py:251
  328.6 1.4 collective-permute-start.31
  330.0 1.5 collective-permute-start.32
  332.8 7.9 %block_out.4.rest_0_ = bf16[1824,768]{1,0:T(8,128)(2,1)} custom-call(s32[3]{0:T(128)} %get-tuple-element.361.valid, bf16[1824,3072]{1,0:T(8,128)(2,1)} %get-tuple-element.187.active, bf16[768,6144]{1,0:T(8,128)(2,1)} %all-gather.2.cloned.1.call-done.up.down.ups.downs, f32[1824,768]{1,0:T(8,128)} %get-tuple-element.300.middle, ...), custom_call_target="tpu_custom_call", output_to_operand_aliasing={{}: (5, {})} | custom-call | flops 1 | bytes 1 | tf_op jit(solution)/shard_map/block_out/pallas_call | solution.py:846
  342.9 2.7 line_sum.3
  345.6 2.4 collective-permute-start.33
  348.5 1.9 collective-permute-start.35
  350.5 7.9 %block_out.5 = bf16[1824,768]{1,0:T(8,128)(2,1)} custom-call(s32[3]{0:T(128)} %get-tuple-element.361.valid, bf16[1824,3072]{1,0:T(8,128)(2,1)} %get-tuple-element.187.active, bf16[768,6144]{1,0:T(8,128)(2,1)} %all-gather.2.cloned.1.call-done.up.down.ups.downs, f32[1824,768]{1,0:T(8,128)} %get-tuple-element.300.middle, ...), custom_call_target="tpu_custom_call", output_to_operand_aliasing={{}: (5, {})} | custom-call | flops 1 | bytes 1 | tf_op jit(solution)/shard_map/block_out/pallas_call | solution.py:846
  358.4 1.1 select_n.92
  359.5 1.2 copy.30
  360.8 2.5 reshape.174
  364.3 0.9 add_add_fusion.1
  (236 shorter events, 27.1 us)
Async XLA Ops:
  7.2 11.1 %copy-start.19 = (bf16[73728]{0:T(1024)(128)(2,1)S(1)}, bf16[73728]{0:T(1024)(128)(2,1)}, u32[]{:S(2)}) copy-start(bf16[73728]{0:T(1024)(128)(2,1)} %param.17) | copy-start | bytes 442372
  7.2 106.4 %all-gather.2.cloned.1.call-start = ((), (), s32[]{:S(2)}) async-start(), calls=%async_computation | async-start | bytes 9732096 | tf_op jit(solution)/shard_map/all_gather | solution.py:1013
  9.2 10.0 %collective-permute-start = (bf16[1,1,1,1,1,24,1280]{6,5,4,3,2,1,0:T(8,128)(2,1)S(1)}, bf16[1,1,1,1,1,24,1280]{6,5,4,3,2,1,0:T(8,128)(2,1)S(1)}, u32[]{:S(2)}, u32[]{:S(2)}) collective-permute-start(bf16[1,1,1,1,1,24,1280]{6,5,4,3,2,1,0:T(8,128)(2,1)S(1)} %bitcast.78), channel_id=1, source_target_pairs={{0,2},{1,3},{2,0},{3,1},{4,6},{5,7},{6,4},{7,5},{8,10},{9,11},{10,... | collective-permute-start | bytes 184328 | tf_op jit(solution)/shard_map/ppermute | solution.py:83
  12.3 7.0 %collective-permute-start.1 = (bf16[1,1,1,1,1,24,1280]{6,5,4,3,2,1,0:T(8,128)(2,1)S(1)}, bf16[1,1,1,1,1,24,1280]{6,5,4,3,2,1,0:T(8,128)(2,1)S(1)}, u32[]{:S(2)}, u32[]{:S(2)}) collective-permute-start(bf16[1,1,1,1,1,24,1280]{6,5,4,3,2,1,0:T(8,128)(2,1)S(1)} %bitcast.79), channel_id=1, source_target_pairs={{0,4},{1,5},{2,6},{3,7},{4,0},{5,1},{6,2},{7,3},{8,12},{9,13},{10,... | collective-permute-start | bytes 184328 | tf_op jit(solution)/shard_map/ppermute | solution.py:83
  14.9 6.0 %collective-permute-start.2 = (bf16[1,1,1,1,1,24,1280]{6,5,4,3,2,1,0:T(8,128)(2,1)S(1)}, bf16[1,1,1,1,1,24,1280]{6,5,4,3,2,1,0:T(8,128)(2,1)S(1)}, u32[]{:S(2)}, u32[]{:S(2)}) collective-permute-start(bf16[1,1,1,1,1,24,1280]{6,5,4,3,2,1,0:T(8,128)(2,1)S(1)} %bitcast.80), channel_id=1, source_target_pairs={{0,6},{1,7},{2,4},{3,5},{4,2},{5,3},{6,0},{7,1},{8,14},{9,15},{10,... | collective-permute-start | bytes 184328 | tf_op jit(solution)/shard_map/ppermute | solution.py:83
  17.0 4.0 %copy-start.22 = (bf16[18432]{0:T(1024)(128)(2,1)S(1)}, bf16[18432]{0:T(1024)(128)(2,1)}, u32[]{:S(2)}) copy-start(bf16[18432]{0:T(1024)(128)(2,1)} %param.15) | copy-start | bytes 110596
  20.9 14.2 %copy-start.30 = (s32[3]{0:T(128)S(1)}, s32[3]{0:T(128)}, u32[]{:S(2)}) copy-start(s32[3]{0:T(128)} %param.13) | copy-start | bytes 40
  20.9 14.2 %copy-start.31 = (s32[3]{0:T(128)S(1)}, s32[3]{0:T(128)}, u32[]{:S(2)}) copy-start(s32[3]{0:T(128)} %param.12) | copy-start | bytes 40
  21.1 9.3 %collective-permute-start.3 = (bf16[1,1,2,2,1,24,1280]{6,5,4,3,2,1,0:T(8,128)(2,1)S(1)}, bf16[1,1,2,2,1,24,1280]{6,5,4,3,2,1,0:T(8,128)(2,1)S(1)}, u32[]{:S(2)}, u32[]{:S(2)}) collective-permute-start(bf16[1,1,2,2,1,24,1280]{6,5,4,3,2,1,0:T(8,128)(2,1)S(1)} %constant_dynamic-update-slice_fusion.88), channel_id=1, source_target_pairs={{0,8},{1,9},{2,10},{3,11},{4,12},{5,13},{6,14},{7,15},{8,0},{9,1},... | collective-permute-start | bytes 737288 | tf_op jit(solution)/shard_map/ppermute | solution.py:83
  22.6 12.2 %collective-permute-start.4 = (bf16[1,1,2,2,1,24,1280]{6,5,4,3,2,1,0:T(8,128)(2,1)S(1)}, bf16[1,1,2,2,1,24,1280]{6,5,4,3,2,1,0:T(8,128)(2,1)S(1)}, u32[]{:S(2)}, u32[]{:S(2)}) collective-permute-start(bf16[1,1,2,2,1,24,1280]{6,5,4,3,2,1,0:T(8,128)(2,1)S(1)} %constant_dynamic-update-slice_fusion.88), channel_id=1, source_target_pairs={{0,16},{1,17},{2,18},{3,19},{4,20},{5,21},{6,22},{7,23},{8,24},{9,... | collective-permute-start | bytes 737288 | tf_op jit(solution)/shard_map/ppermute | solution.py:83
  24.1 10.7 %collective-permute-start.5 = (bf16[1,1,2,2,1,24,1280]{6,5,4,3,2,1,0:T(8,128)(2,1)S(1)}, bf16[1,1,2,2,1,24,1280]{6,5,4,3,2,1,0:T(8,128)(2,1)S(1)}, u32[]{:S(2)}, u32[]{:S(2)}) collective-permute-start(bf16[1,1,2,2,1,24,1280]{6,5,4,3,2,1,0:T(8,128)(2,1)S(1)} %constant_dynamic-update-slice_fusion.88), channel_id=1, source_target_pairs={{0,24},{1,25},{2,26},{3,27},{4,28},{5,29},{6,30},{7,31},{8,16},{9,... | collective-permute-start | bytes 737288 | tf_op jit(solution)/shard_map/ppermute | solution.py:83
  24.6 5.7 %collective-permute-start.6 = (bf16[1,1,1,1,1,24,1920]{6,5,4,3,2,1,0:T(8,128)(2,1)S(1)}, bf16[1,1,1,1,1,24,1920]{6,5,4,3,2,1,0:T(8,128)(2,1)S(1)}, u32[]{:S(2)}, u32[]{:S(2)}) collective-permute-start(bf16[1,1,1,1,1,24,1920]{6,5,4,3,2,1,0:T(8,128)(2,1)S(1)} %bitcast.76), channel_id=1, source_target_pairs={{0,4},{1,5},{2,6},{3,7},{4,0},{5,1},{6,2},{7,3},{8,12},{9,13},{10,... | collective-permute-start | bytes 276488 | tf_op jit(solution)/shard_map/ppermute | solution.py:83
  34.9 10.3 %collective-permute-start.7 = (bf16[2,2,2,2,1,24,1280]{6,5,4,3,2,1,0:T(8,128)(2,1)S(1)}, bf16[2,2,2,2,1,24,1280]{6,5,4,3,2,1,0:T(8,128)(2,1)}, u32[]{:S(2)}, u32[]{:S(2)}) collective-permute-start(bf16[2,2,2,2,1,24,1280]{6,5,4,3,2,1,0:T(8,128)(2,1)S(1)} %constant_dynamic-update-slice_fusion.82), channel_id=1, source_target_pairs={{0,1},{1,0},{2,3},{3,2},{4,5},{5,4},{6,7},{7,6},{8,9},{9,8},{10,11... | collective-permute-start | bytes 2949128 | tf_op jit(solution)/shard_map/ppermute | solution.py:83
  35.7 9.5 %collective-permute-start.8 = (bf16[1,1,2,1,1,24,1920]{6,5,4,3,2,1,0:T(8,128)(2,1)S(1)}, bf16[1,1,2,1,1,24,1920]{6,5,4,3,2,1,0:T(8,128)(2,1)S(1)}, u32[]{:S(2)}, u32[]{:S(2)}) collective-permute-start(bf16[1,1,2,1,1,24,1920]{6,5,4,3,2,1,0:T(8,128)(2,1)S(1)} %constant_dynamic-update-slice_fusion.87), channel_id=1, source_target_pairs={{0,2},{1,3},{2,0},{3,1},{4,6},{5,7},{6,4},{7,5},{8,10},{9,11},{10,... | collective-permute-start | bytes 552968 | tf_op jit(solution)/shard_map/ppermute | solution.py:83
  45.2 1.4 copy-start.18
  46.6 5.8 %copy-start.1 = (bf16[2,2,2,2,2,24,1280]{6,5,4,3,2,1,0:T(8,128)(2,1)}, bf16[2,2,2,2,2,24,1280]{6,5,4,3,2,1,0:T(8,128)(2,1)S(1)}, u32[]{:S(2)}) copy-start(bf16[2,2,2,2,2,24,1280]{6,5,4,3,2,1,0:T(8,128)(2,1)S(1)} %constant_dynamic-update-slice_fusion.79) | copy-start | bytes 5898244
  48.1 26.6 %collective-permute-start.10 = (bf16[1,1,2,2,1,24,1920]{6,5,4,3,2,1,0:T(8,128)(2,1)S(1)}, bf16[1,1,2,2,1,24,1920]{6,5,4,3,2,1,0:T(8,128)(2,1)S(1)}, u32[]{:S(2)}, u32[]{:S(2)}) collective-permute-start(bf16[1,1,2,2,1,24,1920]{6,5,4,3,2,1,0:T(8,128)(2,1)S(1)} %constant_dynamic-update-slice_fusion.81), channel_id=1, source_target_pairs={{0,16},{1,17},{2,18},{3,19},{4,20},{5,21},{6,22},{7,23},{8,24},{9,... | collective-permute-start | bytes 1105928 | tf_op jit(solution)/shard_map/ppermute | solution.py:83
  50.1 24.6 %collective-permute-start.11 = (bf16[1,1,2,2,1,24,1920]{6,5,4,3,2,1,0:T(8,128)(2,1)S(1)}, bf16[1,1,2,2,1,24,1920]{6,5,4,3,2,1,0:T(8,128)(2,1)S(1)}, u32[]{:S(2)}, u32[]{:S(2)}) collective-permute-start(bf16[1,1,2,2,1,24,1920]{6,5,4,3,2,1,0:T(8,128)(2,1)S(1)} %constant_dynamic-update-slice_fusion.81), channel_id=1, source_target_pairs={{0,24},{1,25},{2,26},{3,27},{4,28},{5,29},{6,30},{7,31},{8,16},{9,... | collective-permute-start | bytes 1105928 | tf_op jit(solution)/shard_map/ppermute | solution.py:83
  51.4 24.3 %collective-permute-start.9 = (bf16[1,1,2,2,1,24,1920]{6,5,4,3,2,1,0:T(8,128)(2,1)S(1)}, bf16[1,1,2,2,1,24,1920]{6,5,4,3,2,1,0:T(8,128)(2,1)S(1)}, u32[]{:S(2)}, u32[]{:S(2)}) collective-permute-start(bf16[1,1,2,2,1,24,1920]{6,5,4,3,2,1,0:T(8,128)(2,1)S(1)} %constant_dynamic-update-slice_fusion.81), channel_id=1, source_target_pairs={{0,8},{1,9},{2,10},{3,11},{4,12},{5,13},{6,14},{7,15},{8,0},{9,1},... | collective-permute-start | bytes 1105928 | tf_op jit(solution)/shard_map/ppermute | solution.py:83
  52.4 20.3 %copy-start.24 = (f32[1,1152]{1,0:T(1,128)}, f32[1,1152]{1,0:T(1,128)S(1)}, u32[]{:S(2)}) copy-start(f32[1,1152]{1,0:T(1,128)S(1)} %get-tuple-element.342.refs_2_) | copy-start | bytes 13828
  78.0 3.6 collective-permute-start.12
  83.2 1.6 copy-start
  166.1 21.0 %collective-permute-start.13 = (bf16[768,3072]{1,0:T(8,128)(2,1)}, bf16[768,3072]{1,0:T(8,128)(2,1)}, u32[]{:S(2)}, u32[]{:S(2)}) collective-permute-start(bf16[768,3072]{1,0:T(8,128)(2,1)} %get-tuple-element.199), channel_id=1, source_target_pairs={{0,1},{1,0},{2,3},{3,2},{4,5},{5,4},{6,7},{7,6},{8,9},{9,8},{10,11... | collective-permute-start | bytes 14155784 | tf_op jit(solution)/shard_map/ppermute | solution.py:83
  194.0 35.1 %collective-permute-start.14 = (bf16[2,4,48,1536]{3,2,1,0:T(8,128)(2,1)}, bf16[2,4,48,1536]{3,2,1,0:T(8,128)(2,1)S(1)}, u32[]{:S(2)}, u32[]{:S(2)}) collective-permute-start(bf16[2,4,48,1536]{3,2,1,0:T(8,128)(2,1)} %get-tuple-element.216), channel_id=1, source_target_pairs={{0,16},{1,17},{2,18},{3,19},{4,20},{5,21},{6,22},{7,23},{8,24},{9,... | collective-permute-start | bytes 3538952 | tf_op jit(solution)/shard_map/ppermute | solution.py:83
  195.4 33.6 %collective-permute-start.15 = (bf16[2,4,48,1536]{3,2,1,0:T(8,128)(2,1)}, bf16[2,4,48,1536]{3,2,1,0:T(8,128)(2,1)S(1)}, u32[]{:S(2)}, u32[]{:S(2)}) collective-permute-start(bf16[2,4,48,1536]{3,2,1,0:T(8,128)(2,1)} %get-tuple-element.217), channel_id=1, source_target_pairs={{0,8},{1,9},{2,10},{3,11},{4,12},{5,13},{6,14},{7,15},{8,0},{9,1},... | collective-permute-start | bytes 3538952 | tf_op jit(solution)/shard_map/ppermute | solution.py:83
  230.5 5.7 %copy-start.23 = (f32[1,3072]{1,0:T(1,128)S(1)}, f32[1,3072]{1,0:T(1,128)}, u32[]{:S(2)}) copy-start(f32[1,3072]{1,0:T(1,128)} %get-tuple-element.265) | copy-start | bytes 36868
  235.6 29.4 %collective-permute-start.18 = (bf16[16,24,1920]{2,1,0:T(8,128)(2,1)}, bf16[16,24,1920]{2,1,0:T(8,128)(2,1)S(1)}, u32[]{:S(2)}, u32[]{:S(2)}) collective-permute-start(bf16[16,24,1920]{2,1,0:T(8,128)(2,1)} %get-tuple-element.233), channel_id=1, source_target_pairs={{0,1},{1,0},{2,3},{3,2},{4,5},{5,4},{6,7},{7,6},{8,9},{9,8},{10,11... | collective-permute-start | bytes 4423688 | tf_op jit(solution)/shard_map/ppermute | solution.py:83
  237.1 27.9 %collective-permute-start.16 = (bf16[4,48,1536]{2,1,0:T(8,128)(2,1)}, bf16[4,48,1536]{2,1,0:T(8,128)(2,1)S(1)}, u32[]{:S(2)}, u32[]{:S(2)}) collective-permute-start(bf16[4,48,1536]{2,1,0:T(8,128)(2,1)} %get-tuple-element.231), channel_id=1, source_target_pairs={{0,8},{1,9},{2,10},{3,11},{4,12},{5,13},{6,14},{7,15},{8,0},{9,1},... | collective-permute-start | bytes 1769480 | tf_op jit(solution)/shard_map/ppermute | solution.py:83
  238.6 26.4 %collective-permute-start.17 = (bf16[4,48,1536]{2,1,0:T(8,128)(2,1)}, bf16[4,48,1536]{2,1,0:T(8,128)(2,1)S(1)}, u32[]{:S(2)}, u32[]{:S(2)}) collective-permute-start(bf16[4,48,1536]{2,1,0:T(8,128)(2,1)} %get-tuple-element.232), channel_id=1, source_target_pairs={{0,16},{1,17},{2,18},{3,19},{4,20},{5,21},{6,22},{7,23},{8,24},{9,... | collective-permute-start | bytes 1769480 | tf_op jit(solution)/shard_map/ppermute | solution.py:83
  239.2 25.7 %copy-start.33 = (f32[1,1152]{1,0:T(1,128)S(1)}, f32[1,1152]{1,0:T(1,128)}, u32[]{:S(2)}) copy-start(f32[1,1152]{1,0:T(1,128)} %get-tuple-element.259) | copy-start | bytes 13828
  265.0 5.9 %copy-start.7 = (bf16[4,48,1536]{2,1,0:T(8,128)(2,1)}, bf16[4,48,1536]{2,1,0:T(8,128)(2,1)S(1)}, u32[]{:S(2)}) copy-start(bf16[4,48,1536]{2,1,0:T(8,128)(2,1)S(1)} %collective-permute-done.16.refs_1_) | copy-start | bytes 1769476
  265.0 5.9 %copy-start.8 = (bf16[4,48,1536]{2,1,0:T(8,128)(2,1)}, bf16[4,48,1536]{2,1,0:T(8,128)(2,1)S(1)}, u32[]{:S(2)}) copy-start(bf16[4,48,1536]{2,1,0:T(8,128)(2,1)S(1)} %collective-permute-done.17.refs_3_) | copy-start | bytes 1769476
  266.2 13.2 %copy-start.34 = (f32[1,1152]{1,0:T(1,128)S(1)}, f32[1,1152]{1,0:T(1,128)}, u32[]{:S(2)}) copy-start(f32[1,1152]{1,0:T(1,128)} %get-tuple-element.260) | copy-start | bytes 13828
  270.9 7.0 %copy-start.32 = (bf16[4,24,1920]{2,1,0:T(8,128)(2,1)S(1)}, bf16[4,24,1920]{2,1,0:T(8,128)(2,1)}, u32[]{:S(2)}) copy-start(bf16[4,24,1920]{2,1,0:T(8,128)(2,1)} %get-tuple-element.255) | copy-start | bytes 1105924
  274.4 21.5 %collective-permute-start.23 = (bf16[16,24,1152]{2,1,0:T(8,128)(2,1)}, bf16[16,24,1152]{2,1,0:T(8,128)(2,1)S(1)}, u32[]{:S(2)}, u32[]{:S(2)}) collective-permute-start(bf16[16,24,1152]{2,1,0:T(8,128)(2,1)} %get-tuple-element.256), channel_id=1, source_target_pairs={{0,1},{1,0},{2,3},{3,2},{4,5},{5,4},{6,7},{7,6},{8,9},{9,8},{10,11... | collective-permute-start | bytes 2654216 | tf_op jit(solution)/shard_map/ppermute | solution.py:83
  274.4 21.4 %collective-permute-start.19 = (bf16[2,48,3072]{2,1,0:T(8,128)(2,1)}, bf16[2,48,3072]{2,1,0:T(8,128)(2,1)S(1)}, u32[]{:S(2)}, u32[]{:S(2)}) collective-permute-start(bf16[2,48,3072]{2,1,0:T(8,128)(2,1)} %get-tuple-element.252), channel_id=1, source_target_pairs={{0,2},{1,3},{2,0},{3,1},{4,6},{5,7},{6,4},{7,5},{8,10},{9,11},{10,... | collective-permute-start | bytes 1769480 | tf_op jit(solution)/shard_map/ppermute | solution.py:83
  275.9 18.3 %collective-permute-start.20 = (bf16[4,24,1920]{2,1,0:T(8,128)(2,1)}, bf16[4,24,1920]{2,1,0:T(8,128)(2,1)S(1)}, u32[]{:S(2)}, u32[]{:S(2)}) collective-permute-start(bf16[4,24,1920]{2,1,0:T(8,128)(2,1)} %get-tuple-element.253), channel_id=1, source_target_pairs={{0,8},{1,9},{2,10},{3,11},{4,12},{5,13},{6,14},{7,15},{8,0},{9,1},... | collective-permute-start | bytes 1105928 | tf_op jit(solution)/shard_map/ppermute | solution.py:83
  277.3 18.6 %collective-permute-start.21 = (bf16[4,24,1920]{2,1,0:T(8,128)(2,1)}, bf16[4,24,1920]{2,1,0:T(8,128)(2,1)S(1)}, u32[]{:S(2)}, u32[]{:S(2)}) collective-permute-start(bf16[4,24,1920]{2,1,0:T(8,128)(2,1)} %get-tuple-element.254), channel_id=1, source_target_pairs={{0,16},{1,17},{2,18},{3,19},{4,20},{5,21},{6,22},{7,23},{8,24},{9,... | collective-permute-start | bytes 1105928 | tf_op jit(solution)/shard_map/ppermute | solution.py:83
  277.9 18.0 %collective-permute-start.22 = (bf16[4,24,1920]{2,1,0:T(8,128)(2,1)S(1)}, bf16[4,24,1920]{2,1,0:T(8,128)(2,1)S(1)}, u32[]{:S(2)}, u32[]{:S(2)}) collective-permute-start(bf16[4,24,1920]{2,1,0:T(8,128)(2,1)S(1)} %copy-done.32), channel_id=1, source_target_pairs={{0,24},{1,25},{2,26},{3,27},{4,28},{5,29},{6,30},{7,31},{8,16},{9,... | collective-permute-start | bytes 1105928 | tf_op jit(solution)/shard_map/ppermute | solution.py:83
  279.4 14.7 %copy-start.28 = (f32[1,768]{1,0:T(1,128)S(1)}, f32[1,768]{1,0:T(1,128)}, u32[]{:S(2)}) copy-start(f32[1,768]{1,0:T(1,128)} %get-tuple-element.261) | copy-start | bytes 9220
  279.5 16.4 %copy-start.29 = (f32[1,768]{1,0:T(1,128)S(1)}, f32[1,768]{1,0:T(1,128)}, u32[]{:S(2)}) copy-start(f32[1,768]{1,0:T(1,128)} %get-tuple-element.258) | copy-start | bytes 9220
  279.5 18.0 %copy-start.27 = (f32[1,768]{1,0:T(1,128)S(1)}, f32[1,768]{1,0:T(1,128)}, u32[]{:S(2)}) copy-start(f32[1,768]{1,0:T(1,128)} %get-tuple-element.263) | copy-start | bytes 9220
  279.5 18.0 %copy-start.26 = (f32[1,768]{1,0:T(1,128)S(1)}, f32[1,768]{1,0:T(1,128)}, u32[]{:S(2)}) copy-start(f32[1,768]{1,0:T(1,128)} %get-tuple-element.264) | copy-start | bytes 9220
  279.5 18.3 %copy-start.9 = (bf16[2,48,3072]{2,1,0:T(8,128)(2,1)S(1)}, bf16[2,48,3072]{2,1,0:T(8,128)(2,1)}, u32[]{:S(2)}) copy-start(bf16[2,48,3072]{2,1,0:T(8,128)(2,1)} %get-tuple-element.267) | copy-start | bytes 1769476
  294.2 4.4 %copy-start.10 = (bf16[4,24,1920]{2,1,0:T(8,128)(2,1)}, bf16[4,24,1920]{2,1,0:T(8,128)(2,1)S(1)}, u32[]{:S(2)}) copy-start(bf16[4,24,1920]{2,1,0:T(8,128)(2,1)S(1)} %collective-permute-done.20.refs_1_) | copy-start | bytes 1105924
  295.9 2.8 copy-start.11
  295.9 2.8 copy-start.12
  295.9 19.1 %copy-start.5 = (bf16[16,24,1152]{2,1,0:T(8,128)(2,1)}, bf16[16,24,1152]{2,1,0:T(8,128)(2,1)S(1)}, u32[]{:S(2)}) copy-start(bf16[16,24,1152]{2,1,0:T(8,128)(2,1)S(1)} %collective-permute-done.23) | copy-start | bytes 2654212
  301.5 21.6 %collective-permute-start.24 = (bf16[1,48,3072]{2,1,0:T(8,128)(2,1)}, bf16[1,48,3072]{2,1,0:T(8,128)(2,1)S(1)}, u32[]{:S(2)}, u32[]{:S(2)}) collective-permute-start(bf16[1,48,3072]{2,1,0:T(8,128)(2,1)} %add_convert_fusion), channel_id=1, source_target_pairs={{0,4},{1,5},{2,6},{3,7},{4,0},{5,1},{6,2},{7,3},{8,12},{9,13},{10,... | collective-permute-start | bytes 884744 | tf_op jit(solution)/shard_map/ppermute | solution.py:83
  302.4 20.6 %collective-permute-start.28 = (bf16[16,24,128]{2,1,0:T(8,128)(2,1)S(1)}, bf16[16,24,128]{2,1,0:T(8,128)(2,1)S(1)}, u32[]{:S(2)}, u32[]{:S(2)}) collective-permute-start(bf16[16,24,128]{2,1,0:T(8,128)(2,1)S(1)} %pad.25), channel_id=1, source_target_pairs={{0,1},{1,0},{2,3},{3,2},{4,5},{5,4},{6,7},{7,6},{8,9},{9,8},{10,11... | collective-permute-start | bytes 294920 | tf_op jit(solution)/shard_map/ppermute | solution.py:83
  302.5 13.2 %collective-permute-start.25 = (bf16[24,1920]{1,0:T(8,128)(2,1)}, bf16[24,1920]{1,0:T(8,128)(2,1)S(1)}, u32[]{:S(2)}, u32[]{:S(2)}) collective-permute-start(bf16[24,1920]{1,0:T(8,128)(2,1)} %get-tuple-element.278), channel_id=1, source_target_pairs={{0,2},{1,3},{2,0},{3,1},{4,6},{5,7},{6,4},{7,5},{8,10},{9,11},{10,... | collective-permute-start | bytes 276488 | tf_op jit(solution)/shard_map/ppermute | solution.py:83
  303.9 19.1 %collective-permute-start.26 = (bf16[24,1920]{1,0:T(8,128)(2,1)}, bf16[24,1920]{1,0:T(8,128)(2,1)S(1)}, u32[]{:S(2)}, u32[]{:S(2)}) collective-permute-start(bf16[24,1920]{1,0:T(8,128)(2,1)} %get-tuple-element.279), channel_id=1, source_target_pairs={{0,4},{1,5},{2,6},{3,7},{4,0},{5,1},{6,2},{7,3},{8,12},{9,13},{10,... | collective-permute-start | bytes 276488 | tf_op jit(solution)/shard_map/ppermute | solution.py:83
  305.0 18.1 %collective-permute-start.27 = (bf16[24,1920]{1,0:T(8,128)(2,1)}, bf16[24,1920]{1,0:T(8,128)(2,1)S(1)}, u32[]{:S(2)}, u32[]{:S(2)}) collective-permute-start(bf16[24,1920]{1,0:T(8,128)(2,1)} %get-tuple-element.280), channel_id=1, source_target_pairs={{0,6},{1,7},{2,4},{3,5},{4,2},{5,3},{6,0},{7,1},{8,14},{9,15},{10,... | collective-permute-start | bytes 276488 | tf_op jit(solution)/shard_map/ppermute | solution.py:83
  315.7 15.9 %copy-start.17 = (f32[24,1920]{1,0:T(8,128)S(1)}, f32[24,1920]{1,0:T(8,128)}, u32[]{:S(2)}) copy-start(f32[24,1920]{1,0:T(8,128)} %get-tuple-element.307) | copy-start | bytes 552964
  327.9 14.2 %collective-permute-start.29 = (f32[1,24,3072]{2,1,0:T(8,128)S(1)}, f32[1,24,3072]{2,1,0:T(8,128)S(1)}, u32[]{:S(2)}, u32[]{:S(2)}) collective-permute-start(f32[1,24,3072]{2,1,0:T(8,128)S(1)} %constant_dynamic-slice_fusion), channel_id=1, source_target_pairs={{0,1},{1,0},{2,3},{3,2},{4,5},{5,4},{6,7},{7,6},{8,9},{9,8},{10,11... | collective-permute-start | bytes 884744 | tf_op jit(solution)/shard_map/ppermute | solution.py:83
  328.0 14.0 %collective-permute-start.30 = (bf16[4,24,1280]{2,1,0:T(8,128)(2,1)}, bf16[4,24,1280]{2,1,0:T(8,128)(2,1)S(1)}, u32[]{:S(2)}, u32[]{:S(2)}) collective-permute-start(bf16[4,24,1280]{2,1,0:T(8,128)(2,1)} %get-tuple-element.291), channel_id=1, source_target_pairs={{0,8},{1,9},{2,10},{3,11},{4,12},{5,13},{6,14},{7,15},{8,0},{9,1},... | collective-permute-start | bytes 737288 | tf_op jit(solution)/shard_map/ppermute | solution.py:83
  328.6 13.5 %collective-permute-start.31 = (bf16[4,24,1280]{2,1,0:T(8,128)(2,1)}, bf16[4,24,1280]{2,1,0:T(8,128)(2,1)S(1)}, u32[]{:S(2)}, u32[]{:S(2)}) collective-permute-start(bf16[4,24,1280]{2,1,0:T(8,128)(2,1)} %get-tuple-element.292), channel_id=1, source_target_pairs={{0,16},{1,17},{2,18},{3,19},{4,20},{5,21},{6,22},{7,23},{8,24},{9,... | collective-permute-start | bytes 737288 | tf_op jit(solution)/shard_map/ppermute | solution.py:83
  330.0 12.1 %collective-permute-start.32 = (bf16[4,24,1280]{2,1,0:T(8,128)(2,1)}, bf16[4,24,1280]{2,1,0:T(8,128)(2,1)S(1)}, u32[]{:S(2)}, u32[]{:S(2)}) collective-permute-start(bf16[4,24,1280]{2,1,0:T(8,128)(2,1)} %get-tuple-element.293), channel_id=1, source_target_pairs={{0,24},{1,25},{2,26},{3,27},{4,28},{5,29},{6,30},{7,31},{8,16},{9,... | collective-permute-start | bytes 737288 | tf_op jit(solution)/shard_map/ppermute | solution.py:83
  331.6 9.8 %copy-start.6 = (f32[24,1920]{1,0:T(8,128)}, f32[24,1920]{1,0:T(8,128)S(1)}, u32[]{:S(2)}) copy-start(f32[24,1920]{1,0:T(8,128)S(1)} %add_add_fusion) | copy-start | bytes 552964
  345.6 18.7 %collective-permute-start.33 = (bf16[24,1280]{1,0:T(8,128)(2,1)}, bf16[24,1280]{1,0:T(8,128)(2,1)S(1)}, u32[]{:S(2)}, u32[]{:S(2)}) collective-permute-start(bf16[24,1280]{1,0:T(8,128)(2,1)} %get-tuple-element.302), channel_id=1, source_target_pairs={{0,2},{1,3},{2,0},{3,1},{4,6},{5,7},{6,4},{7,5},{8,10},{9,11},{10,... | collective-permute-start | bytes 184328 | tf_op jit(solution)/shard_map/ppermute | solution.py:83
  348.0 16.3 %collective-permute-start.34 = (bf16[24,1280]{1,0:T(8,128)(2,1)}, bf16[24,1280]{1,0:T(8,128)(2,1)}, u32[]{:S(2)}, u32[]{:S(2)}) collective-permute-start(bf16[24,1280]{1,0:T(8,128)(2,1)} %get-tuple-element.303), channel_id=1, source_target_pairs={{0,4},{1,5},{2,6},{3,7},{4,0},{5,1},{6,2},{7,3},{8,12},{9,13},{10,... | collective-permute-start | bytes 184328 | tf_op jit(solution)/shard_map/ppermute | solution.py:83
  348.5 15.8 %collective-permute-start.35 = (bf16[24,1280]{1,0:T(8,128)(2,1)}, bf16[24,1280]{1,0:T(8,128)(2,1)}, u32[]{:S(2)}, u32[]{:S(2)}) collective-permute-start(bf16[24,1280]{1,0:T(8,128)(2,1)} %get-tuple-element.304), channel_id=1, source_target_pairs={{0,6},{1,7},{2,4},{3,5},{4,2},{5,3},{6,0},{7,1},{8,14},{9,15},{10,... | collective-permute-start | bytes 184328 | tf_op jit(solution)/shard_map/ppermute | solution.py:83
  360.8 3.5 copy-start.20
  360.8 5.6 %copy-start.13 = (f32[24,2304]{1,0:T(8,128)S(1)}, f32[24,2304]{1,0:T(8,128)}, u32[]{:S(2)}) copy-start(f32[24,2304]{1,0:T(8,128)} %constant_dynamic-update-slice_fusion.70) | copy-start | bytes 663556
  (8 other events, 7.0 us)
Sparse Core Ops, SparseCore 0:
  21.1 92.4 all-gather.1

commit v3 on v2

--- a/solution.py
+++ b/solution.py
@@ -105,20 +105,15 @@
                 self.advance(flight[0], got)
         return out
 
-    def behind(self, value):
-        value, _ = lax.optimization_barrier((value, [array for _, sends, _ in self.waiting for array, _ in sends]))
-        return value
-
-    def land(self):
-        held, self.flying = self.flying, []
-        self.finish(1)
-        self.flying += held
-
-    def finish(self, turns=1 << 30):
-        while (self.waiting or self.flying) and turns > 0:
-            turns -= 1
+    def finish(self, turns=None):
+        turn = 0
+        while (self.waiting or self.flying) and turn != turns:
+            turn += 1
             self.depart()
-            landed, self.flying = self.flying, []
+            for flight in self.flying:
+                flight[2] -= 1
+            landed = [flight for flight in self.flying if turns is None or flight[2] <= 0]
+            self.flying = [flight for flight in self.flying if not (turns is None or flight[2] <= 0)]
             cames = lax.optimization_barrier([flight[1] for flight in landed])
             for flight, came in zip(landed, cames):
                 self.advance(flight[0], came)
@@ -298,102 +293,93 @@
     )(where, *arrays)
 
 
-def fold_first_kernel(where, keep, came, keep_a, send_a, keep_b, send_b):
-    slow, fast = where[1] // 2, where[1] % 2
-    cut = keep_a.shape[-1]
-    for other in range(2):
-        for place, out, lanes in (
-            (slow * 2 + other, keep_a, slice(0, cut)),
-            ((slow ^ 1) * 2 + other, send_a, slice(0, cut)),
-            (other * 2 + fast, keep_b, slice(cut, None)),
-            (other * 2 + (fast ^ 1), send_b, slice(cut, None)),
-        ):
-            out[other] = keep[place, :, lanes] + came[place, :, lanes]
+def send_sum_kernel(where, *refs, sizes):
+    at = 0
+    for size, out in zip(sizes, refs[sum(sizes) :]):
+        out[...] = sum(term[...].astype(f32) for term in refs[at : at + size]).astype(out.dtype)
+        at += size
 
 
 def fold_first(where, keep, came):
-    blocks, rows, columns = keep.shape
-    left = blocks // 4
-    cut = columns // 256 * 128
-    whole = pl.BlockSpec((4, None, rows, columns), lambda j, where: (0, j, 0, 0))
-    spec = lambda w: pl.BlockSpec((2, None, rows, w), lambda j, where: (0, j, 0, 0))
-    widths = [cut, cut, columns - cut, columns - cut]
+    _, _, left, rows, columns = keep.shape
+    cut = columns // 2
+    spec_a = pl.BlockSpec((None, 2, None, rows, cut), lambda j, where: ((where[1] // 2) ^ 1, 0, j, 0, 0))
+    spec_b = pl.BlockSpec((2, None, None, rows, cut), lambda j, where: (0, (where[1] % 2) ^ 1, j, 0, 1))
     return pl.pallas_call(
-        fold_first_kernel,
+        functools.partial(send_sum_kernel, sizes=[2, 2]),
         grid_spec=pltpu.PrefetchScalarGridSpec(
             num_scalar_prefetch=1,
             grid=(left,),
-            in_specs=[whole, whole],
-            out_specs=[spec(w) for w in widths],
-        ),
-        out_shape=[shape_of((2, left, rows, w), bf16) for w in widths],
+            in_specs=[spec_a, spec_a, spec_b, spec_b],
+            out_specs=[pl.BlockSpec((2, None, rows, cut), lambda j, where: (0, j, 0, 0))] * 2,
+        ),
+        out_shape=[shape_of((2, left, rows, cut), bf16)] * 2,
         compiler_params=params(1),
         cost_estimate=cost(),
         name="fold_first",
-    )(where, *(array.reshape(4, left, rows, columns) for array in (keep, came)))
-
-
-def fold_second_kernel(where, keep_a, came_a, keep_b, came_b, own_a, send_a, own_b, send_b):
-    slow, fast = where[1] // 2, where[1] % 2
-    for keep, came, mine, own, send in (
-        (keep_a, came_a, fast, own_a, send_a),
-        (keep_b, came_b, slow, own_b, send_b),
-    ):
-        for place, out in ((mine, own), (mine ^ 1, send)):
-            out[...] = keep[place] + came[place]
-
-
-def fold_second(where, keep_a, came_a, keep_b, came_b):
-    arrays = (keep_a, came_a, keep_b, came_b)
-    _, left, rows, _ = keep_a.shape
-    widths = [keep_a.shape[3], keep_a.shape[3], keep_b.shape[3], keep_b.shape[3]]
+    )(where, keep, came, keep, came)
+
+
+def fold_second(where, keep, came, came_a, came_b):
+    _, _, left, rows, columns = keep.shape
+    cut = columns // 2
+    spec_a = pl.BlockSpec(
+        (None, None, None, rows, cut), lambda j, where: (where[1] // 2, (where[1] % 2) ^ 1, j, 0, 0)
+    )
+    spec_b = pl.BlockSpec(
+        (None, None, None, rows, cut), lambda j, where: ((where[1] // 2) ^ 1, where[1] % 2, j, 0, 1)
+    )
+    half_a = pl.BlockSpec((None, None, rows, cut), lambda j, where: ((where[1] % 2) ^ 1, j, 0, 0))
+    half_b = pl.BlockSpec((None, None, rows, cut), lambda j, where: ((where[1] // 2) ^ 1, j, 0, 0))
     return pl.pallas_call(
-        fold_second_kernel,
+        functools.partial(send_sum_kernel, sizes=[3, 3]),
         grid_spec=pltpu.PrefetchScalarGridSpec(
             num_scalar_prefetch=1,
             grid=(left,),
-            in_specs=[pl.BlockSpec((2, None, rows, w), lambda j, where: (0, j, 0, 0)) for w in widths],
-            out_specs=[pl.BlockSpec((None, rows, w), lambda j, where: (j, 0, 0)) for w in widths],
-        ),
-        out_shape=[shape_of((left, rows, w), bf16) for w in widths],
+            in_specs=[spec_a, spec_a, half_a, spec_b, spec_b, half_b],
+            out_specs=[pl.BlockSpec((None, rows, cut), lambda j, where: (j, 0, 0))] * 2,
+        ),
+        out_shape=[shape_of((left, rows, cut), bf16)] * 2,
         compiler_params=params(1),
         cost_estimate=cost(),
         name="fold_second",
-    )(where, *arrays)
-
-
-def line_first_kernel(where, *refs, sizes):
-    keep, send = refs[sum(sizes) :]
+    )(where, keep, came, came_a, keep, came, came_b)
+
+
+def line_first_kernel(where, *refs):
+    *terms, keep, send = refs
     fast = where[2] % 2
+    cut = terms[0].shape[-1]
     for slow in range(2):
         for place, out in ((slow * 2 + fast, keep), (slow * 2 + (fast ^ 1), send)):
-            at = start = 0
-            for size in sizes:
-                terms = refs[at : at + size]
-                at += size
-                lanes = slice(start, start + terms[0].shape[2])
-                start += terms[0].shape[2]
-                first, second = terms
-                out[slow, :, lanes] = first[place] + second[place]
-
-
-def line_first(where, groups):
-    size, rows, _ = groups[0][0].shape
-    columns = sum(group[0].shape[2] for group in groups)
-    arrays = [array for group in groups for array in group]
+            for half in range(2):
+                own = terms[4 * half : 4 * half + 4]
+                lanes = slice(half * cut, (half + 1) * cut)
+                out[slow, :, lanes] = sum(term[place].astype(f32) for term in own).astype(out.dtype)
+
+
+def line_first(where, keep, came, came_a, came_b, last_a, last_b):
+    _, _, size, rows, columns = keep.shape
+    cut = columns // 2
+    whole = lambda half: pl.BlockSpec(
+        (None, None, size, rows, cut), lambda j, where: (where[1] // 2, where[1] % 2, 0, 0, half)
+    )
+    half_a = pl.BlockSpec((None, size, rows, cut), lambda j, where: (where[1] % 2, 0, 0, 0))
+    half_b = pl.BlockSpec((None, size, rows, cut), lambda j, where: (where[1] // 2, 0, 0, 0))
+    last = pl.BlockSpec((size, rows, cut), lambda j, where: (0, 0, 0))
     return pl.pallas_call(
-        functools.partial(line_first_kernel, sizes=[len(group) for group in groups]),
+        line_first_kernel,
         grid_spec=pltpu.PrefetchScalarGridSpec(
             num_scalar_prefetch=1,
             grid=(1,),
-            in_specs=[once(array.shape) for array in arrays],
+            in_specs=[whole(0), whole(0), half_a, last, whole(1), whole(1), half_b, last],
             out_specs=[once((size // 2, rows, columns))] * 2,
         ),
         out_shape=[shape_of((size // 2, rows, columns), bf16)] * 2,
         compiler_params=params(1),
         cost_estimate=cost(),
         name="line_first",
-    )(where, *arrays)
+    )(where, keep, came, came_a, last_a, keep, came, came_b, last_b)
 
 
 def swap_steps(send, mesh):
@@ -416,19 +402,20 @@
     count = mesh.size
     core, outer, rest = bit_groups(mesh)
     (came,) = yield [(send, partners(count, core)[0][1])]
-    shape = (count // 2, keep.shape[0] * 2 // count, keep.shape[1])
+    shape = (2, 2, 1 << len(rest[0]), keep.shape[0] * 2 // count, keep.shape[1])
+    keep, came = keep.reshape(shape), came.reshape(shape)
     fast, slow = (partners(count, [bit])[0][1] for bit in outer)
-    keep_a, send_a, keep_b, send_b = fold_first(where, keep.reshape(shape), came.reshape(shape))
+    send_a, send_b = fold_first(where, keep, came)
     came_a, came_b = yield [(send_a, slow), (send_b, fast)]
-    own_a, send_a, own_b, send_b = fold_second(where, keep_a, came_a, keep_b, came_b)
-    came_a, came_b = yield [(send_a, fast), (send_b, slow)]
-    keep, send = line_first(where, [[own_a, came_a], [own_b, came_b]])
+    send_a, send_b = fold_second(where, keep, came, came_a, came_b)
+    last_a, last_b = yield [(send_a, fast), (send_b, slow)]
+    keep, send = line_first(where, keep, came, came_a, came_b, last_a, last_b)
     (came,) = yield [(send, partners(count, [rest[0][0]])[0][1])]
     me = lax.axis_index(AXES)
     spot = position(me, [rest[0][1]])
     both = [keep, came]
     (last,) = yield [(total(both, 0, spot ^ 1, bf16), partners(count, [rest[0][1]])[0][1])]
-    done = (total(both, 0, spot, f32) + last.astype(f32)).reshape(2, shape[1] // 2, shape[2])
+    done = (total(both, 0, spot, f32) + last.astype(f32)).reshape(2, shape[3] // 2, shape[4])
     spot = position(me, core)
     (came,) = yield [(pick(done, 0, spot ^ 1), partners(count, core)[0][1])]
     own, came = pick(done, 0, spot)[0], came[0]
@@ -630,28 +617,29 @@
     )(valid, *arrays)
 
 
-def attend_back_kernel(
-    where, joined, mixed_grad, mixed, raised, inverse, normed, *rest, pairs, extra, cut
-):
+def attend_back_kernel(where, *refs, pairs, extra, cut):
+    lists = [refs[kind * pairs : (kind + 1) * pairs] for kind in range(5)]
+    joined, mixed_grad, mixed, raised, inverse = lists
+    normed, *rest = refs[5 * pairs :]
     if extra:
         mixed_a, mixed_b, low_grad, joined_grad, column, *outs, held, scaled, total, total_out = rest
     else:
         joined_grad, column, *outs, held, scaled, total = rest
     item = pl.program_id(0)
-    seq, span = joined.shape
-    padded = raised.shape[2] // 2
-    first = lax.broadcasted_iota(jnp.int32, (BTILE, 128), 1) < 64
-    places = [(pair, start) for pair in range(pairs) for start in range(0, seq, BTILE)]
+    seq, span = joined_grad.shape
+    padded = raised[0].shape[1] // 2
+    tile = BTILE if seq % BTILE == 0 else seq
+    first = lax.broadcasted_iota(jnp.int32, (tile, 128), 1) < 64
+    places = [(pair, start) for pair in range(pairs) for start in range(0, seq, tile)]
     keys, values = {}, {}
 
     def prob_grad_at(pair, start):
-        at = pair * 384
         if pair not in keys:
-            keys[pair] = two_heads(joined[:, at + 128 : at + 256], padded)
-            values[pair] = two_heads(joined[:, at + 256 : at + 384], padded)
-        rows, lanes = slice(start, start + BTILE), slice(pair * 128, (pair + 1) * 128)
-        grad = (mixed_grad[rows, lanes].astype(f32) * inverse[rows, lanes]).astype(bf16)
-        scaled[rows, lanes] = grad
+            keys[pair] = two_heads(joined[pair][:, 128:256], padded)
+            values[pair] = two_heads(joined[pair][:, 256:], padded)
+        rows = slice(start, start + tile)
+        grad = (mixed_grad[pair][rows, :].astype(f32) * inverse[pair][rows, :]).astype(bf16)
+        scaled[pair, rows, :] = grad
         return grad, dot(grad, values[pair], NT)
 
     def own_half(both):
@@ -659,28 +647,28 @@
 
     ahead = [prob_grad_at(*place) for place in places[:BAHEAD]]
     for index, (pair, start) in enumerate(places):
-        rows, lanes = slice(start, start + BTILE), slice(pair * 128, (pair + 1) * 128)
+        rows = slice(start, start + tile)
         at = pair * 384
         if index + BAHEAD < len(places):
             ahead.append(prob_grad_at(*places[index + BAHEAD]))
         grad, prob_grad = ahead.pop(0)
-        product = grad.astype(f32) * mixed[rows, lanes].astype(f32)
+        product = grad.astype(f32) * mixed[pair][rows, :].astype(f32)
         zero = jnp.zeros_like(product)
         halves = []
         for head in range(2):
             own = jnp.where(first, product, zero) if head == 0 else jnp.where(first, zero, product)
             centre = jnp.sum(own, 1, keepdims=True)
             half = slice(head * padded, (head + 1) * padded)
-            halves.append((raised[pair, rows, half].astype(f32) * (prob_grad[:, half] - centre)).astype(bf16))
+            halves.append((raised[pair][rows, half].astype(f32) * (prob_grad[:, half] - centre)).astype(bf16))
         score_grad = jnp.concatenate(halves, 1)
         held[rows, :] = score_grad
         joined_grad[rows, at : at + 128] = (dot(score_grad, keys[pair], NN) * 0.125).astype(bf16)
-        if start + BTILE == seq:
+        if start + tile == seq:
             joined_grad[:, at + 128 : at + 256] = (
-                own_half(dot(joined[:, at : at + 128].T, held[...], NN)) * 0.125
+                own_half(dot(joined[pair][:, :128].T, held[...], NN)) * 0.125
             ).astype(bf16)
             joined_grad[:, at + 256 : at + 384] = own_half(
-                dot(scaled[:, lanes].T, raised[pair], NN)
+                dot(scaled[pair].T, raised[pair][...], NN)
             ).astype(bf16)
 
     value = joined_grad[...]
@@ -697,11 +685,17 @@
             store_cut(where[0], outs, slice(span, span + total_out.shape[1]), total_out[...], cut)
 
 
-def attend_back(mixed_grad, where, joined, mixed, raised, inverse, normed, seq, part, cut, others=()):
-    rows, span = joined.shape
-    width = normed.shape[1]
-    items, pairs, _, keys = raised.shape
+def attend_back(mixed_grad, where, joined, mixed, raised, inverse, normed, seq, part, chosen, cut, others=()):
+    rows, width = normed.shape
+    items, in_part, _, keys = raised.shape
+    pairs = len(chosen)
+    span = 384 * pairs
     row = lambda w, off=0: pl.BlockSpec((seq, w), lambda i, *_: (i, off))
+    each = lambda w, off=0: [row(w, off + pair) for pair in chosen]
+    weights = [
+        pl.BlockSpec((None, None, seq, keys), functools.partial(lambda at, i, *_: (i, at, 0, 0), pair))
+        for pair in chosen
+    ]
     columns = span + (width if others else 0)
     specs, shapes = cut_shapes(width, columns, columns, lambda j: 0, cut)
     return pl.pallas_call(
@@ -710,18 +704,13 @@
             num_scalar_prefetch=1,
             grid=(items,),
             in_specs=[
-                row(span),
-                row(span // 3, part),
-                row(span // 3),
-                pl.BlockSpec((None, pairs, seq, keys), lambda i, *_: (i, 0, 0, 0)),
-                row(span // 3),
-                row(width),
+                *each(384), *each(128, part * in_part), *each(128), *weights, *each(128), row(width)
             ]
             + [row(array.shape[1]) for array in others],
             out_specs=[row(span), pl.BlockSpec((1, span), lambda i, *_: (0, 0))] + specs,
             scratch_shapes=[
                 pltpu.VMEM((seq, keys), bf16),
-                pltpu.VMEM((seq, span // 3), bf16),
+                pltpu.VMEM((pairs, seq, 128), bf16),
                 pltpu.VMEM((width, span), f32),
             ]
             + ([pltpu.VMEM((width, width), f32)] if others else []),
@@ -730,7 +719,10 @@
         compiler_params=params(1),
         cost_estimate=cost(),
         name="attend_back",
-    )(where, joined, mixed_grad, mixed, raised, inverse, normed, *others)
+    )(
+        where, *[joined] * pairs, *[mixed_grad] * pairs, *[mixed] * pairs, *[raised] * pairs,
+        *[inverse] * pairs, normed, *others,
+    )
 
 
 def mlp_kernel(
@@ -910,15 +902,18 @@
     )(valid, hidden_grad, both, middle, cotangent, gain, weight)
 
 
-def input_back_kernel(
-    grad_a, grad_b, weight_a, weight_b, tokens, low_grad, gain, input_grad, gain_sum, shift_sum, *, sub
-):
-    span = grad_a.shape[1]
+def input_back_kernel(*refs, spans, sub):
+    grads = refs[: len(spans)]
+    weights = refs[len(spans) : len(spans) + 2]
+    tokens, low_grad, gain, input_grad, gain_sum, shift_sum = refs[len(spans) + 2 :]
     tile, width = tokens.shape
 
     def ahead_of(start):
         rows = slice(start, start + sub)
-        return dot(grad_a[rows, :], weight_a[:, :span], NT) + dot(grad_b[rows, :], weight_b[:, :span], NT)
+        terms = [
+            dot(grad[rows, :], weights[which][:, lanes], NT) for grad, (which, lanes) in zip(grads, spans)
+        ]
+        return sum(terms[1:], terms[0])
 
     starts = list(range(0, tile, sub))
     ahead = [ahead_of(0)]
@@ -936,23 +931,25 @@
         accumulate(ref, value, pl.program_id(0) == 0)
 
 
-def input_back(grad_a, grad_b, weight_a, weight_b, tokens, low_grad, gain, seq):
+def input_back(last, others, spans, weights, tokens, low_grad, gain, seq):
     rows, width = tokens.shape
     tile = LTILE if seq % LTILE == 0 else seq
     sub = LSUB if tile % LSUB == 0 else tile
     row = lambda w: pl.BlockSpec((tile, w), lambda i: (i, 0))
     fixed = pl.BlockSpec((1, width), lambda i: (0, 0))
+    grads = [*others, last]
     return pl.pallas_call(
-        functools.partial(input_back_kernel, sub=sub),
+        functools.partial(input_back_kernel, spans=spans, sub=sub),
         grid=(rows // tile,),
-        in_specs=[row(grad_a.shape[1]), row(grad_b.shape[1]), once(weight_a.shape), once(weight_b.shape)]
+        in_specs=[row(grad.shape[1]) for grad in grads]
+        + [once(weight.shape) for weight in weights]
         + [row(width), row(width), once((1, width))],
         out_specs=[row(width), fixed, fixed],
         out_shape=[shape_of((rows, width), bf16)] + [shape_of((1, width), f32)] * 2,
         compiler_params=params(1),
         cost_estimate=cost(),
         name="input_back",
-    )(grad_a, grad_b, weight_a, weight_b, tokens, low_grad, gain)
+    )(*grads, *weights, tokens, low_grad, gain)
 
 
 def local(mesh, tokens, cotangent, group, text_len, qkv_w, out_w, mlp_in, mlp_out, gains, biases):
@@ -989,12 +986,14 @@
 
 
     def by_pairs(matrix, part):
-        pieces = []
-        for pair in range(part * 3, part * 3 + 3):
-            for place in range(3):
-                at = place * width + pair * 128
-                pieces.append(matrix[:, at : at + 128])
-        return jnp.concatenate(pieces, 1)
+        rows = matrix.shape[0]
+        cubes = matrix.reshape(rows, 3, 2, half // 128, 128)[:, :, part]
+        return cubes.transpose(0, 2, 1, 3).reshape(rows, span)
+
+    def by_kind(part_a, part_b):
+        rows = part_a.shape[0]
+        cubes = [piece[:, :span].reshape(rows, half // 128, 3, 128) for piece in (part_a, part_b)]
+        return jnp.stack(cubes, 1).transpose(0, 3, 1, 2, 4).reshape(rows, 3 * width)
 
     own_up = mlp_in.reshape(share, count, chunks, share).transpose(0, 2, 1, 3).reshape(share, wide)
     own_down = mlp_out.reshape(chunks, share, width).transpose(1, 0, 2).reshape(share, wide)
@@ -1005,18 +1004,14 @@
     small_rows = -(-small.shape[0] // 128)
     padded = jnp.pad(small, (0, small_rows * 128 - small.shape[0])).reshape(small_rows, 128)
     padded = jnp.pad(padded, ((0, share - small_rows), (0, 0)))
-    job = flights.add(
-        gather_steps(jnp.concatenate([by_pairs(own_qkv, 0), padded], 1), mesh, [*others, outer, core]), []
-    )
-    flights.finish(len(others))
-    own_both = flights.behind(own_both)
     both = lax.all_gather(own_both, AXES, axis=0, tiled=True)
+    own_first = jnp.concatenate([by_pairs(own_qkv, 0), padded], 1)
     own_second = jnp.concatenate([by_pairs(own_qkv, 1), out_w.reshape(share, width)], 1)
     singles = [[bit] for group in reversed(others) for bit in reversed(group)]
-    second_job = flights.add(gather_steps(own_second, mesh, [*singles, outer, core]), [])
-    flights.finish(2)
+    job = flights.add(gather_steps(own_first, mesh, [*others, outer, core]), [])
+    second_job = flights.add(gather_steps(own_second, mesh, [*singles, outer, core]), [1] * len(singles) + [2])
+    flights.finish(len(others) + 2)
     first = job["result"]
-
     small = first[:, span:].reshape(count, share, 128)[:, :small_rows]
     small = small.reshape(count, small_rows * 128).astype(f32)
     edge = gains.shape[0]
@@ -1050,31 +1045,35 @@
     )
     joined_grad_a, qkv_sum_a, *grads_a = flights.run(
         lambda x: attend_back(
-            x, where, joined_a, mixed_a, raised_a, inverse_a, normed, seq, 0, cut, (mixed_a, mixed_b, low_grad)
+            x, where, joined_a, mixed_a, raised_a, inverse_a, normed, seq, 0, range(half // 128), cut,
+            (mixed_a, mixed_b, low_grad),
         ),
         mixed_grad,
     )
     swap_a = swap(grads_a)
     joined_grad_b, qkv_sum_b, *grads_b = flights.run(
-        lambda x: attend_back(x, where, joined_b, mixed_b, raised_b, inverse_b, normed, seq, 1, cut), mixed_grad
+        lambda x: attend_back(
+            x, where, joined_b, mixed_b, raised_b, inverse_b, normed, seq, 1, range(1), cut
+        ),
+        mixed_grad,
     )
     sum_a = sums_after([grads_a], [swap_a])
     swap_b = swap(grads_b)
+    joined_grad_c, qkv_sum_c, *grads_c = flights.run(
+        lambda x: attend_back(
+            x, where, joined_b, mixed_b, raised_b, inverse_b, normed, seq, 1, range(1, half // 128), cut
+        ),
+        mixed_grad,
+    )
+    swap_c = swap(grads_c)
+    spans = ((0, slice(0, span)), (1, slice(0, 384)), (1, slice(384, span)))
     input_grad, gain_one_sum, shift_one_sum = flights.run(
-        lambda x: input_back(joined_grad_a, x, first, second, flat, low_grad, gain_one, seq),
-        joined_grad_b,
-    )
-
-    def by_kind(part_a, part_b):
-        return jnp.concatenate(
-            [
-                piece[:, (3 * pair + place) * 128 : (3 * pair + place + 1) * 128]
-                for place in range(3)
-                for piece in (part_a, part_b)
-                for pair in range(3)
-            ],
-            1,
-        )
+        lambda x: input_back(
+            x, [joined_grad_a, joined_grad_b], spans, [first, second], flat, low_grad, gain_one, seq
+        ),
+        joined_grad_c,
+    )
+    qkv_sum_b = jnp.concatenate([qkv_sum_b, qkv_sum_c], 1)
 
     joined_sums = by_kind(qkv_sum_a, qkv_sum_b)
     up_sum = up_sum.reshape(chunks, count, share).transpose(1, 0, 2).reshape(1, wide)
@@ -1103,8 +1102,9 @@
         swap_small = swap(small)
     else:
         small_job = flights.add(small_sum_steps(small, mesh), [])
-        sum_b = sums_after([grads_b], [swap_b])
-    cuts = [item * seq for item in range(items + 1)]
+        grads_b = [jnp.concatenate([grads_b[0], grads_c[0]], 1)]
+        sum_b = sums_after([grads_b], [None])
+    cuts = [0, items // 2 * seq, rows]
     block_out = None
     for begin, end in zip(cuts, cuts[1:]):
         if begin < end:
@@ -1115,7 +1115,7 @@
                 middle,
             )
             if cut and begin == 0:
-                sum_b = sums_after([grads_b, small], [swap_b, swap_small])
+                sum_b = sums_after([grads_b, grads_c, small], [swap_b, swap_c, swap_small])
     flights.finish()
     total_a, total_b = sum_a["result"], sum_b["result"]
     if cut:

time: 384 us -> 366 us (0.953)
  waiting for transfers between devices: 34.5 us -> 21.3 us
  Pallas kernels: 245 us -> 241 us
    ppermute x36 -> x37, waiting for transfers between devices: 30.5 us -> 21.3 us  [depart(): came = [lax.ppermute(array, AXES, pairs) for array, pairs in sends]]
    unnamed x123 -> x89, local copies, waits for them, and re-layouts: 13.2 us -> 7.33 us
    pallas_call x3 -> x2, Pallas kernels: 24 us -> 19.5 us  [block_out_of(): pl.pallas_call(functools.partial(block_out_kernel, seq=seq, begin=begin),...]
    all_gather x1, waiting for transfers between devices: 3.91 us -> 0.01 us  [local(): both = lax.all_gather(own_both, AXES, axis=0, tiled=True)]
    ppermute x36 -> x37, starting transfers between devices: 37.3 us -> 40.8 us  [depart(): came = [lax.ppermute(array, AXES, pairs) for array, pairs in sends]]
    dynamic_update_slice x20 -> x18, local copies, waits for them, and re-layouts: 9.05 us -> 11 us  [gather_steps(): whole = lax.dynamic_update_slice(whole, got, start)]
    pallas_call x2 -> x3, Pallas kernels: 58.8 us -> 59.6 us  [attend_back(): pl.pallas_call(functools.partial(attend_back_kernel, pairs=pairs, extra=b...]
  transfers between devices with their start and end apart: 37 -> 38, of which waited for: 10 -> 7; matrix products, arithmetic and copies ran while one was open for 7% -> 7% of each run, Pallas kernels for 43% -> 44%
where the time goes in v3:
time: 366 us; the launch traced here: 361 us
  Pallas kernels  241 us (66%)
  starting transfers between devices  40.8 us (11%)
  local copies, waits for them, and re-layouts  38.2 us (10%)
  waiting for transfers between devices  21.3 us (6%)
  between operations  15.5 us (4%)
  other arithmetic  3.66 us (1%)
    pallas_call x3, Pallas kernels, attend_back(): pl.pallas_call(functools.partial(attend_back_kernel, pairs=pairs, extra=b...  59.6 us
    pallas_call x1, Pallas kernels, mlp(): pl.pallas_call(functools.partial(mlp_kernel, seq=seq, tile=tile_of(seq),...  52.5 us
    pallas_call x2, Pallas kernels, attend(): pl.pallas_call(functools.partial(attend_kernel, tile=tile_of(seq), padded...  44.5 us
    ppermute x37, starting transfers between devices, depart(): came = [lax.ppermute(array, AXES, pairs) for array, pairs in sends]  40.8 us
    ppermute x37, waiting for transfers between devices, depart(): came = [lax.ppermute(array, AXES, pairs) for array, pairs in sends]  21.3 us
    pallas_call x1, Pallas kernels, middle_back(): pl.pallas_call(functools.partial(middle_back_kernel, seq=seq, sub=sub), g...  20.6 us
    pallas_call x2, Pallas kernels, block_out_of(): pl.pallas_call(functools.partial(block_out_kernel, seq=seq, begin=begin),...  19.5 us
    pallas_call x1, Pallas kernels, input_back(): pl.pallas_call(functools.partial(input_back_kernel, spans=spans, sub=sub)...  15.1 us
  transfers between devices with their start and end apart: 38, of which 7 were waited for; matrix products, arithmetic and copies ran while one was open for 7% of the time, Pallas kernels for 44%

profile of v3, /device:TPU:0, one launch (start us, length us, event | category | flops | bytes accessed | tf_op | source)
XLA Modules:
  0.0 360.9 jit_solution(9321888072937073518)
XLA Ops:
  7.2 2.0 reshape.181
  9.4 1.3 reshape.182
  10.9 0.7 pad_maximum_fusion
  12.0 3.1 collective-permute-start
  15.1 2.6 collective-permute-start.1
  17.8 2.0 collective-permute-start.3
  20.0 4.9 %collective-permute-done.1 = bf16[1,1,1,1,1,24,1280]{6,5,4,3,2,1,0:T(8,128)(2,1)S(1)} collective-permute-done((bf16[1,1,1,1,1,24,1280]{6,5,4,3,2,1,0:T(8,128)(2,1)S(1)}, bf16[1,1,1,1,1,24,1280]{6,5,4,3,2,1,0:T(8,128)(2,1)S(1)}, u32[]{:S(2)}, u32[]{:S(2)}) %collective-permute-start.1) | collective-permute-done | bytes 61472 | tf_op jit(solution)/shard_map/ppermute | solution.py:83
  24.8 4.0 %collective-permute-done.3 = bf16[1,1,1,1,1,24,1920]{6,5,4,3,2,1,0:T(8,128)(2,1)S(1)} collective-permute-done((bf16[1,1,1,1,1,24,1920]{6,5,4,3,2,1,0:T(8,128)(2,1)S(1)}, bf16[1,1,1,1,1,24,1920]{6,5,4,3,2,1,0:T(8,128)(2,1)S(1)}, u32[]{:S(2)}, u32[]{:S(2)}) %collective-permute-start.3) | collective-permute-done | bytes 92192 | tf_op jit(solution)/shard_map/ppermute | solution.py:83
  28.9 1.6 collective-permute-start.4
  30.5 1.6 collective-permute-start.5
  33.0 5.8 %collective-permute-done.7 = bf16[1,1,2,1,1,24,1920]{6,5,4,3,2,1,0:T(8,128)(2,1)S(1)} collective-permute-done((bf16[1,1,2,1,1,24,1920]{6,5,4,3,2,1,0:T(8,128)(2,1)S(1)}, bf16[1,1,2,1,1,24,1920]{6,5,4,3,2,1,0:T(8,128)(2,1)S(1)}, u32[]{:S(2)}, u32[]{:S(2)}) %collective-permute-start.7) | collective-permute-done | bytes 184352 | tf_op jit(solution)/shard_map/ppermute | solution.py:83
  38.8 2.3 collective-permute-done.5
  42.0 1.6 collective-permute-start.10
  43.6 1.2 collective-permute-start.11
  44.7 0.8 collective-permute-start.9
  45.5 1.2 broadcast_in_dim.31
  46.8 0.8 constant_dynamic-update-slice_fusion.12
  47.8 1.3 constant_dynamic-update-slice_fusion.15
  49.5 0.9 fusion.11
  51.1 19.7 %attend.2 = (bf16[1824,768]{1,0:T(8,128)(2,1)}, bf16[1824,1152]{1,0:T(8,128)(2,1)}, bf16[1824,384]{1,0:T(8,128)(2,1)}, bf16[3,3,608,1280]{3,2,1,0:T(8,128)(2,1)}, f32[1824,384]{1,0:T(8,128)}) custom-call(s32[3]{0:T(128)} %get-tuple-element.327.valid, bf16[1824,768]{1,0:T(8,128)(2,1)} %bitcast.80, f32[1,768]{1,0:T(1,128)} %get-tuple-element.324.refs_1_.refs_7_, ...), custom_call_target="tpu_custom_call" | custom-call | flops 1 | bytes 1 | tf_op jit(solution)/shard_map/attend/pallas_call | solution.py:608
  70.8 1.8 constant_dynamic-update-slice_fusion.11
  72.6 1.8 constant_dynamic-update-slice_fusion.10
  74.4 1.9 constant_dynamic-update-slice_fusion.9
  77.9 1.6 constant_dynamic-update-slice_fusion.8
  79.8 1.6 constant_dynamic-update-slice_fusion.7
  81.5 1.6 copy-done
  83.0 24.8 %attend.3 = (bf16[1824,1152]{1,0:T(8,128)(2,1)}, bf16[1824,384]{1,0:T(8,128)(2,1)}, bf16[3,3,608,1280]{3,2,1,0:T(8,128)(2,1)}, f32[1824,384]{1,0:T(8,128)}, f32[...) custom-call(s32[3]{0:T(128)} %get-tuple-element.327.valid, ...), custom_call_target="tpu_custom_call" | custom-call | flops 1 | bytes 1 | tf_op jit(solution)/shard_map/attend/pallas_call | solution.py:608
  107.9 52.5 %mlp.1 = (bf16[1824,3072]{1,0:T(8,128)(2,1)}, bf16[1824,3072]{1,0:T(8,128)(2,1)}, f32[1,3072]{1,0:T(1,128)}, bf16[768,3072]{1,0:T(8,128)(2,1)}, bf16[768,3072]{1,0:T(8,128)(2,1)}) custom-call(s32[3]{0:T(128)} %get-tuple-element.327.valid, s32[3]{0:T(128)} %get-tuple-element.326.where, bf16[1824,768]{1,0:T(8,128)(2,1)} %get-tuple-element.176.normed, ...), custom_call_target="tpu_custom_call" | custom-call | flops 1 | bytes 1 | tf_op jit(solution)/shard_map/mlp/pallas_call | solution.py:787
  160.6 20.6 %middle_back.1 = (bf16[1824,768]{1,0:T(8,128)(2,1)}, bf16[1824,768]{1,0:T(8,128)(2,1)}, f32[1,768]{1,0:T(1,128)}, f32[1,768]{1,0:T(1,128)}, f32[1,768]{1,0:T(1,128)}, /*index=5*/f32[1,768]{1,0:T(1,128)}) custom-call(s32[3]{0:T(128)} %get-tuple-element.327.valid, bf16[1824,3072]{1,0:T(8,128)(2,1)} %get-tuple-element.180.hidden_grad, ...), custom_call_target="tpu_custom_call" | custom-call | flops 1 | bytes 1 | tf_op jit(solution)/shard_map/middle_back/pallas_call | solution.py:887
  181.1 5.2 %fold_first.1 = (bf16[2,4,48,1536]{3,2,1,0:T(8,128)(2,1)}, bf16[2,4,48,1536]{3,2,1,0:T(8,128)(2,1)}) custom-call(s32[3]{0:T(128)} %get-tuple-element.326.where, bf16[2,2,4,48,3072]{4,3,2,1,0:T(8,128)(2,1)} %bitcast.71, bf16[2,2,4,48,3072]{4,3,2,1,0:T(8,128)(2,1)} %bitcast.23.refs_1_.refs_3_.refs_4_.refs_5_, bf16[2,2,4,48,3072]{4,3,2,1,0:T(8,128)(2,1)} %bitcast.72, ...), custom_call_target="tpu_custom_call" | custom-call | flops 1 | bytes 1 | tf_op jit(solution)/shard_map/fold_first/pallas_call | solution.py:308
  186.3 1.6 collective-permute-start.14
  188.0 1.5 collective-permute-start.15
  189.5 30.5 %attend_back.3 = (bf16[1824,1152]{1,0:T(8,128)(2,1)}, f32[1,1152]{1,0:T(1,128)}, bf16[16,24,1920]{2,1,0:T(8,128)(2,1)}, bf16[16,24,1920]{2,1,0:T(8,128)(2,1)}) custom-call(s32[3]{0:T(128)} %get-tuple-element.326.where, bf16[1824,1152]{1,0:T(8,128)(2,1)} %get-tuple-element.193.refs_0_.refs_1_.refs_2_, ...), custom_call_target="tpu_custom_call" | custom-call | flops 1 | bytes 1 | tf_op jit(solution)/shard_map/attend_back/pallas_call | solution.py:701
  220.0 1.0 copy-done.2
  221.4 4.8 %fold_second.1 = (bf16[4,48,1536]{2,1,0:T(8,128)(2,1)}, bf16[4,48,1536]{2,1,0:T(8,128)(2,1)}) custom-call(s32[3]{0:T(128)} %get-tuple-element.326.where, bf16[2,2,4,48,3072]{4,3,2,1,0:T(8,128)(2,1)} %bitcast.73, bf16[2,2,4,48,3072]{4,3,2,1,0:T(8,128)(2,1)} %bitcast.23.refs_1_.refs_3_.refs_4_.refs_5_, bf16[2,4,48,1536]{3,2,1,0:T(8,128)(2,1)} %copy-done.2, ...), custom_call_target="tpu_custom_call" | custom-call | flops 1 | bytes 1 | tf_op jit(solution)/shard_map/fold_second/pallas_call | solution.py:334
  227.4 11.2 %attend_back.4 = (bf16[1824,384]{1,0:T(8,128)(2,1)}, f32[1,384]{1,0:T(1,128)}, bf16[16,24,384]{2,1,0:T(8,128)(2,1)}, bf16[16,24,384]{2,1,0:T(8,128)(2,1)}) custom-call(s32[3]{0:T(128)} %get-tuple-element.326.where, bf16[1824,1152]{1,0:T(8,128)(2,1)} %get-tuple-element.179.refs_0_.refs_1_, ...), custom_call_target="tpu_custom_call" | custom-call | flops 1 | bytes 1 | tf_op jit(solution)/shard_map/attend_back/pallas_call | solution.py:701
  238.6 3.7 %collective-permute-done.16.refs_3_ = bf16[4,48,1536]{2,1,0:T(8,128)(2,1)S(1)} collective-permute-done((bf16[4,48,1536]{2,1,0:T(8,128)(2,1)}, bf16[4,48,1536]{2,1,0:T(8,128)(2,1)S(1)}, u32[]{:S(2)}, u32[]{:S(2)}) %collective-permute-start.16) | collective-permute-done | bytes 589856 | tf_op jit(solution)/shard_map/ppermute | solution.py:83
  242.6 1.1 copy-done.4
  243.7 4.7 %plane_sum.2 = (bf16[4,24,1920]{2,1,0:T(8,128)(2,1)}, bf16[4,24,1920]{2,1,0:T(8,128)(2,1)}, bf16[4,24,1920]{2,1,0:T(8,128)(2,1)}, bf16[4,24,1920]{2,1,0:T(8,128)(2,1)}) custom-call(s32[3]{0:T(128)} %get-tuple-element.326.where, bf16[4,4,24,1920]{3,2,1,0:T(8,128)(2,1)} %bitcast.93, bf16[4,4,24,1920]{3,2,1,0:T(8,128)(2,1)} %bitcast.94), custom_call_target="tpu_custom_call" | custom-call | flops 1 | bytes 1 | tf_op jit(solution)/shard_map/plane_sum/pallas_call | solution.py:246
  248.5 4.6 %line_first.1 = (bf16[2,48,3072]{2,1,0:T(8,128)(2,1)}, bf16[2,48,3072]{2,1,0:T(8,128)(2,1)}) custom-call(s32[3]{0:T(128)} %get-tuple-element.326.where, bf16[2,2,4,48,3072]{4,3,2,1,0:T(8,128)(2,1)} %bitcast.75, bf16[2,2,4,48,3072]{4,3,2,1,0:T(8,128)(2,1)} %bitcast.23.refs_1_.refs_3_.refs_4_.refs_5_, bf16[2,4,48,1536]{3,2,1,0:T(8,128)(2,1)} %copy-done.2, ...), custom_call_target="tpu_custom_call" | custom-call | flops 1 | bytes 1 | tf_op jit(solution)/shard_map/line_first/pallas_call | solution.py:370
  253.1 1.3 collective-permute-start.19
  254.7 1.0 collective-permute-start.21
  255.7 2.2 collective-permute-start.22
  259.4 17.8 %attend_back.5 = (bf16[1824,768]{1,0:T(8,128)(2,1)}, f32[1,768]{1,0:T(1,128)}, bf16[16,24,768]{2,1,0:T(8,128)(2,1)}, bf16[16,24,768]{2,1,0:T(8,128)(2,1)}) custom-call(s32[3]{0:T(128)} %get-tuple-element.326.where, bf16[1824,1152]{1,0:T(8,128)(2,1)} %get-tuple-element.179.refs_0_.refs_1_, bf16[1824,1152]{1,0:T(8,128)(2,1)} %get-tuple-element.179.refs_0_.refs_1_, ...), custom_call_target="tpu_custom_call" | custom-call | flops 1 | bytes 1 | tf_op jit(solution)/shard_map/attend_back/pallas_call | solution.py:701
  278.4 2.8 line_sum.2
  281.7 2.7 collective-permute-start.24
  284.6 0.8 collective-permute-start.26
  285.4 3.4 collective-permute-start.27
  288.9 15.1 %input_back.1 = (bf16[1824,768]{1,0:T(8,128)(2,1)}, f32[1,768]{1,0:T(1,128)}, f32[1,768]{1,0:T(1,128)}) custom-call(bf16[1824,1152]{1,0:T(8,128)(2,1)} %get-tuple-element.243.refs_0_, bf16[1824,384]{1,0:T(8,128)(2,1)} %get-tuple-element.244.refs_1_, bf16[1824,768]{1,0:T(8,128)(2,1)} %get-tuple-element.256.refs_2_, bf16[768,1280]{1,0:T(8,128)(2,1)} %bitcast.85, ...), custom_call_target="tpu_custom_call" | custom-call | flops 1 | bytes 1 | tf_op jit(solution)/shard_map/input_back/pallas_call | solution.py:941
  306.1 7.9 %block_out.2.rest_0_ = bf16[1824,768]{1,0:T(8,128)(2,1)} custom-call(s32[3]{0:T(128)} %get-tuple-element.327.valid, bf16[1824,3072]{1,0:T(8,128)(2,1)} %get-tuple-element.177.active, bf16[768,6144]{1,0:T(8,128)(2,1)} %all-gather.2.cloned.1.call-done.up.down.ups.downs, f32[1824,768]{1,0:T(8,128)} %get-tuple-element.285.middle, ...), custom_call_target="tpu_custom_call" | custom-call | flops 1 | bytes 1 | tf_op jit(solution)/shard_map/block_out/pallas_call | solution.py:838
  315.3 4.6 %plane_sum.3 = (bf16[4,24,1280]{2,1,0:T(8,128)(2,1)}, bf16[4,24,1280]{2,1,0:T(8,128)(2,1)}, bf16[4,24,1280]{2,1,0:T(8,128)(2,1)}, bf16[4,24,1280]{2,1,0:T(8,128)(2,1)}) custom-call(s32[3]{0:T(128)} %get-tuple-element.326.where, bf16[4,4,24,384]{3,2,1,0:T(8,128)(2,1)} %bitcast.101, bf16[4,4,24,768]{3,2,1,0:T(8,128)(2,1)} %bitcast.98, ...), custom_call_target="tpu_custom_call" | custom-call | flops 1 | bytes 1 | tf_op jit(solution)/shard_map/plane_sum/pallas_call | solution.py:246
  319.9 1.6 collective-permute-start.31
  321.9 1.6 collective-permute-start.33
  324.9 11.6 %block_out.3 = bf16[1824,768]{1,0:T(8,128)(2,1)} custom-call(s32[3]{0:T(128)} %get-tuple-element.327.valid, bf16[1824,3072]{1,0:T(8,128)(2,1)} %get-tuple-element.177.active, bf16[768,6144]{1,0:T(8,128)(2,1)} %all-gather.2.cloned.1.call-done.up.down.ups.downs, f32[1824,768]{1,0:T(8,128)} %get-tuple-element.285.middle, ...), custom_call_target="tpu_custom_call", output_to_operand_aliasing={{}: (5, {})} | custom-call | flops 1 | bytes 1 | tf_op jit(solution)/shard_map/block_out/pallas_call | solution.py:838
  337.4 2.7 line_sum.3
  340.1 2.2 collective-permute-start.34
  342.3 1.2 collective-permute-start.35
  343.5 1.2 collective-permute-start.36
  344.7 1.1 select_n.92
  345.9 1.2 copy.43
  347.2 2.5 reshape.207
  349.9 0.7 reshape.208
  350.7 0.9 add_add_fusion.1
  353.0 0.8 reshape_reshape.8
  (229 shorter events, 18.9 us)
Async XLA Ops:
  7.2 3.5 copy-start.18
  7.2 100.7 %all-gather.2.cloned.1.call-start = ((), (), s32[]{:S(2)}) async-start(), calls=%async_computation | async-start | bytes 9732096 | tf_op jit(solution)/shard_map/all_gather | solution.py:1007
  9.2 2.4 copy-start.20
  9.4 2.5 copy-start.37
  9.4 2.5 copy-start.38
  9.4 8.3 %copy-start.24 = (bf16[18432]{0:T(1024)(128)(2,1)S(1)}, bf16[18432]{0:T(1024)(128)(2,1)}, u32[]{:S(2)}) copy-start(bf16[18432]{0:T(1024)(128)(2,1)} %param.15) | copy-start | bytes 110596
  12.0 8.0 %collective-permute-start = (bf16[1,1,1,1,1,24,1280]{6,5,4,3,2,1,0:T(8,128)(2,1)S(1)}, bf16[1,1,1,1,1,24,1280]{6,5,4,3,2,1,0:T(8,128)(2,1)S(1)}, u32[]{:S(2)}, u32[]{:S(2)}) collective-permute-start(bf16[1,1,1,1,1,24,1280]{6,5,4,3,2,1,0:T(8,128)(2,1)S(1)} %fusion.2), channel_id=1, source_target_pairs={{0,2},{1,3},{2,0},{3,1},{4,6},{5,7},{6,4},{7,5},{8,10},{9,11},{10,... | collective-permute-start | bytes 184328 | tf_op jit(solution)/shard_map/ppermute | solution.py:83
  15.1 9.8 %collective-permute-start.1 = (bf16[1,1,1,1,1,24,1280]{6,5,4,3,2,1,0:T(8,128)(2,1)S(1)}, bf16[1,1,1,1,1,24,1280]{6,5,4,3,2,1,0:T(8,128)(2,1)S(1)}, u32[]{:S(2)}, u32[]{:S(2)}) collective-permute-start(bf16[1,1,1,1,1,24,1280]{6,5,4,3,2,1,0:T(8,128)(2,1)S(1)} %fusion.2), channel_id=1, source_target_pairs={{0,4},{1,5},{2,6},{3,7},{4,0},{5,1},{6,2},{7,3},{8,12},{9,13},{10,... | collective-permute-start | bytes 184328 | tf_op jit(solution)/shard_map/ppermute | solution.py:83
  17.6 7.2 %collective-permute-start.2 = (bf16[1,1,1,1,1,24,1280]{6,5,4,3,2,1,0:T(8,128)(2,1)S(1)}, bf16[1,1,1,1,1,24,1280]{6,5,4,3,2,1,0:T(8,128)(2,1)S(1)}, u32[]{:S(2)}, u32[]{:S(2)}) collective-permute-start(bf16[1,1,1,1,1,24,1280]{6,5,4,3,2,1,0:T(8,128)(2,1)S(1)} %fusion.2), channel_id=1, source_target_pairs={{0,6},{1,7},{2,4},{3,5},{4,2},{5,3},{6,0},{7,1},{8,14},{9,15},{10,... | collective-permute-start | bytes 184328 | tf_op jit(solution)/shard_map/ppermute | solution.py:83
  17.8 11.0 %collective-permute-start.3 = (bf16[1,1,1,1,1,24,1920]{6,5,4,3,2,1,0:T(8,128)(2,1)S(1)}, bf16[1,1,1,1,1,24,1920]{6,5,4,3,2,1,0:T(8,128)(2,1)S(1)}, u32[]{:S(2)}, u32[]{:S(2)}) collective-permute-start(bf16[1,1,1,1,1,24,1920]{6,5,4,3,2,1,0:T(8,128)(2,1)S(1)} %maximum_bitcast_fusion.1), channel_id=1, source_target_pairs={{0,4},{1,5},{2,6},{3,7},{4,0},{5,1},{6,2},{7,3},{8,12},{9,13},{10,... | collective-permute-start | bytes 276488 | tf_op jit(solution)/shard_map/ppermute | solution.py:83
  19.8 21.4 %copy-start.35 = (s32[3]{0:T(128)S(1)}, s32[3]{0:T(128)}, u32[]{:S(2)}) copy-start(s32[3]{0:T(128)} %param.13) | copy-start | bytes 40
  19.9 21.4 %copy-start.36 = (s32[3]{0:T(128)S(1)}, s32[3]{0:T(128)}, u32[]{:S(2)}) copy-start(s32[3]{0:T(128)} %param.12) | copy-start | bytes 40
  28.9 9.9 %collective-permute-start.4 = (bf16[1,1,2,2,1,24,1280]{6,5,4,3,2,1,0:T(8,128)(2,1)S(1)}, bf16[1,1,2,2,1,24,1280]{6,5,4,3,2,1,0:T(8,128)(2,1)S(1)}, u32[]{:S(2)}, u32[]{:S(2)}) collective-permute-start(bf16[1,1,2,2,1,24,1280]{6,5,4,3,2,1,0:T(8,128)(2,1)S(1)} %constant_dynamic-update-slice_fusion.23), channel_id=1, source_target_pairs={{0,8},{1,9},{2,10},{3,11},{4,12},{5,13},{6,14},{7,15},{8,0},{9,1},... | collective-permute-start | bytes 737288 | tf_op jit(solution)/shard_map/ppermute | solution.py:83
  30.5 10.5 %collective-permute-start.5 = (bf16[1,1,2,2,1,24,1280]{6,5,4,3,2,1,0:T(8,128)(2,1)S(1)}, bf16[1,1,2,2,1,24,1280]{6,5,4,3,2,1,0:T(8,128)(2,1)S(1)}, u32[]{:S(2)}, u32[]{:S(2)}) collective-permute-start(bf16[1,1,2,2,1,24,1280]{6,5,4,3,2,1,0:T(8,128)(2,1)S(1)} %constant_dynamic-update-slice_fusion.23), channel_id=1, source_target_pairs={{0,16},{1,17},{2,18},{3,19},{4,20},{5,21},{6,22},{7,23},{8,24},{9,... | collective-permute-start | bytes 737288 | tf_op jit(solution)/shard_map/ppermute | solution.py:83
  32.1 9.0 %collective-permute-start.6 = (bf16[1,1,2,2,1,24,1280]{6,5,4,3,2,1,0:T(8,128)(2,1)S(1)}, bf16[1,1,2,2,1,24,1280]{6,5,4,3,2,1,0:T(8,128)(2,1)S(1)}, u32[]{:S(2)}, u32[]{:S(2)}) collective-permute-start(bf16[1,1,2,2,1,24,1280]{6,5,4,3,2,1,0:T(8,128)(2,1)S(1)} %constant_dynamic-update-slice_fusion.23), channel_id=1, source_target_pairs={{0,24},{1,25},{2,26},{3,27},{4,28},{5,29},{6,30},{7,31},{8,16},{9,... | collective-permute-start | bytes 737288 | tf_op jit(solution)/shard_map/ppermute | solution.py:83
  32.5 6.3 %collective-permute-start.7 = (bf16[1,1,2,1,1,24,1920]{6,5,4,3,2,1,0:T(8,128)(2,1)S(1)}, bf16[1,1,2,1,1,24,1920]{6,5,4,3,2,1,0:T(8,128)(2,1)S(1)}, u32[]{:S(2)}, u32[]{:S(2)}) collective-permute-start(bf16[1,1,2,1,1,24,1920]{6,5,4,3,2,1,0:T(8,128)(2,1)S(1)} %constant_dynamic-update-slice_fusion.20), channel_id=1, source_target_pairs={{0,2},{1,3},{2,0},{3,1},{4,6},{5,7},{6,4},{7,5},{8,10},{9,11},{10,... | collective-permute-start | bytes 552968 | tf_op jit(solution)/shard_map/ppermute | solution.py:83
  41.2 6.6 %collective-permute-start.8 = (bf16[2,2,2,2,1,24,1280]{6,5,4,3,2,1,0:T(8,128)(2,1)S(1)}, bf16[2,2,2,2,1,24,1280]{6,5,4,3,2,1,0:T(8,128)(2,1)}, u32[]{:S(2)}, u32[]{:S(2)}) collective-permute-start(bf16[2,2,2,2,1,24,1280]{6,5,4,3,2,1,0:T(8,128)(2,1)S(1)} %constant_dynamic-update-slice_fusion.17), channel_id=1, source_target_pairs={{0,1},{1,0},{2,3},{3,2},{4,5},{5,4},{6,7},{7,6},{8,9},{9,8},{10,11... | collective-permute-start | bytes 2949128 | tf_op jit(solution)/shard_map/ppermute | solution.py:83
  42.0 28.8 %collective-permute-start.10 = (bf16[1,1,2,2,1,24,1920]{6,5,4,3,2,1,0:T(8,128)(2,1)S(1)}, bf16[1,1,2,2,1,24,1920]{6,5,4,3,2,1,0:T(8,128)(2,1)}, u32[]{:S(2)}, u32[]{:S(2)}) collective-permute-start(bf16[1,1,2,2,1,24,1920]{6,5,4,3,2,1,0:T(8,128)(2,1)S(1)} %constant_dynamic-update-slice_fusion.13), channel_id=1, source_target_pairs={{0,16},{1,17},{2,18},{3,19},{4,20},{5,21},{6,22},{7,23},{8,24},{9,... | collective-permute-start | bytes 1105928 | tf_op jit(solution)/shard_map/ppermute | solution.py:83
  43.6 27.2 %collective-permute-start.11 = (bf16[1,1,2,2,1,24,1920]{6,5,4,3,2,1,0:T(8,128)(2,1)S(1)}, bf16[1,1,2,2,1,24,1920]{6,5,4,3,2,1,0:T(8,128)(2,1)}, u32[]{:S(2)}, u32[]{:S(2)}) collective-permute-start(bf16[1,1,2,2,1,24,1920]{6,5,4,3,2,1,0:T(8,128)(2,1)S(1)} %constant_dynamic-update-slice_fusion.13), channel_id=1, source_target_pairs={{0,24},{1,25},{2,26},{3,27},{4,28},{5,29},{6,30},{7,31},{8,16},{9,... | collective-permute-start | bytes 1105928 | tf_op jit(solution)/shard_map/ppermute | solution.py:83
  44.7 26.1 %collective-permute-start.9 = (bf16[1,1,2,2,1,24,1920]{6,5,4,3,2,1,0:T(8,128)(2,1)S(1)}, bf16[1,1,2,2,1,24,1920]{6,5,4,3,2,1,0:T(8,128)(2,1)}, u32[]{:S(2)}, u32[]{:S(2)}) collective-permute-start(bf16[1,1,2,2,1,24,1920]{6,5,4,3,2,1,0:T(8,128)(2,1)S(1)} %constant_dynamic-update-slice_fusion.13), channel_id=1, source_target_pairs={{0,8},{1,9},{2,10},{3,11},{4,12},{5,13},{6,14},{7,15},{8,0},{9,1},... | collective-permute-start | bytes 1105928 | tf_op jit(solution)/shard_map/ppermute | solution.py:83
  49.1 1.9 copy-start.1
  76.2 3.6 %collective-permute-start.12 = (bf16[2,2,2,2,1,24,1920]{6,5,4,3,2,1,0:T(8,128)(2,1)}, bf16[2,2,2,2,1,24,1920]{6,5,4,3,2,1,0:T(8,128)(2,1)}, u32[]{:S(2)}, u32[]{:S(2)}) collective-permute-start(bf16[2,2,2,2,1,24,1920]{6,5,4,3,2,1,0:T(8,128)(2,1)} %constant_dynamic-update-slice_fusion.9), channel_id=1, source_target_pairs={{0,1},{1,0},{2,3},{3,2},{4,5},{5,4},{6,7},{7,6},{8,9},{9,8},{10,11... | collective-permute-start | bytes 4423688 | tf_op jit(solution)/shard_map/ppermute | solution.py:83
  81.4 1.6 copy-start
  160.3 20.8 %collective-permute-start.13 = (bf16[768,3072]{1,0:T(8,128)(2,1)}, bf16[768,3072]{1,0:T(8,128)(2,1)}, u32[]{:S(2)}, u32[]{:S(2)}) collective-permute-start(bf16[768,3072]{1,0:T(8,128)(2,1)} %get-tuple-element.189), channel_id=1, source_target_pairs={{0,1},{1,0},{2,3},{3,2},{4,5},{5,4},{6,7},{7,6},{8,9},{9,8},{10,11... | collective-permute-start | bytes 14155784 | tf_op jit(solution)/shard_map/ppermute | solution.py:83
  186.3 33.6 %collective-permute-start.14 = (bf16[2,4,48,1536]{3,2,1,0:T(8,128)(2,1)}, bf16[2,4,48,1536]{3,2,1,0:T(8,128)(2,1)S(1)}, u32[]{:S(2)}, u32[]{:S(2)}) collective-permute-start(bf16[2,4,48,1536]{3,2,1,0:T(8,128)(2,1)} %get-tuple-element.205), channel_id=1, source_target_pairs={{0,16},{1,17},{2,18},{3,19},{4,20},{5,21},{6,22},{7,23},{8,24},{9,... | collective-permute-start | bytes 3538952 | tf_op jit(solution)/shard_map/ppermute | solution.py:83
  188.0 32.0 %collective-permute-start.15 = (bf16[2,4,48,1536]{3,2,1,0:T(8,128)(2,1)}, bf16[2,4,48,1536]{3,2,1,0:T(8,128)(2,1)S(1)}, u32[]{:S(2)}, u32[]{:S(2)}) collective-permute-start(bf16[2,4,48,1536]{3,2,1,0:T(8,128)(2,1)} %get-tuple-element.206), channel_id=1, source_target_pairs={{0,8},{1,9},{2,10},{3,11},{4,12},{5,13},{6,14},{7,15},{8,0},{9,1},... | collective-permute-start | bytes 3538952 | tf_op jit(solution)/shard_map/ppermute | solution.py:83
  220.0 1.4 copy-start.3
  221.4 4.8 %copy-start.39 = (bf16[16,24,1920]{2,1,0:T(8,128)(2,1)S(1)}, bf16[16,24,1920]{2,1,0:T(8,128)(2,1)}, u32[]{:S(2)}) copy-start(bf16[16,24,1920]{2,1,0:T(8,128)(2,1)} %get-tuple-element.221) | copy-start | bytes 4423684
  226.3 16.3 %collective-permute-start.18 = (bf16[16,24,1920]{2,1,0:T(8,128)(2,1)S(1)}, bf16[16,24,1920]{2,1,0:T(8,128)(2,1)S(1)}, u32[]{:S(2)}, u32[]{:S(2)}) collective-permute-start(bf16[16,24,1920]{2,1,0:T(8,128)(2,1)S(1)} %copy-done.39), channel_id=1, source_target_pairs={{0,1},{1,0},{2,3},{3,2},{4,5},{5,4},{6,7},{7,6},{8,9},{9,8},{10,11... | collective-permute-start | bytes 4423688 | tf_op jit(solution)/shard_map/ppermute | solution.py:83
  226.4 16.0 %collective-permute-start.16 = (bf16[4,48,1536]{2,1,0:T(8,128)(2,1)}, bf16[4,48,1536]{2,1,0:T(8,128)(2,1)S(1)}, u32[]{:S(2)}, u32[]{:S(2)}) collective-permute-start(bf16[4,48,1536]{2,1,0:T(8,128)(2,1)} %get-tuple-element.219), channel_id=1, source_target_pairs={{0,8},{1,9},{2,10},{3,11},{4,12},{5,13},{6,14},{7,15},{8,0},{9,1},... | collective-permute-start | bytes 1769480 | tf_op jit(solution)/shard_map/ppermute | solution.py:83
  227.0 15.6 %collective-permute-start.17 = (bf16[4,48,1536]{2,1,0:T(8,128)(2,1)}, bf16[4,48,1536]{2,1,0:T(8,128)(2,1)S(1)}, u32[]{:S(2)}, u32[]{:S(2)}) collective-permute-start(bf16[4,48,1536]{2,1,0:T(8,128)(2,1)} %get-tuple-element.220), channel_id=1, source_target_pairs={{0,16},{1,17},{2,18},{3,19},{4,20},{5,21},{6,22},{7,23},{8,24},{9,... | collective-permute-start | bytes 1769480 | tf_op jit(solution)/shard_map/ppermute | solution.py:83
  242.3 6.1 %copy-start.5 = (bf16[4,48,1536]{2,1,0:T(8,128)(2,1)}, bf16[4,48,1536]{2,1,0:T(8,128)(2,1)S(1)}, u32[]{:S(2)}) copy-start(bf16[4,48,1536]{2,1,0:T(8,128)(2,1)S(1)} %collective-permute-done.16.refs_3_) | copy-start | bytes 1769476
  242.6 5.9 %copy-start.6 = (bf16[4,48,1536]{2,1,0:T(8,128)(2,1)}, bf16[4,48,1536]{2,1,0:T(8,128)(2,1)S(1)}, u32[]{:S(2)}) copy-start(bf16[4,48,1536]{2,1,0:T(8,128)(2,1)S(1)} %collective-permute-done.17.refs_7_) | copy-start | bytes 1769476
  248.5 7.2 %copy-start.40 = (bf16[4,24,1920]{2,1,0:T(8,128)(2,1)S(1)}, bf16[4,24,1920]{2,1,0:T(8,128)(2,1)}, u32[]{:S(2)}) copy-start(bf16[4,24,1920]{2,1,0:T(8,128)(2,1)} %get-tuple-element.240) | copy-start | bytes 1105924
  248.5 9.9 %copy-start.25 = (f32[1,3072]{1,0:T(1,128)S(1)}, f32[1,3072]{1,0:T(1,128)}, u32[]{:S(2)}) copy-start(f32[1,3072]{1,0:T(1,128)} %get-tuple-element.274) | copy-start | bytes 36868
  248.5 10.9 %copy-start.26 = (f32[1,1152]{1,0:T(1,128)S(1)}, f32[1,1152]{1,0:T(1,128)}, u32[]{:S(2)}) copy-start(f32[1,1152]{1,0:T(1,128)} %get-tuple-element.267) | copy-start | bytes 13828
  253.1 24.2 %collective-permute-start.19 = (bf16[2,48,3072]{2,1,0:T(8,128)(2,1)}, bf16[2,48,3072]{2,1,0:T(8,128)(2,1)S(1)}, u32[]{:S(2)}, u32[]{:S(2)}) collective-permute-start(bf16[2,48,3072]{2,1,0:T(8,128)(2,1)} %get-tuple-element.237), channel_id=1, source_target_pairs={{0,2},{1,3},{2,0},{3,1},{4,6},{5,7},{6,4},{7,5},{8,10},{9,11},{10,... | collective-permute-start | bytes 1769480 | tf_op jit(solution)/shard_map/ppermute | solution.py:83
  254.4 22.9 %collective-permute-start.20 = (bf16[4,24,1920]{2,1,0:T(8,128)(2,1)}, bf16[4,24,1920]{2,1,0:T(8,128)(2,1)S(1)}, u32[]{:S(2)}, u32[]{:S(2)}) collective-permute-start(bf16[4,24,1920]{2,1,0:T(8,128)(2,1)} %get-tuple-element.238), channel_id=1, source_target_pairs={{0,8},{1,9},{2,10},{3,11},{4,12},{5,13},{6,14},{7,15},{8,0},{9,1},... | collective-permute-start | bytes 1105928 | tf_op jit(solution)/shard_map/ppermute | solution.py:83
  254.7 22.6 %collective-permute-start.21 = (bf16[4,24,1920]{2,1,0:T(8,128)(2,1)}, bf16[4,24,1920]{2,1,0:T(8,128)(2,1)S(1)}, u32[]{:S(2)}, u32[]{:S(2)}) collective-permute-start(bf16[4,24,1920]{2,1,0:T(8,128)(2,1)} %get-tuple-element.239), channel_id=1, source_target_pairs={{0,16},{1,17},{2,18},{3,19},{4,20},{5,21},{6,22},{7,23},{8,24},{9,... | collective-permute-start | bytes 1105928 | tf_op jit(solution)/shard_map/ppermute | solution.py:83
  255.7 21.6 %collective-permute-start.22 = (bf16[4,24,1920]{2,1,0:T(8,128)(2,1)S(1)}, bf16[4,24,1920]{2,1,0:T(8,128)(2,1)S(1)}, u32[]{:S(2)}, u32[]{:S(2)}) collective-permute-start(bf16[4,24,1920]{2,1,0:T(8,128)(2,1)S(1)} %copy-done.40), channel_id=1, source_target_pairs={{0,24},{1,25},{2,26},{3,27},{4,28},{5,29},{6,30},{7,31},{8,16},{9,... | collective-permute-start | bytes 1105928 | tf_op jit(solution)/shard_map/ppermute | solution.py:83
  257.9 19.3 %collective-permute-start.23 = (bf16[16,24,384]{2,1,0:T(8,128)(2,1)}, bf16[16,24,384]{2,1,0:T(8,128)(2,1)S(1)}, u32[]{:S(2)}, u32[]{:S(2)}) collective-permute-start(bf16[16,24,384]{2,1,0:T(8,128)(2,1)} %get-tuple-element.241), channel_id=1, source_target_pairs={{0,1},{1,0},{2,3},{3,2},{4,5},{5,4},{6,7},{7,6},{8,9},{9,8},{10,11... | collective-permute-start | bytes 884744 | tf_op jit(solution)/shard_map/ppermute | solution.py:83
  259.4 17.9 %copy-start.7 = (bf16[2,48,3072]{2,1,0:T(8,128)(2,1)S(1)}, bf16[2,48,3072]{2,1,0:T(8,128)(2,1)}, u32[]{:S(2)}) copy-start(bf16[2,48,3072]{2,1,0:T(8,128)(2,1)} %get-tuple-element.246) | copy-start | bytes 1769476
  277.2 11.6 %copy-start.32 = (f32[1,768]{1,0:T(1,128)S(1)}, f32[1,768]{1,0:T(1,128)}, u32[]{:S(2)}) copy-start(f32[1,768]{1,0:T(1,128)} %get-tuple-element.269) | copy-start | bytes 9220
  277.2 11.6 %copy-start.34 = (f32[1,384]{1,0:T(1,128)S(1)}, f32[1,384]{1,0:T(1,128)}, u32[]{:S(2)}) copy-start(f32[1,384]{1,0:T(1,128)} %get-tuple-element.268) | copy-start | bytes 4612
  277.2 26.8 %copy-start.13 = (bf16[16,24,384]{2,1,0:T(8,128)(2,1)}, bf16[16,24,384]{2,1,0:T(8,128)(2,1)S(1)}, u32[]{:S(2)}) copy-start(bf16[16,24,384]{2,1,0:T(8,128)(2,1)S(1)} %collective-permute-done.23) | copy-start | bytes 884740
  281.2 23.0 %collective-permute-start.28 = (bf16[16,24,768]{2,1,0:T(8,128)(2,1)}, bf16[16,24,768]{2,1,0:T(8,128)(2,1)S(1)}, u32[]{:S(2)}, u32[]{:S(2)}) collective-permute-start(bf16[16,24,768]{2,1,0:T(8,128)(2,1)} %get-tuple-element.264), channel_id=1, source_target_pairs={{0,1},{1,0},{2,3},{3,2},{4,5},{5,4},{6,7},{7,6},{8,9},{9,8},{10,11... | collective-permute-start | bytes 1769480 | tf_op jit(solution)/shard_map/ppermute | solution.py:83
  281.7 22.5 %collective-permute-start.24 = (bf16[1,48,3072]{2,1,0:T(8,128)(2,1)S(1)}, bf16[1,48,3072]{2,1,0:T(8,128)(2,1)S(1)}, u32[]{:S(2)}, u32[]{:S(2)}) collective-permute-start(bf16[1,48,3072]{2,1,0:T(8,128)(2,1)S(1)} %add_convert_fusion), channel_id=1, source_target_pairs={{0,4},{1,5},{2,6},{3,7},{4,0},{5,1},{6,2},{7,3},{8,12},{9,13},{10,... | collective-permute-start | bytes 884744 | tf_op jit(solution)/shard_map/ppermute | solution.py:83
  284.4 19.7 %collective-permute-start.25 = (bf16[24,1920]{1,0:T(8,128)(2,1)}, bf16[24,1920]{1,0:T(8,128)(2,1)S(1)}, u32[]{:S(2)}, u32[]{:S(2)}) collective-permute-start(bf16[24,1920]{1,0:T(8,128)(2,1)} %get-tuple-element.261), channel_id=1, source_target_pairs={{0,2},{1,3},{2,0},{3,1},{4,6},{5,7},{6,4},{7,5},{8,10},{9,11},{10,... | collective-permute-start | bytes 276488 | tf_op jit(solution)/shard_map/ppermute | solution.py:83
  284.6 19.6 %collective-permute-start.26 = (bf16[24,1920]{1,0:T(8,128)(2,1)}, bf16[24,1920]{1,0:T(8,128)(2,1)S(1)}, u32[]{:S(2)}, u32[]{:S(2)}) collective-permute-start(bf16[24,1920]{1,0:T(8,128)(2,1)} %get-tuple-element.262), channel_id=1, source_target_pairs={{0,4},{1,5},{2,6},{3,7},{4,0},{5,1},{6,2},{7,3},{8,12},{9,13},{10,... | collective-permute-start | bytes 276488 | tf_op jit(solution)/shard_map/ppermute | solution.py:83
  285.4 18.8 %collective-permute-start.27 = (bf16[24,1920]{1,0:T(8,128)(2,1)}, bf16[24,1920]{1,0:T(8,128)(2,1)S(1)}, u32[]{:S(2)}, u32[]{:S(2)}) collective-permute-start(bf16[24,1920]{1,0:T(8,128)(2,1)} %get-tuple-element.263), channel_id=1, source_target_pairs={{0,6},{1,7},{2,4},{3,5},{4,2},{5,3},{6,0},{7,1},{8,14},{9,15},{10,... | collective-permute-start | bytes 276488 | tf_op jit(solution)/shard_map/ppermute | solution.py:83
  288.9 15.3 %copy-start.29 = (f32[1,768]{1,0:T(1,128)S(1)}, f32[1,768]{1,0:T(1,128)}, u32[]{:S(2)}) copy-start(f32[1,768]{1,0:T(1,128)} %get-tuple-element.270) | copy-start | bytes 9220
  304.2 9.8 %copy-start.8 = (bf16[16,24,768]{2,1,0:T(8,128)(2,1)}, bf16[16,24,768]{2,1,0:T(8,128)(2,1)S(1)}, u32[]{:S(2)}) copy-start(bf16[16,24,768]{2,1,0:T(8,128)(2,1)S(1)} %collective-permute-done.28) | copy-start | bytes 1769476
  305.5 9.2 %collective-permute-start.29 = (f32[1,24,3072]{2,1,0:T(8,128)S(1)}, f32[1,24,3072]{2,1,0:T(8,128)S(1)}, u32[]{:S(2)}, u32[]{:S(2)}) collective-permute-start(f32[1,24,3072]{2,1,0:T(8,128)S(1)} %constant_dynamic-slice_fusion), channel_id=1, source_target_pairs={{0,1},{1,0},{2,3},{3,2},{4,5},{5,4},{6,7},{7,6},{8,9},{9,8},{10,11... | collective-permute-start | bytes 884744 | tf_op jit(solution)/shard_map/ppermute | solution.py:83
  305.6 9.1 %collective-permute-start.30 = (bf16[16,24,128]{2,1,0:T(8,128)(2,1)S(1)}, bf16[16,24,128]{2,1,0:T(8,128)(2,1)S(1)}, u32[]{:S(2)}, u32[]{:S(2)}) collective-permute-start(bf16[16,24,128]{2,1,0:T(8,128)(2,1)S(1)} %pad.25), channel_id=1, source_target_pairs={{0,1},{1,0},{2,3},{3,2},{4,5},{5,4},{6,7},{7,6},{8,9},{9,8},{10,11... | collective-permute-start | bytes 294920 | tf_op jit(solution)/shard_map/ppermute | solution.py:83
  314.0 9.4 %copy-start.17 = (f32[24,1920]{1,0:T(8,128)S(1)}, f32[24,1920]{1,0:T(8,128)}, u32[]{:S(2)}) copy-start(f32[24,1920]{1,0:T(8,128)} %get-tuple-element.292) | copy-start | bytes 552964
  314.0 9.4 %copy-start.23 = (bf16[24,1920]{1,0:T(8,128)(2,1)S(1)}, bf16[24,1920]{1,0:T(8,128)(2,1)}, u32[]{:S(2)}) copy-start(bf16[24,1920]{1,0:T(8,128)(2,1)} %copy-done.22) | copy-start | bytes 276484
  319.9 16.6 %collective-permute-start.31 = (bf16[4,24,1280]{2,1,0:T(8,128)(2,1)}, bf16[4,24,1280]{2,1,0:T(8,128)(2,1)S(1)}, u32[]{:S(2)}, u32[]{:S(2)}) collective-permute-start(bf16[4,24,1280]{2,1,0:T(8,128)(2,1)} %get-tuple-element.287), channel_id=1, source_target_pairs={{0,8},{1,9},{2,10},{3,11},{4,12},{5,13},{6,14},{7,15},{8,0},{9,1},... | collective-permute-start | bytes 737288 | tf_op jit(solution)/shard_map/ppermute | solution.py:83
  321.5 15.0 %collective-permute-start.32 = (bf16[4,24,1280]{2,1,0:T(8,128)(2,1)}, bf16[4,24,1280]{2,1,0:T(8,128)(2,1)S(1)}, u32[]{:S(2)}, u32[]{:S(2)}) collective-permute-start(bf16[4,24,1280]{2,1,0:T(8,128)(2,1)} %get-tuple-element.288), channel_id=1, source_target_pairs={{0,16},{1,17},{2,18},{3,19},{4,20},{5,21},{6,22},{7,23},{8,24},{9,... | collective-permute-start | bytes 737288 | tf_op jit(solution)/shard_map/ppermute | solution.py:83
  321.9 14.6 %collective-permute-start.33 = (bf16[4,24,1280]{2,1,0:T(8,128)(2,1)}, bf16[4,24,1280]{2,1,0:T(8,128)(2,1)S(1)}, u32[]{:S(2)}, u32[]{:S(2)}) collective-permute-start(bf16[4,24,1280]{2,1,0:T(8,128)(2,1)} %get-tuple-element.289), channel_id=1, source_target_pairs={{0,24},{1,25},{2,26},{3,27},{4,28},{5,29},{6,30},{7,31},{8,16},{9,... | collective-permute-start | bytes 737288 | tf_op jit(solution)/shard_map/ppermute | solution.py:83
  340.1 10.6 %collective-permute-start.34 = (bf16[24,1280]{1,0:T(8,128)(2,1)}, bf16[24,1280]{1,0:T(8,128)(2,1)S(1)}, u32[]{:S(2)}, u32[]{:S(2)}) collective-permute-start(bf16[24,1280]{1,0:T(8,128)(2,1)} %get-tuple-element.301), channel_id=1, source_target_pairs={{0,2},{1,3},{2,0},{3,1},{4,6},{5,7},{6,4},{7,5},{8,10},{9,11},{10,... | collective-permute-start | bytes 184328 | tf_op jit(solution)/shard_map/ppermute | solution.py:83
  342.3 8.4 %collective-permute-start.35 = (bf16[24,1280]{1,0:T(8,128)(2,1)}, bf16[24,1280]{1,0:T(8,128)(2,1)}, u32[]{:S(2)}, u32[]{:S(2)}) collective-permute-start(bf16[24,1280]{1,0:T(8,128)(2,1)} %get-tuple-element.302), channel_id=1, source_target_pairs={{0,4},{1,5},{2,6},{3,7},{4,0},{5,1},{6,2},{7,3},{8,12},{9,13},{10,... | collective-permute-start | bytes 184328 | tf_op jit(solution)/shard_map/ppermute | solution.py:83
  343.5 7.2 %collective-permute-start.36 = (bf16[24,1280]{1,0:T(8,128)(2,1)}, bf16[24,1280]{1,0:T(8,128)(2,1)}, u32[]{:S(2)}, u32[]{:S(2)}) collective-permute-start(bf16[24,1280]{1,0:T(8,128)(2,1)} %get-tuple-element.303), channel_id=1, source_target_pairs={{0,6},{1,7},{2,4},{3,5},{4,2},{5,3},{6,0},{7,1},{8,14},{9,15},{10,... | collective-permute-start | bytes 184328 | tf_op jit(solution)/shard_map/ppermute | solution.py:83
  347.1 3.5 copy-start.19
  347.1 5.6 %copy-start.9 = (f32[24,1,3,3,128]{4,3,2,0,1:T(4,128)S(1)}, f32[24,1,3,3,128]{4,3,2,0,1:T(4,128)}, u32[]{:S(2)}) copy-start(f32[24,1,3,3,128]{4,3,2,0,1:T(4,128)} %stack_reshape.14) | copy-start | bytes 331780
  (15 other events, 13.6 us)
Sparse Core Ops, SparseCore 0:
  11.7 95.2 all-gather.1

commit v4 on v3

--- a/solution.py
+++ b/solution.py
@@ -73,7 +73,7 @@
         try:
             sends = job["steps"].send(came) if came is not None else next(job["steps"])
         except StopIteration as stop:
-            job["result"] = stop.value
+            job["result"] = lax.optimization_barrier(stop.value)
             return
         length = job["lengths"].pop(0) if job["lengths"] else 1
         self.waiting.append((job, sends, length))
@@ -226,73 +226,6 @@
     return jnp.concatenate(sums, -1)
 
 
-def plane_sum_kernel(where, *refs, parts):
-    keeps, cames, outs = refs[:parts], refs[parts : 2 * parts], refs[2 * parts :]
-    for step, out in enumerate(outs):
-        place = where[1] ^ step
-        start = 0
-        for keep, came in zip(keeps, cames):
-            lanes = slice(start, start + keep.shape[-1])
-            start += keep.shape[-1]
-            out[:, lanes] = keep[place] + came[place]
-
-
-def plane_sum(where, keeps, cames, size):
-    blocks, rows, _ = keeps[0].shape
-    left = blocks // size
-    columns = sum(keep.shape[2] for keep in keeps)
-    arrays = [array.reshape(size, left, rows, array.shape[2]) for array in (*keeps, *cames)]
-    part = pl.BlockSpec((None, rows, columns), lambda j, where: (j, 0, 0))
-    return pl.pallas_call(
-        functools.partial(plane_sum_kernel, parts=len(keeps)),
-        grid_spec=pltpu.PrefetchScalarGridSpec(
-            num_scalar_prefetch=1,
-            grid=(left,),
-            in_specs=[
-                pl.BlockSpec((size, None, rows, array.shape[3]), lambda j, where: (0, j, 0, 0))
-                for array in arrays
-            ],
-            out_specs=[part] * size,
-        ),
-        out_shape=[shape_of((left, rows, columns), bf16)] * size,
-        compiler_params=params(1),
-        cost_estimate=cost(blocks * rows * columns, blocks * rows * columns * 6),
-        name="plane_sum",
-    )(where, *arrays)
-
-
-def line_sum_kernel(where, *refs, sizes):
-    outs = refs[sum(sizes) :]
-    for step, out in enumerate(outs):
-        place = where[2] ^ step
-        at = start = 0
-        for size in sizes:
-            terms = refs[at : at + size]
-            at += size
-            lanes = slice(start, start + terms[0].shape[2])
-            start += terms[0].shape[2]
-            out[:, lanes] = sum(term[place].astype(f32) for term in terms).astype(out.dtype)
-
-
-def line_sum(where, groups):
-    size, rows, _ = groups[0][0].shape
-    columns = sum(group[0].shape[2] for group in groups)
-    arrays = [array for group in groups for array in group]
-    return pl.pallas_call(
-        functools.partial(line_sum_kernel, sizes=[len(group) for group in groups]),
-        grid_spec=pltpu.PrefetchScalarGridSpec(
-            num_scalar_prefetch=1,
-            grid=(1,),
-            in_specs=[once(array.shape) for array in arrays],
-            out_specs=[once((rows, columns))] * size,
-        ),
-        out_shape=[shape_of((rows, columns), f32)] + [shape_of((rows, columns), bf16)] * (size - 1),
-        compiler_params=params(1),
-        cost_estimate=cost(),
-        name="line_sum",
-    )(where, *arrays)
-
-
 def send_sum_kernel(where, *refs, sizes):
     at = 0
     for size, out in zip(sizes, refs[sum(sizes) :]):
@@ -303,15 +236,15 @@
 def fold_first(where, keep, came):
     _, _, left, rows, columns = keep.shape
     cut = columns // 2
-    spec_a = pl.BlockSpec((None, 2, None, rows, cut), lambda j, where: ((where[1] // 2) ^ 1, 0, j, 0, 0))
-    spec_b = pl.BlockSpec((2, None, None, rows, cut), lambda j, where: (0, (where[1] % 2) ^ 1, j, 0, 1))
+    spec_a = pl.BlockSpec((None, 2, 2, rows, cut), lambda j, where: ((where[1] // 2) ^ 1, 0, j, 0, 0))
+    spec_b = pl.BlockSpec((2, None, 2, rows, cut), lambda j, where: (0, (where[1] % 2) ^ 1, j, 0, 1))
     return pl.pallas_call(
         functools.partial(send_sum_kernel, sizes=[2, 2]),
         grid_spec=pltpu.PrefetchScalarGridSpec(
             num_scalar_prefetch=1,
-            grid=(left,),
+            grid=(left // 2,),
             in_specs=[spec_a, spec_a, spec_b, spec_b],
-            out_specs=[pl.BlockSpec((2, None, rows, cut), lambda j, where: (0, j, 0, 0))] * 2,
+            out_specs=[pl.BlockSpec((2, 2, rows, cut), lambda j, where: (0, j, 0, 0))] * 2,
         ),
         out_shape=[shape_of((2, left, rows, cut), bf16)] * 2,
         compiler_params=params(1),
@@ -324,20 +257,20 @@
     _, _, left, rows, columns = keep.shape
     cut = columns // 2
     spec_a = pl.BlockSpec(
-        (None, None, None, rows, cut), lambda j, where: (where[1] // 2, (where[1] % 2) ^ 1, j, 0, 0)
+        (None, None, 2, rows, cut), lambda j, where: (where[1] // 2, (where[1] % 2) ^ 1, j, 0, 0)
     )
     spec_b = pl.BlockSpec(
-        (None, None, None, rows, cut), lambda j, where: ((where[1] // 2) ^ 1, where[1] % 2, j, 0, 1)
-    )
-    half_a = pl.BlockSpec((None, None, rows, cut), lambda j, where: ((where[1] % 2) ^ 1, j, 0, 0))
-    half_b = pl.BlockSpec((None, None, rows, cut), lambda j, where: ((where[1] // 2) ^ 1, j, 0, 0))
+        (None, None, 2, rows, cut), lambda j, where: ((where[1] // 2) ^ 1, where[1] % 2, j, 0, 1)
+    )
+    half_a = pl.BlockSpec((None, 2, rows, cut), lambda j, where: ((where[1] % 2) ^ 1, j, 0, 0))
+    half_b = pl.BlockSpec((None, 2, rows, cut), lambda j, where: ((where[1] // 2) ^ 1, j, 0, 0))
     return pl.pallas_call(
         functools.partial(send_sum_kernel, sizes=[3, 3]),
         grid_spec=pltpu.PrefetchScalarGridSpec(
             num_scalar_prefetch=1,
-            grid=(left,),
+            grid=(left // 2,),
             in_specs=[spec_a, spec_a, half_a, spec_b, spec_b, half_b],
-            out_specs=[pl.BlockSpec((None, rows, cut), lambda j, where: (j, 0, 0))] * 2,
+            out_specs=[pl.BlockSpec((2, rows, cut), lambda j, where: (j, 0, 0))] * 2,
         ),
         out_shape=[shape_of((left, rows, cut), bf16)] * 2,
         compiler_params=params(1),
@@ -388,14 +321,36 @@
     return came
 
 
+def part_of(terms, axis, index, kind):
+    total = None
+    for term in terms:
+        if term.shape[axis] != 1:
+            term = pick(term, axis, index)
+        total = term.astype(f32) if total is None else total + term.astype(f32)
+    return total.astype(kind)
+
+
 def fast_sum_steps(keeps, cames, where, mesh):
     count = mesh.size
     _, outer, rest = bit_groups(mesh)
-    own, *sends = plane_sum(where, keeps, cames, 1 << len(outer))
+    me = lax.axis_index(AXES)
+    spot = position(me, outer)
+    size, line = 1 << len(outer), 1 << len(rest[0])
+    terms = []
+    for pair in zip(keeps, cames):
+        for array in pair:
+            lead = keeps[0].shape[2] - array.shape[2]
+            array = jnp.pad(array, ((0, 0), (0, 0), (lead, 0))) if lead else array
+            terms.append(array.reshape((size, line) + array.shape[1:]))
+    sends = [part_of(terms, 0, spot ^ step, bf16)[0] for step in range(1, size)]
+    terms = [pick(term, 0, spot)[0] for term in terms]
     came = yield [(array, pairs) for array, (_, pairs) in zip(sends, partners(count, outer))]
-    own, *sends = line_sum(where, [[own, *came]])
-    came = yield [(array, pairs) for array, (_, pairs) in zip(sends, partners(count, rest[0]))]
-    return own + sum(array.astype(f32) for array in came)
+    terms = terms + came
+    spot = position(me, rest[0])
+    came = yield [
+        (part_of(terms, 0, spot ^ step, bf16)[0], pairs) for step, pairs in partners(count, rest[0])
+    ]
+    return part_of(terms, 0, spot, f32)[0] + sum(array.astype(f32) for array in came)
 
 
 def fold_sum_steps(keep, send, where, mesh):
@@ -617,10 +572,11 @@
     )(valid, *arrays)
 
 
-def attend_back_kernel(where, *refs, pairs, extra, cut):
+def attend_back_kernel(where, *refs, pairs, extra, carry, cut):
     lists = [refs[kind * pairs : (kind + 1) * pairs] for kind in range(5)]
     joined, mixed_grad, mixed, raised, inverse = lists
     normed, *rest = refs[5 * pairs :]
+    carried, rest = rest[:carry], rest[carry:]
     if extra:
         mixed_a, mixed_b, low_grad, joined_grad, column, *outs, held, scaled, total, total_out = rest
     else:
@@ -680,12 +636,18 @@
 
     @pl.when(item == pl.num_programs(0) - 1)
     def _():
-        store_cut(where[0], outs, slice(0, span), total[...], cut)
+        begin = 0
+        for before, out in zip(carried, outs):
+            begin = before.shape[-1]
+            out[..., :begin] = before[...]
+            if out.shape[-1] > begin + span:
+                out[..., begin + span :] = jnp.zeros(out.shape[:-1] + (out.shape[-1] - begin - span,), bf16)
+        store_cut(where[0], outs, slice(begin, begin + span), total[...], cut)
         if extra:
             store_cut(where[0], outs, slice(span, span + total_out.shape[1]), total_out[...], cut)
 
 
-def attend_back(mixed_grad, where, joined, mixed, raised, inverse, normed, seq, part, chosen, cut, others=()):
+def attend_back(mixed_grad, where, joined, mixed, raised, inverse, normed, seq, part, chosen, cut, others=(), carried=()):
     rows, width = normed.shape
     items, in_part, _, keys = raised.shape
     pairs = len(chosen)
@@ -696,16 +658,19 @@
         pl.BlockSpec((None, None, seq, keys), functools.partial(lambda at, i, *_: (i, at, 0, 0), pair))
         for pair in chosen
     ]
-    columns = span + (width if others else 0)
+    columns = span + (width if others else 0) + (carried[0].shape[-1] + 128 if carried else 0)
     specs, shapes = cut_shapes(width, columns, columns, lambda j: 0, cut)
     return pl.pallas_call(
-        functools.partial(attend_back_kernel, pairs=pairs, extra=bool(others), cut=cut),
+        functools.partial(
+            attend_back_kernel, pairs=pairs, extra=bool(others), carry=len(carried), cut=cut
+        ),
         grid_spec=pltpu.PrefetchScalarGridSpec(
             num_scalar_prefetch=1,
             grid=(items,),
             in_specs=[
                 *each(384), *each(128, part * in_part), *each(128), *weights, *each(128), row(width)
             ]
+            + [once(array.shape) for array in carried]
             + [row(array.shape[1]) for array in others],
             out_specs=[row(span), pl.BlockSpec((1, span), lambda i, *_: (0, 0))] + specs,
             scratch_shapes=[
@@ -721,7 +686,7 @@
         name="attend_back",
     )(
         where, *[joined] * pairs, *[mixed_grad] * pairs, *[mixed] * pairs, *[raised] * pairs,
-        *[inverse] * pairs, normed, *others,
+        *[inverse] * pairs, normed, *carried, *others,
     )
 
 
@@ -1058,14 +1023,14 @@
         mixed_grad,
     )
     sum_a = sums_after([grads_a], [swap_a])
+    joined_grad_c, qkv_sum_c, *grads_b = flights.run(
+        lambda x: attend_back(
+            x, where, joined_b, mixed_b, raised_b, inverse_b, normed, seq, 1, range(1, half // 128), cut,
+            carried=grads_b,
+        ),
+        mixed_grad,
+    )
     swap_b = swap(grads_b)
-    joined_grad_c, qkv_sum_c, *grads_c = flights.run(
-        lambda x: attend_back(
-            x, where, joined_b, mixed_b, raised_b, inverse_b, normed, seq, 1, range(1, half // 128), cut
-        ),
-        mixed_grad,
-    )
-    swap_c = swap(grads_c)
     spans = ((0, slice(0, span)), (1, slice(0, 384)), (1, slice(384, span)))
     input_grad, gain_one_sum, shift_one_sum = flights.run(
         lambda x: input_back(
@@ -1102,7 +1067,6 @@
         swap_small = swap(small)
     else:
         small_job = flights.add(small_sum_steps(small, mesh), [])
-        grads_b = [jnp.concatenate([grads_b[0], grads_c[0]], 1)]
         sum_b = sums_after([grads_b], [None])
     cuts = [0, items // 2 * seq, rows]
     block_out = None
@@ -1115,7 +1079,7 @@
                 middle,
             )
             if cut and begin == 0:
-                sum_b = sums_after([grads_b, grads_c, small], [swap_b, swap_c, swap_small])
+                sum_b = sums_after([grads_b, small], [swap_b, swap_small])
     flights.finish()
     total_a, total_b = sum_a["result"], sum_b["result"]
     if cut:

time: 366 us -> 365 us (level)
  Pallas kernels: 241 us -> 226 us
  other arithmetic: 3.66 us -> 16.5 us
    pallas_call x4 -> x0, Pallas kernels: 14.8 us -> none  [the longest x2 9.27 us: plane_sum(): pl.pallas_call(functools.partial(plane_sum_kernel, parts=len(keeps)), gri...]
    squeeze x0 -> x4, other arithmetic: none -> 6.37 us  [the longest x2 4.06 us: fast_sum_steps(): part_of(terms, 0, spot ^ step, bf16)[0]]
    unnamed x89 -> x79, local copies, waits for them, and re-layouts: 7.33 us -> 5.26 us
    ppermute x37 -> x36, starting transfers between devices: 40.8 us -> 40.2 us  [depart(): came = [lax.ppermute(array, AXES, pairs) for array, pairs in sends]]
    ppermute x37 -> x36, waiting for transfers between devices: 21.3 us -> 21.8 us  [depart(): came = [lax.ppermute(array, AXES, pairs) for array, pairs in sends]]
  transfers between devices with their start and end apart: 38 -> 37, of which waited for: 7 -> 8; matrix products, arithmetic and copies ran while one was open for 7% -> 9% of each run, Pallas kernels for 44% -> 45%
where the time goes in v4:
time: 365 us; the launch traced here: 360 us
  Pallas kernels  226 us (62%)
  starting transfers between devices  40.3 us (11%)
  local copies, waits for them, and re-layouts  39.8 us (11%)
  waiting for transfers between devices  21.8 us (6%)
  other arithmetic  16.5 us (5%)
  between operations  15.6 us (4%)
    pallas_call x3, Pallas kernels, attend_back(): pl.pallas_call(functools.partial(attend_back_kernel, pairs=pairs, extra=b...  61.1 us
    pallas_call x1, Pallas kernels, mlp(): pl.pallas_call(functools.partial(mlp_kernel, seq=seq, tile=tile_of(seq),...  52.5 us
    pallas_call x2, Pallas kernels, attend(): pl.pallas_call(functools.partial(attend_kernel, tile=tile_of(seq), padded...  44.6 us
    ppermute x36, starting transfers between devices, depart(): came = [lax.ppermute(array, AXES, pairs) for array, pairs in sends]  40.2 us
    ppermute x36, waiting for transfers between devices, depart(): came = [lax.ppermute(array, AXES, pairs) for array, pairs in sends]  21.8 us
    pallas_call x1, Pallas kernels, middle_back(): pl.pallas_call(functools.partial(middle_back_kernel, seq=seq, sub=sub), g...  20.6 us
    pallas_call x2, Pallas kernels, block_out_of(): pl.pallas_call(functools.partial(block_out_kernel, seq=seq, begin=begin),...  19.8 us
    pallas_call x1, Pallas kernels, input_back(): pl.pallas_call(functools.partial(input_back_kernel, spans=spans, sub=sub)...  15.1 us
  transfers between devices with their start and end apart: 37, of which 8 were waited for; matrix products, arithmetic and copies ran while one was open for 9% of the time, Pallas kernels for 45%

profile of v4, /device:TPU:0, one launch (start us, length us, event | category | flops | bytes accessed | tf_op | source)
XLA Modules:
  0.0 360.2 jit_solution(7805252237378984256)
XLA Ops:
  7.2 2.0 reshape.591
  9.4 1.3 reshape.592
  12.0 3.1 collective-permute-start
  15.1 2.6 collective-permute-start.1
  17.8 2.0 collective-permute-start.3
  20.0 4.9 %collective-permute-done.1 = bf16[1,1,1,1,1,24,1280]{6,5,4,3,2,1,0:T(8,128)(2,1)S(1)} collective-permute-done((bf16[1,1,1,1,1,24,1280]{6,5,4,3,2,1,0:T(8,128)(2,1)S(1)}, bf16[1,1,1,1,1,24,1280]{6,5,4,3,2,1,0:T(8,128)(2,1)S(1)}, u32[]{:S(2)}, u32[]{:S(2)}) %collective-permute-start.1) | collective-permute-done | bytes 61472 | tf_op jit(solution)/shard_map/ppermute | solution.py:83
  24.8 4.0 %collective-permute-done.3 = bf16[1,1,1,1,1,24,1920]{6,5,4,3,2,1,0:T(8,128)(2,1)S(1)} collective-permute-done((bf16[1,1,1,1,1,24,1920]{6,5,4,3,2,1,0:T(8,128)(2,1)S(1)}, bf16[1,1,1,1,1,24,1920]{6,5,4,3,2,1,0:T(8,128)(2,1)S(1)}, u32[]{:S(2)}, u32[]{:S(2)}) %collective-permute-start.3) | collective-permute-done | bytes 92192 | tf_op jit(solution)/shard_map/ppermute | solution.py:83
  28.9 1.6 collective-permute-start.4
  30.5 1.6 collective-permute-start.5
  33.0 5.8 %collective-permute-done.7 = bf16[1,1,2,1,1,24,1920]{6,5,4,3,2,1,0:T(8,128)(2,1)S(1)} collective-permute-done((bf16[1,1,2,1,1,24,1920]{6,5,4,3,2,1,0:T(8,128)(2,1)S(1)}, bf16[1,1,2,1,1,24,1920]{6,5,4,3,2,1,0:T(8,128)(2,1)S(1)}, u32[]{:S(2)}, u32[]{:S(2)}) %collective-permute-start.7) | collective-permute-done | bytes 184352 | tf_op jit(solution)/shard_map/ppermute | solution.py:83
  38.8 2.3 collective-permute-done.5
  42.0 1.6 collective-permute-start.10
  43.6 1.2 collective-permute-start.11
  45.6 1.2 broadcast_in_dim.31
  47.9 1.3 constant_dynamic-update-slice_fusion.8
  49.5 0.9 fusion.45
  51.1 19.7 %attend.2 = (bf16[1824,768]{1,0:T(8,128)(2,1)}, bf16[1824,1152]{1,0:T(8,128)(2,1)}, bf16[1824,384]{1,0:T(8,128)(2,1)}, bf16[3,3,608,1280]{3,2,1,0:T(8,128)(2,1)}, f32[1824,384]{1,0:T(8,128)}) custom-call(s32[3]{0:T(128)} %get-tuple-element.307.valid, bf16[1824,768]{1,0:T(8,128)(2,1)} %bitcast.186, f32[1,768]{1,0:T(1,128)} %get-tuple-element.304.refs_1_.refs_7_, ...), custom_call_target="tpu_custom_call" | custom-call | flops 1 | bytes 1 | tf_op jit(solution)/shard_map/attend/pallas_call | solution.py:563
  70.9 1.8 constant_dynamic-update-slice_fusion.4
  72.6 1.8 constant_dynamic-update-slice_fusion.3
  74.4 1.9 constant_dynamic-update-slice_fusion.2
  78.0 1.6 constant_dynamic-update-slice_fusion.1
  79.9 1.6 constant_dynamic-update-slice_fusion
  81.5 1.5 copy-done
  83.0 24.9 %attend.3 = (bf16[1824,1152]{1,0:T(8,128)(2,1)}, bf16[1824,384]{1,0:T(8,128)(2,1)}, bf16[3,3,608,1280]{3,2,1,0:T(8,128)(2,1)}, f32[1824,384]{1,0:T(8,128)}, f32[...) custom-call(s32[3]{0:T(128)} %get-tuple-element.307.valid, ...), custom_call_target="tpu_custom_call" | custom-call | flops 1 | bytes 1 | tf_op jit(solution)/shard_map/attend/pallas_call | solution.py:563
  107.9 52.5 %mlp.1 = (bf16[1824,3072]{1,0:T(8,128)(2,1)}, bf16[1824,3072]{1,0:T(8,128)(2,1)}, f32[1,3072]{1,0:T(1,128)}, bf16[768,3072]{1,0:T(8,128)(2,1)}, bf16[768,3072]{1,0:T(8,128)(2,1)}) custom-call(s32[3]{0:T(128)} %get-tuple-element.307.valid, s32[3]{0:T(128)} %get-tuple-element.306.where, bf16[1824,768]{1,0:T(8,128)(2,1)} %get-tuple-element.160.normed, ...), custom_call_target="tpu_custom_call" | custom-call | flops 1 | bytes 1 | tf_op jit(solution)/shard_map/mlp/pallas_call | solution.py:752
  160.6 20.6 %middle_back.1 = (bf16[1824,768]{1,0:T(8,128)(2,1)}, bf16[1824,768]{1,0:T(8,128)(2,1)}, f32[1,768]{1,0:T(1,128)}, f32[1,768]{1,0:T(1,128)}, f32[1,768]{1,0:T(1,128)}, /*index=5*/f32[1,768]{1,0:T(1,128)}) custom-call(s32[3]{0:T(128)} %get-tuple-element.307.valid, bf16[1824,3072]{1,0:T(8,128)(2,1)} %get-tuple-element.164.hidden_grad, ...), custom_call_target="tpu_custom_call" | custom-call | flops 1 | bytes 1 | tf_op jit(solution)/shard_map/middle_back/pallas_call | solution.py:852
  181.2 4.4 %fold_first.1 = (bf16[2,4,48,1536]{3,2,1,0:T(8,128)(2,1)}, bf16[2,4,48,1536]{3,2,1,0:T(8,128)(2,1)}) custom-call(s32[3]{0:T(128)} %get-tuple-element.306.where, bf16[2,2,4,48,3072]{4,3,2,1,0:T(8,128)(2,1)} %bitcast.177, bf16[2,2,4,48,3072]{4,3,2,1,0:T(8,128)(2,1)} %bitcast.23.refs_1_.refs_3_.refs_4_.refs_5_, bf16[2,2,4,48,3072]{4,3,2,1,0:T(8,128)(2,1)} %bitcast.178, ...), custom_call_target="tpu_custom_call" | custom-call | flops 1 | bytes 1 | tf_op jit(solution)/shard_map/fold_first/pallas_call | solution.py:241
  185.6 1.6 collective-permute-start.14
  187.2 1.5 collective-permute-start.15
  188.7 30.6 %attend_back.3 = (bf16[1824,1152]{1,0:T(8,128)(2,1)}, f32[1,1152]{1,0:T(1,128)}, bf16[16,24,1920]{2,1,0:T(8,128)(2,1)}, bf16[16,24,1920]{2,1,0:T(8,128)(2,1)}) custom-call(s32[3]{0:T(128)} %get-tuple-element.306.where, bf16[1824,1152]{1,0:T(8,128)(2,1)} %get-tuple-element.177.refs_0_.refs_1_.refs_2_, ...), custom_call_target="tpu_custom_call" | custom-call | flops 1 | bytes 1 | tf_op jit(solution)/shard_map/attend_back/pallas_call | solution.py:663
  219.3 1.0 copy-done.2
  220.7 3.7 %fold_second.1 = (bf16[4,48,1536]{2,1,0:T(8,128)(2,1)}, bf16[4,48,1536]{2,1,0:T(8,128)(2,1)}) custom-call(s32[3]{0:T(128)} %get-tuple-element.306.where, bf16[2,2,4,48,3072]{4,3,2,1,0:T(8,128)(2,1)} %bitcast.179, bf16[2,2,4,48,3072]{4,3,2,1,0:T(8,128)(2,1)} %bitcast.23.refs_1_.refs_3_.refs_4_.refs_5_, bf16[2,4,48,1536]{3,2,1,0:T(8,128)(2,1)} %copy-done.2, ...), custom_call_target="tpu_custom_call" | custom-call | flops 1 | bytes 1 | tf_op jit(solution)/shard_map/fold_second/pallas_call | solution.py:267
  225.4 11.4 %attend_back.4 = (bf16[1824,384]{1,0:T(8,128)(2,1)}, f32[1,384]{1,0:T(1,128)}, bf16[16,24,384]{2,1,0:T(8,128)(2,1)}, bf16[16,24,384]{2,1,0:T(8,128)(2,1)}) custom-call(s32[3]{0:T(128)} %get-tuple-element.306.where, bf16[1824,1152]{1,0:T(8,128)(2,1)} %get-tuple-element.163.refs_0_.refs_1_, ...), custom_call_target="tpu_custom_call" | custom-call | flops 1 | bytes 1 | tf_op jit(solution)/shard_map/attend_back/pallas_call | solution.py:663
  236.8 3.5 collective-permute-done.16.refs_3_
  240.6 0.8 copy-done.12
  241.4 4.6 %line_first.1 = (bf16[2,48,3072]{2,1,0:T(8,128)(2,1)}, bf16[2,48,3072]{2,1,0:T(8,128)(2,1)}) custom-call(s32[3]{0:T(128)} %get-tuple-element.306.where, bf16[2,2,4,48,3072]{4,3,2,1,0:T(8,128)(2,1)} %bitcast.181, bf16[2,2,4,48,3072]{4,3,2,1,0:T(8,128)(2,1)} %bitcast.23.refs_1_.refs_3_.refs_4_.refs_5_, bf16[2,4,48,1536]{3,2,1,0:T(8,128)(2,1)} %copy-done.2, ...), custom_call_target="tpu_custom_call" | custom-call | flops 1 | bytes 1 | tf_op jit(solution)/shard_map/line_first/pallas_call | solution.py:303
  246.0 1.1 fusion.2
  247.2 1.3 collective-permute-start.19
  249.8 2.2 collective-permute-start.22
  252.0 19.1 %attend_back.5 = (bf16[1824,768]{1,0:T(8,128)(2,1)}, f32[1,768]{1,0:T(1,128)}, bf16[16,24,1280]{2,1,0:T(8,128)(2,1)}, bf16[16,24,1280]{2,1,0:T(8,128)(2,1)}) custom-call(s32[3]{0:T(128)} %get-tuple-element.306.where, bf16[1824,1152]{1,0:T(8,128)(2,1)} %get-tuple-element.163.refs_0_.refs_1_, bf16[1824,1152]{1,0:T(8,128)(2,1)} %get-tuple-element.163.refs_0_.refs_1_, ...), custom_call_target="tpu_custom_call" | custom-call | flops 1 | bytes 1 | tf_op jit(solution)/shard_map/attend_back/pallas_call | solution.py:663
  271.1 1.8 add_convert_fusion.3
  272.9 2.1 fusion.31
  277.2 2.7 collective-permute-start.23
  280.9 3.4 collective-permute-start.26
  284.3 15.1 %input_back.1 = (bf16[1824,768]{1,0:T(8,128)(2,1)}, f32[1,768]{1,0:T(1,128)}, f32[1,768]{1,0:T(1,128)}) custom-call(bf16[1824,1152]{1,0:T(8,128)(2,1)} %get-tuple-element.223.refs_0_, bf16[1824,384]{1,0:T(8,128)(2,1)} %get-tuple-element.224.refs_1_, bf16[1824,768]{1,0:T(8,128)(2,1)} %get-tuple-element.232.refs_2_, bf16[768,1280]{1,0:T(8,128)(2,1)} %bitcast.191, ...), custom_call_target="tpu_custom_call" | custom-call | flops 1 | bytes 1 | tf_op jit(solution)/shard_map/input_back/pallas_call | solution.py:906
  302.2 1.1 convert_add_fusion
  304.0 8.2 %block_out.2.rest_0_ = bf16[1824,768]{1,0:T(8,128)(2,1)} custom-call(s32[3]{0:T(128)} %get-tuple-element.307.valid, bf16[1824,3072]{1,0:T(8,128)(2,1)} %get-tuple-element.161.active, bf16[768,6144]{1,0:T(8,128)(2,1)} %all-gather.2.cloned.1.call-done.up.down.ups.downs, f32[1824,768]{1,0:T(8,128)} %get-tuple-element.257.middle, ...), custom_call_target="tpu_custom_call" | custom-call | flops 1 | bytes 1 | tf_op jit(solution)/shard_map/block_out/pallas_call | solution.py:803
  312.9 1.2 pad.34
  314.1 1.2 fusion.5
  315.3 1.4 collective-permute-start.30
  317.2 1.6 collective-permute-start.32
  318.8 1.2 bitcast_add_fusion
  321.2 1.6 stack_reshape.14
  322.8 1.5 reshape.614
  324.4 11.6 %block_out.3 = bf16[1824,768]{1,0:T(8,128)(2,1)} custom-call(s32[3]{0:T(128)} %get-tuple-element.307.valid, bf16[1824,3072]{1,0:T(8,128)(2,1)} %get-tuple-element.161.active, bf16[768,6144]{1,0:T(8,128)(2,1)} %all-gather.2.cloned.1.call-done.up.down.ups.downs, f32[1824,768]{1,0:T(8,128)} %get-tuple-element.257.middle, ...), custom_call_target="tpu_custom_call", output_to_operand_aliasing={{}: (5, {})} | custom-call | flops 1 | bytes 1 | tf_op jit(solution)/shard_map/block_out/pallas_call | solution.py:803
  336.0 2.0 fusion.36
  338.0 2.3 collective-permute-start.33
  340.3 0.9 collective-permute-start.34
  341.2 1.5 collective-permute-start.35
  342.7 1.0 select_bitcast_fusion
  343.7 1.1 reshape.615
  344.8 1.2 copy.43
  346.1 2.5 reshape.616
  349.6 1.2 bitcast_add_fusion.8
  (218 shorter events, 23.6 us)
Async XLA Ops:
  7.2 3.5 copy-start.15
  7.2 100.7 %all-gather.2.cloned.1.call-start = ((), (), s32[]{:S(2)}) async-start(), calls=%async_computation | async-start | bytes 9732096 | tf_op jit(solution)/shard_map/all_gather | solution.py:972
  9.2 2.4 copy-start.16
  9.4 2.5 copy-start.34
  9.4 2.5 copy-start.35
  9.4 8.3 %copy-start.24 = (bf16[18432]{0:T(1024)(128)(2,1)S(1)}, bf16[18432]{0:T(1024)(128)(2,1)}, u32[]{:S(2)}) copy-start(bf16[18432]{0:T(1024)(128)(2,1)} %param.15) | copy-start | bytes 110596
  12.0 8.0 %collective-permute-start = (bf16[1,1,1,1,1,24,1280]{6,5,4,3,2,1,0:T(8,128)(2,1)S(1)}, bf16[1,1,1,1,1,24,1280]{6,5,4,3,2,1,0:T(8,128)(2,1)S(1)}, u32[]{:S(2)}, u32[]{:S(2)}) collective-permute-start(bf16[1,1,1,1,1,24,1280]{6,5,4,3,2,1,0:T(8,128)(2,1)S(1)} %fusion.33), channel_id=1, source_target_pairs={{0,2},{1,3},{2,0},{3,1},{4,6},{5,7},{6,4},{7,5},{8,10},{9,11},{10,... | collective-permute-start | bytes 184328 | tf_op jit(solution)/shard_map/ppermute | solution.py:83
  15.1 9.8 %collective-permute-start.1 = (bf16[1,1,1,1,1,24,1280]{6,5,4,3,2,1,0:T(8,128)(2,1)S(1)}, bf16[1,1,1,1,1,24,1280]{6,5,4,3,2,1,0:T(8,128)(2,1)S(1)}, u32[]{:S(2)}, u32[]{:S(2)}) collective-permute-start(bf16[1,1,1,1,1,24,1280]{6,5,4,3,2,1,0:T(8,128)(2,1)S(1)} %fusion.33), channel_id=1, source_target_pairs={{0,4},{1,5},{2,6},{3,7},{4,0},{5,1},{6,2},{7,3},{8,12},{9,13},{10,... | collective-permute-start | bytes 184328 | tf_op jit(solution)/shard_map/ppermute | solution.py:83
  17.6 7.2 %collective-permute-start.2 = (bf16[1,1,1,1,1,24,1280]{6,5,4,3,2,1,0:T(8,128)(2,1)S(1)}, bf16[1,1,1,1,1,24,1280]{6,5,4,3,2,1,0:T(8,128)(2,1)S(1)}, u32[]{:S(2)}, u32[]{:S(2)}) collective-permute-start(bf16[1,1,1,1,1,24,1280]{6,5,4,3,2,1,0:T(8,128)(2,1)S(1)} %fusion.33), channel_id=1, source_target_pairs={{0,6},{1,7},{2,4},{3,5},{4,2},{5,3},{6,0},{7,1},{8,14},{9,15},{10,... | collective-permute-start | bytes 184328 | tf_op jit(solution)/shard_map/ppermute | solution.py:83
  17.8 11.0 %collective-permute-start.3 = (bf16[1,1,1,1,1,24,1920]{6,5,4,3,2,1,0:T(8,128)(2,1)S(1)}, bf16[1,1,1,1,1,24,1920]{6,5,4,3,2,1,0:T(8,128)(2,1)S(1)}, u32[]{:S(2)}, u32[]{:S(2)}) collective-permute-start(bf16[1,1,1,1,1,24,1920]{6,5,4,3,2,1,0:T(8,128)(2,1)S(1)} %maximum_bitcast_fusion.1), channel_id=1, source_target_pairs={{0,4},{1,5},{2,6},{3,7},{4,0},{5,1},{6,2},{7,3},{8,12},{9,13},{10,... | collective-permute-start | bytes 276488 | tf_op jit(solution)/shard_map/ppermute | solution.py:83
  19.8 21.4 %copy-start.32 = (s32[3]{0:T(128)S(1)}, s32[3]{0:T(128)}, u32[]{:S(2)}) copy-start(s32[3]{0:T(128)} %param.13) | copy-start | bytes 40
  19.9 21.4 %copy-start.33 = (s32[3]{0:T(128)S(1)}, s32[3]{0:T(128)}, u32[]{:S(2)}) copy-start(s32[3]{0:T(128)} %param.12) | copy-start | bytes 40
  28.9 9.9 %collective-permute-start.4 = (bf16[1,1,2,2,1,24,1280]{6,5,4,3,2,1,0:T(8,128)(2,1)S(1)}, bf16[1,1,2,2,1,24,1280]{6,5,4,3,2,1,0:T(8,128)(2,1)S(1)}, u32[]{:S(2)}, u32[]{:S(2)}) collective-permute-start(bf16[1,1,2,2,1,24,1280]{6,5,4,3,2,1,0:T(8,128)(2,1)S(1)} %constant_dynamic-update-slice_fusion.16), channel_id=1, source_target_pairs={{0,8},{1,9},{2,10},{3,11},{4,12},{5,13},{6,14},{7,15},{8,0},{9,1},... | collective-permute-start | bytes 737288 | tf_op jit(solution)/shard_map/ppermute | solution.py:83
  30.5 10.5 %collective-permute-start.5 = (bf16[1,1,2,2,1,24,1280]{6,5,4,3,2,1,0:T(8,128)(2,1)S(1)}, bf16[1,1,2,2,1,24,1280]{6,5,4,3,2,1,0:T(8,128)(2,1)S(1)}, u32[]{:S(2)}, u32[]{:S(2)}) collective-permute-start(bf16[1,1,2,2,1,24,1280]{6,5,4,3,2,1,0:T(8,128)(2,1)S(1)} %constant_dynamic-update-slice_fusion.16), channel_id=1, source_target_pairs={{0,16},{1,17},{2,18},{3,19},{4,20},{5,21},{6,22},{7,23},{8,24},{9,... | collective-permute-start | bytes 737288 | tf_op jit(solution)/shard_map/ppermute | solution.py:83
  32.1 9.0 %collective-permute-start.6 = (bf16[1,1,2,2,1,24,1280]{6,5,4,3,2,1,0:T(8,128)(2,1)S(1)}, bf16[1,1,2,2,1,24,1280]{6,5,4,3,2,1,0:T(8,128)(2,1)S(1)}, u32[]{:S(2)}, u32[]{:S(2)}) collective-permute-start(bf16[1,1,2,2,1,24,1280]{6,5,4,3,2,1,0:T(8,128)(2,1)S(1)} %constant_dynamic-update-slice_fusion.16), channel_id=1, source_target_pairs={{0,24},{1,25},{2,26},{3,27},{4,28},{5,29},{6,30},{7,31},{8,16},{9,... | collective-permute-start | bytes 737288 | tf_op jit(solution)/shard_map/ppermute | solution.py:83
  32.5 6.3 %collective-permute-start.7 = (bf16[1,1,2,1,1,24,1920]{6,5,4,3,2,1,0:T(8,128)(2,1)S(1)}, bf16[1,1,2,1,1,24,1920]{6,5,4,3,2,1,0:T(8,128)(2,1)S(1)}, u32[]{:S(2)}, u32[]{:S(2)}) collective-permute-start(bf16[1,1,2,1,1,24,1920]{6,5,4,3,2,1,0:T(8,128)(2,1)S(1)} %constant_dynamic-update-slice_fusion.13), channel_id=1, source_target_pairs={{0,2},{1,3},{2,0},{3,1},{4,6},{5,7},{6,4},{7,5},{8,10},{9,11},{10,... | collective-permute-start | bytes 552968 | tf_op jit(solution)/shard_map/ppermute | solution.py:83
  41.2 6.7 %collective-permute-start.8 = (bf16[2,2,2,2,1,24,1280]{6,5,4,3,2,1,0:T(8,128)(2,1)S(1)}, bf16[2,2,2,2,1,24,1280]{6,5,4,3,2,1,0:T(8,128)(2,1)}, u32[]{:S(2)}, u32[]{:S(2)}) collective-permute-start(bf16[2,2,2,2,1,24,1280]{6,5,4,3,2,1,0:T(8,128)(2,1)S(1)} %constant_dynamic-update-slice_fusion.10), channel_id=1, source_target_pairs={{0,1},{1,0},{2,3},{3,2},{4,5},{5,4},{6,7},{7,6},{8,9},{9,8},{10,11... | collective-permute-start | bytes 2949128 | tf_op jit(solution)/shard_map/ppermute | solution.py:83
  42.0 28.9 %collective-permute-start.10 = (bf16[1,1,2,2,1,24,1920]{6,5,4,3,2,1,0:T(8,128)(2,1)S(1)}, bf16[1,1,2,2,1,24,1920]{6,5,4,3,2,1,0:T(8,128)(2,1)}, u32[]{:S(2)}, u32[]{:S(2)}) collective-permute-start(bf16[1,1,2,2,1,24,1920]{6,5,4,3,2,1,0:T(8,128)(2,1)S(1)} %constant_dynamic-update-slice_fusion.6), channel_id=1, source_target_pairs={{0,16},{1,17},{2,18},{3,19},{4,20},{5,21},{6,22},{7,23},{8,24},{9,... | collective-permute-start | bytes 1105928 | tf_op jit(solution)/shard_map/ppermute | solution.py:83
  43.6 27.3 %collective-permute-start.11 = (bf16[1,1,2,2,1,24,1920]{6,5,4,3,2,1,0:T(8,128)(2,1)S(1)}, bf16[1,1,2,2,1,24,1920]{6,5,4,3,2,1,0:T(8,128)(2,1)}, u32[]{:S(2)}, u32[]{:S(2)}) collective-permute-start(bf16[1,1,2,2,1,24,1920]{6,5,4,3,2,1,0:T(8,128)(2,1)S(1)} %constant_dynamic-update-slice_fusion.6), channel_id=1, source_target_pairs={{0,24},{1,25},{2,26},{3,27},{4,28},{5,29},{6,30},{7,31},{8,16},{9,... | collective-permute-start | bytes 1105928 | tf_op jit(solution)/shard_map/ppermute | solution.py:83
  44.8 26.1 %collective-permute-start.9 = (bf16[1,1,2,2,1,24,1920]{6,5,4,3,2,1,0:T(8,128)(2,1)S(1)}, bf16[1,1,2,2,1,24,1920]{6,5,4,3,2,1,0:T(8,128)(2,1)}, u32[]{:S(2)}, u32[]{:S(2)}) collective-permute-start(bf16[1,1,2,2,1,24,1920]{6,5,4,3,2,1,0:T(8,128)(2,1)S(1)} %constant_dynamic-update-slice_fusion.6), channel_id=1, source_target_pairs={{0,8},{1,9},{2,10},{3,11},{4,12},{5,13},{6,14},{7,15},{8,0},{9,1},... | collective-permute-start | bytes 1105928 | tf_op jit(solution)/shard_map/ppermute | solution.py:83
  76.3 3.6 %collective-permute-start.12 = (bf16[2,2,2,2,1,24,1920]{6,5,4,3,2,1,0:T(8,128)(2,1)}, bf16[2,2,2,2,1,24,1920]{6,5,4,3,2,1,0:T(8,128)(2,1)}, u32[]{:S(2)}, u32[]{:S(2)}) collective-permute-start(bf16[2,2,2,2,1,24,1920]{6,5,4,3,2,1,0:T(8,128)(2,1)} %constant_dynamic-update-slice_fusion.2), channel_id=1, source_target_pairs={{0,1},{1,0},{2,3},{3,2},{4,5},{5,4},{6,7},{7,6},{8,9},{9,8},{10,11... | collective-permute-start | bytes 4423688 | tf_op jit(solution)/shard_map/ppermute | solution.py:83
  160.4 20.8 %collective-permute-start.13 = (bf16[768,3072]{1,0:T(8,128)(2,1)}, bf16[768,3072]{1,0:T(8,128)(2,1)}, u32[]{:S(2)}, u32[]{:S(2)}) collective-permute-start(bf16[768,3072]{1,0:T(8,128)(2,1)} %get-tuple-element.173), channel_id=1, source_target_pairs={{0,1},{1,0},{2,3},{3,2},{4,5},{5,4},{6,7},{7,6},{8,9},{9,8},{10,11... | collective-permute-start | bytes 14155784 | tf_op jit(solution)/shard_map/ppermute | solution.py:83
  185.6 33.6 %collective-permute-start.14 = (bf16[2,4,48,1536]{3,2,1,0:T(8,128)(2,1)}, bf16[2,4,48,1536]{3,2,1,0:T(8,128)(2,1)S(1)}, u32[]{:S(2)}, u32[]{:S(2)}) collective-permute-start(bf16[2,4,48,1536]{3,2,1,0:T(8,128)(2,1)} %get-tuple-element.189), channel_id=1, source_target_pairs={{0,16},{1,17},{2,18},{3,19},{4,20},{5,21},{6,22},{7,23},{8,24},{9,... | collective-permute-start | bytes 3538952 | tf_op jit(solution)/shard_map/ppermute | solution.py:83
  187.2 32.0 %collective-permute-start.15 = (bf16[2,4,48,1536]{3,2,1,0:T(8,128)(2,1)}, bf16[2,4,48,1536]{3,2,1,0:T(8,128)(2,1)S(1)}, u32[]{:S(2)}, u32[]{:S(2)}) collective-permute-start(bf16[2,4,48,1536]{3,2,1,0:T(8,128)(2,1)} %get-tuple-element.190), channel_id=1, source_target_pairs={{0,8},{1,9},{2,10},{3,11},{4,12},{5,13},{6,14},{7,15},{8,0},{9,1},... | collective-permute-start | bytes 3538952 | tf_op jit(solution)/shard_map/ppermute | solution.py:83
  224.3 16.3 %collective-permute-start.18 = (bf16[16,24,1920]{2,1,0:T(8,128)(2,1)}, bf16[16,24,1920]{2,1,0:T(8,128)(2,1)S(1)}, u32[]{:S(2)}, u32[]{:S(2)}) collective-permute-start(bf16[16,24,1920]{2,1,0:T(8,128)(2,1)} %get-tuple-element.205), channel_id=1, source_target_pairs={{0,1},{1,0},{2,3},{3,2},{4,5},{5,4},{6,7},{7,6},{8,9},{9,8},{10,11... | collective-permute-start | bytes 4423688 | tf_op jit(solution)/shard_map/ppermute | solution.py:83
  224.3 15.9 %collective-permute-start.16 = (bf16[4,48,1536]{2,1,0:T(8,128)(2,1)}, bf16[4,48,1536]{2,1,0:T(8,128)(2,1)S(1)}, u32[]{:S(2)}, u32[]{:S(2)}) collective-permute-start(bf16[4,48,1536]{2,1,0:T(8,128)(2,1)} %get-tuple-element.203), channel_id=1, source_target_pairs={{0,8},{1,9},{2,10},{3,11},{4,12},{5,13},{6,14},{7,15},{8,0},{9,1},... | collective-permute-start | bytes 1769480 | tf_op jit(solution)/shard_map/ppermute | solution.py:83
  225.0 15.6 %collective-permute-start.17 = (bf16[4,48,1536]{2,1,0:T(8,128)(2,1)}, bf16[4,48,1536]{2,1,0:T(8,128)(2,1)S(1)}, u32[]{:S(2)}, u32[]{:S(2)}) collective-permute-start(bf16[4,48,1536]{2,1,0:T(8,128)(2,1)} %get-tuple-element.204), channel_id=1, source_target_pairs={{0,16},{1,17},{2,18},{3,19},{4,20},{5,21},{6,22},{7,23},{8,24},{9,... | collective-permute-start | bytes 1769480 | tf_op jit(solution)/shard_map/ppermute | solution.py:83
  240.6 32.3 %copy-start.7 = (bf16[16,24,1920]{2,1,0:T(8,128)(2,1)}, bf16[16,24,1920]{2,1,0:T(8,128)(2,1)S(1)}, u32[]{:S(2)}) copy-start(bf16[16,24,1920]{2,1,0:T(8,128)(2,1)S(1)} %collective-permute-done.18) | copy-start | bytes 4423684
  241.4 4.6 %copy-start.6 = (bf16[16,24,1920]{2,1,0:T(8,128)(2,1)S(1)}, bf16[16,24,1920]{2,1,0:T(8,128)(2,1)}, u32[]{:S(2)}) copy-start(bf16[16,24,1920]{2,1,0:T(8,128)(2,1)} %get-tuple-element.209) | copy-start | bytes 4423684
  247.2 24.0 %collective-permute-start.19 = (bf16[2,48,3072]{2,1,0:T(8,128)(2,1)}, bf16[2,48,3072]{2,1,0:T(8,128)(2,1)}, u32[]{:S(2)}, u32[]{:S(2)}) collective-permute-start(bf16[2,48,3072]{2,1,0:T(8,128)(2,1)} %get-tuple-element.218), channel_id=1, source_target_pairs={{0,2},{1,3},{2,0},{3,1},{4,6},{5,7},{6,4},{7,5},{8,10},{9,11},{10,... | collective-permute-start | bytes 1769480 | tf_op jit(solution)/shard_map/ppermute | solution.py:83
  248.5 22.6 %collective-permute-start.20 = (bf16[4,24,1920]{2,1,0:T(8,128)(2,1)}, bf16[4,24,1920]{2,1,0:T(8,128)(2,1)}, u32[]{:S(2)}, u32[]{:S(2)}) collective-permute-start(bf16[4,24,1920]{2,1,0:T(8,128)(2,1)} %get-tuple-element.219), channel_id=1, source_target_pairs={{0,8},{1,9},{2,10},{3,11},{4,12},{5,13},{6,14},{7,15},{8,0},{9,1},... | collective-permute-start | bytes 1105928 | tf_op jit(solution)/shard_map/ppermute | solution.py:83
  249.0 22.1 %collective-permute-start.21 = (bf16[4,24,1920]{2,1,0:T(8,128)(2,1)}, bf16[4,24,1920]{2,1,0:T(8,128)(2,1)}, u32[]{:S(2)}, u32[]{:S(2)}) collective-permute-start(bf16[4,24,1920]{2,1,0:T(8,128)(2,1)} %get-tuple-element.220), channel_id=1, source_target_pairs={{0,16},{1,17},{2,18},{3,19},{4,20},{5,21},{6,22},{7,23},{8,24},{9,... | collective-permute-start | bytes 1105928 | tf_op jit(solution)/shard_map/ppermute | solution.py:83
  249.8 21.3 %collective-permute-start.22 = (bf16[4,24,1920]{2,1,0:T(8,128)(2,1)}, bf16[4,24,1920]{2,1,0:T(8,128)(2,1)}, u32[]{:S(2)}, u32[]{:S(2)}) collective-permute-start(bf16[4,24,1920]{2,1,0:T(8,128)(2,1)} %get-tuple-element.221), channel_id=1, source_target_pairs={{0,24},{1,25},{2,26},{3,27},{4,28},{5,29},{6,30},{7,31},{8,16},{9,... | collective-permute-start | bytes 1105928 | tf_op jit(solution)/shard_map/ppermute | solution.py:83
  252.0 19.2 %copy-start.13 = (bf16[2,48,3072]{2,1,0:T(8,128)(2,1)S(1)}, bf16[2,48,3072]{2,1,0:T(8,128)(2,1)}, u32[]{:S(2)}) copy-start(bf16[2,48,3072]{2,1,0:T(8,128)(2,1)} %get-tuple-element.226) | copy-start | bytes 1769476
  271.1 4.4 %copy-start.25 = (f32[1,3072]{1,0:T(1,128)S(1)}, f32[1,3072]{1,0:T(1,128)}, u32[]{:S(2)}) copy-start(f32[1,3072]{1,0:T(1,128)} %get-tuple-element.251) | copy-start | bytes 36868
  275.0 25.3 %collective-permute-start.27 = (bf16[16,24,1280]{2,1,0:T(8,128)(2,1)}, bf16[16,24,1280]{2,1,0:T(8,128)(2,1)S(1)}, u32[]{:S(2)}, u32[]{:S(2)}) collective-permute-start(bf16[16,24,1280]{2,1,0:T(8,128)(2,1)} %get-tuple-element.240), channel_id=1, source_target_pairs={{0,1},{1,0},{2,3},{3,2},{4,5},{5,4},{6,7},{7,6},{8,9},{9,8},{10,11... | collective-permute-start | bytes 2949128 | tf_op jit(solution)/shard_map/ppermute | solution.py:83
  277.2 22.3 %copy-start.30 = (f32[1,768]{1,0:T(1,128)S(1)}, f32[1,768]{1,0:T(1,128)}, u32[]{:S(2)}) copy-start(f32[1,768]{1,0:T(1,128)} %get-tuple-element.246) | copy-start | bytes 9220
  277.2 22.3 %copy-start.31 = (f32[1,384]{1,0:T(1,128)S(1)}, f32[1,384]{1,0:T(1,128)}, u32[]{:S(2)}) copy-start(f32[1,384]{1,0:T(1,128)} %get-tuple-element.245) | copy-start | bytes 4612
  277.2 22.4 %copy-start.28 = (f32[1,768]{1,0:T(1,128)S(1)}, f32[1,768]{1,0:T(1,128)}, u32[]{:S(2)}) copy-start(f32[1,768]{1,0:T(1,128)} %get-tuple-element.247) | copy-start | bytes 9220
  277.2 23.1 %copy-start.29 = (f32[1,768]{1,0:T(1,128)S(1)}, f32[1,768]{1,0:T(1,128)}, u32[]{:S(2)}) copy-start(f32[1,768]{1,0:T(1,128)} %get-tuple-element.243) | copy-start | bytes 9220
  277.2 24.7 %copy-start.27 = (f32[1,768]{1,0:T(1,128)S(1)}, f32[1,768]{1,0:T(1,128)}, u32[]{:S(2)}) copy-start(f32[1,768]{1,0:T(1,128)} %get-tuple-element.249) | copy-start | bytes 9220
  277.2 24.7 %copy-start.26 = (f32[1,768]{1,0:T(1,128)S(1)}, f32[1,768]{1,0:T(1,128)}, u32[]{:S(2)}) copy-start(f32[1,768]{1,0:T(1,128)} %get-tuple-element.250) | copy-start | bytes 9220
  277.2 23.1 %collective-permute-start.23 = (bf16[1,48,3072]{2,1,0:T(8,128)(2,1)}, bf16[1,48,3072]{2,1,0:T(8,128)(2,1)S(1)}, u32[]{:S(2)}, u32[]{:S(2)}) collective-permute-start(bf16[1,48,3072]{2,1,0:T(8,128)(2,1)} %add_convert_fusion.3), channel_id=1, source_target_pairs={{0,4},{1,5},{2,6},{3,7},{4,0},{5,1},{6,2},{7,3},{8,12},{9,13},{10,... | collective-permute-start | bytes 884744 | tf_op jit(solution)/shard_map/ppermute | solution.py:83
  279.9 19.7 %collective-permute-start.24 = (bf16[24,1920]{1,0:T(8,128)(2,1)}, bf16[24,1920]{1,0:T(8,128)(2,1)S(1)}, u32[]{:S(2)}, u32[]{:S(2)}) collective-permute-start(bf16[24,1920]{1,0:T(8,128)(2,1)} %get-tuple-element.237), channel_id=1, source_target_pairs={{0,2},{1,3},{2,0},{3,1},{4,6},{5,7},{6,4},{7,5},{8,10},{9,11},{10,... | collective-permute-start | bytes 276488 | tf_op jit(solution)/shard_map/ppermute | solution.py:83
  280.1 20.2 %collective-permute-start.25 = (bf16[24,1920]{1,0:T(8,128)(2,1)}, bf16[24,1920]{1,0:T(8,128)(2,1)S(1)}, u32[]{:S(2)}, u32[]{:S(2)}) collective-permute-start(bf16[24,1920]{1,0:T(8,128)(2,1)} %get-tuple-element.238), channel_id=1, source_target_pairs={{0,4},{1,5},{2,6},{3,7},{4,0},{5,1},{6,2},{7,3},{8,12},{9,13},{10,... | collective-permute-start | bytes 276488 | tf_op jit(solution)/shard_map/ppermute | solution.py:83
  280.9 19.4 %collective-permute-start.26 = (bf16[24,1920]{1,0:T(8,128)(2,1)}, bf16[24,1920]{1,0:T(8,128)(2,1)S(1)}, u32[]{:S(2)}, u32[]{:S(2)}) collective-permute-start(bf16[24,1920]{1,0:T(8,128)(2,1)} %get-tuple-element.239), channel_id=1, source_target_pairs={{0,6},{1,7},{2,4},{3,5},{4,2},{5,3},{6,0},{7,1},{8,14},{9,15},{10,... | collective-permute-start | bytes 276488 | tf_op jit(solution)/shard_map/ppermute | solution.py:83
  299.6 2.4 copy-start.18
  300.3 3.0 copy-start.20
  300.3 3.0 copy-start.22
  300.3 11.8 %copy-start.9 = (bf16[16,24,1280]{2,1,0:T(8,128)(2,1)}, bf16[16,24,1280]{2,1,0:T(8,128)(2,1)S(1)}, u32[]{:S(2)}) copy-start(bf16[16,24,1280]{2,1,0:T(8,128)(2,1)S(1)} %collective-permute-done.27) | copy-start | bytes 2949124
  303.4 9.5 %collective-permute-start.28 = (f32[1,24,3072]{2,1,0:T(8,128)S(1)}, f32[1,24,3072]{2,1,0:T(8,128)}, u32[]{:S(2)}, u32[]{:S(2)}) collective-permute-start(f32[1,24,3072]{2,1,0:T(8,128)S(1)} %constant_dynamic-slice_fusion), channel_id=1, source_target_pairs={{0,1},{1,0},{2,3},{3,2},{4,5},{5,4},{6,7},{7,6},{8,9},{9,8},{10,11... | collective-permute-start | bytes 884744 | tf_op jit(solution)/shard_map/ppermute | solution.py:83
  303.5 8.8 %collective-permute-start.29 = (bf16[16,24,128]{2,1,0:T(8,128)(2,1)S(1)}, bf16[16,24,128]{2,1,0:T(8,128)(2,1)S(1)}, u32[]{:S(2)}, u32[]{:S(2)}) collective-permute-start(bf16[16,24,128]{2,1,0:T(8,128)(2,1)S(1)} %pad.33), channel_id=1, source_target_pairs={{0,1},{1,0},{2,3},{3,2},{4,5},{5,4},{6,7},{7,6},{8,9},{9,8},{10,11... | collective-permute-start | bytes 294920 | tf_op jit(solution)/shard_map/ppermute | solution.py:83
  312.2 23.8 %copy-start.4 = (bf16[16,24,1280]{2,1,0:T(8,128)(2,1)}, bf16[16,24,1280]{2,1,0:T(8,128)(2,1)S(1)}, u32[]{:S(2)}) copy-start(bf16[16,24,1280]{2,1,0:T(8,128)(2,1)S(1)} %pad.64) | copy-start | bytes 2949124
  314.1 21.9 %copy-start.5 = (bf16[16,24,1280]{2,1,0:T(8,128)(2,1)}, bf16[16,24,1280]{2,1,0:T(8,128)(2,1)S(1)}, u32[]{:S(2)}) copy-start(bf16[16,24,1280]{2,1,0:T(8,128)(2,1)S(1)} %pad.34) | copy-start | bytes 2949124
  314.1 4.7 %copy-start.19 = (bf16[24,1920]{1,0:T(8,128)(2,1)S(1)}, bf16[24,1920]{1,0:T(8,128)(2,1)}, u32[]{:S(2)}) copy-start(bf16[24,1920]{1,0:T(8,128)(2,1)} %copy-done.18) | copy-start | bytes 276484
  314.1 4.7 %copy-start.21 = (bf16[24,1920]{1,0:T(8,128)(2,1)S(1)}, bf16[24,1920]{1,0:T(8,128)(2,1)}, u32[]{:S(2)}) copy-start(bf16[24,1920]{1,0:T(8,128)(2,1)} %copy-done.20) | copy-start | bytes 276484
  314.1 4.7 %copy-start.23 = (bf16[24,1920]{1,0:T(8,128)(2,1)S(1)}, bf16[24,1920]{1,0:T(8,128)(2,1)}, u32[]{:S(2)}) copy-start(bf16[24,1920]{1,0:T(8,128)(2,1)} %copy-done.22) | copy-start | bytes 276484
  315.3 20.7 %collective-permute-start.30 = (bf16[4,24,1280]{2,1,0:T(8,128)(2,1)}, bf16[4,24,1280]{2,1,0:T(8,128)(2,1)}, u32[]{:S(2)}, u32[]{:S(2)}) collective-permute-start(bf16[4,24,1280]{2,1,0:T(8,128)(2,1)} %get-tuple-element.259), channel_id=1, source_target_pairs={{0,8},{1,9},{2,10},{3,11},{4,12},{5,13},{6,14},{7,15},{8,0},{9,1},... | collective-permute-start | bytes 737288 | tf_op jit(solution)/shard_map/ppermute | solution.py:83
  316.7 19.2 %collective-permute-start.31 = (bf16[4,24,1280]{2,1,0:T(8,128)(2,1)}, bf16[4,24,1280]{2,1,0:T(8,128)(2,1)}, u32[]{:S(2)}, u32[]{:S(2)}) collective-permute-start(bf16[4,24,1280]{2,1,0:T(8,128)(2,1)} %get-tuple-element.260), channel_id=1, source_target_pairs={{0,16},{1,17},{2,18},{3,19},{4,20},{5,21},{6,22},{7,23},{8,24},{9,... | collective-permute-start | bytes 737288 | tf_op jit(solution)/shard_map/ppermute | solution.py:83
  317.2 18.8 %collective-permute-start.32 = (bf16[4,24,1280]{2,1,0:T(8,128)(2,1)}, bf16[4,24,1280]{2,1,0:T(8,128)(2,1)}, u32[]{:S(2)}, u32[]{:S(2)}) collective-permute-start(bf16[4,24,1280]{2,1,0:T(8,128)(2,1)} %get-tuple-element.261), channel_id=1, source_target_pairs={{0,24},{1,25},{2,26},{3,27},{4,28},{5,29},{6,30},{7,31},{8,16},{9,... | collective-permute-start | bytes 737288 | tf_op jit(solution)/shard_map/ppermute | solution.py:83
  338.0 11.6 %collective-permute-start.33 = (bf16[24,1280]{1,0:T(8,128)(2,1)}, bf16[24,1280]{1,0:T(8,128)(2,1)S(1)}, u32[]{:S(2)}, u32[]{:S(2)}) collective-permute-start(bf16[24,1280]{1,0:T(8,128)(2,1)} %get-tuple-element.278), channel_id=1, source_target_pairs={{0,2},{1,3},{2,0},{3,1},{4,6},{5,7},{6,4},{7,5},{8,10},{9,11},{10,... | collective-permute-start | bytes 184328 | tf_op jit(solution)/shard_map/ppermute | solution.py:83
  340.3 9.3 %collective-permute-start.34 = (bf16[24,1280]{1,0:T(8,128)(2,1)}, bf16[24,1280]{1,0:T(8,128)(2,1)}, u32[]{:S(2)}, u32[]{:S(2)}) collective-permute-start(bf16[24,1280]{1,0:T(8,128)(2,1)} %get-tuple-element.277), channel_id=1, source_target_pairs={{0,4},{1,5},{2,6},{3,7},{4,0},{5,1},{6,2},{7,3},{8,12},{9,13},{10,... | collective-permute-start | bytes 184328 | tf_op jit(solution)/shard_map/ppermute | solution.py:83
  341.2 8.4 %collective-permute-start.35 = (bf16[24,1280]{1,0:T(8,128)(2,1)}, bf16[24,1280]{1,0:T(8,128)(2,1)}, u32[]{:S(2)}, u32[]{:S(2)}) collective-permute-start(bf16[24,1280]{1,0:T(8,128)(2,1)} %get-tuple-element.276), channel_id=1, source_target_pairs={{0,6},{1,7},{2,4},{3,5},{4,2},{5,3},{6,0},{7,1},{8,14},{9,15},{10,... | collective-permute-start | bytes 184328 | tf_op jit(solution)/shard_map/ppermute | solution.py:83
  346.1 5.9 %copy-start.14 = (f32[24,1,3,3,128]{4,3,2,0,1:T(4,128)S(1)}, f32[24,1,3,3,128]{4,3,2,0,1:T(4,128)}, u32[]{:S(2)}) copy-start(f32[24,1,3,3,128]{4,3,2,0,1:T(4,128)} %stack_reshape.14) | copy-start | bytes 331780
  (9 other events, 12.5 us)
Sparse Core Ops, SparseCore 0:
  11.7 95.2 all-gather.1

commit v5 on v4

--- a/solution.py
+++ b/solution.py
@@ -330,27 +330,24 @@
     return total.astype(kind)
 
 
-def fast_sum_steps(keeps, cames, where, mesh):
+def plane_steps(keep, came, mesh):
     count = mesh.size
     _, outer, rest = bit_groups(mesh)
-    me = lax.axis_index(AXES)
-    spot = position(me, outer)
-    size, line = 1 << len(outer), 1 << len(rest[0])
-    terms = []
-    for pair in zip(keeps, cames):
-        for array in pair:
-            lead = keeps[0].shape[2] - array.shape[2]
-            array = jnp.pad(array, ((0, 0), (0, 0), (lead, 0))) if lead else array
-            terms.append(array.reshape((size, line) + array.shape[1:]))
+    spot = position(lax.axis_index(AXES), outer)
+    size = 1 << len(outer)
+    terms = [array.reshape((size, 1 << len(rest[0])) + keep.shape[1:]) for array in (keep, came)]
     sends = [part_of(terms, 0, spot ^ step, bf16)[0] for step in range(1, size)]
-    terms = [pick(term, 0, spot)[0] for term in terms]
     came = yield [(array, pairs) for array, (_, pairs) in zip(sends, partners(count, outer))]
-    terms = terms + came
-    spot = position(me, rest[0])
-    came = yield [
-        (part_of(terms, 0, spot ^ step, bf16)[0], pairs) for step, pairs in partners(count, rest[0])
-    ]
-    return part_of(terms, 0, spot, f32)[0] + sum(array.astype(f32) for array in came)
+    return [pick(term, 0, spot)[0] for term in terms] + came
+
+
+def line_steps(groups, mesh):
+    count = mesh.size
+    _, _, rest = bit_groups(mesh)
+    spot = position(lax.axis_index(AXES), rest[0])
+    side = lambda index, kind: jnp.concatenate([part_of(terms, 0, index, kind)[0] for terms in groups], -1)
+    came = yield [(side(spot ^ step, bf16), pairs) for step, pairs in partners(count, rest[0])]
+    return side(spot, f32) + sum(array.astype(f32) for array in came)
 
 
 def fold_sum_steps(keep, send, where, mesh):
@@ -572,15 +569,13 @@
     )(valid, *arrays)
 
 
-def attend_back_kernel(where, *refs, pairs, extra, carry, cut):
+def attend_back_kernel(where, *refs, pairs, extra, spare, cut):
     lists = [refs[kind * pairs : (kind + 1) * pairs] for kind in range(5)]
     joined, mixed_grad, mixed, raised, inverse = lists
-    normed, *rest = refs[5 * pairs :]
-    carried, rest = rest[:carry], rest[carry:]
+    normed, weight, *rest = refs[5 * pairs :]
     if extra:
-        mixed_a, mixed_b, low_grad, joined_grad, column, *outs, held, scaled, total, total_out = rest
-    else:
-        joined_grad, column, *outs, held, scaled, total = rest
+        mixed_a, mixed_b, low_grad, *rest, total_out = rest
+    joined_grad, column, gain_sum, shift_sum, *outs, held, scaled, total = rest
     item = pl.program_id(0)
     seq, span = joined_grad.shape
     padded = raised[0].shape[1] // 2
@@ -636,21 +631,23 @@
 
     @pl.when(item == pl.num_programs(0) - 1)
     def _():
-        begin = 0
-        for before, out in zip(carried, outs):
-            begin = before.shape[-1]
-            out[..., :begin] = before[...]
-            if out.shape[-1] > begin + span:
-                out[..., begin + span :] = jnp.zeros(out.shape[:-1] + (out.shape[-1] - begin - span,), bf16)
-        store_cut(where[0], outs, slice(begin, begin + span), total[...], cut)
+        store_cut(where[0], outs, slice(0, span), total[...], cut)
+        if spare:
+            for out in outs:
+                out[..., span:] = jnp.zeros(out.shape[:-1] + (spare,), bf16)
+        wide = weight[...].astype(f32)
+        for ref, product in ((gain_sum, wide * total[...]), (shift_sum, wide * column[...])):
+            row = jnp.sum(product, 1, keepdims=True)
+            ref[...] = jnp.broadcast_to(row, (row.shape[0], 128)).T[:1]
         if extra:
             store_cut(where[0], outs, slice(span, span + total_out.shape[1]), total_out[...], cut)
 
 
-def attend_back(mixed_grad, where, joined, mixed, raised, inverse, normed, seq, part, chosen, cut, others=(), carried=()):
+def attend_back(mixed_grad, where, joined, mixed, raised, inverse, normed, weight, seq, part, cut, others=(), spare=0):
     rows, width = normed.shape
     items, in_part, _, keys = raised.shape
-    pairs = len(chosen)
+    pairs = in_part
+    chosen = range(pairs)
     span = 384 * pairs
     row = lambda w, off=0: pl.BlockSpec((seq, w), lambda i, *_: (i, off))
     each = lambda w, off=0: [row(w, off + pair) for pair in chosen]
@@ -658,11 +655,12 @@
         pl.BlockSpec((None, None, seq, keys), functools.partial(lambda at, i, *_: (i, at, 0, 0), pair))
         for pair in chosen
     ]
-    columns = span + (width if others else 0) + (carried[0].shape[-1] + 128 if carried else 0)
+    columns = span + (width if others else 0) + spare
+    one = pl.BlockSpec((1, width), lambda i, *_: (0, 0))
     specs, shapes = cut_shapes(width, columns, columns, lambda j: 0, cut)
     return pl.pallas_call(
         functools.partial(
-            attend_back_kernel, pairs=pairs, extra=bool(others), carry=len(carried), cut=cut
+            attend_back_kernel, pairs=pairs, extra=bool(others), spare=spare, cut=cut
         ),
         grid_spec=pltpu.PrefetchScalarGridSpec(
             num_scalar_prefetch=1,
@@ -670,9 +668,9 @@
             in_specs=[
                 *each(384), *each(128, part * in_part), *each(128), *weights, *each(128), row(width)
             ]
-            + [once(array.shape) for array in carried]
+            + [once((width, span))]
             + [row(array.shape[1]) for array in others],
-            out_specs=[row(span), pl.BlockSpec((1, span), lambda i, *_: (0, 0))] + specs,
+            out_specs=[row(span), pl.BlockSpec((1, span), lambda i, *_: (0, 0)), one, one] + specs,
             scratch_shapes=[
                 pltpu.VMEM((seq, keys), bf16),
                 pltpu.VMEM((pairs, seq, 128), bf16),
@@ -680,13 +678,15 @@
             ]
             + ([pltpu.VMEM((width, width), f32)] if others else []),
         ),
-        out_shape=[shape_of((rows, span), bf16), shape_of((1, span), f32)] + shapes,
+        out_shape=[shape_of((rows, span), bf16), shape_of((1, span), f32)]
+        + [shape_of((1, width), f32)] * 2
+        + shapes,
         compiler_params=params(1),
         cost_estimate=cost(),
         name="attend_back",
     )(
         where, *[joined] * pairs, *[mixed_grad] * pairs, *[mixed] * pairs, *[raised] * pairs,
-        *[inverse] * pairs, normed, *carried, *others,
+        *[inverse] * pairs, normed, weight, *others,
     )
 
 
@@ -817,7 +817,7 @@
 
 
 def middle_back_kernel(
-    valid, hidden_grad, ups, middle, cotangent, gain, weight,
+    valid, hidden_grad, ups, middle, cotangent, gain, weight_a, weight_b,
     low_grad, mixed_grad, gain_sum, shift_sum, bias_sum, down_sum, *, seq, sub,
 ):
     step = pl.program_id(0)
@@ -836,7 +836,9 @@
         kept = jnp.where(place < valid[step // each], cotangent[rows, :].astype(f32), 0.0)
         low = (kept + norm_back(grad, gain[...], unit, scale)).astype(bf16)
         low_grad[rows, :] = low
-        mixed_grad[rows, :] = dot(low, weight[:, -width:], NT).astype(bf16)
+        mixed_grad[rows, :] = (
+            dot(low[:, : width // 2], weight_a[...], NT) + dot(low[:, width // 2 :], weight_b[...], NT)
+        ).astype(bf16)
         terms = (grad * unit, grad, low.astype(f32), kept)
         sums = [before + column_sum(term) for before, term in zip(sums, terms)]
     for ref, value in zip((gain_sum, shift_sum, bias_sum, down_sum), sums):
@@ -849,6 +851,12 @@
     sub = LSUB if tile % LSUB == 0 else tile
     row = lambda w: pl.BlockSpec((tile, w), lambda j, *_: (j, 0))
     one = pl.BlockSpec((1, width), lambda j, *_: (0, 0))
+    half = width // 2
+    at = weight.shape[1] // half - 2
+    halves = [
+        pl.BlockSpec((width, half), lambda j, *_: (0, at), pipeline_mode=pl.Buffered(buffer_count=1)),
+        pl.BlockSpec((width, half), lambda j, *_: (0, at + 1), pipeline_mode=pl.Buffered(buffer_count=1)),
+    ]
     return pl.pallas_call(
         functools.partial(middle_back_kernel, seq=seq, sub=sub),
         grid_spec=pltpu.PrefetchScalarGridSpec(
@@ -856,7 +864,7 @@
             grid=(rows // tile,),
             in_specs=[
                 row(hidden_grad.shape[1]), half_of(both, 0), row(width), row(width),
-                once((1, width)), once(weight.shape),
+                once((1, width)), *halves,
             ],
             out_specs=[row(width), row(width)] + [one] * 4,
         ),
@@ -864,13 +872,13 @@
         compiler_params=params(1),
         cost_estimate=cost(),
         name="middle_back",
-    )(valid, hidden_grad, both, middle, cotangent, gain, weight)
+    )(valid, hidden_grad, both, middle, cotangent, gain, weight, weight)
 
 
 def input_back_kernel(*refs, spans, sub):
     grads = refs[: len(spans)]
     weights = refs[len(spans) : len(spans) + 2]
-    tokens, low_grad, gain, input_grad, gain_sum, shift_sum = refs[len(spans) + 2 :]
+    tokens, low_grad, gain, input_grad = refs[len(spans) + 2 :]
     tile, width = tokens.shape
 
     def ahead_of(start):
@@ -882,18 +890,14 @@
 
     starts = list(range(0, tile, sub))
     ahead = [ahead_of(0)]
-    sums = [jnp.zeros((1, width), f32)] * 2
     for index, start in enumerate(starts):
         rows = slice(start, start + sub)
         if index + 1 < len(starts):
             ahead.append(ahead_of(start + sub))
         grad = ahead.pop(0)
         unit, scale = normalize(tokens[rows, :].astype(f32))
-        sums = [before + column_sum(term) for before, term in zip(sums, (grad * unit, grad))]
         full = low_grad[rows, :].astype(f32) + norm_back(grad, gain[...], unit, scale)
         input_grad[rows, :] = full.astype(bf16)
-    for ref, value in zip((gain_sum, shift_sum), sums):
-        accumulate(ref, value, pl.program_id(0) == 0)
 
 
 def input_back(last, others, spans, weights, tokens, low_grad, gain, seq):
@@ -901,16 +905,15 @@
     tile = LTILE if seq % LTILE == 0 else seq
     sub = LSUB if tile % LSUB == 0 else tile
     row = lambda w: pl.BlockSpec((tile, w), lambda i: (i, 0))
-    fixed = pl.BlockSpec((1, width), lambda i: (0, 0))
     grads = [*others, last]
     return pl.pallas_call(
         functools.partial(input_back_kernel, spans=spans, sub=sub),
         grid=(rows // tile,),
         in_specs=[row(grad.shape[1]) for grad in grads]
-        + [once(weight.shape) for weight in weights]
+        + [once((width, spans[0][1].stop))] * 2
         + [row(width), row(width), once((1, width))],
-        out_specs=[row(width), fixed, fixed],
-        out_shape=[shape_of((rows, width), bf16)] + [shape_of((1, width), f32)] * 2,
+        out_specs=row(width),
+        out_shape=shape_of((rows, width), bf16),
         compiler_params=params(1),
         cost_estimate=cost(),
         name="input_back",
@@ -942,13 +945,6 @@
 
     def swap(arrays):
         return flights.add(swap_steps(arrays[1], mesh), []) if cut else None
-
-    def sums_after(arrays, swaps):
-        if cut:
-            keeps, cames = [keep for keep, _ in arrays], [job["result"] for job in swaps]
-            return flights.add(fast_sum_steps(keeps, cames, where, mesh), [])
-        return flights.add(sum_steps(arrays[0][0], mesh, bf16), [])
-
 
     def by_pairs(matrix, part):
         rows = matrix.shape[0]
@@ -1008,38 +1004,23 @@
     low_grad, mixed_grad, gain_two_sum, shift_two_sum, bias_out_sum, down_sum = flights.run(
         lambda x: middle_back(x, valid, hidden_grad, both, cot, gain_two, second, seq), middle
     )
-    joined_grad_a, qkv_sum_a, *grads_a = flights.run(
+    joined_grad_a, qkv_sum_a, gain_sum_a, shift_sum_a, *grads_a = flights.run(
         lambda x: attend_back(
-            x, where, joined_a, mixed_a, raised_a, inverse_a, normed, seq, 0, range(half // 128), cut,
-            (mixed_a, mixed_b, low_grad),
+            x, where, joined_a, mixed_a, raised_a, inverse_a, normed, first, seq, 0, cut,
+            others=(mixed_a, mixed_b, low_grad),
         ),
         mixed_grad,
     )
     swap_a = swap(grads_a)
-    joined_grad_b, qkv_sum_b, *grads_b = flights.run(
+    joined_grad_b, qkv_sum_b, gain_sum_b, shift_sum_b, *grads_b = flights.run(
         lambda x: attend_back(
-            x, where, joined_b, mixed_b, raised_b, inverse_b, normed, seq, 1, range(1), cut
+            x, where, joined_b, mixed_b, raised_b, inverse_b, normed, second, seq, 1, cut,
+            spare=128 if cut else 0,
         ),
         mixed_grad,
     )
-    sum_a = sums_after([grads_a], [swap_a])
-    joined_grad_c, qkv_sum_c, *grads_b = flights.run(
-        lambda x: attend_back(
-            x, where, joined_b, mixed_b, raised_b, inverse_b, normed, seq, 1, range(1, half // 128), cut,
-            carried=grads_b,
-        ),
-        mixed_grad,
-    )
-    swap_b = swap(grads_b)
-    spans = ((0, slice(0, span)), (1, slice(0, 384)), (1, slice(384, span)))
-    input_grad, gain_one_sum, shift_one_sum = flights.run(
-        lambda x: input_back(
-            x, [joined_grad_a, joined_grad_b], spans, [first, second], flat, low_grad, gain_one, seq
-        ),
-        joined_grad_c,
-    )
-    qkv_sum_b = jnp.concatenate([qkv_sum_b, qkv_sum_c], 1)
-
+    shift_one_sum = shift_sum_a + shift_sum_b
+    gain_one_sum = (gain_sum_a + gain_sum_b - shift_one * shift_one_sum) / gain_one
     joined_sums = by_kind(qkv_sum_a, qkv_sum_b)
     up_sum = up_sum.reshape(chunks, count, share).transpose(1, 0, 2).reshape(1, wide)
     gain_sums = jnp.concatenate([gain_one_sum, gain_two_sum], 1).reshape(count, edge)
@@ -1060,32 +1041,35 @@
         small = jnp.pad(small, ((0, 0), (0, small_rows * 128 - small.shape[1])))
         small = small.reshape(count // 2, 2, small_rows, 128)
         spot = position(me, core)
-        small = [
-            jnp.pad(pick(small, 1, place)[:, 0], ((0, 0), (0, share - small_rows), (0, 0))).astype(bf16)
-            for place in (spot, spot ^ 1)
+        grads_b = [
+            lax.dynamic_update_slice(grads, pick(small, 1, place)[:, 0].astype(bf16), (0, 0, span))
+            for grads, place in zip(grads_b, (spot, spot ^ 1))
         ]
-        swap_small = swap(small)
+        swap_b = swap(grads_b)
+        plane_a = flights.add(plane_steps(grads_a[0], swap_a["result"], mesh), [])
     else:
         small_job = flights.add(small_sum_steps(small, mesh), [])
-        sum_b = sums_after([grads_b], [None])
-    cuts = [0, items // 2 * seq, rows]
-    block_out = None
-    for begin, end in zip(cuts, cuts[1:]):
-        if begin < end:
-            block_out = flights.run(
-                lambda x: block_out_of(
-                    x, valid, active, both, bias_down, seq, begin, end, block_out
-                ),
-                middle,
-            )
-            if cut and begin == 0:
-                sum_b = sums_after([grads_b, small], [swap_b, swap_small])
+        sum_a, sum_b = (flights.add(sum_steps(grads, mesh, bf16), []) for (grads,) in (grads_a, grads_b))
+    spans = ((0, slice(0, span)), (1, slice(0, span)))
+    input_grad = flights.run(
+        lambda x: input_back(x, [joined_grad_a], spans, [first, second], flat, low_grad, gain_one, seq),
+        joined_grad_b,
+    )
+    if cut:
+        plane_b = flights.add(plane_steps(grads_b[0], swap_b["result"], mesh), [])
+    block_out = flights.run(
+        lambda x: block_out_of(x, valid, active, both, bias_down, seq, 0, rows), middle
+    )
+    if cut:
+        line = flights.add(line_steps([plane_a["result"], plane_b["result"]], mesh), [])
     flights.finish()
-    total_a, total_b = sum_a["result"], sum_b["result"]
     if cut:
+        edge_a = grads_a[0].shape[-1]
+        total_a, total_b = line["result"][:, :edge_a], line["result"][:, edge_a:]
         small_total = total_b[:small_rows, span:].reshape(-1)
         small_total = small_total[: edge + biases.shape[0]]
     else:
+        total_a, total_b = sum_a["result"], sum_b["result"]
         small_total = small_job["result"]
     if cut:
         up_total, down_total = mlp_job["result"]

time: 365 us -> 352 us (0.964)
  Pallas kernels: 226 us -> 220 us
  starting transfers between devices: 40.3 us -> 35.2 us
  waiting for transfers between devices: 21.8 us -> 26.7 us
  other arithmetic: 16.5 us -> 12.4 us
    ppermute x36 -> x32, starting transfers between devices: 40.2 us -> 35.2 us  [depart(): came = [lax.ppermute(array, AXES, pairs) for array, pairs in sends]]
    ppermute x36 -> x32, waiting for transfers between devices: 21.8 us -> 26.6 us  [depart(): came = [lax.ppermute(array, AXES, pairs) for array, pairs in sends]]
    pallas_call x2 -> x1, Pallas kernels: 19.8 us -> 15.2 us  [block_out_of(): pl.pallas_call(functools.partial(block_out_kernel, seq=seq, begin=begin),...]
    pallas_call x3 -> x2, Pallas kernels: 61.1 us -> 59.3 us  [attend_back(): pl.pallas_call(functools.partial(attend_back_kernel, pairs=pairs, extra=b...]
  transfers between devices with their start and end apart: 37 -> 33, of which waited for: 8 -> 8; matrix products, arithmetic and copies ran while one was open for 9% -> 7% of each run, Pallas kernels for 45% -> 44%
where the time goes in v5:
time: 352 us; the launch traced here: 347 us
  Pallas kernels  220 us (62%)
  local copies, waits for them, and re-layouts  37.9 us (11%)
  starting transfers between devices  35.2 us (10%)
  waiting for transfers between devices  26.7 us (8%)
  between operations  15.6 us (4%)
  other arithmetic  12.4 us (4%)
    pallas_call x2, Pallas kernels, attend_back(): pl.pallas_call(functools.partial(attend_back_kernel, pairs=pairs, extra=b...  59.3 us
    pallas_call x1, Pallas kernels, mlp(): pl.pallas_call(functools.partial(mlp_kernel, seq=seq, tile=tile_of(seq),...  52.5 us
    pallas_call x2, Pallas kernels, attend(): pl.pallas_call(functools.partial(attend_kernel, tile=tile_of(seq), padded...  44.7 us
    ppermute x32, starting transfers between devices, depart(): came = [lax.ppermute(array, AXES, pairs) for array, pairs in sends]  35.2 us
    ppermute x32, waiting for transfers between devices, depart(): came = [lax.ppermute(array, AXES, pairs) for array, pairs in sends]  26.6 us
    pallas_call x1, Pallas kernels, middle_back(): pl.pallas_call(functools.partial(middle_back_kernel, seq=seq, sub=sub), g...  20.7 us
    pallas_call x1, Pallas kernels, block_out_of(): pl.pallas_call(functools.partial(block_out_kernel, seq=seq, begin=begin),...  15.2 us
    pallas_call x1, Pallas kernels, input_back(): pl.pallas_call(functools.partial(input_back_kernel, spans=spans, sub=sub)...  14.3 us
  transfers between devices with their start and end apart: 33, of which 8 were waited for; matrix products, arithmetic and copies ran while one was open for 7% of the time, Pallas kernels for 44%

profile of v5, /device:TPU:0, one launch (start us, length us, event | category | flops | bytes accessed | tf_op | source)
XLA Modules:
  0.0 347.2 jit_solution(5114970802493510396)
XLA Ops:
  7.2 2.0 reshape.171
  9.4 1.3 reshape.172
  12.0 3.1 collective-permute-start
  15.1 2.6 collective-permute-start.1
  17.8 2.0 collective-permute-start.3
  20.0 4.9 %collective-permute-done.1 = bf16[1,1,1,1,1,24,1280]{6,5,4,3,2,1,0:T(8,128)(2,1)S(1)} collective-permute-done((bf16[1,1,1,1,1,24,1280]{6,5,4,3,2,1,0:T(8,128)(2,1)S(1)}, bf16[1,1,1,1,1,24,1280]{6,5,4,3,2,1,0:T(8,128)(2,1)S(1)}, u32[]{:S(2)}, u32[]{:S(2)}) %collective-permute-start.1) | collective-permute-done | bytes 61472 | tf_op jit(solution)/shard_map/ppermute | solution.py:83
  24.8 4.0 %collective-permute-done.3 = bf16[1,1,1,1,1,24,1920]{6,5,4,3,2,1,0:T(8,128)(2,1)S(1)} collective-permute-done((bf16[1,1,1,1,1,24,1920]{6,5,4,3,2,1,0:T(8,128)(2,1)S(1)}, bf16[1,1,1,1,1,24,1920]{6,5,4,3,2,1,0:T(8,128)(2,1)S(1)}, u32[]{:S(2)}, u32[]{:S(2)}) %collective-permute-start.3) | collective-permute-done | bytes 92192 | tf_op jit(solution)/shard_map/ppermute | solution.py:83
  28.9 1.6 collective-permute-start.4
  30.5 1.6 collective-permute-start.5
  33.0 5.8 %collective-permute-done.7 = bf16[1,1,2,1,1,24,1920]{6,5,4,3,2,1,0:T(8,128)(2,1)S(1)} collective-permute-done((bf16[1,1,2,1,1,24,1920]{6,5,4,3,2,1,0:T(8,128)(2,1)S(1)}, bf16[1,1,2,1,1,24,1920]{6,5,4,3,2,1,0:T(8,128)(2,1)S(1)}, u32[]{:S(2)}, u32[]{:S(2)}) %collective-permute-start.7) | collective-permute-done | bytes 184352 | tf_op jit(solution)/shard_map/ppermute | solution.py:83
  38.8 2.3 collective-permute-done.5
  42.0 1.6 collective-permute-start.10
  43.6 1.2 collective-permute-start.11
  44.7 0.8 collective-permute-start.9
  45.5 1.3 broadcast_in_dim.31
  47.8 1.3 constant_dynamic-update-slice_fusion.8
  49.4 0.8 fusion.25
  51.6 19.8 %attend.2 = (bf16[1824,768]{1,0:T(8,128)(2,1)}, bf16[1824,1152]{1,0:T(8,128)(2,1)}, bf16[1824,384]{1,0:T(8,128)(2,1)}, bf16[3,3,608,1280]{3,2,1,0:T(8,128)(2,1)}, f32[1824,384]{1,0:T(8,128)}) custom-call(s32[3]{0:T(128)} %get-tuple-element.297.valid, bf16[1824,768]{1,0:T(8,128)(2,1)} %bitcast.130, f32[1,768]{1,0:T(1,128)} %get-tuple-element.295.refs_1_.refs_6_, ...), custom_call_target="tpu_custom_call" | custom-call | flops 1 | bytes 1 | tf_op jit(solution)/shard_map/attend/pallas_call | solution.py:560
  71.4 1.8 constant_dynamic-update-slice_fusion.4
  73.2 1.7 constant_dynamic-update-slice_fusion.3
  74.9 1.8 constant_dynamic-update-slice_fusion.2
  78.4 1.6 constant_dynamic-update-slice_fusion.1
  80.3 1.6 constant_dynamic-update-slice_fusion
  81.9 1.6 copy-done
  83.5 24.9 %attend.3 = (bf16[1824,1152]{1,0:T(8,128)(2,1)}, bf16[1824,384]{1,0:T(8,128)(2,1)}, bf16[3,3,608,1280]{3,2,1,0:T(8,128)(2,1)}, f32[1824,384]{1,0:T(8,128)}, f32[...) custom-call(s32[3]{0:T(128)} %get-tuple-element.297.valid, bf16[1824,768]{1,0:T(8,128)(2,1)} %get-tuple-element.148.refs_0_.refs_15_, ...), custom_call_target="tpu_custom_call" | custom-call | flops 1 | bytes 1 | tf_op jit(solution)/shard_map/attend/pallas_call | solution.py:560
  108.4 52.5 %mlp.1 = (bf16[1824,3072]{1,0:T(8,128)(2,1)}, bf16[1824,3072]{1,0:T(8,128)(2,1)}, f32[1,3072]{1,0:T(1,128)}, bf16[768,3072]{1,0:T(8,128)(2,1)}, bf16[768,3072]{1,0:T(8,128)(2,1)}) custom-call(s32[3]{0:T(128)} %get-tuple-element.297.valid, s32[3]{0:T(128)} %get-tuple-element.296.where, bf16[1824,768]{1,0:T(8,128)(2,1)} %get-tuple-element.153.normed, ...), custom_call_target="tpu_custom_call" | custom-call | flops 1 | bytes 1 | tf_op jit(solution)/shard_map/mlp/pallas_call | solution.py:752
  160.9 20.7 %middle_back.1 = (bf16[1824,768]{1,0:T(8,128)(2,1)}, bf16[1824,768]{1,0:T(8,128)(2,1)}, f32[1,768]{1,0:T(1,128)}, f32[1,768]{1,0:T(1,128)}, f32[1,768]{1,0:T(1,128)}, /*index=5*/f32[1,768]{1,0:T(1,128)}) custom-call(s32[3]{0:T(128)} %get-tuple-element.297.valid, bf16[1824,3072]{1,0:T(8,128)(2,1)} %get-tuple-element.157.hidden_grad, ...), custom_call_target="tpu_custom_call" | custom-call | flops 1 | bytes 1 | tf_op jit(solution)/shard_map/middle_back/pallas_call | solution.py:860
  181.7 4.4 %fold_first.1 = (bf16[2,4,48,1536]{3,2,1,0:T(8,128)(2,1)}, bf16[2,4,48,1536]{3,2,1,0:T(8,128)(2,1)}) custom-call(s32[3]{0:T(128)} %get-tuple-element.296.where, bf16[2,2,4,48,3072]{4,3,2,1,0:T(8,128)(2,1)} %bitcast.115, bf16[2,2,4,48,3072]{4,3,2,1,0:T(8,128)(2,1)} %bitcast.23.refs_1_.refs_3_.refs_4_.refs_5_, bf16[2,2,4,48,3072]{4,3,2,1,0:T(8,128)(2,1)} %bitcast.116, ...), custom_call_target="tpu_custom_call" | custom-call | flops 1 | bytes 1 | tf_op jit(solution)/shard_map/fold_first/pallas_call | solution.py:241
  186.0 1.6 collective-permute-start.14
  187.6 1.1 collective-permute-start.15
  188.7 32.1 %attend_back.2 = (bf16[1824,1152]{1,0:T(8,128)(2,1)}, f32[1,1152]{1,0:T(1,128)}, f32[1,768]{1,0:T(1,128)}, f32[1,768]{1,0:T(1,128)}, bf16[16,24,1920]{2,1,0:T(8,128)(2,1)}, /*index=5*/bf16[16,24,1920]{2,1,0:T(8,128)(2,1)}) custom-call(s32[3]{0:T(128)} %get-tuple-element.296.where, bf16[1824,1152]{1,0:T(8,128)(2,1)} %get-tuple-element.168.refs_0_.refs_1_.refs_2_, ...), custom_call_target="tpu_custom_call" | custom-call | flops 1 | bytes 1 | tf_op jit(solution)/shard_map/attend_back/pallas_call | solution.py:661
  220.9 1.0 copy-done.2
  222.3 3.8 %fold_second.1 = (bf16[4,48,1536]{2,1,0:T(8,128)(2,1)}, bf16[4,48,1536]{2,1,0:T(8,128)(2,1)}) custom-call(s32[3]{0:T(128)} %get-tuple-element.296.where, bf16[2,2,4,48,3072]{4,3,2,1,0:T(8,128)(2,1)} %bitcast.117, bf16[2,2,4,48,3072]{4,3,2,1,0:T(8,128)(2,1)} %bitcast.23.refs_1_.refs_3_.refs_4_.refs_5_, bf16[2,4,48,1536]{3,2,1,0:T(8,128)(2,1)} %copy-done.2, ...), custom_call_target="tpu_custom_call" | custom-call | flops 1 | bytes 1 | tf_op jit(solution)/shard_map/fold_second/pallas_call | solution.py:267
  226.1 1.0 collective-permute-start.16
  228.9 27.2 %attend_back.3 = (bf16[1824,1152]{1,0:T(8,128)(2,1)}, f32[1,1152]{1,0:T(1,128)}, f32[1,768]{1,0:T(1,128)}, f32[1,768]{1,0:T(1,128)}, bf16[16,24,1280]{2,1,0:T(8,128)(2,1)}, /*index=5*/bf16[16,24,1280]{2,1,0:T(8,128)(2,1)}) custom-call(s32[3]{0:T(128)} %get-tuple-element.296.where, bf16[1824,1152]{1,0:T(8,128)(2,1)} %get-tuple-element.186.refs_0_.refs_1_.refs_2_, ...), custom_call_target="tpu_custom_call" | custom-call | flops 1 | bytes 1 | tf_op jit(solution)/shard_map/attend_back/pallas_call | solution.py:661
  257.2 1.3 fusion.24
  259.0 4.7 %line_first.1 = (bf16[2,48,3072]{2,1,0:T(8,128)(2,1)}, bf16[2,48,3072]{2,1,0:T(8,128)(2,1)}) custom-call(s32[3]{0:T(128)} %get-tuple-element.296.where, bf16[2,2,4,48,3072]{4,3,2,1,0:T(8,128)(2,1)} %bitcast.119, bf16[2,2,4,48,3072]{4,3,2,1,0:T(8,128)(2,1)} %bitcast.23.refs_1_.refs_3_.refs_4_.refs_5_, bf16[2,4,48,1536]{3,2,1,0:T(8,128)(2,1)} %copy-done.2, ...), custom_call_target="tpu_custom_call" | custom-call | flops 1 | bytes 1 | tf_op jit(solution)/shard_map/line_first/pallas_call | solution.py:303
  263.6 2.3 dynamic_update_slice.86
  266.0 1.1 fusion.2
  267.1 1.3 collective-permute-start.19
  268.4 1.2 collective-permute-start.21
  269.6 1.1 collective-permute-start.22
  270.7 1.3 collective-permute-start.23
  272.0 14.3 %input_back.1 = bf16[1824,768]{1,0:T(8,128)(2,1)} custom-call(bf16[1824,1152]{1,0:T(8,128)(2,1)} %get-tuple-element.206.refs_0_, bf16[1824,1152]{1,0:T(8,128)(2,1)} %get-tuple-element.223.refs_1_, bf16[768,1280]{1,0:T(8,128)(2,1)} %bitcast.129, bf16[768,1920]{1,0:T(8,128)(2,1)} %bitcast.125, bf16[1824,768]{1,0:T(8,128)(2,1)} %bitcast.132, ...), custom_call_target="tpu_custom_call" | custom-call | flops 1 | bytes 1 | tf_op jit(solution)/shard_map/input_back/pallas_call | solution.py:909
  287.0 1.3 collective-permute-done.23
  288.3 2.1 fusion.5
  290.5 1.0 add_convert_fusion.3
  291.5 2.8 collective-permute-start.24
  294.3 1.2 collective-permute-start.25
  295.5 1.0 collective-permute-start.26
  296.5 1.3 collective-permute-start.27
  297.8 1.0 dynamic-slice_bitcast_fusion.2
  298.7 15.2 %block_out.1 = bf16[1824,768]{1,0:T(8,128)(2,1)} custom-call(s32[3]{0:T(128)} %get-tuple-element.297.valid, bf16[1824,3072]{1,0:T(8,128)(2,1)} %get-tuple-element.154.active, bf16[768,6144]{1,0:T(8,128)(2,1)} %all-gather.2.cloned.1.call-done.up.down.ups.downs, f32[1824,768]{1,0:T(8,128)} %get-tuple-element.232.middle, f32[1,768]{1,0:T(1,128)} %get-tuple-element.284.bias_down), custom_call_target="tpu_custom_call" | custom-call | flops 1 | bytes 1 | tf_op jit(solution)/shard_map/block_out/pallas_call | solution.py:803
  313.9 1.6 fusion.9
  316.3 1.3 collective-permute-start.30
  317.6 1.1 convert_add_fusion
  318.8 2.7 collective-permute-start.29
  321.5 2.0 collective-permute-done.31
  323.5 6.0 %collective-permute-done.30 = bf16[24,3200]{1,0:T(8,128)(2,1)S(1)} collective-permute-done((bf16[24,3200]{1,0:T(8,128)(2,1)S(1)}, bf16[24,3200]{1,0:T(8,128)(2,1)S(1)}, u32[]{:S(2)}, u32[]{:S(2)}) %collective-permute-start.30) | collective-permute-done | bytes 153632 | tf_op jit(solution)/shard_map/ppermute | solution.py:83
  329.6 0.8 fusion.23
  332.3 1.1 reshape.193
  333.4 1.2 copy.46
  334.7 2.5 reshape.194
  338.5 0.8 reshape_reshape.8
  (198 shorter events, 17.2 us)
Async XLA Ops:
  7.2 3.5 %copy-start.13 = (bf16[73728]{0:T(1024)(128)(2,1)S(1)}, bf16[73728]{0:T(1024)(128)(2,1)}, u32[]{:S(2)}) copy-start(bf16[73728]{0:T(1024)(128)(2,1)} %param.17) | copy-start | bytes 442372
  7.2 101.2 %all-gather.2.cloned.1.call-start = ((), (), s32[]{:S(2)}) async-start(), calls=%async_computation | async-start | bytes 9732096 | tf_op jit(solution)/shard_map/all_gather | solution.py:968
  9.2 2.4 copy-start.14
  9.4 2.5 copy-start.26
  9.4 2.5 copy-start.27
  9.4 8.3 %copy-start.15 = (bf16[18432]{0:T(1024)(128)(2,1)S(1)}, bf16[18432]{0:T(1024)(128)(2,1)}, u32[]{:S(2)}) copy-start(bf16[18432]{0:T(1024)(128)(2,1)} %param.15) | copy-start | bytes 110596
  12.0 8.0 %collective-permute-start = (bf16[1,1,1,1,1,24,1280]{6,5,4,3,2,1,0:T(8,128)(2,1)S(1)}, bf16[1,1,1,1,1,24,1280]{6,5,4,3,2,1,0:T(8,128)(2,1)S(1)}, u32[]{:S(2)}, u32[]{:S(2)}) collective-permute-start(bf16[1,1,1,1,1,24,1280]{6,5,4,3,2,1,0:T(8,128)(2,1)S(1)} %fusion.11), channel_id=1, source_target_pairs={{0,2},{1,3},{2,0},{3,1},{4,6},{5,7},{6,4},{7,5},{8,10},{9,11},{10,... | collective-permute-start | bytes 184328 | tf_op jit(solution)/shard_map/ppermute | solution.py:83
  15.1 9.8 %collective-permute-start.1 = (bf16[1,1,1,1,1,24,1280]{6,5,4,3,2,1,0:T(8,128)(2,1)S(1)}, bf16[1,1,1,1,1,24,1280]{6,5,4,3,2,1,0:T(8,128)(2,1)S(1)}, u32[]{:S(2)}, u32[]{:S(2)}) collective-permute-start(bf16[1,1,1,1,1,24,1280]{6,5,4,3,2,1,0:T(8,128)(2,1)S(1)} %fusion.11), channel_id=1, source_target_pairs={{0,4},{1,5},{2,6},{3,7},{4,0},{5,1},{6,2},{7,3},{8,12},{9,13},{10,... | collective-permute-start | bytes 184328 | tf_op jit(solution)/shard_map/ppermute | solution.py:83
  17.6 7.2 %collective-permute-start.2 = (bf16[1,1,1,1,1,24,1280]{6,5,4,3,2,1,0:T(8,128)(2,1)S(1)}, bf16[1,1,1,1,1,24,1280]{6,5,4,3,2,1,0:T(8,128)(2,1)S(1)}, u32[]{:S(2)}, u32[]{:S(2)}) collective-permute-start(bf16[1,1,1,1,1,24,1280]{6,5,4,3,2,1,0:T(8,128)(2,1)S(1)} %fusion.11), channel_id=1, source_target_pairs={{0,6},{1,7},{2,4},{3,5},{4,2},{5,3},{6,0},{7,1},{8,14},{9,15},{10,... | collective-permute-start | bytes 184328 | tf_op jit(solution)/shard_map/ppermute | solution.py:83
  17.8 11.0 %collective-permute-start.3 = (bf16[1,1,1,1,1,24,1920]{6,5,4,3,2,1,0:T(8,128)(2,1)S(1)}, bf16[1,1,1,1,1,24,1920]{6,5,4,3,2,1,0:T(8,128)(2,1)S(1)}, u32[]{:S(2)}, u32[]{:S(2)}) collective-permute-start(bf16[1,1,1,1,1,24,1920]{6,5,4,3,2,1,0:T(8,128)(2,1)S(1)} %maximum_bitcast_fusion.1), channel_id=1, source_target_pairs={{0,4},{1,5},{2,6},{3,7},{4,0},{5,1},{6,2},{7,3},{8,12},{9,13},{10,... | collective-permute-start | bytes 276488 | tf_op jit(solution)/shard_map/ppermute | solution.py:83
  19.8 21.4 %copy-start.24 = (s32[3]{0:T(128)S(1)}, s32[3]{0:T(128)}, u32[]{:S(2)}) copy-start(s32[3]{0:T(128)} %param.13) | copy-start | bytes 40
  19.9 21.4 %copy-start.25 = (s32[3]{0:T(128)S(1)}, s32[3]{0:T(128)}, u32[]{:S(2)}) copy-start(s32[3]{0:T(128)} %param.12) | copy-start | bytes 40
  28.9 9.9 %collective-permute-start.4 = (bf16[1,1,2,2,1,24,1280]{6,5,4,3,2,1,0:T(8,128)(2,1)S(1)}, bf16[1,1,2,2,1,24,1280]{6,5,4,3,2,1,0:T(8,128)(2,1)S(1)}, u32[]{:S(2)}, u32[]{:S(2)}) collective-permute-start(bf16[1,1,2,2,1,24,1280]{6,5,4,3,2,1,0:T(8,128)(2,1)S(1)} %constant_dynamic-update-slice_fusion.16), channel_id=1, source_target_pairs={{0,8},{1,9},{2,10},{3,11},{4,12},{5,13},{6,14},{7,15},{8,0},{9,1},... | collective-permute-start | bytes 737288 | tf_op jit(solution)/shard_map/ppermute | solution.py:83
  30.5 10.5 %collective-permute-start.5 = (bf16[1,1,2,2,1,24,1280]{6,5,4,3,2,1,0:T(8,128)(2,1)S(1)}, bf16[1,1,2,2,1,24,1280]{6,5,4,3,2,1,0:T(8,128)(2,1)S(1)}, u32[]{:S(2)}, u32[]{:S(2)}) collective-permute-start(bf16[1,1,2,2,1,24,1280]{6,5,4,3,2,1,0:T(8,128)(2,1)S(1)} %constant_dynamic-update-slice_fusion.16), channel_id=1, source_target_pairs={{0,16},{1,17},{2,18},{3,19},{4,20},{5,21},{6,22},{7,23},{8,24},{9,... | collective-permute-start | bytes 737288 | tf_op jit(solution)/shard_map/ppermute | solution.py:83
  32.1 9.0 %collective-permute-start.6 = (bf16[1,1,2,2,1,24,1280]{6,5,4,3,2,1,0:T(8,128)(2,1)S(1)}, bf16[1,1,2,2,1,24,1280]{6,5,4,3,2,1,0:T(8,128)(2,1)S(1)}, u32[]{:S(2)}, u32[]{:S(2)}) collective-permute-start(bf16[1,1,2,2,1,24,1280]{6,5,4,3,2,1,0:T(8,128)(2,1)S(1)} %constant_dynamic-update-slice_fusion.16), channel_id=1, source_target_pairs={{0,24},{1,25},{2,26},{3,27},{4,28},{5,29},{6,30},{7,31},{8,16},{9,... | collective-permute-start | bytes 737288 | tf_op jit(solution)/shard_map/ppermute | solution.py:83
  32.5 6.3 %collective-permute-start.7 = (bf16[1,1,2,1,1,24,1920]{6,5,4,3,2,1,0:T(8,128)(2,1)S(1)}, bf16[1,1,2,1,1,24,1920]{6,5,4,3,2,1,0:T(8,128)(2,1)S(1)}, u32[]{:S(2)}, u32[]{:S(2)}) collective-permute-start(bf16[1,1,2,1,1,24,1920]{6,5,4,3,2,1,0:T(8,128)(2,1)S(1)} %constant_dynamic-update-slice_fusion.13), channel_id=1, source_target_pairs={{0,2},{1,3},{2,0},{3,1},{4,6},{5,7},{6,4},{7,5},{8,10},{9,11},{10,... | collective-permute-start | bytes 552968 | tf_op jit(solution)/shard_map/ppermute | solution.py:83
  41.2 6.6 %collective-permute-start.8 = (bf16[2,2,2,2,1,24,1280]{6,5,4,3,2,1,0:T(8,128)(2,1)S(1)}, bf16[2,2,2,2,1,24,1280]{6,5,4,3,2,1,0:T(8,128)(2,1)}, u32[]{:S(2)}, u32[]{:S(2)}) collective-permute-start(bf16[2,2,2,2,1,24,1280]{6,5,4,3,2,1,0:T(8,128)(2,1)S(1)} %constant_dynamic-update-slice_fusion.10), channel_id=1, source_target_pairs={{0,1},{1,0},{2,3},{3,2},{4,5},{5,4},{6,7},{7,6},{8,9},{9,8},{10,11... | collective-permute-start | bytes 2949128 | tf_op jit(solution)/shard_map/ppermute | solution.py:83
  42.0 29.4 %collective-permute-start.10 = (bf16[1,1,2,2,1,24,1920]{6,5,4,3,2,1,0:T(8,128)(2,1)S(1)}, bf16[1,1,2,2,1,24,1920]{6,5,4,3,2,1,0:T(8,128)(2,1)}, u32[]{:S(2)}, u32[]{:S(2)}) collective-permute-start(bf16[1,1,2,2,1,24,1920]{6,5,4,3,2,1,0:T(8,128)(2,1)S(1)} %constant_dynamic-update-slice_fusion.6), channel_id=1, source_target_pairs={{0,16},{1,17},{2,18},{3,19},{4,20},{5,21},{6,22},{7,23},{8,24},{9,... | collective-permute-start | bytes 1105928 | tf_op jit(solution)/shard_map/ppermute | solution.py:83
  43.6 27.8 %collective-permute-start.11 = (bf16[1,1,2,2,1,24,1920]{6,5,4,3,2,1,0:T(8,128)(2,1)S(1)}, bf16[1,1,2,2,1,24,1920]{6,5,4,3,2,1,0:T(8,128)(2,1)}, u32[]{:S(2)}, u32[]{:S(2)}) collective-permute-start(bf16[1,1,2,2,1,24,1920]{6,5,4,3,2,1,0:T(8,128)(2,1)S(1)} %constant_dynamic-update-slice_fusion.6), channel_id=1, source_target_pairs={{0,24},{1,25},{2,26},{3,27},{4,28},{5,29},{6,30},{7,31},{8,16},{9,... | collective-permute-start | bytes 1105928 | tf_op jit(solution)/shard_map/ppermute | solution.py:83
  44.7 26.6 %collective-permute-start.9 = (bf16[1,1,2,2,1,24,1920]{6,5,4,3,2,1,0:T(8,128)(2,1)S(1)}, bf16[1,1,2,2,1,24,1920]{6,5,4,3,2,1,0:T(8,128)(2,1)}, u32[]{:S(2)}, u32[]{:S(2)}) collective-permute-start(bf16[1,1,2,2,1,24,1920]{6,5,4,3,2,1,0:T(8,128)(2,1)S(1)} %constant_dynamic-update-slice_fusion.6), channel_id=1, source_target_pairs={{0,8},{1,9},{2,10},{3,11},{4,12},{5,13},{6,14},{7,15},{8,0},{9,1},... | collective-permute-start | bytes 1105928 | tf_op jit(solution)/shard_map/ppermute | solution.py:83
  49.1 2.5 copy-start.1
  76.7 3.6 %collective-permute-start.12 = (bf16[2,2,2,2,1,24,1920]{6,5,4,3,2,1,0:T(8,128)(2,1)}, bf16[2,2,2,2,1,24,1920]{6,5,4,3,2,1,0:T(8,128)(2,1)}, u32[]{:S(2)}, u32[]{:S(2)}) collective-permute-start(bf16[2,2,2,2,1,24,1920]{6,5,4,3,2,1,0:T(8,128)(2,1)} %constant_dynamic-update-slice_fusion.2), channel_id=1, source_target_pairs={{0,1},{1,0},{2,3},{3,2},{4,5},{5,4},{6,7},{7,6},{8,9},{9,8},{10,11... | collective-permute-start | bytes 4423688 | tf_op jit(solution)/shard_map/ppermute | solution.py:83
  81.9 1.6 copy-start
  160.9 20.8 %collective-permute-start.13 = (bf16[768,3072]{1,0:T(8,128)(2,1)}, bf16[768,3072]{1,0:T(8,128)(2,1)}, u32[]{:S(2)}, u32[]{:S(2)}) collective-permute-start(bf16[768,3072]{1,0:T(8,128)(2,1)} %get-tuple-element.166), channel_id=1, source_target_pairs={{0,1},{1,0},{2,3},{3,2},{4,5},{5,4},{6,7},{7,6},{8,9},{9,8},{10,11... | collective-permute-start | bytes 14155784 | tf_op jit(solution)/shard_map/ppermute | solution.py:83
  186.0 34.8 %collective-permute-start.14 = (bf16[2,4,48,1536]{3,2,1,0:T(8,128)(2,1)}, bf16[2,4,48,1536]{3,2,1,0:T(8,128)(2,1)S(1)}, u32[]{:S(2)}, u32[]{:S(2)}) collective-permute-start(bf16[2,4,48,1536]{3,2,1,0:T(8,128)(2,1)} %get-tuple-element.183), channel_id=1, source_target_pairs={{0,16},{1,17},{2,18},{3,19},{4,20},{5,21},{6,22},{7,23},{8,24},{9,... | collective-permute-start | bytes 3538952 | tf_op jit(solution)/shard_map/ppermute | solution.py:83
  187.6 33.2 %collective-permute-start.15 = (bf16[2,4,48,1536]{3,2,1,0:T(8,128)(2,1)}, bf16[2,4,48,1536]{3,2,1,0:T(8,128)(2,1)S(1)}, u32[]{:S(2)}, u32[]{:S(2)}) collective-permute-start(bf16[2,4,48,1536]{3,2,1,0:T(8,128)(2,1)} %get-tuple-element.184), channel_id=1, source_target_pairs={{0,8},{1,9},{2,10},{3,11},{4,12},{5,13},{6,14},{7,15},{8,0},{9,1},... | collective-permute-start | bytes 3538952 | tf_op jit(solution)/shard_map/ppermute | solution.py:83
  220.9 1.0 copy-start.2
  220.9 1.4 copy-start.3
  222.3 5.7 %copy-start.16 = (f32[1,3072]{1,0:T(1,128)S(1)}, f32[1,3072]{1,0:T(1,128)}, u32[]{:S(2)}) copy-start(f32[1,3072]{1,0:T(1,128)} %get-tuple-element.220) | copy-start | bytes 36868
  226.1 30.2 %collective-permute-start.18 = (bf16[16,24,1920]{2,1,0:T(8,128)(2,1)}, bf16[16,24,1920]{2,1,0:T(8,128)(2,1)S(1)}, u32[]{:S(2)}, u32[]{:S(2)}) collective-permute-start(bf16[16,24,1920]{2,1,0:T(8,128)(2,1)} %get-tuple-element.202), channel_id=1, source_target_pairs={{0,1},{1,0},{2,3},{3,2},{4,5},{5,4},{6,7},{7,6},{8,9},{9,8},{10,11... | collective-permute-start | bytes 4423688 | tf_op jit(solution)/shard_map/ppermute | solution.py:83
  226.1 30.2 %collective-permute-start.16 = (bf16[4,48,1536]{2,1,0:T(8,128)(2,1)}, bf16[4,48,1536]{2,1,0:T(8,128)(2,1)S(1)}, u32[]{:S(2)}, u32[]{:S(2)}) collective-permute-start(bf16[4,48,1536]{2,1,0:T(8,128)(2,1)} %get-tuple-element.200), channel_id=1, source_target_pairs={{0,8},{1,9},{2,10},{3,11},{4,12},{5,13},{6,14},{7,15},{8,0},{9,1},... | collective-permute-start | bytes 1769480 | tf_op jit(solution)/shard_map/ppermute | solution.py:83
  227.1 29.2 %collective-permute-start.17 = (bf16[4,48,1536]{2,1,0:T(8,128)(2,1)}, bf16[4,48,1536]{2,1,0:T(8,128)(2,1)S(1)}, u32[]{:S(2)}, u32[]{:S(2)}) collective-permute-start(bf16[4,48,1536]{2,1,0:T(8,128)(2,1)} %get-tuple-element.201), channel_id=1, source_target_pairs={{0,16},{1,17},{2,18},{3,19},{4,20},{5,21},{6,22},{7,23},{8,24},{9,... | collective-permute-start | bytes 1769480 | tf_op jit(solution)/shard_map/ppermute | solution.py:83
  228.9 27.3 %copy-start.17 = (f32[1,1152]{1,0:T(1,128)S(1)}, f32[1,1152]{1,0:T(1,128)}, u32[]{:S(2)}) copy-start(f32[1,1152]{1,0:T(1,128)} %get-tuple-element.215) | copy-start | bytes 13828
  228.9 28.3 %copy-start.20 = (f32[1,768]{1,0:T(1,128)S(1)}, f32[1,768]{1,0:T(1,128)}, u32[]{:S(2)}) copy-start(f32[1,768]{1,0:T(1,128)} %get-tuple-element.217) | copy-start | bytes 9220
  228.9 28.3 %copy-start.22 = (f32[1,768]{1,0:T(1,128)S(1)}, f32[1,768]{1,0:T(1,128)}, u32[]{:S(2)}) copy-start(f32[1,768]{1,0:T(1,128)} %get-tuple-element.210) | copy-start | bytes 9220
  228.9 28.3 %copy-start.23 = (f32[1,768]{1,0:T(1,128)S(1)}, f32[1,768]{1,0:T(1,128)}, u32[]{:S(2)}) copy-start(f32[1,768]{1,0:T(1,128)} %get-tuple-element.212) | copy-start | bytes 9220
  228.9 29.5 %copy-start.21 = (f32[1,768]{1,0:T(1,128)S(1)}, f32[1,768]{1,0:T(1,128)}, u32[]{:S(2)}) copy-start(f32[1,768]{1,0:T(1,128)} %get-tuple-element.214) | copy-start | bytes 9220
  228.9 29.6 %copy-start.19 = (f32[1,768]{1,0:T(1,128)S(1)}, f32[1,768]{1,0:T(1,128)}, u32[]{:S(2)}) copy-start(f32[1,768]{1,0:T(1,128)} %get-tuple-element.218) | copy-start | bytes 9220
  228.9 29.7 %copy-start.18 = (f32[1,768]{1,0:T(1,128)S(1)}, f32[1,768]{1,0:T(1,128)}, u32[]{:S(2)}) copy-start(f32[1,768]{1,0:T(1,128)} %get-tuple-element.219) | copy-start | bytes 9220
  256.2 2.7 copy-start.8
  256.3 2.7 copy-start.9
  259.0 7.0 %copy-start.4 = (bf16[16,24,1920]{2,1,0:T(8,128)(2,1)S(1)}, bf16[16,24,1920]{2,1,0:T(8,128)(2,1)}, u32[]{:S(2)}) copy-start(bf16[16,24,1920]{2,1,0:T(8,128)(2,1)} %get-tuple-element.221) | copy-start | bytes 4423684
  267.1 21.2 %collective-permute-start.20 = (bf16[16,24,1280]{2,1,0:T(8,128)(2,1)}, bf16[16,24,1280]{2,1,0:T(8,128)(2,1)}, u32[]{:S(2)}, u32[]{:S(2)}) collective-permute-start(bf16[16,24,1280]{2,1,0:T(8,128)(2,1)} %dynamic_update_slice.86), channel_id=1, source_target_pairs={{0,1},{1,0},{2,3},{3,2},{4,5},{5,4},{6,7},{7,6},{8,9},{9,8},{10,11... | collective-permute-start | bytes 2949128 | tf_op jit(solution)/shard_map/ppermute | solution.py:83
  267.1 21.2 %collective-permute-start.19 = (bf16[2,48,3072]{2,1,0:T(8,128)(2,1)}, bf16[2,48,3072]{2,1,0:T(8,128)(2,1)}, u32[]{:S(2)}, u32[]{:S(2)}) collective-permute-start(bf16[2,48,3072]{2,1,0:T(8,128)(2,1)} %get-tuple-element.224), channel_id=1, source_target_pairs={{0,2},{1,3},{2,0},{3,1},{4,6},{5,7},{6,4},{7,5},{8,10},{9,11},{10,... | collective-permute-start | bytes 1769480 | tf_op jit(solution)/shard_map/ppermute | solution.py:83
  268.4 17.9 %copy-start.7 = (bf16[16,24,1280]{2,1,0:T(8,128)(2,1)S(1)}, bf16[16,24,1280]{2,1,0:T(8,128)(2,1)}, u32[]{:S(2)}) copy-start(bf16[16,24,1280]{2,1,0:T(8,128)(2,1)} %get-tuple-element.230) | copy-start | bytes 2949124
  268.4 18.6 %collective-permute-start.21 = (bf16[4,24,1920]{2,1,0:T(8,128)(2,1)}, bf16[4,24,1920]{2,1,0:T(8,128)(2,1)}, u32[]{:S(2)}, u32[]{:S(2)}) collective-permute-start(bf16[4,24,1920]{2,1,0:T(8,128)(2,1)} %get-tuple-element.226), channel_id=1, source_target_pairs={{0,8},{1,9},{2,10},{3,11},{4,12},{5,13},{6,14},{7,15},{8,0},{9,1},... | collective-permute-start | bytes 1105928 | tf_op jit(solution)/shard_map/ppermute | solution.py:83
  269.6 17.4 %collective-permute-start.22 = (bf16[4,24,1920]{2,1,0:T(8,128)(2,1)}, bf16[4,24,1920]{2,1,0:T(8,128)(2,1)}, u32[]{:S(2)}, u32[]{:S(2)}) collective-permute-start(bf16[4,24,1920]{2,1,0:T(8,128)(2,1)} %get-tuple-element.227), channel_id=1, source_target_pairs={{0,16},{1,17},{2,18},{3,19},{4,20},{5,21},{6,22},{7,23},{8,24},{9,... | collective-permute-start | bytes 1105928 | tf_op jit(solution)/shard_map/ppermute | solution.py:83
  270.7 17.6 %collective-permute-start.23 = (bf16[4,24,1920]{2,1,0:T(8,128)(2,1)}, bf16[4,24,1920]{2,1,0:T(8,128)(2,1)}, u32[]{:S(2)}, u32[]{:S(2)}) collective-permute-start(bf16[4,24,1920]{2,1,0:T(8,128)(2,1)} %get-tuple-element.228), channel_id=1, source_target_pairs={{0,24},{1,25},{2,26},{3,27},{4,28},{5,29},{6,30},{7,31},{8,16},{9,... | collective-permute-start | bytes 1105928 | tf_op jit(solution)/shard_map/ppermute | solution.py:83
  286.3 4.2 %copy-start.10 = (bf16[2,48,3072]{2,1,0:T(8,128)(2,1)S(1)}, bf16[2,48,3072]{2,1,0:T(8,128)(2,1)}, u32[]{:S(2)}) copy-start(bf16[2,48,3072]{2,1,0:T(8,128)(2,1)} %get-tuple-element.205) | copy-start | bytes 1769476
  291.5 24.0 %collective-permute-start.24 = (bf16[1,48,3072]{2,1,0:T(8,128)(2,1)S(1)}, bf16[1,48,3072]{2,1,0:T(8,128)(2,1)S(1)}, u32[]{:S(2)}, u32[]{:S(2)}) collective-permute-start(bf16[1,48,3072]{2,1,0:T(8,128)(2,1)S(1)} %add_convert_fusion.3), channel_id=1, source_target_pairs={{0,4},{1,5},{2,6},{3,7},{4,0},{5,1},{6,2},{7,3},{8,12},{9,13},{10,... | collective-permute-start | bytes 884744 | tf_op jit(solution)/shard_map/ppermute | solution.py:83
  294.3 21.2 %collective-permute-start.25 = (bf16[4,24,1280]{2,1,0:T(8,128)(2,1)}, bf16[4,24,1280]{2,1,0:T(8,128)(2,1)S(1)}, u32[]{:S(2)}, u32[]{:S(2)}) collective-permute-start(bf16[4,24,1280]{2,1,0:T(8,128)(2,1)} %get-tuple-element.234), channel_id=1, source_target_pairs={{0,8},{1,9},{2,10},{3,11},{4,12},{5,13},{6,14},{7,15},{8,0},{9,1},... | collective-permute-start | bytes 737288 | tf_op jit(solution)/shard_map/ppermute | solution.py:83
  295.5 20.0 %collective-permute-start.26 = (bf16[4,24,1280]{2,1,0:T(8,128)(2,1)}, bf16[4,24,1280]{2,1,0:T(8,128)(2,1)S(1)}, u32[]{:S(2)}, u32[]{:S(2)}) collective-permute-start(bf16[4,24,1280]{2,1,0:T(8,128)(2,1)} %get-tuple-element.235), channel_id=1, source_target_pairs={{0,16},{1,17},{2,18},{3,19},{4,20},{5,21},{6,22},{7,23},{8,24},{9,... | collective-permute-start | bytes 737288 | tf_op jit(solution)/shard_map/ppermute | solution.py:83
  296.5 19.0 %collective-permute-start.27 = (bf16[4,24,1280]{2,1,0:T(8,128)(2,1)}, bf16[4,24,1280]{2,1,0:T(8,128)(2,1)S(1)}, u32[]{:S(2)}, u32[]{:S(2)}) collective-permute-start(bf16[4,24,1280]{2,1,0:T(8,128)(2,1)} %get-tuple-element.236), channel_id=1, source_target_pairs={{0,24},{1,25},{2,26},{3,27},{4,28},{5,29},{6,30},{7,31},{8,16},{9,... | collective-permute-start | bytes 737288 | tf_op jit(solution)/shard_map/ppermute | solution.py:83
  315.7 7.8 %collective-permute-start.31 = (bf16[24,3200]{1,0:T(8,128)(2,1)S(1)}, bf16[24,3200]{1,0:T(8,128)(2,1)S(1)}, u32[]{:S(2)}, u32[]{:S(2)}) collective-permute-start(bf16[24,3200]{1,0:T(8,128)(2,1)S(1)} %pad_maximum_fusion.3), channel_id=1, source_target_pairs={{0,6},{1,7},{2,4},{3,5},{4,2},{5,3},{6,0},{7,1},{8,14},{9,15},{10,... | collective-permute-start | bytes 460808 | tf_op jit(solution)/shard_map/ppermute | solution.py:83
  316.3 13.2 %collective-permute-start.30 = (bf16[24,3200]{1,0:T(8,128)(2,1)S(1)}, bf16[24,3200]{1,0:T(8,128)(2,1)S(1)}, u32[]{:S(2)}, u32[]{:S(2)}) collective-permute-start(bf16[24,3200]{1,0:T(8,128)(2,1)S(1)} %pad_maximum_fusion.2), channel_id=1, source_target_pairs={{0,4},{1,5},{2,6},{3,7},{4,0},{5,1},{6,2},{7,3},{8,12},{9,13},{10,... | collective-permute-start | bytes 460808 | tf_op jit(solution)/shard_map/ppermute | solution.py:83
  318.7 10.8 %collective-permute-start.28 = (f32[1,24,3072]{2,1,0:T(8,128)S(1)}, f32[1,24,3072]{2,1,0:T(8,128)S(1)}, u32[]{:S(2)}, u32[]{:S(2)}) collective-permute-start(f32[1,24,3072]{2,1,0:T(8,128)S(1)} %constant_dynamic-slice_fusion), channel_id=1, source_target_pairs={{0,1},{1,0},{2,3},{3,2},{4,5},{5,4},{6,7},{7,6},{8,9},{9,8},{10,11... | collective-permute-start | bytes 884744 | tf_op jit(solution)/shard_map/ppermute | solution.py:83
  318.8 10.7 %collective-permute-start.29 = (bf16[24,3200]{1,0:T(8,128)(2,1)S(1)}, bf16[24,3200]{1,0:T(8,128)(2,1)S(1)}, u32[]{:S(2)}, u32[]{:S(2)}) collective-permute-start(bf16[24,3200]{1,0:T(8,128)(2,1)S(1)} %pad_maximum_fusion.1), channel_id=1, source_target_pairs={{0,2},{1,3},{2,0},{3,1},{4,6},{5,7},{6,4},{7,5},{8,10},{9,11},{10,... | collective-permute-start | bytes 460808 | tf_op jit(solution)/shard_map/ppermute | solution.py:83
  329.6 5.1 %copy-start.5 = (f32[24,3200]{1,0:T(8,128)}, f32[24,3200]{1,0:T(8,128)S(1)}, u32[]{:S(2)}) copy-start(f32[24,3200]{1,0:T(8,128)S(1)} %maximum_add_fusion) | copy-start | bytes 921604
  334.7 2.6 copy-start.6
  334.7 3.5 %copy-start.12 = (f32[24,1152]{1,0:T(8,128)S(1)}, f32[24,1152]{1,0:T(8,128)}, u32[]{:S(2)}) copy-start(f32[24,1152]{1,0:T(8,128)} %get-tuple-element.278) | copy-start | bytes 331780
  334.7 3.6 %copy-start.11 = (f32[24,1152]{1,0:T(8,128)S(1)}, f32[24,1152]{1,0:T(8,128)}, u32[]{:S(2)}) copy-start(f32[24,1152]{1,0:T(8,128)} %get-tuple-element.279) | copy-start | bytes 331780
  337.3 2.0 slice-start
Sparse Core Ops, SparseCore 0:
  11.7 95.2 all-gather.1

commit v6 on v5

--- a/solution.py
+++ b/solution.py
@@ -105,6 +105,19 @@
                 self.advance(flight[0], got)
         return out
 
+    def land(self, job):
+        self.depart()
+        for flight in [flight for flight in self.flying if flight[0] is job]:
+            self.flying.remove(flight)
+            self.advance(job, flight[1])
+
+    def finish_after(self, values):
+        cames, values = lax.optimization_barrier(([flight[1] for flight in self.flying], values))
+        for flight, came in zip(self.flying, cames):
+            flight[1] = came
+        self.finish()
+        return values
+
     def finish(self, turns=None):
         turn = 0
         while (self.waiting or self.flying) and turn != turns:
@@ -114,7 +127,9 @@
                 flight[2] -= 1
             landed = [flight for flight in self.flying if turns is None or flight[2] <= 0]
             self.flying = [flight for flight in self.flying if not (turns is None or flight[2] <= 0)]
-            cames = lax.optimization_barrier([flight[1] for flight in landed])
+            cames = [flight[1] for flight in landed]
+            if turns is not None:
+                cames = lax.optimization_barrier(cames)
             for flight, came in zip(landed, cames):
                 self.advance(flight[0], came)
 
@@ -1062,7 +1077,15 @@
     )
     if cut:
         line = flights.add(line_steps([plane_a["result"], plane_b["result"]], mesh), [])
-    flights.finish()
+        flights.land(mlp_job)
+        up_total, down_total = mlp_job["result"]
+    else:
+        flights.finish()
+        mlp_total = mlp_job["result"].reshape(share, chunks, 2, width)
+        up_total, down_total = mlp_total[:, :, 0], mlp_total[:, :, 1]
+    up_total = up_total.reshape(share, chunks, count, share).transpose(0, 2, 1, 3).reshape(-1)
+    down_total = down_total.reshape(share, chunks, width).transpose(1, 0, 2).reshape(-1)
+    up_total, down_total = flights.finish_after((up_total, down_total))
     if cut:
         edge_a = grads_a[0].shape[-1]
         total_a, total_b = line["result"][:, :edge_a], line["result"][:, edge_a:]
@@ -1071,20 +1094,13 @@
     else:
         total_a, total_b = sum_a["result"], sum_b["result"]
         small_total = small_job["result"]
-    if cut:
-        up_total, down_total = mlp_job["result"]
-    else:
-        mlp_total = mlp_job["result"].reshape(share, chunks, 2, width)
-        up_total, down_total = mlp_total[:, :, 0], mlp_total[:, :, 1]
-    up_total = up_total.reshape(share, chunks, count, share).transpose(0, 2, 1, 3)
-    down_total = down_total.reshape(share, chunks, width).transpose(1, 0, 2)
     return (
         block_out.reshape(tokens.shape),
         input_grad.reshape(tokens.shape),
         by_kind(total_a, total_b).reshape(-1),
         total_a[:, span:].reshape(-1),
-        up_total.reshape(-1),
-        down_total.reshape(-1),
+        up_total,
+        down_total,
         small_total[:edge],
         small_total[edge:],
     )

time: 352 us -> 352 us (level)
  other arithmetic: 12.4 us -> 16.1 us
  transfers between devices with their start and end apart: 33 -> 33, of which waited for: 8 -> 7; matrix products, arithmetic and copies ran while one was open for 7% -> 9% of each run, Pallas kernels for 44% -> 44%
where the time goes in v6:
time: 352 us; the launch traced here: 347 us
  Pallas kernels  220 us (62%)
  local copies, waits for them, and re-layouts  37.2 us (11%)
  starting transfers between devices  35 us (10%)
  waiting for transfers between devices  23.2 us (7%)
  other arithmetic  16.1 us (5%)
  between operations  15.5 us (4%)
    pallas_call x2, Pallas kernels, attend_back(): pl.pallas_call(functools.partial(attend_back_kernel, pairs=pairs, extra=b...  59.3 us
    pallas_call x1, Pallas kernels, mlp(): pl.pallas_call(functools.partial(mlp_kernel, seq=seq, tile=tile_of(seq),...  52.6 us
    pallas_call x2, Pallas kernels, attend(): pl.pallas_call(functools.partial(attend_kernel, tile=tile_of(seq), padded...  44.7 us
    ppermute x32, starting transfers between devices, depart(): came = [lax.ppermute(array, AXES, pairs) for array, pairs in sends]  34.9 us
    ppermute x32, waiting for transfers between devices, depart(): came = [lax.ppermute(array, AXES, pairs) for array, pairs in sends]  23.2 us
    pallas_call x1, Pallas kernels, middle_back(): pl.pallas_call(functools.partial(middle_back_kernel, seq=seq, sub=sub), g...  20.7 us
    pallas_call x1, Pallas kernels, block_out_of(): pl.pallas_call(functools.partial(block_out_kernel, seq=seq, begin=begin),...  15.2 us
    pallas_call x1, Pallas kernels, input_back(): pl.pallas_call(functools.partial(input_back_kernel, spans=spans, sub=sub)...  14.3 us
  transfers between devices with their start and end apart: 33, of which 7 were waited for; matrix products, arithmetic and copies ran while one was open for 9% of the time, Pallas kernels for 44%

profile of v6, /device:TPU:0, one launch (start us, length us, event | category | flops | bytes accessed | tf_op | source)
XLA Modules:
  0.0 346.7 jit_solution(11475833010969767557)
XLA Ops:
  7.2 2.0 reshape.171
  9.4 1.3 reshape.172
  12.0 3.1 collective-permute-start
  15.1 2.6 collective-permute-start.1
  17.8 2.0 collective-permute-start.3
  20.0 4.9 %collective-permute-done.1 = bf16[1,1,1,1,1,24,1280]{6,5,4,3,2,1,0:T(8,128)(2,1)S(1)} collective-permute-done((bf16[1,1,1,1,1,24,1280]{6,5,4,3,2,1,0:T(8,128)(2,1)S(1)}, bf16[1,1,1,1,1,24,1280]{6,5,4,3,2,1,0:T(8,128)(2,1)S(1)}, u32[]{:S(2)}, u32[]{:S(2)}) %collective-permute-start.1) | collective-permute-done | bytes 61472 | tf_op jit(solution)/shard_map/ppermute | solution.py:83
  24.8 4.0 %collective-permute-done.3 = bf16[1,1,1,1,1,24,1920]{6,5,4,3,2,1,0:T(8,128)(2,1)S(1)} collective-permute-done((bf16[1,1,1,1,1,24,1920]{6,5,4,3,2,1,0:T(8,128)(2,1)S(1)}, bf16[1,1,1,1,1,24,1920]{6,5,4,3,2,1,0:T(8,128)(2,1)S(1)}, u32[]{:S(2)}, u32[]{:S(2)}) %collective-permute-start.3) | collective-permute-done | bytes 92192 | tf_op jit(solution)/shard_map/ppermute | solution.py:83
  28.9 1.6 collective-permute-start.4
  30.5 1.6 collective-permute-start.5
  33.0 5.8 %collective-permute-done.7 = bf16[1,1,2,1,1,24,1920]{6,5,4,3,2,1,0:T(8,128)(2,1)S(1)} collective-permute-done((bf16[1,1,2,1,1,24,1920]{6,5,4,3,2,1,0:T(8,128)(2,1)S(1)}, bf16[1,1,2,1,1,24,1920]{6,5,4,3,2,1,0:T(8,128)(2,1)S(1)}, u32[]{:S(2)}, u32[]{:S(2)}) %collective-permute-start.7) | collective-permute-done | bytes 184352 | tf_op jit(solution)/shard_map/ppermute | solution.py:83
  38.8 2.3 collective-permute-done.5
  42.0 1.6 collective-permute-start.10
  43.6 1.2 collective-permute-start.11
  44.7 0.8 collective-permute-start.9
  45.5 1.3 broadcast_in_dim.31
  47.8 1.3 constant_dynamic-update-slice_fusion.8
  49.4 0.8 fusion.25
  51.6 19.7 %attend.2 = (bf16[1824,768]{1,0:T(8,128)(2,1)}, bf16[1824,1152]{1,0:T(8,128)(2,1)}, bf16[1824,384]{1,0:T(8,128)(2,1)}, bf16[3,3,608,1280]{3,2,1,0:T(8,128)(2,1)}, f32[1824,384]{1,0:T(8,128)}) custom-call(s32[3]{0:T(128)} %get-tuple-element.299.valid, bf16[1824,768]{1,0:T(8,128)(2,1)} %bitcast.130, f32[1,768]{1,0:T(1,128)} %get-tuple-element.297.refs_1_.refs_6_, ...), custom_call_target="tpu_custom_call" | custom-call | flops 1 | bytes 1 | tf_op jit(solution)/shard_map/attend/pallas_call | solution.py:575
  71.4 1.8 constant_dynamic-update-slice_fusion.4
  73.2 1.8 constant_dynamic-update-slice_fusion.3
  74.9 1.8 constant_dynamic-update-slice_fusion.2
  78.4 1.6 constant_dynamic-update-slice_fusion.1
  80.3 1.6 constant_dynamic-update-slice_fusion
  81.9 1.6 copy-done
  83.5 24.9 %attend.3 = (bf16[1824,1152]{1,0:T(8,128)(2,1)}, bf16[1824,384]{1,0:T(8,128)(2,1)}, bf16[3,3,608,1280]{3,2,1,0:T(8,128)(2,1)}, f32[1824,384]{1,0:T(8,128)}, f32[...) custom-call(s32[3]{0:T(128)} %get-tuple-element.299.valid, bf16[1824,768]{1,0:T(8,128)(2,1)} %get-tuple-element.149.refs_0_.refs_15_, ...), custom_call_target="tpu_custom_call" | custom-call | flops 1 | bytes 1 | tf_op jit(solution)/shard_map/attend/pallas_call | solution.py:575
  108.4 52.6 %mlp.1 = (bf16[1824,3072]{1,0:T(8,128)(2,1)}, bf16[1824,3072]{1,0:T(8,128)(2,1)}, f32[1,3072]{1,0:T(1,128)}, bf16[768,3072]{1,0:T(8,128)(2,1)}, bf16[768,3072]{1,0:T(8,128)(2,1)}) custom-call(s32[3]{0:T(128)} %get-tuple-element.299.valid, s32[3]{0:T(128)} %get-tuple-element.298.where, bf16[1824,768]{1,0:T(8,128)(2,1)} %get-tuple-element.154.normed, ...), custom_call_target="tpu_custom_call" | custom-call | flops 1 | bytes 1 | tf_op jit(solution)/shard_map/mlp/pallas_call | solution.py:767
  161.1 20.7 %middle_back.1 = (bf16[1824,768]{1,0:T(8,128)(2,1)}, bf16[1824,768]{1,0:T(8,128)(2,1)}, f32[1,768]{1,0:T(1,128)}, f32[1,768]{1,0:T(1,128)}, f32[1,768]{1,0:T(1,128)}, /*index=5*/f32[1,768]{1,0:T(1,128)}) custom-call(s32[3]{0:T(128)} %get-tuple-element.299.valid, bf16[1824,3072]{1,0:T(8,128)(2,1)} %get-tuple-element.158.hidden_grad, ...), custom_call_target="tpu_custom_call" | custom-call | flops 1 | bytes 1 | tf_op jit(solution)/shard_map/middle_back/pallas_call | solution.py:875
  181.8 4.4 %fold_first.1 = (bf16[2,4,48,1536]{3,2,1,0:T(8,128)(2,1)}, bf16[2,4,48,1536]{3,2,1,0:T(8,128)(2,1)}) custom-call(s32[3]{0:T(128)} %get-tuple-element.298.where, bf16[2,2,4,48,3072]{4,3,2,1,0:T(8,128)(2,1)} %bitcast.115, bf16[2,2,4,48,3072]{4,3,2,1,0:T(8,128)(2,1)} %bitcast.23.refs_1_.refs_3_.refs_4_.refs_5_, bf16[2,2,4,48,3072]{4,3,2,1,0:T(8,128)(2,1)} %bitcast.116, ...), custom_call_target="tpu_custom_call" | custom-call | flops 1 | bytes 1 | tf_op jit(solution)/shard_map/fold_first/pallas_call | solution.py:256
  186.2 1.7 collective-permute-start.14
  187.9 1.0 collective-permute-start.15
  188.9 32.1 %attend_back.2 = (bf16[1824,1152]{1,0:T(8,128)(2,1)}, f32[1,1152]{1,0:T(1,128)}, f32[1,768]{1,0:T(1,128)}, f32[1,768]{1,0:T(1,128)}, bf16[16,24,1920]{2,1,0:T(8,128)(2,1)}, /*index=5*/bf16[16,24,1920]{2,1,0:T(8,128)(2,1)}) custom-call(s32[3]{0:T(128)} %get-tuple-element.298.where, bf16[1824,1152]{1,0:T(8,128)(2,1)} %get-tuple-element.169.refs_0_.refs_1_.refs_2_, ...), custom_call_target="tpu_custom_call" | custom-call | flops 1 | bytes 1 | tf_op jit(solution)/shard_map/attend_back/pallas_call | solution.py:676
  221.1 1.0 copy-done.2
  222.5 3.8 %fold_second.1 = (bf16[4,48,1536]{2,1,0:T(8,128)(2,1)}, bf16[4,48,1536]{2,1,0:T(8,128)(2,1)}) custom-call(s32[3]{0:T(128)} %get-tuple-element.298.where, bf16[2,2,4,48,3072]{4,3,2,1,0:T(8,128)(2,1)} %bitcast.117, bf16[2,2,4,48,3072]{4,3,2,1,0:T(8,128)(2,1)} %bitcast.23.refs_1_.refs_3_.refs_4_.refs_5_, bf16[2,4,48,1536]{3,2,1,0:T(8,128)(2,1)} %copy-done.2, ...), custom_call_target="tpu_custom_call" | custom-call | flops 1 | bytes 1 | tf_op jit(solution)/shard_map/fold_second/pallas_call | solution.py:282
  226.3 1.0 collective-permute-start.16
  229.2 27.2 %attend_back.3 = (bf16[1824,1152]{1,0:T(8,128)(2,1)}, f32[1,1152]{1,0:T(1,128)}, f32[1,768]{1,0:T(1,128)}, f32[1,768]{1,0:T(1,128)}, bf16[16,24,1280]{2,1,0:T(8,128)(2,1)}, /*index=5*/bf16[16,24,1280]{2,1,0:T(8,128)(2,1)}) custom-call(s32[3]{0:T(128)} %get-tuple-element.298.where, bf16[1824,1152]{1,0:T(8,128)(2,1)} %get-tuple-element.187.refs_0_.refs_1_.refs_2_, ...), custom_call_target="tpu_custom_call" | custom-call | flops 1 | bytes 1 | tf_op jit(solution)/shard_map/attend_back/pallas_call | solution.py:676
  257.4 1.3 fusion.24
  259.2 4.7 %line_first.1 = (bf16[2,48,3072]{2,1,0:T(8,128)(2,1)}, bf16[2,48,3072]{2,1,0:T(8,128)(2,1)}) custom-call(s32[3]{0:T(128)} %get-tuple-element.298.where, bf16[2,2,4,48,3072]{4,3,2,1,0:T(8,128)(2,1)} %bitcast.119, bf16[2,2,4,48,3072]{4,3,2,1,0:T(8,128)(2,1)} %bitcast.23.refs_1_.refs_3_.refs_4_.refs_5_, bf16[2,4,48,1536]{3,2,1,0:T(8,128)(2,1)} %copy-done.2, ...), custom_call_target="tpu_custom_call" | custom-call | flops 1 | bytes 1 | tf_op jit(solution)/shard_map/line_first/pallas_call | solution.py:318
  263.9 2.3 dynamic_update_slice.86
  266.3 1.1 fusion.2
  267.4 1.2 collective-permute-start.19
  268.7 1.3 collective-permute-start.21
  269.9 1.1 collective-permute-start.22
  271.0 1.2 collective-permute-start.23
  272.2 14.3 %input_back.1 = bf16[1824,768]{1,0:T(8,128)(2,1)} custom-call(bf16[1824,1152]{1,0:T(8,128)(2,1)} %get-tuple-element.207.refs_0_, bf16[1824,1152]{1,0:T(8,128)(2,1)} %get-tuple-element.224.refs_1_, bf16[768,1280]{1,0:T(8,128)(2,1)} %bitcast.129, bf16[768,1920]{1,0:T(8,128)(2,1)} %bitcast.125, bf16[1824,768]{1,0:T(8,128)(2,1)} %bitcast.132, ...), custom_call_target="tpu_custom_call" | custom-call | flops 1 | bytes 1 | tf_op jit(solution)/shard_map/input_back/pallas_call | solution.py:924
  287.3 1.3 collective-permute-done.23
  288.6 2.1 fusion.5
  290.8 1.0 add_convert_fusion.3
  291.8 2.7 collective-permute-start.24
  294.5 1.2 collective-permute-start.25
  295.8 1.0 collective-permute-start.26
  296.8 1.2 collective-permute-start.27
  298.0 1.0 dynamic-slice_bitcast_fusion.2
  299.0 15.2 %block_out.1 = bf16[1824,768]{1,0:T(8,128)(2,1)} custom-call(s32[3]{0:T(128)} %get-tuple-element.299.valid, bf16[1824,3072]{1,0:T(8,128)(2,1)} %get-tuple-element.155.active, bf16[768,6144]{1,0:T(8,128)(2,1)} %all-gather.2.cloned.1.call-done.up.down.ups.downs, f32[1824,768]{1,0:T(8,128)} %get-tuple-element.233.middle, f32[1,768]{1,0:T(1,128)} %get-tuple-element.286.bias_down), custom_call_target="tpu_custom_call" | custom-call | flops 1 | bytes 1 | tf_op jit(solution)/shard_map/block_out/pallas_call | solution.py:818
  314.1 2.2 fusion.9
  316.4 1.1 convert_add_fusion
  317.6 0.8 fusion.14
  320.4 1.1 collective-permute-start.29
  322.2 2.6 collective-permute-start.28
  324.9 1.1 reshape.192
  326.0 1.2 copy.45
  327.3 2.5 reshape.193
  330.8 4.6 %collective-permute-done.29 = bf16[24,3200]{1,0:T(8,128)(2,1)} collective-permute-done((bf16[24,3200]{1,0:T(8,128)(2,1)}, bf16[24,3200]{1,0:T(8,128)(2,1)}, u32[]{:S(2)}, u32[]{:S(2)}) %collective-permute-start.29) | collective-permute-done | bytes 153632 | tf_op jit(solution)/shard_map/ppermute | solution.py:83
  335.4 1.1 maximum_add_fusion
  338.0 0.8 reshape_reshape.8
  (193 shorter events, 18.3 us)
Async XLA Ops:
  7.2 3.5 %copy-start.11 = (bf16[73728]{0:T(1024)(128)(2,1)S(1)}, bf16[73728]{0:T(1024)(128)(2,1)}, u32[]{:S(2)}) copy-start(bf16[73728]{0:T(1024)(128)(2,1)} %param.17) | copy-start | bytes 442372
  7.2 101.3 %all-gather.2.cloned.1.call-start = ((), (), s32[]{:S(2)}) async-start(), calls=%async_computation | async-start | bytes 9732096 | tf_op jit(solution)/shard_map/all_gather | solution.py:983
  9.2 2.4 copy-start.12
  9.4 2.5 copy-start.24
  9.4 2.5 copy-start.25
  9.4 8.3 %copy-start.13 = (bf16[18432]{0:T(1024)(128)(2,1)S(1)}, bf16[18432]{0:T(1024)(128)(2,1)}, u32[]{:S(2)}) copy-start(bf16[18432]{0:T(1024)(128)(2,1)} %param.15) | copy-start | bytes 110596
  12.0 8.0 %collective-permute-start = (bf16[1,1,1,1,1,24,1280]{6,5,4,3,2,1,0:T(8,128)(2,1)S(1)}, bf16[1,1,1,1,1,24,1280]{6,5,4,3,2,1,0:T(8,128)(2,1)S(1)}, u32[]{:S(2)}, u32[]{:S(2)}) collective-permute-start(bf16[1,1,1,1,1,24,1280]{6,5,4,3,2,1,0:T(8,128)(2,1)S(1)} %fusion.11), channel_id=1, source_target_pairs={{0,2},{1,3},{2,0},{3,1},{4,6},{5,7},{6,4},{7,5},{8,10},{9,11},{10,... | collective-permute-start | bytes 184328 | tf_op jit(solution)/shard_map/ppermute | solution.py:83
  15.1 9.8 %collective-permute-start.1 = (bf16[1,1,1,1,1,24,1280]{6,5,4,3,2,1,0:T(8,128)(2,1)S(1)}, bf16[1,1,1,1,1,24,1280]{6,5,4,3,2,1,0:T(8,128)(2,1)S(1)}, u32[]{:S(2)}, u32[]{:S(2)}) collective-permute-start(bf16[1,1,1,1,1,24,1280]{6,5,4,3,2,1,0:T(8,128)(2,1)S(1)} %fusion.11), channel_id=1, source_target_pairs={{0,4},{1,5},{2,6},{3,7},{4,0},{5,1},{6,2},{7,3},{8,12},{9,13},{10,... | collective-permute-start | bytes 184328 | tf_op jit(solution)/shard_map/ppermute | solution.py:83
  17.6 7.2 %collective-permute-start.2 = (bf16[1,1,1,1,1,24,1280]{6,5,4,3,2,1,0:T(8,128)(2,1)S(1)}, bf16[1,1,1,1,1,24,1280]{6,5,4,3,2,1,0:T(8,128)(2,1)S(1)}, u32[]{:S(2)}, u32[]{:S(2)}) collective-permute-start(bf16[1,1,1,1,1,24,1280]{6,5,4,3,2,1,0:T(8,128)(2,1)S(1)} %fusion.11), channel_id=1, source_target_pairs={{0,6},{1,7},{2,4},{3,5},{4,2},{5,3},{6,0},{7,1},{8,14},{9,15},{10,... | collective-permute-start | bytes 184328 | tf_op jit(solution)/shard_map/ppermute | solution.py:83
  17.8 11.0 %collective-permute-start.3 = (bf16[1,1,1,1,1,24,1920]{6,5,4,3,2,1,0:T(8,128)(2,1)S(1)}, bf16[1,1,1,1,1,24,1920]{6,5,4,3,2,1,0:T(8,128)(2,1)S(1)}, u32[]{:S(2)}, u32[]{:S(2)}) collective-permute-start(bf16[1,1,1,1,1,24,1920]{6,5,4,3,2,1,0:T(8,128)(2,1)S(1)} %maximum_bitcast_fusion.1), channel_id=1, source_target_pairs={{0,4},{1,5},{2,6},{3,7},{4,0},{5,1},{6,2},{7,3},{8,12},{9,13},{10,... | collective-permute-start | bytes 276488 | tf_op jit(solution)/shard_map/ppermute | solution.py:83
  19.8 21.4 %copy-start.22 = (s32[3]{0:T(128)S(1)}, s32[3]{0:T(128)}, u32[]{:S(2)}) copy-start(s32[3]{0:T(128)} %param.13) | copy-start | bytes 40
  19.9 21.4 %copy-start.23 = (s32[3]{0:T(128)S(1)}, s32[3]{0:T(128)}, u32[]{:S(2)}) copy-start(s32[3]{0:T(128)} %param.12) | copy-start | bytes 40
  28.9 9.9 %collective-permute-start.4 = (bf16[1,1,2,2,1,24,1280]{6,5,4,3,2,1,0:T(8,128)(2,1)S(1)}, bf16[1,1,2,2,1,24,1280]{6,5,4,3,2,1,0:T(8,128)(2,1)S(1)}, u32[]{:S(2)}, u32[]{:S(2)}) collective-permute-start(bf16[1,1,2,2,1,24,1280]{6,5,4,3,2,1,0:T(8,128)(2,1)S(1)} %constant_dynamic-update-slice_fusion.16), channel_id=1, source_target_pairs={{0,8},{1,9},{2,10},{3,11},{4,12},{5,13},{6,14},{7,15},{8,0},{9,1},... | collective-permute-start | bytes 737288 | tf_op jit(solution)/shard_map/ppermute | solution.py:83
  30.5 10.5 %collective-permute-start.5 = (bf16[1,1,2,2,1,24,1280]{6,5,4,3,2,1,0:T(8,128)(2,1)S(1)}, bf16[1,1,2,2,1,24,1280]{6,5,4,3,2,1,0:T(8,128)(2,1)S(1)}, u32[]{:S(2)}, u32[]{:S(2)}) collective-permute-start(bf16[1,1,2,2,1,24,1280]{6,5,4,3,2,1,0:T(8,128)(2,1)S(1)} %constant_dynamic-update-slice_fusion.16), channel_id=1, source_target_pairs={{0,16},{1,17},{2,18},{3,19},{4,20},{5,21},{6,22},{7,23},{8,24},{9,... | collective-permute-start | bytes 737288 | tf_op jit(solution)/shard_map/ppermute | solution.py:83
  32.1 9.0 %collective-permute-start.6 = (bf16[1,1,2,2,1,24,1280]{6,5,4,3,2,1,0:T(8,128)(2,1)S(1)}, bf16[1,1,2,2,1,24,1280]{6,5,4,3,2,1,0:T(8,128)(2,1)S(1)}, u32[]{:S(2)}, u32[]{:S(2)}) collective-permute-start(bf16[1,1,2,2,1,24,1280]{6,5,4,3,2,1,0:T(8,128)(2,1)S(1)} %constant_dynamic-update-slice_fusion.16), channel_id=1, source_target_pairs={{0,24},{1,25},{2,26},{3,27},{4,28},{5,29},{6,30},{7,31},{8,16},{9,... | collective-permute-start | bytes 737288 | tf_op jit(solution)/shard_map/ppermute | solution.py:83
  32.5 6.3 %collective-permute-start.7 = (bf16[1,1,2,1,1,24,1920]{6,5,4,3,2,1,0:T(8,128)(2,1)S(1)}, bf16[1,1,2,1,1,24,1920]{6,5,4,3,2,1,0:T(8,128)(2,1)S(1)}, u32[]{:S(2)}, u32[]{:S(2)}) collective-permute-start(bf16[1,1,2,1,1,24,1920]{6,5,4,3,2,1,0:T(8,128)(2,1)S(1)} %constant_dynamic-update-slice_fusion.13), channel_id=1, source_target_pairs={{0,2},{1,3},{2,0},{3,1},{4,6},{5,7},{6,4},{7,5},{8,10},{9,11},{10,... | collective-permute-start | bytes 552968 | tf_op jit(solution)/shard_map/ppermute | solution.py:83
  41.2 6.7 %collective-permute-start.8 = (bf16[2,2,2,2,1,24,1280]{6,5,4,3,2,1,0:T(8,128)(2,1)S(1)}, bf16[2,2,2,2,1,24,1280]{6,5,4,3,2,1,0:T(8,128)(2,1)}, u32[]{:S(2)}, u32[]{:S(2)}) collective-permute-start(bf16[2,2,2,2,1,24,1280]{6,5,4,3,2,1,0:T(8,128)(2,1)S(1)} %constant_dynamic-update-slice_fusion.10), channel_id=1, source_target_pairs={{0,1},{1,0},{2,3},{3,2},{4,5},{5,4},{6,7},{7,6},{8,9},{9,8},{10,11... | collective-permute-start | bytes 2949128 | tf_op jit(solution)/shard_map/ppermute | solution.py:83
  42.0 29.4 %collective-permute-start.10 = (bf16[1,1,2,2,1,24,1920]{6,5,4,3,2,1,0:T(8,128)(2,1)S(1)}, bf16[1,1,2,2,1,24,1920]{6,5,4,3,2,1,0:T(8,128)(2,1)}, u32[]{:S(2)}, u32[]{:S(2)}) collective-permute-start(bf16[1,1,2,2,1,24,1920]{6,5,4,3,2,1,0:T(8,128)(2,1)S(1)} %constant_dynamic-update-slice_fusion.6), channel_id=1, source_target_pairs={{0,16},{1,17},{2,18},{3,19},{4,20},{5,21},{6,22},{7,23},{8,24},{9,... | collective-permute-start | bytes 1105928 | tf_op jit(solution)/shard_map/ppermute | solution.py:83
  43.6 27.8 %collective-permute-start.11 = (bf16[1,1,2,2,1,24,1920]{6,5,4,3,2,1,0:T(8,128)(2,1)S(1)}, bf16[1,1,2,2,1,24,1920]{6,5,4,3,2,1,0:T(8,128)(2,1)}, u32[]{:S(2)}, u32[]{:S(2)}) collective-permute-start(bf16[1,1,2,2,1,24,1920]{6,5,4,3,2,1,0:T(8,128)(2,1)S(1)} %constant_dynamic-update-slice_fusion.6), channel_id=1, source_target_pairs={{0,24},{1,25},{2,26},{3,27},{4,28},{5,29},{6,30},{7,31},{8,16},{9,... | collective-permute-start | bytes 1105928 | tf_op jit(solution)/shard_map/ppermute | solution.py:83
  44.7 26.6 %collective-permute-start.9 = (bf16[1,1,2,2,1,24,1920]{6,5,4,3,2,1,0:T(8,128)(2,1)S(1)}, bf16[1,1,2,2,1,24,1920]{6,5,4,3,2,1,0:T(8,128)(2,1)}, u32[]{:S(2)}, u32[]{:S(2)}) collective-permute-start(bf16[1,1,2,2,1,24,1920]{6,5,4,3,2,1,0:T(8,128)(2,1)S(1)} %constant_dynamic-update-slice_fusion.6), channel_id=1, source_target_pairs={{0,8},{1,9},{2,10},{3,11},{4,12},{5,13},{6,14},{7,15},{8,0},{9,1},... | collective-permute-start | bytes 1105928 | tf_op jit(solution)/shard_map/ppermute | solution.py:83
  49.2 2.5 copy-start.1
  76.7 3.6 %collective-permute-start.12 = (bf16[2,2,2,2,1,24,1920]{6,5,4,3,2,1,0:T(8,128)(2,1)}, bf16[2,2,2,2,1,24,1920]{6,5,4,3,2,1,0:T(8,128)(2,1)}, u32[]{:S(2)}, u32[]{:S(2)}) collective-permute-start(bf16[2,2,2,2,1,24,1920]{6,5,4,3,2,1,0:T(8,128)(2,1)} %constant_dynamic-update-slice_fusion.2), channel_id=1, source_target_pairs={{0,1},{1,0},{2,3},{3,2},{4,5},{5,4},{6,7},{7,6},{8,9},{9,8},{10,11... | collective-permute-start | bytes 4423688 | tf_op jit(solution)/shard_map/ppermute | solution.py:83
  81.9 1.6 copy-start
  161.0 20.8 %collective-permute-start.13 = (bf16[768,3072]{1,0:T(8,128)(2,1)}, bf16[768,3072]{1,0:T(8,128)(2,1)}, u32[]{:S(2)}, u32[]{:S(2)}) collective-permute-start(bf16[768,3072]{1,0:T(8,128)(2,1)} %get-tuple-element.167), channel_id=1, source_target_pairs={{0,1},{1,0},{2,3},{3,2},{4,5},{5,4},{6,7},{7,6},{8,9},{9,8},{10,11... | collective-permute-start | bytes 14155784 | tf_op jit(solution)/shard_map/ppermute | solution.py:83
  186.2 34.8 %collective-permute-start.14 = (bf16[2,4,48,1536]{3,2,1,0:T(8,128)(2,1)}, bf16[2,4,48,1536]{3,2,1,0:T(8,128)(2,1)S(1)}, u32[]{:S(2)}, u32[]{:S(2)}) collective-permute-start(bf16[2,4,48,1536]{3,2,1,0:T(8,128)(2,1)} %get-tuple-element.184), channel_id=1, source_target_pairs={{0,16},{1,17},{2,18},{3,19},{4,20},{5,21},{6,22},{7,23},{8,24},{9,... | collective-permute-start | bytes 3538952 | tf_op jit(solution)/shard_map/ppermute | solution.py:83
  187.9 33.2 %collective-permute-start.15 = (bf16[2,4,48,1536]{3,2,1,0:T(8,128)(2,1)}, bf16[2,4,48,1536]{3,2,1,0:T(8,128)(2,1)S(1)}, u32[]{:S(2)}, u32[]{:S(2)}) collective-permute-start(bf16[2,4,48,1536]{3,2,1,0:T(8,128)(2,1)} %get-tuple-element.185), channel_id=1, source_target_pairs={{0,8},{1,9},{2,10},{3,11},{4,12},{5,13},{6,14},{7,15},{8,0},{9,1},... | collective-permute-start | bytes 3538952 | tf_op jit(solution)/shard_map/ppermute | solution.py:83
  221.0 1.0 copy-start.2
  221.1 1.4 copy-start.3
  222.5 5.7 %copy-start.14 = (f32[1,3072]{1,0:T(1,128)S(1)}, f32[1,3072]{1,0:T(1,128)}, u32[]{:S(2)}) copy-start(f32[1,3072]{1,0:T(1,128)} %get-tuple-element.221) | copy-start | bytes 36868
  226.3 30.3 %collective-permute-start.18 = (bf16[16,24,1920]{2,1,0:T(8,128)(2,1)}, bf16[16,24,1920]{2,1,0:T(8,128)(2,1)S(1)}, u32[]{:S(2)}, u32[]{:S(2)}) collective-permute-start(bf16[16,24,1920]{2,1,0:T(8,128)(2,1)} %get-tuple-element.203), channel_id=1, source_target_pairs={{0,1},{1,0},{2,3},{3,2},{4,5},{5,4},{6,7},{7,6},{8,9},{9,8},{10,11... | collective-permute-start | bytes 4423688 | tf_op jit(solution)/shard_map/ppermute | solution.py:83
  226.3 30.2 %collective-permute-start.16 = (bf16[4,48,1536]{2,1,0:T(8,128)(2,1)}, bf16[4,48,1536]{2,1,0:T(8,128)(2,1)S(1)}, u32[]{:S(2)}, u32[]{:S(2)}) collective-permute-start(bf16[4,48,1536]{2,1,0:T(8,128)(2,1)} %get-tuple-element.201), channel_id=1, source_target_pairs={{0,8},{1,9},{2,10},{3,11},{4,12},{5,13},{6,14},{7,15},{8,0},{9,1},... | collective-permute-start | bytes 1769480 | tf_op jit(solution)/shard_map/ppermute | solution.py:83
  227.3 29.2 %collective-permute-start.17 = (bf16[4,48,1536]{2,1,0:T(8,128)(2,1)}, bf16[4,48,1536]{2,1,0:T(8,128)(2,1)S(1)}, u32[]{:S(2)}, u32[]{:S(2)}) collective-permute-start(bf16[4,48,1536]{2,1,0:T(8,128)(2,1)} %get-tuple-element.202), channel_id=1, source_target_pairs={{0,16},{1,17},{2,18},{3,19},{4,20},{5,21},{6,22},{7,23},{8,24},{9,... | collective-permute-start | bytes 1769480 | tf_op jit(solution)/shard_map/ppermute | solution.py:83
  229.1 27.3 %copy-start.15 = (f32[1,1152]{1,0:T(1,128)S(1)}, f32[1,1152]{1,0:T(1,128)}, u32[]{:S(2)}) copy-start(f32[1,1152]{1,0:T(1,128)} %get-tuple-element.216) | copy-start | bytes 13828
  229.1 28.3 %copy-start.18 = (f32[1,768]{1,0:T(1,128)S(1)}, f32[1,768]{1,0:T(1,128)}, u32[]{:S(2)}) copy-start(f32[1,768]{1,0:T(1,128)} %get-tuple-element.218) | copy-start | bytes 9220
  229.1 28.3 %copy-start.20 = (f32[1,768]{1,0:T(1,128)S(1)}, f32[1,768]{1,0:T(1,128)}, u32[]{:S(2)}) copy-start(f32[1,768]{1,0:T(1,128)} %get-tuple-element.211) | copy-start | bytes 9220
  229.2 28.3 %copy-start.21 = (f32[1,768]{1,0:T(1,128)S(1)}, f32[1,768]{1,0:T(1,128)}, u32[]{:S(2)}) copy-start(f32[1,768]{1,0:T(1,128)} %get-tuple-element.213) | copy-start | bytes 9220
  229.2 29.5 %copy-start.19 = (f32[1,768]{1,0:T(1,128)S(1)}, f32[1,768]{1,0:T(1,128)}, u32[]{:S(2)}) copy-start(f32[1,768]{1,0:T(1,128)} %get-tuple-element.215) | copy-start | bytes 9220
  229.2 29.7 %copy-start.17 = (f32[1,768]{1,0:T(1,128)S(1)}, f32[1,768]{1,0:T(1,128)}, u32[]{:S(2)}) copy-start(f32[1,768]{1,0:T(1,128)} %get-tuple-element.219) | copy-start | bytes 9220
  229.2 29.7 %copy-start.16 = (f32[1,768]{1,0:T(1,128)S(1)}, f32[1,768]{1,0:T(1,128)}, u32[]{:S(2)}) copy-start(f32[1,768]{1,0:T(1,128)} %get-tuple-element.220) | copy-start | bytes 9220
  256.5 2.7 copy-start.7
  256.5 2.7 copy-start.8
  259.2 7.0 %copy-start.4 = (bf16[16,24,1920]{2,1,0:T(8,128)(2,1)S(1)}, bf16[16,24,1920]{2,1,0:T(8,128)(2,1)}, u32[]{:S(2)}) copy-start(bf16[16,24,1920]{2,1,0:T(8,128)(2,1)} %get-tuple-element.222) | copy-start | bytes 4423684
  267.4 21.2 %collective-permute-start.20 = (bf16[16,24,1280]{2,1,0:T(8,128)(2,1)}, bf16[16,24,1280]{2,1,0:T(8,128)(2,1)}, u32[]{:S(2)}, u32[]{:S(2)}) collective-permute-start(bf16[16,24,1280]{2,1,0:T(8,128)(2,1)} %dynamic_update_slice.86), channel_id=1, source_target_pairs={{0,1},{1,0},{2,3},{3,2},{4,5},{5,4},{6,7},{7,6},{8,9},{9,8},{10,11... | collective-permute-start | bytes 2949128 | tf_op jit(solution)/shard_map/ppermute | solution.py:83
  267.4 21.2 %collective-permute-start.19 = (bf16[2,48,3072]{2,1,0:T(8,128)(2,1)}, bf16[2,48,3072]{2,1,0:T(8,128)(2,1)}, u32[]{:S(2)}, u32[]{:S(2)}) collective-permute-start(bf16[2,48,3072]{2,1,0:T(8,128)(2,1)} %get-tuple-element.225), channel_id=1, source_target_pairs={{0,2},{1,3},{2,0},{3,1},{4,6},{5,7},{6,4},{7,5},{8,10},{9,11},{10,... | collective-permute-start | bytes 1769480 | tf_op jit(solution)/shard_map/ppermute | solution.py:83
  268.7 17.9 %copy-start.5 = (bf16[16,24,1280]{2,1,0:T(8,128)(2,1)S(1)}, bf16[16,24,1280]{2,1,0:T(8,128)(2,1)}, u32[]{:S(2)}) copy-start(bf16[16,24,1280]{2,1,0:T(8,128)(2,1)} %get-tuple-element.231) | copy-start | bytes 2949124
  268.7 18.6 %collective-permute-start.21 = (bf16[4,24,1920]{2,1,0:T(8,128)(2,1)}, bf16[4,24,1920]{2,1,0:T(8,128)(2,1)}, u32[]{:S(2)}, u32[]{:S(2)}) collective-permute-start(bf16[4,24,1920]{2,1,0:T(8,128)(2,1)} %get-tuple-element.227), channel_id=1, source_target_pairs={{0,8},{1,9},{2,10},{3,11},{4,12},{5,13},{6,14},{7,15},{8,0},{9,1},... | collective-permute-start | bytes 1105928 | tf_op jit(solution)/shard_map/ppermute | solution.py:83
  269.9 17.4 %collective-permute-start.22 = (bf16[4,24,1920]{2,1,0:T(8,128)(2,1)}, bf16[4,24,1920]{2,1,0:T(8,128)(2,1)}, u32[]{:S(2)}, u32[]{:S(2)}) collective-permute-start(bf16[4,24,1920]{2,1,0:T(8,128)(2,1)} %get-tuple-element.228), channel_id=1, source_target_pairs={{0,16},{1,17},{2,18},{3,19},{4,20},{5,21},{6,22},{7,23},{8,24},{9,... | collective-permute-start | bytes 1105928 | tf_op jit(solution)/shard_map/ppermute | solution.py:83
  271.0 17.6 %collective-permute-start.23 = (bf16[4,24,1920]{2,1,0:T(8,128)(2,1)}, bf16[4,24,1920]{2,1,0:T(8,128)(2,1)}, u32[]{:S(2)}, u32[]{:S(2)}) collective-permute-start(bf16[4,24,1920]{2,1,0:T(8,128)(2,1)} %get-tuple-element.229), channel_id=1, source_target_pairs={{0,24},{1,25},{2,26},{3,27},{4,28},{5,29},{6,30},{7,31},{8,16},{9,... | collective-permute-start | bytes 1105928 | tf_op jit(solution)/shard_map/ppermute | solution.py:83
  286.6 4.2 %copy-start.9 = (bf16[2,48,3072]{2,1,0:T(8,128)(2,1)S(1)}, bf16[2,48,3072]{2,1,0:T(8,128)(2,1)}, u32[]{:S(2)}) copy-start(bf16[2,48,3072]{2,1,0:T(8,128)(2,1)} %get-tuple-element.206) | copy-start | bytes 1769476
  291.8 24.6 %collective-permute-start.24 = (bf16[1,48,3072]{2,1,0:T(8,128)(2,1)S(1)}, bf16[1,48,3072]{2,1,0:T(8,128)(2,1)S(1)}, u32[]{:S(2)}, u32[]{:S(2)}) collective-permute-start(bf16[1,48,3072]{2,1,0:T(8,128)(2,1)S(1)} %add_convert_fusion.3), channel_id=1, source_target_pairs={{0,4},{1,5},{2,6},{3,7},{4,0},{5,1},{6,2},{7,3},{8,12},{9,13},{10,... | collective-permute-start | bytes 884744 | tf_op jit(solution)/shard_map/ppermute | solution.py:83
  294.5 21.8 %collective-permute-start.25 = (bf16[4,24,1280]{2,1,0:T(8,128)(2,1)}, bf16[4,24,1280]{2,1,0:T(8,128)(2,1)S(1)}, u32[]{:S(2)}, u32[]{:S(2)}) collective-permute-start(bf16[4,24,1280]{2,1,0:T(8,128)(2,1)} %get-tuple-element.235), channel_id=1, source_target_pairs={{0,8},{1,9},{2,10},{3,11},{4,12},{5,13},{6,14},{7,15},{8,0},{9,1},... | collective-permute-start | bytes 737288 | tf_op jit(solution)/shard_map/ppermute | solution.py:83
  295.8 20.6 %collective-permute-start.26 = (bf16[4,24,1280]{2,1,0:T(8,128)(2,1)}, bf16[4,24,1280]{2,1,0:T(8,128)(2,1)S(1)}, u32[]{:S(2)}, u32[]{:S(2)}) collective-permute-start(bf16[4,24,1280]{2,1,0:T(8,128)(2,1)} %get-tuple-element.236), channel_id=1, source_target_pairs={{0,16},{1,17},{2,18},{3,19},{4,20},{5,21},{6,22},{7,23},{8,24},{9,... | collective-permute-start | bytes 737288 | tf_op jit(solution)/shard_map/ppermute | solution.py:83
  296.8 19.6 %collective-permute-start.27 = (bf16[4,24,1280]{2,1,0:T(8,128)(2,1)}, bf16[4,24,1280]{2,1,0:T(8,128)(2,1)S(1)}, u32[]{:S(2)}, u32[]{:S(2)}) collective-permute-start(bf16[4,24,1280]{2,1,0:T(8,128)(2,1)} %get-tuple-element.237), channel_id=1, source_target_pairs={{0,24},{1,25},{2,26},{3,27},{4,28},{5,29},{6,30},{7,31},{8,16},{9,... | collective-permute-start | bytes 737288 | tf_op jit(solution)/shard_map/ppermute | solution.py:83
  317.5 7.3 %collective-permute-start.31 = (f32[1,24,3072]{2,1,0:T(8,128)S(1)}, f32[1,24,3072]{2,1,0:T(8,128)S(1)}, u32[]{:S(2)}, u32[]{:S(2)}) collective-permute-start(f32[1,24,3072]{2,1,0:T(8,128)S(1)} %constant_dynamic-slice_fusion), channel_id=1, source_target_pairs={{0,1},{1,0},{2,3},{3,2},{4,5},{5,4},{6,7},{7,6},{8,9},{9,8},{10,11... | collective-permute-start | bytes 884744 | tf_op jit(solution)/shard_map/ppermute | solution.py:83
  319.1 11.7 %collective-permute-start.30 = (bf16[24,3200]{1,0:T(8,128)(2,1)}, bf16[24,3200]{1,0:T(8,128)(2,1)}, u32[]{:S(2)}, u32[]{:S(2)}) collective-permute-start(bf16[24,3200]{1,0:T(8,128)(2,1)} %pad_maximum_fusion.3), channel_id=1, source_target_pairs={{0,6},{1,7},{2,4},{3,5},{4,2},{5,3},{6,0},{7,1},{8,14},{9,15},{10,... | collective-permute-start | bytes 460808 | tf_op jit(solution)/shard_map/ppermute | solution.py:83
  320.4 15.0 %collective-permute-start.29 = (bf16[24,3200]{1,0:T(8,128)(2,1)}, bf16[24,3200]{1,0:T(8,128)(2,1)}, u32[]{:S(2)}, u32[]{:S(2)}) collective-permute-start(bf16[24,3200]{1,0:T(8,128)(2,1)} %pad_maximum_fusion.2), channel_id=1, source_target_pairs={{0,4},{1,5},{2,6},{3,7},{4,0},{5,1},{6,2},{7,3},{8,12},{9,13},{10,... | collective-permute-start | bytes 460808 | tf_op jit(solution)/shard_map/ppermute | solution.py:83
  322.2 13.2 %collective-permute-start.28 = (bf16[24,3200]{1,0:T(8,128)(2,1)}, bf16[24,3200]{1,0:T(8,128)(2,1)}, u32[]{:S(2)}, u32[]{:S(2)}) collective-permute-start(bf16[24,3200]{1,0:T(8,128)(2,1)} %pad_maximum_fusion.1), channel_id=1, source_target_pairs={{0,2},{1,3},{2,0},{3,1},{4,6},{5,7},{6,4},{7,5},{8,10},{9,11},{10,... | collective-permute-start | bytes 460808 | tf_op jit(solution)/shard_map/ppermute | solution.py:83
  327.3 8.1 %copy-start.6 = (f32[24,1920]{1,0:T(8,128)S(1)}, f32[24,1920]{1,0:T(8,128)}, u32[]{:S(2)}) copy-start(f32[24,1920]{1,0:T(8,128)} %get-tuple-element.273) | copy-start | bytes 552964
  327.3 8.1 %copy-start.10 = (f32[24,1280]{1,0:T(8,128)S(1)}, f32[24,1280]{1,0:T(8,128)}, u32[]{:S(2)}) copy-start(f32[24,1280]{1,0:T(8,128)} %get-tuple-element.277) | copy-start | bytes 368644
Sparse Core Ops, SparseCore 0:
  11.7 95.2 all-gather.1

commit v7 on v6

--- a/solution.py
+++ b/solution.py
@@ -298,30 +298,29 @@
     *terms, keep, send = refs
     fast = where[2] % 2
     cut = terms[0].shape[-1]
-    for slow in range(2):
-        for place, out in ((slow * 2 + fast, keep), (slow * 2 + (fast ^ 1), send)):
-            for half in range(2):
-                own = terms[4 * half : 4 * half + 4]
-                lanes = slice(half * cut, (half + 1) * cut)
-                out[slow, :, lanes] = sum(term[place].astype(f32) for term in own).astype(out.dtype)
+    for place, out in ((fast, keep), (fast ^ 1, send)):
+        for half in range(2):
+            own = terms[4 * half : 4 * half + 4]
+            lanes = slice(half * cut, (half + 1) * cut)
+            out[:, lanes] = sum(term[place].astype(f32) for term in own).astype(out.dtype)
 
 
 def line_first(where, keep, came, came_a, came_b, last_a, last_b):
     _, _, size, rows, columns = keep.shape
     cut = columns // 2
     whole = lambda half: pl.BlockSpec(
-        (None, None, size, rows, cut), lambda j, where: (where[1] // 2, where[1] % 2, 0, 0, half)
-    )
-    half_a = pl.BlockSpec((None, size, rows, cut), lambda j, where: (where[1] % 2, 0, 0, 0))
-    half_b = pl.BlockSpec((None, size, rows, cut), lambda j, where: (where[1] // 2, 0, 0, 0))
-    last = pl.BlockSpec((size, rows, cut), lambda j, where: (0, 0, 0))
+        (None, None, 2, rows, cut), lambda j, where: (where[1] // 2, where[1] % 2, j, 0, half)
+    )
+    half_a = pl.BlockSpec((None, 2, rows, cut), lambda j, where: (where[1] % 2, j, 0, 0))
+    half_b = pl.BlockSpec((None, 2, rows, cut), lambda j, where: (where[1] // 2, j, 0, 0))
+    last = pl.BlockSpec((2, rows, cut), lambda j, where: (j, 0, 0))
     return pl.pallas_call(
         line_first_kernel,
         grid_spec=pltpu.PrefetchScalarGridSpec(
             num_scalar_prefetch=1,
-            grid=(1,),
+            grid=(size // 2,),
             in_specs=[whole(0), whole(0), half_a, last, whole(1), whole(1), half_b, last],
-            out_specs=[once((size // 2, rows, columns))] * 2,
+            out_specs=[pl.BlockSpec((None, rows, columns), lambda j, where: (j, 0, 0))] * 2,
         ),
         out_shape=[shape_of((size // 2, rows, columns), bf16)] * 2,
         compiler_params=params(1),
@@ -356,13 +355,26 @@
     return [pick(term, 0, spot)[0] for term in terms] + came
 
 
-def line_steps(groups, mesh):
+def line_steps(terms, mesh):
     count = mesh.size
     _, _, rest = bit_groups(mesh)
     spot = position(lax.axis_index(AXES), rest[0])
-    side = lambda index, kind: jnp.concatenate([part_of(terms, 0, index, kind)[0] for terms in groups], -1)
-    came = yield [(side(spot ^ step, bf16), pairs) for step, pairs in partners(count, rest[0])]
-    return side(spot, f32) + sum(array.astype(f32) for array in came)
+    came = yield [
+        (part_of(terms, 0, spot ^ step, bf16)[0], pairs) for step, pairs in partners(count, rest[0])
+    ]
+    return part_of(terms, 0, spot, f32)[0] + sum(array.astype(f32) for array in came)
+
+
+def line_fold_steps(terms, mesh):
+    count = mesh.size
+    _, _, rest = bit_groups(mesh)
+    me = lax.axis_index(AXES)
+    terms = [term.reshape((2, 2) + term.shape[1:]) for term in terms]
+    for axis, bit in ((1, rest[0][0]), (0, rest[0][1])):
+        spot = position(me, [bit])
+        came = yield [(part_of(terms, axis, spot ^ 1, bf16), partners(count, [bit])[0][1])]
+        terms = [pick(term, axis, spot) for term in terms] + came
+    return sum(term.astype(f32) for term in terms)[0, 0]
 
 
 def fold_sum_steps(keep, send, where, mesh):
@@ -1072,11 +1084,12 @@
     )
     if cut:
         plane_b = flights.add(plane_steps(grads_b[0], swap_b["result"], mesh), [])
+        line_a = flights.add(line_fold_steps(plane_a["result"], mesh), [])
     block_out = flights.run(
         lambda x: block_out_of(x, valid, active, both, bias_down, seq, 0, rows), middle
     )
     if cut:
-        line = flights.add(line_steps([plane_a["result"], plane_b["result"]], mesh), [])
+        line_b = flights.add(line_steps(plane_b["result"], mesh), [])
         flights.land(mlp_job)
         up_total, down_total = mlp_job["result"]
     else:
@@ -1087,8 +1100,7 @@
     down_total = down_total.reshape(share, chunks, width).transpose(1, 0, 2).reshape(-1)
     up_total, down_total = flights.finish_after((up_total, down_total))
     if cut:
-        edge_a = grads_a[0].shape[-1]
-        total_a, total_b = line["result"][:, :edge_a], line["result"][:, edge_a:]
+        total_a, total_b = line_a["result"], line_b["result"]
         small_total = total_b[:small_rows, span:].reshape(-1)
         small_total = small_total[: edge + biases.shape[0]]
     else:

time: 352 us -> 351 us (level)
    convert_element_type x0 -> x2, other arithmetic: none -> 3.66 us  [part_of(): return total.astype(kind)]
    ppermute x32 -> x34, waiting for transfers between devices: 23.2 us -> 20.2 us  [depart(): came = [lax.ppermute(array, AXES, pairs) for array, pairs in sends]]
    ppermute x32 -> x34, starting transfers between devices: 34.9 us -> 35.5 us  [depart(): came = [lax.ppermute(array, AXES, pairs) for array, pairs in sends]]
  transfers between devices with their start and end apart: 33 -> 35, of which waited for: 7 -> 7; matrix products, arithmetic and copies ran while one was open for 9% -> 9% of each run, Pallas kernels for 44% -> 45%
where the time goes in v7:
time: 351 us; the launch traced here: 346 us
  Pallas kernels  219 us (62%)
  local copies, waits for them, and re-layouts  37.8 us (11%)
  starting transfers between devices  35.5 us (10%)
  waiting for transfers between devices  20.2 us (6%)
  other arithmetic  17.8 us (5%)
  between operations  15.6 us (4%)
    pallas_call x2, Pallas kernels, attend_back(): pl.pallas_call(functools.partial(attend_back_kernel, pairs=pairs, extra=b...  59.3 us
    pallas_call x1, Pallas kernels, mlp(): pl.pallas_call(functools.partial(mlp_kernel, seq=seq, tile=tile_of(seq),...  52.5 us
    pallas_call x2, Pallas kernels, attend(): pl.pallas_call(functools.partial(attend_kernel, tile=tile_of(seq), padded...  44.7 us
    ppermute x34, starting transfers between devices, depart(): came = [lax.ppermute(array, AXES, pairs) for array, pairs in sends]  35.5 us
    pallas_call x1, Pallas kernels, middle_back(): pl.pallas_call(functools.partial(middle_back_kernel, seq=seq, sub=sub), g...  20.7 us
    ppermute x34, waiting for transfers between devices, depart(): came = [lax.ppermute(array, AXES, pairs) for array, pairs in sends]  20.2 us
    pallas_call x1, Pallas kernels, block_out_of(): pl.pallas_call(functools.partial(block_out_kernel, seq=seq, begin=begin),...  15.3 us
    pallas_call x1, Pallas kernels, input_back(): pl.pallas_call(functools.partial(input_back_kernel, spans=spans, sub=sub)...  14.4 us
  transfers between devices with their start and end apart: 35, of which 7 were waited for; matrix products, arithmetic and copies ran while one was open for 9% of the time, Pallas kernels for 45%

profile of v7, /device:TPU:0, one launch (start us, length us, event | category | flops | bytes accessed | tf_op | source)
XLA Modules:
  0.0 345.9 jit_solution(11123387535813935214)
XLA Ops:
  7.2 2.0 reshape.186
  9.4 1.3 reshape.187
  12.0 3.1 collective-permute-start
  15.1 2.6 collective-permute-start.1
  17.8 2.0 collective-permute-start.3
  20.0 4.9 %collective-permute-done.1 = bf16[1,1,1,1,1,24,1280]{6,5,4,3,2,1,0:T(8,128)(2,1)S(1)} collective-permute-done((bf16[1,1,1,1,1,24,1280]{6,5,4,3,2,1,0:T(8,128)(2,1)S(1)}, bf16[1,1,1,1,1,24,1280]{6,5,4,3,2,1,0:T(8,128)(2,1)S(1)}, u32[]{:S(2)}, u32[]{:S(2)}) %collective-permute-start.1) | collective-permute-done | bytes 61472 | tf_op jit(solution)/shard_map/ppermute | solution.py:83
  24.8 4.0 %collective-permute-done.3 = bf16[1,1,1,1,1,24,1920]{6,5,4,3,2,1,0:T(8,128)(2,1)S(1)} collective-permute-done((bf16[1,1,1,1,1,24,1920]{6,5,4,3,2,1,0:T(8,128)(2,1)S(1)}, bf16[1,1,1,1,1,24,1920]{6,5,4,3,2,1,0:T(8,128)(2,1)S(1)}, u32[]{:S(2)}, u32[]{:S(2)}) %collective-permute-start.3) | collective-permute-done | bytes 92192 | tf_op jit(solution)/shard_map/ppermute | solution.py:83
  28.9 1.6 collective-permute-start.4
  30.5 1.6 collective-permute-start.5
  33.0 5.8 %collective-permute-done.7 = bf16[1,1,2,1,1,24,1920]{6,5,4,3,2,1,0:T(8,128)(2,1)S(1)} collective-permute-done((bf16[1,1,2,1,1,24,1920]{6,5,4,3,2,1,0:T(8,128)(2,1)S(1)}, bf16[1,1,2,1,1,24,1920]{6,5,4,3,2,1,0:T(8,128)(2,1)S(1)}, u32[]{:S(2)}, u32[]{:S(2)}) %collective-permute-start.7) | collective-permute-done | bytes 184352 | tf_op jit(solution)/shard_map/ppermute | solution.py:83
  38.8 2.3 collective-permute-done.5
  42.0 1.6 collective-permute-start.10
  43.6 1.2 collective-permute-start.11
  45.5 1.3 broadcast_in_dim.31
  47.8 1.3 constant_dynamic-update-slice_fusion.8
  49.4 0.9 fusion.21
  51.6 19.8 %attend.2 = (bf16[1824,768]{1,0:T(8,128)(2,1)}, bf16[1824,1152]{1,0:T(8,128)(2,1)}, bf16[1824,384]{1,0:T(8,128)(2,1)}, bf16[3,3,608,1280]{3,2,1,0:T(8,128)(2,1)}, f32[1824,384]{1,0:T(8,128)}) custom-call(s32[3]{0:T(128)} %get-tuple-element.298.valid, bf16[1824,768]{1,0:T(8,128)(2,1)} %bitcast.129, f32[1,768]{1,0:T(1,128)} %get-tuple-element.296.refs_1_.refs_6_, ...), custom_call_target="tpu_custom_call" | custom-call | flops 1 | bytes 1 | tf_op jit(solution)/shard_map/attend/pallas_call | solution.py:587
  71.4 1.8 constant_dynamic-update-slice_fusion.4
  73.2 1.7 constant_dynamic-update-slice_fusion.3
  74.9 1.8 constant_dynamic-update-slice_fusion.2
  78.4 1.6 constant_dynamic-update-slice_fusion.1
  80.3 1.6 constant_dynamic-update-slice_fusion
  81.9 1.6 copy-done
  83.5 24.9 %attend.3 = (bf16[1824,1152]{1,0:T(8,128)(2,1)}, bf16[1824,384]{1,0:T(8,128)(2,1)}, bf16[3,3,608,1280]{3,2,1,0:T(8,128)(2,1)}, f32[1824,384]{1,0:T(8,128)}, f32[...) custom-call(s32[3]{0:T(128)} %get-tuple-element.298.valid, bf16[1824,768]{1,0:T(8,128)(2,1)} %get-tuple-element.152.refs_0_.refs_15_, ...), custom_call_target="tpu_custom_call" | custom-call | flops 1 | bytes 1 | tf_op jit(solution)/shard_map/attend/pallas_call | solution.py:587
  108.4 52.5 %mlp.1 = (bf16[1824,3072]{1,0:T(8,128)(2,1)}, bf16[1824,3072]{1,0:T(8,128)(2,1)}, f32[1,3072]{1,0:T(1,128)}, bf16[768,3072]{1,0:T(8,128)(2,1)}, bf16[768,3072]{1,0:T(8,128)(2,1)}) custom-call(s32[3]{0:T(128)} %get-tuple-element.298.valid, s32[3]{0:T(128)} %get-tuple-element.297.where, bf16[1824,768]{1,0:T(8,128)(2,1)} %get-tuple-element.157.normed, ...), custom_call_target="tpu_custom_call" | custom-call | flops 1 | bytes 1 | tf_op jit(solution)/shard_map/mlp/pallas_call | solution.py:779
  161.0 20.7 %middle_back.1 = (bf16[1824,768]{1,0:T(8,128)(2,1)}, bf16[1824,768]{1,0:T(8,128)(2,1)}, f32[1,768]{1,0:T(1,128)}, f32[1,768]{1,0:T(1,128)}, f32[1,768]{1,0:T(1,128)}, /*index=5*/f32[1,768]{1,0:T(1,128)}) custom-call(s32[3]{0:T(128)} %get-tuple-element.298.valid, bf16[1824,3072]{1,0:T(8,128)(2,1)} %get-tuple-element.161.hidden_grad, ...), custom_call_target="tpu_custom_call" | custom-call | flops 1 | bytes 1 | tf_op jit(solution)/shard_map/middle_back/pallas_call | solution.py:887
  181.7 4.4 %fold_first.1 = (bf16[2,4,48,1536]{3,2,1,0:T(8,128)(2,1)}, bf16[2,4,48,1536]{3,2,1,0:T(8,128)(2,1)}) custom-call(s32[3]{0:T(128)} %get-tuple-element.297.where, bf16[2,2,4,48,3072]{4,3,2,1,0:T(8,128)(2,1)} %bitcast.114, bf16[2,2,4,48,3072]{4,3,2,1,0:T(8,128)(2,1)} %bitcast.23.refs_1_.refs_3_.refs_4_.refs_5_, bf16[2,2,4,48,3072]{4,3,2,1,0:T(8,128)(2,1)} %bitcast.115, ...), custom_call_target="tpu_custom_call" | custom-call | flops 1 | bytes 1 | tf_op jit(solution)/shard_map/fold_first/pallas_call | solution.py:256
  186.0 1.7 collective-permute-start.14
  187.7 1.0 collective-permute-start.15
  188.8 32.1 %attend_back.2 = (bf16[1824,1152]{1,0:T(8,128)(2,1)}, f32[1,1152]{1,0:T(1,128)}, f32[1,768]{1,0:T(1,128)}, f32[1,768]{1,0:T(1,128)}, bf16[16,24,1920]{2,1,0:T(8,128)(2,1)}, /*index=5*/bf16[16,24,1920]{2,1,0:T(8,128)(2,1)}) custom-call(s32[3]{0:T(128)} %get-tuple-element.297.where, bf16[1824,1152]{1,0:T(8,128)(2,1)} %get-tuple-element.172.refs_0_.refs_1_.refs_2_, ...), custom_call_target="tpu_custom_call" | custom-call | flops 1 | bytes 1 | tf_op jit(solution)/shard_map/attend_back/pallas_call | solution.py:688
  220.9 1.0 copy-done.2
  222.3 3.6 %fold_second.1 = (bf16[4,48,1536]{2,1,0:T(8,128)(2,1)}, bf16[4,48,1536]{2,1,0:T(8,128)(2,1)}) custom-call(s32[3]{0:T(128)} %get-tuple-element.297.where, bf16[2,2,4,48,3072]{4,3,2,1,0:T(8,128)(2,1)} %bitcast.116, bf16[2,2,4,48,3072]{4,3,2,1,0:T(8,128)(2,1)} %bitcast.23.refs_1_.refs_3_.refs_4_.refs_5_, bf16[2,4,48,1536]{3,2,1,0:T(8,128)(2,1)} %copy-done.2, ...), custom_call_target="tpu_custom_call" | custom-call | flops 1 | bytes 1 | tf_op jit(solution)/shard_map/fold_second/pallas_call | solution.py:282
  225.9 1.1 collective-permute-start.16
  227.9 1.4 reduce.14
  229.7 27.2 %attend_back.3 = (bf16[1824,1152]{1,0:T(8,128)(2,1)}, f32[1,1152]{1,0:T(1,128)}, f32[1,768]{1,0:T(1,128)}, f32[1,768]{1,0:T(1,128)}, bf16[16,24,1280]{2,1,0:T(8,128)(2,1)}, /*index=5*/bf16[16,24,1280]{2,1,0:T(8,128)(2,1)}) custom-call(s32[3]{0:T(128)} %get-tuple-element.297.where, bf16[1824,1152]{1,0:T(8,128)(2,1)} %get-tuple-element.190.refs_0_.refs_1_.refs_2_, ...), custom_call_target="tpu_custom_call" | custom-call | flops 1 | bytes 1 | tf_op jit(solution)/shard_map/attend_back/pallas_call | solution.py:688
  257.9 1.3 fusion.20
  260.3 4.2 %line_first.1 = (bf16[2,48,3072]{2,1,0:T(8,128)(2,1)}, bf16[2,48,3072]{2,1,0:T(8,128)(2,1)}) custom-call(s32[3]{0:T(128)} %get-tuple-element.297.where, bf16[2,2,4,48,3072]{4,3,2,1,0:T(8,128)(2,1)} %bitcast.118, bf16[2,2,4,48,3072]{4,3,2,1,0:T(8,128)(2,1)} %bitcast.23.refs_1_.refs_3_.refs_4_.refs_5_, bf16[2,4,48,1536]{3,2,1,0:T(8,128)(2,1)} %copy-done.2, ...), custom_call_target="tpu_custom_call" | custom-call | flops 1 | bytes 1 | tf_op jit(solution)/shard_map/line_first/pallas_call | solution.py:317
  264.6 2.3 dynamic_update_slice.86
  266.9 1.1 fusion.2
  268.1 1.3 collective-permute-start.19
  269.3 1.1 collective-permute-start.21
  270.4 1.1 collective-permute-start.22
  271.6 1.2 collective-permute-start.23
  272.8 14.4 %input_back.1 = bf16[1824,768]{1,0:T(8,128)(2,1)} custom-call(bf16[1824,1152]{1,0:T(8,128)(2,1)} %get-tuple-element.210.refs_0_, bf16[1824,1152]{1,0:T(8,128)(2,1)} %get-tuple-element.227.refs_1_, bf16[768,1280]{1,0:T(8,128)(2,1)} %bitcast.128, bf16[768,1920]{1,0:T(8,128)(2,1)} %bitcast.124, bf16[1824,768]{1,0:T(8,128)(2,1)} %bitcast.131, ...), custom_call_target="tpu_custom_call" | custom-call | flops 1 | bytes 1 | tf_op jit(solution)/shard_map/input_back/pallas_call | solution.py:936
  287.9 1.2 collective-permute-done.23
  289.2 1.4 fusion.5
  290.5 1.1 add_convert_fusion.3
  291.7 1.9 add_convert_fusion.7
  293.6 2.7 collective-permute-start.24
  296.3 1.2 collective-permute-start.25
  297.5 1.0 collective-permute-start.26
  298.5 1.3 collective-permute-start.27
  300.2 15.3 %block_out.1 = bf16[1824,768]{1,0:T(8,128)(2,1)} custom-call(s32[3]{0:T(128)} %get-tuple-element.298.valid, bf16[1824,3072]{1,0:T(8,128)(2,1)} %get-tuple-element.158.active, bf16[768,6144]{1,0:T(8,128)(2,1)} %all-gather.2.cloned.1.call-done.up.down.ups.downs, f32[1824,768]{1,0:T(8,128)} %get-tuple-element.244.middle, f32[1,768]{1,0:T(1,128)} %get-tuple-element.285.bias_down), custom_call_target="tpu_custom_call" | custom-call | flops 1 | bytes 1 | tf_op jit(solution)/shard_map/block_out/pallas_call | solution.py:830
  315.5 1.0 dynamic-slice_bitcast_fusion.2
  316.5 1.3 convert_add_fusion
  318.7 1.7 collective-permute-start.30
  320.7 2.4 collective-permute-start.32
  323.1 1.7 add_convert_fusion.8
  325.9 1.1 reshape.212
  327.0 1.2 copy.45
  328.3 2.5 reshape.213
  331.8 1.6 collective-permute-done.29
  333.4 1.2 add_bitcast_fusion
  334.6 1.1 bitcast_add_fusion
  (207 shorter events, 19.5 us)
Async XLA Ops:
  7.2 3.5 %copy-start.16 = (bf16[73728]{0:T(1024)(128)(2,1)S(1)}, bf16[73728]{0:T(1024)(128)(2,1)}, u32[]{:S(2)}) copy-start(bf16[73728]{0:T(1024)(128)(2,1)} %param.17) | copy-start | bytes 442372
  7.2 101.2 %all-gather.2.cloned.1.call-start = ((), (), s32[]{:S(2)}) async-start(), calls=%async_computation | async-start | bytes 9732096 | tf_op jit(solution)/shard_map/all_gather | solution.py:995
  9.2 2.4 copy-start.18
  9.4 2.5 copy-start.29
  9.4 2.5 copy-start.30
  9.4 8.3 %copy-start.19 = (bf16[18432]{0:T(1024)(128)(2,1)S(1)}, bf16[18432]{0:T(1024)(128)(2,1)}, u32[]{:S(2)}) copy-start(bf16[18432]{0:T(1024)(128)(2,1)} %param.15) | copy-start | bytes 110596
  12.0 8.0 %collective-permute-start = (bf16[1,1,1,1,1,24,1280]{6,5,4,3,2,1,0:T(8,128)(2,1)S(1)}, bf16[1,1,1,1,1,24,1280]{6,5,4,3,2,1,0:T(8,128)(2,1)S(1)}, u32[]{:S(2)}, u32[]{:S(2)}) collective-permute-start(bf16[1,1,1,1,1,24,1280]{6,5,4,3,2,1,0:T(8,128)(2,1)S(1)} %fusion.8), channel_id=1, source_target_pairs={{0,2},{1,3},{2,0},{3,1},{4,6},{5,7},{6,4},{7,5},{8,10},{9,11},{10,... | collective-permute-start | bytes 184328 | tf_op jit(solution)/shard_map/ppermute | solution.py:83
  15.1 9.8 %collective-permute-start.1 = (bf16[1,1,1,1,1,24,1280]{6,5,4,3,2,1,0:T(8,128)(2,1)S(1)}, bf16[1,1,1,1,1,24,1280]{6,5,4,3,2,1,0:T(8,128)(2,1)S(1)}, u32[]{:S(2)}, u32[]{:S(2)}) collective-permute-start(bf16[1,1,1,1,1,24,1280]{6,5,4,3,2,1,0:T(8,128)(2,1)S(1)} %fusion.8), channel_id=1, source_target_pairs={{0,4},{1,5},{2,6},{3,7},{4,0},{5,1},{6,2},{7,3},{8,12},{9,13},{10,... | collective-permute-start | bytes 184328 | tf_op jit(solution)/shard_map/ppermute | solution.py:83
  17.6 7.2 %collective-permute-start.2 = (bf16[1,1,1,1,1,24,1280]{6,5,4,3,2,1,0:T(8,128)(2,1)S(1)}, bf16[1,1,1,1,1,24,1280]{6,5,4,3,2,1,0:T(8,128)(2,1)S(1)}, u32[]{:S(2)}, u32[]{:S(2)}) collective-permute-start(bf16[1,1,1,1,1,24,1280]{6,5,4,3,2,1,0:T(8,128)(2,1)S(1)} %fusion.8), channel_id=1, source_target_pairs={{0,6},{1,7},{2,4},{3,5},{4,2},{5,3},{6,0},{7,1},{8,14},{9,15},{10,... | collective-permute-start | bytes 184328 | tf_op jit(solution)/shard_map/ppermute | solution.py:83
  17.8 11.0 %collective-permute-start.3 = (bf16[1,1,1,1,1,24,1920]{6,5,4,3,2,1,0:T(8,128)(2,1)S(1)}, bf16[1,1,1,1,1,24,1920]{6,5,4,3,2,1,0:T(8,128)(2,1)S(1)}, u32[]{:S(2)}, u32[]{:S(2)}) collective-permute-start(bf16[1,1,1,1,1,24,1920]{6,5,4,3,2,1,0:T(8,128)(2,1)S(1)} %maximum_bitcast_fusion.1), channel_id=1, source_target_pairs={{0,4},{1,5},{2,6},{3,7},{4,0},{5,1},{6,2},{7,3},{8,12},{9,13},{10,... | collective-permute-start | bytes 276488 | tf_op jit(solution)/shard_map/ppermute | solution.py:83
  19.8 21.4 %copy-start.27 = (s32[3]{0:T(128)S(1)}, s32[3]{0:T(128)}, u32[]{:S(2)}) copy-start(s32[3]{0:T(128)} %param.13) | copy-start | bytes 40
  19.9 21.4 %copy-start.28 = (s32[3]{0:T(128)S(1)}, s32[3]{0:T(128)}, u32[]{:S(2)}) copy-start(s32[3]{0:T(128)} %param.12) | copy-start | bytes 40
  28.9 9.9 %collective-permute-start.4 = (bf16[1,1,2,2,1,24,1280]{6,5,4,3,2,1,0:T(8,128)(2,1)S(1)}, bf16[1,1,2,2,1,24,1280]{6,5,4,3,2,1,0:T(8,128)(2,1)S(1)}, u32[]{:S(2)}, u32[]{:S(2)}) collective-permute-start(bf16[1,1,2,2,1,24,1280]{6,5,4,3,2,1,0:T(8,128)(2,1)S(1)} %constant_dynamic-update-slice_fusion.16), channel_id=1, source_target_pairs={{0,8},{1,9},{2,10},{3,11},{4,12},{5,13},{6,14},{7,15},{8,0},{9,1},... | collective-permute-start | bytes 737288 | tf_op jit(solution)/shard_map/ppermute | solution.py:83
  30.5 10.5 %collective-permute-start.5 = (bf16[1,1,2,2,1,24,1280]{6,5,4,3,2,1,0:T(8,128)(2,1)S(1)}, bf16[1,1,2,2,1,24,1280]{6,5,4,3,2,1,0:T(8,128)(2,1)S(1)}, u32[]{:S(2)}, u32[]{:S(2)}) collective-permute-start(bf16[1,1,2,2,1,24,1280]{6,5,4,3,2,1,0:T(8,128)(2,1)S(1)} %constant_dynamic-update-slice_fusion.16), channel_id=1, source_target_pairs={{0,16},{1,17},{2,18},{3,19},{4,20},{5,21},{6,22},{7,23},{8,24},{9,... | collective-permute-start | bytes 737288 | tf_op jit(solution)/shard_map/ppermute | solution.py:83
  32.1 9.0 %collective-permute-start.6 = (bf16[1,1,2,2,1,24,1280]{6,5,4,3,2,1,0:T(8,128)(2,1)S(1)}, bf16[1,1,2,2,1,24,1280]{6,5,4,3,2,1,0:T(8,128)(2,1)S(1)}, u32[]{:S(2)}, u32[]{:S(2)}) collective-permute-start(bf16[1,1,2,2,1,24,1280]{6,5,4,3,2,1,0:T(8,128)(2,1)S(1)} %constant_dynamic-update-slice_fusion.16), channel_id=1, source_target_pairs={{0,24},{1,25},{2,26},{3,27},{4,28},{5,29},{6,30},{7,31},{8,16},{9,... | collective-permute-start | bytes 737288 | tf_op jit(solution)/shard_map/ppermute | solution.py:83
  32.5 6.3 %collective-permute-start.7 = (bf16[1,1,2,1,1,24,1920]{6,5,4,3,2,1,0:T(8,128)(2,1)S(1)}, bf16[1,1,2,1,1,24,1920]{6,5,4,3,2,1,0:T(8,128)(2,1)S(1)}, u32[]{:S(2)}, u32[]{:S(2)}) collective-permute-start(bf16[1,1,2,1,1,24,1920]{6,5,4,3,2,1,0:T(8,128)(2,1)S(1)} %constant_dynamic-update-slice_fusion.13), channel_id=1, source_target_pairs={{0,2},{1,3},{2,0},{3,1},{4,6},{5,7},{6,4},{7,5},{8,10},{9,11},{10,... | collective-permute-start | bytes 552968 | tf_op jit(solution)/shard_map/ppermute | solution.py:83
  41.2 6.7 %collective-permute-start.8 = (bf16[2,2,2,2,1,24,1280]{6,5,4,3,2,1,0:T(8,128)(2,1)S(1)}, bf16[2,2,2,2,1,24,1280]{6,5,4,3,2,1,0:T(8,128)(2,1)}, u32[]{:S(2)}, u32[]{:S(2)}) collective-permute-start(bf16[2,2,2,2,1,24,1280]{6,5,4,3,2,1,0:T(8,128)(2,1)S(1)} %constant_dynamic-update-slice_fusion.10), channel_id=1, source_target_pairs={{0,1},{1,0},{2,3},{3,2},{4,5},{5,4},{6,7},{7,6},{8,9},{9,8},{10,11... | collective-permute-start | bytes 2949128 | tf_op jit(solution)/shard_map/ppermute | solution.py:83
  42.0 29.4 %collective-permute-start.10 = (bf16[1,1,2,2,1,24,1920]{6,5,4,3,2,1,0:T(8,128)(2,1)S(1)}, bf16[1,1,2,2,1,24,1920]{6,5,4,3,2,1,0:T(8,128)(2,1)}, u32[]{:S(2)}, u32[]{:S(2)}) collective-permute-start(bf16[1,1,2,2,1,24,1920]{6,5,4,3,2,1,0:T(8,128)(2,1)S(1)} %constant_dynamic-update-slice_fusion.6), channel_id=1, source_target_pairs={{0,16},{1,17},{2,18},{3,19},{4,20},{5,21},{6,22},{7,23},{8,24},{9,... | collective-permute-start | bytes 1105928 | tf_op jit(solution)/shard_map/ppermute | solution.py:83
  43.6 27.8 %collective-permute-start.11 = (bf16[1,1,2,2,1,24,1920]{6,5,4,3,2,1,0:T(8,128)(2,1)S(1)}, bf16[1,1,2,2,1,24,1920]{6,5,4,3,2,1,0:T(8,128)(2,1)}, u32[]{:S(2)}, u32[]{:S(2)}) collective-permute-start(bf16[1,1,2,2,1,24,1920]{6,5,4,3,2,1,0:T(8,128)(2,1)S(1)} %constant_dynamic-update-slice_fusion.6), channel_id=1, source_target_pairs={{0,24},{1,25},{2,26},{3,27},{4,28},{5,29},{6,30},{7,31},{8,16},{9,... | collective-permute-start | bytes 1105928 | tf_op jit(solution)/shard_map/ppermute | solution.py:83
  44.7 26.7 %collective-permute-start.9 = (bf16[1,1,2,2,1,24,1920]{6,5,4,3,2,1,0:T(8,128)(2,1)S(1)}, bf16[1,1,2,2,1,24,1920]{6,5,4,3,2,1,0:T(8,128)(2,1)}, u32[]{:S(2)}, u32[]{:S(2)}) collective-permute-start(bf16[1,1,2,2,1,24,1920]{6,5,4,3,2,1,0:T(8,128)(2,1)S(1)} %constant_dynamic-update-slice_fusion.6), channel_id=1, source_target_pairs={{0,8},{1,9},{2,10},{3,11},{4,12},{5,13},{6,14},{7,15},{8,0},{9,1},... | collective-permute-start | bytes 1105928 | tf_op jit(solution)/shard_map/ppermute | solution.py:83
  49.1 2.5 copy-start.1
  49.4 27.9 %copy-start.17 = (f32[1,7680]{1,0:T(1,128)}, f32[1,7680]{1,0:T(1,128)S(1)}, u32[]{:S(2)}) copy-start(f32[1,7680]{1,0:T(1,128)S(1)} %reshape.180) | copy-start | bytes 92164
  76.7 3.6 %collective-permute-start.12 = (bf16[2,2,2,2,1,24,1920]{6,5,4,3,2,1,0:T(8,128)(2,1)}, bf16[2,2,2,2,1,24,1920]{6,5,4,3,2,1,0:T(8,128)(2,1)}, u32[]{:S(2)}, u32[]{:S(2)}) collective-permute-start(bf16[2,2,2,2,1,24,1920]{6,5,4,3,2,1,0:T(8,128)(2,1)} %constant_dynamic-update-slice_fusion.2), channel_id=1, source_target_pairs={{0,1},{1,0},{2,3},{3,2},{4,5},{5,4},{6,7},{7,6},{8,9},{9,8},{10,11... | collective-permute-start | bytes 4423688 | tf_op jit(solution)/shard_map/ppermute | solution.py:83
  81.9 1.6 copy-start
  160.9 20.8 %collective-permute-start.13 = (bf16[768,3072]{1,0:T(8,128)(2,1)}, bf16[768,3072]{1,0:T(8,128)(2,1)}, u32[]{:S(2)}, u32[]{:S(2)}) collective-permute-start(bf16[768,3072]{1,0:T(8,128)(2,1)} %get-tuple-element.170), channel_id=1, source_target_pairs={{0,1},{1,0},{2,3},{3,2},{4,5},{5,4},{6,7},{7,6},{8,9},{9,8},{10,11... | collective-permute-start | bytes 14155784 | tf_op jit(solution)/shard_map/ppermute | solution.py:83
  186.0 34.8 %collective-permute-start.14 = (bf16[2,4,48,1536]{3,2,1,0:T(8,128)(2,1)}, bf16[2,4,48,1536]{3,2,1,0:T(8,128)(2,1)S(1)}, u32[]{:S(2)}, u32[]{:S(2)}) collective-permute-start(bf16[2,4,48,1536]{3,2,1,0:T(8,128)(2,1)} %get-tuple-element.187), channel_id=1, source_target_pairs={{0,16},{1,17},{2,18},{3,19},{4,20},{5,21},{6,22},{7,23},{8,24},{9,... | collective-permute-start | bytes 3538952 | tf_op jit(solution)/shard_map/ppermute | solution.py:83
  187.7 33.1 %collective-permute-start.15 = (bf16[2,4,48,1536]{3,2,1,0:T(8,128)(2,1)}, bf16[2,4,48,1536]{3,2,1,0:T(8,128)(2,1)S(1)}, u32[]{:S(2)}, u32[]{:S(2)}) collective-permute-start(bf16[2,4,48,1536]{3,2,1,0:T(8,128)(2,1)} %get-tuple-element.188), channel_id=1, source_target_pairs={{0,8},{1,9},{2,10},{3,11},{4,12},{5,13},{6,14},{7,15},{8,0},{9,1},... | collective-permute-start | bytes 3538952 | tf_op jit(solution)/shard_map/ppermute | solution.py:83
  225.9 31.1 %collective-permute-start.18 = (bf16[16,24,1920]{2,1,0:T(8,128)(2,1)}, bf16[16,24,1920]{2,1,0:T(8,128)(2,1)S(1)}, u32[]{:S(2)}, u32[]{:S(2)}) collective-permute-start(bf16[16,24,1920]{2,1,0:T(8,128)(2,1)} %get-tuple-element.206), channel_id=1, source_target_pairs={{0,1},{1,0},{2,3},{3,2},{4,5},{5,4},{6,7},{7,6},{8,9},{9,8},{10,11... | collective-permute-start | bytes 4423688 | tf_op jit(solution)/shard_map/ppermute | solution.py:83
  225.9 31.1 %collective-permute-start.16 = (bf16[4,48,1536]{2,1,0:T(8,128)(2,1)}, bf16[4,48,1536]{2,1,0:T(8,128)(2,1)S(1)}, u32[]{:S(2)}, u32[]{:S(2)}) collective-permute-start(bf16[4,48,1536]{2,1,0:T(8,128)(2,1)} %get-tuple-element.204), channel_id=1, source_target_pairs={{0,8},{1,9},{2,10},{3,11},{4,12},{5,13},{6,14},{7,15},{8,0},{9,1},... | collective-permute-start | bytes 1769480 | tf_op jit(solution)/shard_map/ppermute | solution.py:83
  227.0 30.0 %collective-permute-start.17 = (bf16[4,48,1536]{2,1,0:T(8,128)(2,1)}, bf16[4,48,1536]{2,1,0:T(8,128)(2,1)S(1)}, u32[]{:S(2)}, u32[]{:S(2)}) collective-permute-start(bf16[4,48,1536]{2,1,0:T(8,128)(2,1)} %get-tuple-element.205), channel_id=1, source_target_pairs={{0,16},{1,17},{2,18},{3,19},{4,20},{5,21},{6,22},{7,23},{8,24},{9,... | collective-permute-start | bytes 1769480 | tf_op jit(solution)/shard_map/ppermute | solution.py:83
  229.6 27.3 %copy-start.20 = (f32[1,1152]{1,0:T(1,128)S(1)}, f32[1,1152]{1,0:T(1,128)}, u32[]{:S(2)}) copy-start(f32[1,1152]{1,0:T(1,128)} %get-tuple-element.219) | copy-start | bytes 13828
  229.6 28.2 %copy-start.23 = (f32[1,768]{1,0:T(1,128)S(1)}, f32[1,768]{1,0:T(1,128)}, u32[]{:S(2)}) copy-start(f32[1,768]{1,0:T(1,128)} %get-tuple-element.221) | copy-start | bytes 9220
  229.6 28.3 %copy-start.25 = (f32[1,768]{1,0:T(1,128)S(1)}, f32[1,768]{1,0:T(1,128)}, u32[]{:S(2)}) copy-start(f32[1,768]{1,0:T(1,128)} %get-tuple-element.214) | copy-start | bytes 9220
  229.6 28.3 %copy-start.26 = (f32[1,768]{1,0:T(1,128)S(1)}, f32[1,768]{1,0:T(1,128)}, u32[]{:S(2)}) copy-start(f32[1,768]{1,0:T(1,128)} %get-tuple-element.216) | copy-start | bytes 9220
  229.7 29.6 %copy-start.24 = (f32[1,768]{1,0:T(1,128)S(1)}, f32[1,768]{1,0:T(1,128)}, u32[]{:S(2)}) copy-start(f32[1,768]{1,0:T(1,128)} %get-tuple-element.218) | copy-start | bytes 9220
  229.7 29.7 %copy-start.22 = (f32[1,768]{1,0:T(1,128)S(1)}, f32[1,768]{1,0:T(1,128)}, u32[]{:S(2)}) copy-start(f32[1,768]{1,0:T(1,128)} %get-tuple-element.222) | copy-start | bytes 9220
  229.7 29.7 %copy-start.21 = (f32[1,768]{1,0:T(1,128)S(1)}, f32[1,768]{1,0:T(1,128)}, u32[]{:S(2)}) copy-start(f32[1,768]{1,0:T(1,128)} %get-tuple-element.223) | copy-start | bytes 9220
  257.0 3.3 copy-start.10
  257.0 2.7 copy-start.11
  260.3 6.6 %copy-start.5 = (bf16[16,24,1920]{2,1,0:T(8,128)(2,1)S(1)}, bf16[16,24,1920]{2,1,0:T(8,128)(2,1)}, u32[]{:S(2)}) copy-start(bf16[16,24,1920]{2,1,0:T(8,128)(2,1)} %get-tuple-element.225) | copy-start | bytes 4423684
  268.0 21.1 %collective-permute-start.20 = (bf16[16,24,1280]{2,1,0:T(8,128)(2,1)}, bf16[16,24,1280]{2,1,0:T(8,128)(2,1)}, u32[]{:S(2)}, u32[]{:S(2)}) collective-permute-start(bf16[16,24,1280]{2,1,0:T(8,128)(2,1)} %dynamic_update_slice.86), channel_id=1, source_target_pairs={{0,1},{1,0},{2,3},{3,2},{4,5},{5,4},{6,7},{7,6},{8,9},{9,8},{10,11... | collective-permute-start | bytes 2949128 | tf_op jit(solution)/shard_map/ppermute | solution.py:83
  268.1 21.1 %collective-permute-start.19 = (bf16[2,48,3072]{2,1,0:T(8,128)(2,1)}, bf16[2,48,3072]{2,1,0:T(8,128)(2,1)}, u32[]{:S(2)}, u32[]{:S(2)}) collective-permute-start(bf16[2,48,3072]{2,1,0:T(8,128)(2,1)} %get-tuple-element.228), channel_id=1, source_target_pairs={{0,2},{1,3},{2,0},{3,1},{4,6},{5,7},{6,4},{7,5},{8,10},{9,11},{10,... | collective-permute-start | bytes 1769480 | tf_op jit(solution)/shard_map/ppermute | solution.py:83
  269.3 18.6 %collective-permute-start.21 = (bf16[4,24,1920]{2,1,0:T(8,128)(2,1)}, bf16[4,24,1920]{2,1,0:T(8,128)(2,1)}, u32[]{:S(2)}, u32[]{:S(2)}) collective-permute-start(bf16[4,24,1920]{2,1,0:T(8,128)(2,1)} %get-tuple-element.230), channel_id=1, source_target_pairs={{0,8},{1,9},{2,10},{3,11},{4,12},{5,13},{6,14},{7,15},{8,0},{9,1},... | collective-permute-start | bytes 1105928 | tf_op jit(solution)/shard_map/ppermute | solution.py:83
  270.4 17.5 %collective-permute-start.22 = (bf16[4,24,1920]{2,1,0:T(8,128)(2,1)}, bf16[4,24,1920]{2,1,0:T(8,128)(2,1)}, u32[]{:S(2)}, u32[]{:S(2)}) collective-permute-start(bf16[4,24,1920]{2,1,0:T(8,128)(2,1)} %get-tuple-element.231), channel_id=1, source_target_pairs={{0,16},{1,17},{2,18},{3,19},{4,20},{5,21},{6,22},{7,23},{8,24},{9,... | collective-permute-start | bytes 1105928 | tf_op jit(solution)/shard_map/ppermute | solution.py:83
  271.6 17.6 %collective-permute-start.23 = (bf16[4,24,1920]{2,1,0:T(8,128)(2,1)}, bf16[4,24,1920]{2,1,0:T(8,128)(2,1)}, u32[]{:S(2)}, u32[]{:S(2)}) collective-permute-start(bf16[4,24,1920]{2,1,0:T(8,128)(2,1)} %get-tuple-element.232), channel_id=1, source_target_pairs={{0,24},{1,25},{2,26},{3,27},{4,28},{5,29},{6,30},{7,31},{8,16},{9,... | collective-permute-start | bytes 1105928 | tf_op jit(solution)/shard_map/ppermute | solution.py:83
  272.8 14.4 %copy-start.9 = (bf16[16,24,1280]{2,1,0:T(8,128)(2,1)S(1)}, bf16[16,24,1280]{2,1,0:T(8,128)(2,1)}, u32[]{:S(2)}) copy-start(bf16[16,24,1280]{2,1,0:T(8,128)(2,1)} %get-tuple-element.234) | copy-start | bytes 2949124
  287.9 35.2 %copy-start.4 = (bf16[4,24,1920]{2,1,0:T(8,128)(2,1)}, bf16[4,24,1920]{2,1,0:T(8,128)(2,1)S(1)}, u32[]{:S(2)}) copy-start(bf16[4,24,1920]{2,1,0:T(8,128)(2,1)S(1)} %dynamic-slice_bitcast_fusion) | copy-start | bytes 1105924
  293.6 22.9 %collective-permute-start.24 = (bf16[1,48,3072]{2,1,0:T(8,128)(2,1)S(1)}, bf16[1,48,3072]{2,1,0:T(8,128)(2,1)S(1)}, u32[]{:S(2)}, u32[]{:S(2)}) collective-permute-start(bf16[1,48,3072]{2,1,0:T(8,128)(2,1)S(1)} %add_convert_fusion.3), channel_id=1, source_target_pairs={{0,4},{1,5},{2,6},{3,7},{4,0},{5,1},{6,2},{7,3},{8,12},{9,13},{10,... | collective-permute-start | bytes 884744 | tf_op jit(solution)/shard_map/ppermute | solution.py:83
  296.3 20.2 %collective-permute-start.25 = (bf16[4,24,1280]{2,1,0:T(8,128)(2,1)S(1)}, bf16[4,24,1280]{2,1,0:T(8,128)(2,1)S(1)}, u32[]{:S(2)}, u32[]{:S(2)}) collective-permute-start(bf16[4,24,1280]{2,1,0:T(8,128)(2,1)S(1)} %get-tuple-element.246), channel_id=1, source_target_pairs={{0,8},{1,9},{2,10},{3,11},{4,12},{5,13},{6,14},{7,15},{8,0},{9,1},... | collective-permute-start | bytes 737288 | tf_op jit(solution)/shard_map/ppermute | solution.py:83
  297.5 19.0 %collective-permute-start.26 = (bf16[4,24,1280]{2,1,0:T(8,128)(2,1)S(1)}, bf16[4,24,1280]{2,1,0:T(8,128)(2,1)S(1)}, u32[]{:S(2)}, u32[]{:S(2)}) collective-permute-start(bf16[4,24,1280]{2,1,0:T(8,128)(2,1)S(1)} %get-tuple-element.247), channel_id=1, source_target_pairs={{0,16},{1,17},{2,18},{3,19},{4,20},{5,21},{6,22},{7,23},{8,24},{9,... | collective-permute-start | bytes 737288 | tf_op jit(solution)/shard_map/ppermute | solution.py:83
  298.5 18.0 %collective-permute-start.27 = (bf16[4,24,1280]{2,1,0:T(8,128)(2,1)S(1)}, bf16[4,24,1280]{2,1,0:T(8,128)(2,1)S(1)}, u32[]{:S(2)}, u32[]{:S(2)}) collective-permute-start(bf16[4,24,1280]{2,1,0:T(8,128)(2,1)S(1)} %get-tuple-element.248), channel_id=1, source_target_pairs={{0,24},{1,25},{2,26},{3,27},{4,28},{5,29},{6,30},{7,31},{8,16},{9,... | collective-permute-start | bytes 737288 | tf_op jit(solution)/shard_map/ppermute | solution.py:83
  299.8 18.2 %copy-start.7 = (bf16[4,24,1280]{2,1,0:T(8,128)(2,1)}, bf16[4,24,1280]{2,1,0:T(8,128)(2,1)S(1)}, u32[]{:S(2)}) copy-start(bf16[4,24,1280]{2,1,0:T(8,128)(2,1)S(1)} %dynamic-slice_bitcast_fusion.3) | copy-start | bytes 737284
  299.8 16.7 %collective-permute-start.28 = (bf16[2,1,24,1920]{3,2,1,0:T(8,128)(2,1)}, bf16[2,1,24,1920]{3,2,1,0:T(8,128)(2,1)}, u32[]{:S(2)}, u32[]{:S(2)}) collective-permute-start(bf16[2,1,24,1920]{3,2,1,0:T(8,128)(2,1)} %add_convert_fusion.7), channel_id=1, source_target_pairs={{0,2},{1,3},{2,0},{3,1},{4,6},{5,7},{6,4},{7,5},{8,10},{9,11},{10,... | collective-permute-start | bytes 552968 | tf_op jit(solution)/shard_map/ppermute | solution.py:83
  300.2 16.4 %copy-start.12 = (bf16[2,48,3072]{2,1,0:T(8,128)(2,1)S(1)}, bf16[2,48,3072]{2,1,0:T(8,128)(2,1)}, u32[]{:S(2)}) copy-start(bf16[2,48,3072]{2,1,0:T(8,128)(2,1)} %get-tuple-element.209) | copy-start | bytes 1769476
  316.4 9.5 %copy-start.8 = (bf16[4,24,1280]{2,1,0:T(8,128)(2,1)}, bf16[4,24,1280]{2,1,0:T(8,128)(2,1)S(1)}, u32[]{:S(2)}) copy-start(bf16[4,24,1280]{2,1,0:T(8,128)(2,1)S(1)} %dynamic-slice_bitcast_fusion.2) | copy-start | bytes 737284
  316.5 8.7 %copy-start.13 = (bf16[4,24,1280]{2,1,0:T(8,128)(2,1)}, bf16[4,24,1280]{2,1,0:T(8,128)(2,1)S(1)}, u32[]{:S(2)}) copy-start(bf16[4,24,1280]{2,1,0:T(8,128)(2,1)S(1)} %collective-permute-done.25) | copy-start | bytes 737284
  316.5 8.6 %copy-start.14 = (bf16[4,24,1280]{2,1,0:T(8,128)(2,1)}, bf16[4,24,1280]{2,1,0:T(8,128)(2,1)S(1)}, u32[]{:S(2)}) copy-start(bf16[4,24,1280]{2,1,0:T(8,128)(2,1)S(1)} %collective-permute-done.26) | copy-start | bytes 737284
  316.5 9.4 %copy-start.15 = (bf16[4,24,1280]{2,1,0:T(8,128)(2,1)}, bf16[4,24,1280]{2,1,0:T(8,128)(2,1)S(1)}, u32[]{:S(2)}) copy-start(bf16[4,24,1280]{2,1,0:T(8,128)(2,1)S(1)} %collective-permute-done.27) | copy-start | bytes 737284
  317.9 7.2 %collective-permute-start.33 = (f32[1,24,3072]{2,1,0:T(8,128)S(1)}, f32[1,24,3072]{2,1,0:T(8,128)S(1)}, u32[]{:S(2)}, u32[]{:S(2)}) collective-permute-start(f32[1,24,3072]{2,1,0:T(8,128)S(1)} %constant_dynamic-slice_fusion), channel_id=1, source_target_pairs={{0,1},{1,0},{2,3},{3,2},{4,5},{5,4},{6,7},{7,6},{8,9},{9,8},{10,11... | collective-permute-start | bytes 884744 | tf_op jit(solution)/shard_map/ppermute | solution.py:83
  318.7 13.1 %collective-permute-start.30 = (bf16[24,1280]{1,0:T(8,128)(2,1)}, bf16[24,1280]{1,0:T(8,128)(2,1)}, u32[]{:S(2)}, u32[]{:S(2)}) collective-permute-start(bf16[24,1280]{1,0:T(8,128)(2,1)} %get-tuple-element.278), channel_id=1, source_target_pairs={{0,2},{1,3},{2,0},{3,1},{4,6},{5,7},{6,4},{7,5},{8,10},{9,11},{10,... | collective-permute-start | bytes 184328 | tf_op jit(solution)/shard_map/ppermute | solution.py:83
  320.4 11.4 %collective-permute-start.31 = (bf16[24,1280]{1,0:T(8,128)(2,1)}, bf16[24,1280]{1,0:T(8,128)(2,1)}, u32[]{:S(2)}, u32[]{:S(2)}) collective-permute-start(bf16[24,1280]{1,0:T(8,128)(2,1)} %get-tuple-element.277), channel_id=1, source_target_pairs={{0,4},{1,5},{2,6},{3,7},{4,0},{5,1},{6,2},{7,3},{8,12},{9,13},{10,... | collective-permute-start | bytes 184328 | tf_op jit(solution)/shard_map/ppermute | solution.py:83
  320.7 11.1 %collective-permute-start.32 = (bf16[24,1280]{1,0:T(8,128)(2,1)}, bf16[24,1280]{1,0:T(8,128)(2,1)}, u32[]{:S(2)}, u32[]{:S(2)}) collective-permute-start(bf16[24,1280]{1,0:T(8,128)(2,1)} %get-tuple-element.276), channel_id=1, source_target_pairs={{0,6},{1,7},{2,4},{3,5},{4,2},{5,3},{6,0},{7,1},{8,14},{9,15},{10,... | collective-permute-start | bytes 184328 | tf_op jit(solution)/shard_map/ppermute | solution.py:83
  324.9 8.6 %collective-permute-start.29 = (bf16[1,1,24,1920]{3,2,1,0:T(8,128)(2,1)}, bf16[1,1,24,1920]{3,2,1,0:T(8,128)(2,1)}, u32[]{:S(2)}, u32[]{:S(2)}) collective-permute-start(bf16[1,1,24,1920]{3,2,1,0:T(8,128)(2,1)} %add_convert_fusion.8), channel_id=1, source_target_pairs={{0,4},{1,5},{2,6},{3,7},{4,0},{5,1},{6,2},{7,3},{8,12},{9,13},{10,... | collective-permute-start | bytes 276488 | tf_op jit(solution)/shard_map/ppermute | solution.py:83
  328.3 2.6 copy-start.6
  (2 other events, 2.4 us)
Sparse Core Ops, SparseCore 0:
  11.7 95.2 all-gather.1

commit v8 on v7

--- a/solution.py
+++ b/solution.py
@@ -17,7 +17,7 @@
 NN = (((1,), (0,)), ((), ()))
 NT = (((1,), (1,)), ((), ()))
 TN = (((0,), (0,)), ((), ()))
-VMEM_LIMIT = 60 * 2**20
+VMEM_LIMIT = 63 * 2**20
 TILE = 304
 ATILE = 304
 AHEAD = 1

time: 351 us -> 356 us (1.014)
    squeeze x4, local copies, waits for them, and re-layouts: 1.04 us -> 4.68 us  [plane_steps(): return [pick(term, 0, spot)[0] for term in terms] + came]
  transfers between devices with their start and end apart: 35 -> 35, of which waited for: 7 -> 5; matrix products, arithmetic and copies ran while one was open for 9% -> 10% of each run, Pallas kernels for 45% -> 44%
where the time goes in v8:
time: 356 us; the launch traced here: 351 us
  Pallas kernels  219 us (62%)
  local copies, waits for them, and re-layouts  40.8 us (11%)
  starting transfers between devices  35.5 us (10%)
  other arithmetic  21.2 us (6%)
  waiting for transfers between devices  18.7 us (5%)
  between operations  15.5 us (4%)
    pallas_call x2, Pallas kernels, attend_back(): pl.pallas_call(functools.partial(attend_back_kernel, pairs=pairs, extra=b...  59.3 us
    pallas_call x1, Pallas kernels, mlp(): pl.pallas_call(functools.partial(mlp_kernel, seq=seq, tile=tile_of(seq),...  52.5 us
    pallas_call x2, Pallas kernels, attend(): pl.pallas_call(functools.partial(attend_kernel, tile=tile_of(seq), padded...  44.6 us
    ppermute x34, starting transfers between devices, depart(): came = [lax.ppermute(array, AXES, pairs) for array, pairs in sends]  35.4 us
    pallas_call x1, Pallas kernels, middle_back(): pl.pallas_call(functools.partial(middle_back_kernel, seq=seq, sub=sub), g...  20.9 us
    ppermute x34, waiting for transfers between devices, depart(): came = [lax.ppermute(array, AXES, pairs) for array, pairs in sends]  18.6 us
    pallas_call x1, Pallas kernels, block_out_of(): pl.pallas_call(functools.partial(block_out_kernel, seq=seq, begin=begin),...  15.2 us
    pallas_call x1, Pallas kernels, input_back(): pl.pallas_call(functools.partial(input_back_kernel, spans=spans, sub=sub)...  14.4 us
  transfers between devices with their start and end apart: 35, of which 5 were waited for; matrix products, arithmetic and copies ran while one was open for 10% of the time, Pallas kernels for 44%

profile of v8, /device:TPU:0, one launch (start us, length us, event | category | flops | bytes accessed | tf_op | source)
XLA Modules:
  0.0 350.6 jit_solution(15135653669443926073)
XLA Ops:
  7.2 2.0 reshape.186
  9.4 1.3 reshape.187
  12.0 3.1 collective-permute-start
  15.1 2.6 collective-permute-start.1
  17.8 2.0 collective-permute-start.3
  20.0 4.9 %collective-permute-done.1 = bf16[1,1,1,1,1,24,1280]{6,5,4,3,2,1,0:T(8,128)(2,1)S(1)} collective-permute-done((bf16[1,1,1,1,1,24,1280]{6,5,4,3,2,1,0:T(8,128)(2,1)S(1)}, bf16[1,1,1,1,1,24,1280]{6,5,4,3,2,1,0:T(8,128)(2,1)S(1)}, u32[]{:S(2)}, u32[]{:S(2)}) %collective-permute-start.1) | collective-permute-done | bytes 61472 | tf_op jit(solution)/shard_map/ppermute | solution.py:83
  24.8 4.0 %collective-permute-done.3 = bf16[1,1,1,1,1,24,1920]{6,5,4,3,2,1,0:T(8,128)(2,1)S(1)} collective-permute-done((bf16[1,1,1,1,1,24,1920]{6,5,4,3,2,1,0:T(8,128)(2,1)S(1)}, bf16[1,1,1,1,1,24,1920]{6,5,4,3,2,1,0:T(8,128)(2,1)S(1)}, u32[]{:S(2)}, u32[]{:S(2)}) %collective-permute-start.3) | collective-permute-done | bytes 92192 | tf_op jit(solution)/shard_map/ppermute | solution.py:83
  28.9 1.6 collective-permute-start.4
  30.5 1.6 collective-permute-start.5
  33.0 5.8 %collective-permute-done.7 = bf16[1,1,2,1,1,24,1920]{6,5,4,3,2,1,0:T(8,128)(2,1)S(1)} collective-permute-done((bf16[1,1,2,1,1,24,1920]{6,5,4,3,2,1,0:T(8,128)(2,1)S(1)}, bf16[1,1,2,1,1,24,1920]{6,5,4,3,2,1,0:T(8,128)(2,1)S(1)}, u32[]{:S(2)}, u32[]{:S(2)}) %collective-permute-start.7) | collective-permute-done | bytes 184352 | tf_op jit(solution)/shard_map/ppermute | solution.py:83
  38.8 2.3 collective-permute-done.5
  42.0 1.6 collective-permute-start.10
  43.6 1.2 collective-permute-start.11
  44.8 0.8 collective-permute-start.9
  45.6 1.3 broadcast_in_dim.31
  48.0 1.3 copy-done
  51.4 19.7 %attend.2 = (bf16[1824,768]{1,0:T(8,128)(2,1)}, bf16[1824,1152]{1,0:T(8,128)(2,1)}, bf16[1824,384]{1,0:T(8,128)(2,1)}, bf16[3,3,608,1280]{3,2,1,0:T(8,128)(2,1)}, f32[1824,384]{1,0:T(8,128)}) custom-call(s32[3]{0:T(128)} %get-tuple-element.298.valid, bf16[1824,768]{1,0:T(8,128)(2,1)} %bitcast.124, f32[1,768]{1,0:T(1,128)} %get-tuple-element.296.refs_1_.refs_6_, ...), custom_call_target="tpu_custom_call" | custom-call | flops 1 | bytes 1 | tf_op jit(solution)/shard_map/attend/pallas_call | solution.py:587
  71.2 1.8 constant_dynamic-update-slice_fusion.4
  73.0 1.8 constant_dynamic-update-slice_fusion.3
  74.8 0.8 constant_dynamic-update-slice_fusion.2
  77.0 1.8 broadcast_in_dim.30
  78.8 2.7 constant_dynamic-update-slice_fusion.1
  81.5 1.3 constant_dynamic-update-slice_fusion
  82.8 24.9 %attend.3 = (bf16[1824,1152]{1,0:T(8,128)(2,1)}, bf16[1824,384]{1,0:T(8,128)(2,1)}, bf16[3,3,608,1280]{3,2,1,0:T(8,128)(2,1)}, f32[1824,384]{1,0:T(8,128)}, f32[...) custom-call(s32[3]{0:T(128)} %get-tuple-element.298.valid, bf16[1824,768]{1,0:T(8,128)(2,1)} %get-tuple-element.152.refs_0_.refs_15_, ...), custom_call_target="tpu_custom_call" | custom-call | flops 1 | bytes 1 | tf_op jit(solution)/shard_map/attend/pallas_call | solution.py:587
  107.7 52.5 %mlp.1 = (bf16[1824,3072]{1,0:T(8,128)(2,1)}, bf16[1824,3072]{1,0:T(8,128)(2,1)}, f32[1,3072]{1,0:T(1,128)}, bf16[768,3072]{1,0:T(8,128)(2,1)}, bf16[768,3072]{1,0:T(8,128)(2,1)}) custom-call(s32[3]{0:T(128)} %get-tuple-element.298.valid, s32[3]{0:T(128)} %get-tuple-element.297.where, bf16[1824,768]{1,0:T(8,128)(2,1)} %get-tuple-element.157.normed, ...), custom_call_target="tpu_custom_call" | custom-call | flops 1 | bytes 1 | tf_op jit(solution)/shard_map/mlp/pallas_call | solution.py:779
  160.6 20.9 %middle_back.1 = (bf16[1824,768]{1,0:T(8,128)(2,1)}, bf16[1824,768]{1,0:T(8,128)(2,1)}, f32[1,768]{1,0:T(1,128)}, f32[1,768]{1,0:T(1,128)}, f32[1,768]{1,0:T(1,128)}, /*index=5*/f32[1,768]{1,0:T(1,128)}) custom-call(s32[3]{0:T(128)} %get-tuple-element.298.valid, bf16[1824,3072]{1,0:T(8,128)(2,1)} %get-tuple-element.161.hidden_grad, ...), custom_call_target="tpu_custom_call" | custom-call | flops 1 | bytes 1 | tf_op jit(solution)/shard_map/middle_back/pallas_call | solution.py:887
  181.4 4.4 %fold_first.1 = (bf16[2,4,48,1536]{3,2,1,0:T(8,128)(2,1)}, bf16[2,4,48,1536]{3,2,1,0:T(8,128)(2,1)}) custom-call(s32[3]{0:T(128)} %get-tuple-element.297.where, bf16[2,2,4,48,3072]{4,3,2,1,0:T(8,128)(2,1)} %bitcast.114, bf16[2,2,4,48,3072]{4,3,2,1,0:T(8,128)(2,1)} %bitcast.23.refs_1_.refs_3_.refs_4_.refs_5_, bf16[2,2,4,48,3072]{4,3,2,1,0:T(8,128)(2,1)} %bitcast.115, ...), custom_call_target="tpu_custom_call" | custom-call | flops 1 | bytes 1 | tf_op jit(solution)/shard_map/fold_first/pallas_call | solution.py:256
  185.8 1.5 collective-permute-start.14
  187.9 32.1 %attend_back.2 = (bf16[1824,1152]{1,0:T(8,128)(2,1)}, f32[1,1152]{1,0:T(1,128)}, f32[1,768]{1,0:T(1,128)}, f32[1,768]{1,0:T(1,128)}, bf16[16,24,1920]{2,1,0:T(8,128)(2,1)}, /*index=5*/bf16[16,24,1920]{2,1,0:T(8,128)(2,1)}) custom-call(s32[3]{0:T(128)} %get-tuple-element.297.where, bf16[1824,1152]{1,0:T(8,128)(2,1)} %get-tuple-element.172.refs_0_.refs_1_.refs_2_, ...), custom_call_target="tpu_custom_call" | custom-call | flops 1 | bytes 1 | tf_op jit(solution)/shard_map/attend_back/pallas_call | solution.py:688
  220.0 3.7 %fold_second.1 = (bf16[4,48,1536]{2,1,0:T(8,128)(2,1)}, bf16[4,48,1536]{2,1,0:T(8,128)(2,1)}) custom-call(s32[3]{0:T(128)} %get-tuple-element.297.where, bf16[2,2,4,48,3072]{4,3,2,1,0:T(8,128)(2,1)} %bitcast.116, bf16[2,2,4,48,3072]{4,3,2,1,0:T(8,128)(2,1)} %bitcast.23.refs_1_.refs_3_.refs_4_.refs_5_, ...), custom_call_target="tpu_custom_call" | custom-call | flops 1 | bytes 1 | tf_op jit(solution)/shard_map/fold_second/pallas_call | solution.py:282
  223.7 1.5 collective-permute-start.16
  227.3 27.3 %attend_back.3 = (bf16[1824,1152]{1,0:T(8,128)(2,1)}, f32[1,1152]{1,0:T(1,128)}, f32[1,768]{1,0:T(1,128)}, f32[1,768]{1,0:T(1,128)}, bf16[16,24,1280]{2,1,0:T(8,128)(2,1)}, /*index=5*/bf16[16,24,1280]{2,1,0:T(8,128)(2,1)}) custom-call(s32[3]{0:T(128)} %get-tuple-element.297.where, bf16[1824,1152]{1,0:T(8,128)(2,1)} %get-tuple-element.190.refs_0_.refs_1_.refs_2_, ...), custom_call_target="tpu_custom_call" | custom-call | flops 1 | bytes 1 | tf_op jit(solution)/shard_map/attend_back/pallas_call | solution.py:688
  255.5 1.3 fusion.20
  257.2 4.1 %line_first.1 = (bf16[2,48,3072]{2,1,0:T(8,128)(2,1)}, bf16[2,48,3072]{2,1,0:T(8,128)(2,1)}) custom-call(s32[3]{0:T(128)} %get-tuple-element.297.where, bf16[2,2,4,48,3072]{4,3,2,1,0:T(8,128)(2,1)} %bitcast.118, bf16[2,2,4,48,3072]{4,3,2,1,0:T(8,128)(2,1)} %bitcast.23.refs_1_.refs_3_.refs_4_.refs_5_, ...), custom_call_target="tpu_custom_call" | custom-call | flops 1 | bytes 1 | tf_op jit(solution)/shard_map/line_first/pallas_call | solution.py:317
  261.3 2.3 dynamic_update_slice.86
  263.7 2.7 fusion.2
  267.0 1.4 collective-permute-start.21
  269.0 1.5 collective-permute-start.23
  270.5 1.0 dynamic-slice_bitcast_fusion.1
  271.5 14.4 %input_back.1 = bf16[1824,768]{1,0:T(8,128)(2,1)} custom-call(bf16[1824,1152]{1,0:T(8,128)(2,1)} %get-tuple-element.210.refs_0_, bf16[1824,1152]{1,0:T(8,128)(2,1)} %get-tuple-element.227.refs_1_, bf16[768,1280]{1,0:T(8,128)(2,1)} %bitcast.123, bf16[768,1920]{1,0:T(8,128)(2,1)} %bitcast.15.refs_1_.weight_a.weight_b.refs_16_.refs_3_, ...), custom_call_target="tpu_custom_call" | custom-call | flops 1 | bytes 1 | tf_op jit(solution)/shard_map/input_back/pallas_call | solution.py:936
  285.9 2.4 dynamic_update_slice.87
  288.3 1.0 dynamic-slice_bitcast_fusion
  289.4 2.5 fusion.5
  291.8 1.7 add_convert_fusion.3
  293.6 1.9 add_convert_fusion.7
  295.5 3.0 collective-permute-start.24
  298.5 1.3 collective-permute-start.25
  299.8 0.8 collective-permute-start.26
  300.6 1.4 collective-permute-start.27
  302.0 1.6 dynamic-slice_bitcast_fusion.3
  303.7 15.2 %block_out.1 = bf16[1824,768]{1,0:T(8,128)(2,1)} custom-call(s32[3]{0:T(128)} %get-tuple-element.298.valid, bf16[1824,3072]{1,0:T(8,128)(2,1)} %get-tuple-element.158.active, bf16[768,6144]{1,0:T(8,128)(2,1)} %all-gather.2.cloned.1.call-done.up.down.ups.downs, f32[1824,768]{1,0:T(8,128)} %get-tuple-element.244.middle, f32[1,768]{1,0:T(1,128)} %get-tuple-element.285.bias_down), custom_call_target="tpu_custom_call" | custom-call | flops 1 | bytes 1 | tf_op jit(solution)/shard_map/block_out/pallas_call | solution.py:830
  318.9 1.0 dynamic-slice_bitcast_fusion.2
  320.0 1.3 convert_add_fusion
  321.5 1.8 fusion.11
  323.3 1.9 collective-permute-start.30
  325.2 2.5 collective-permute-start.32
  327.7 1.7 add_convert_fusion.8
  330.6 1.1 reshape.212
  331.7 1.2 copy.45
  333.0 2.5 reshape.213
  336.5 1.6 collective-permute-done.29
  338.1 1.2 add_bitcast_fusion
  339.3 1.1 bitcast_add_fusion
  341.9 0.8 reshape_reshape.8
  (193 shorter events, 18.2 us)
Async XLA Ops:
  7.2 3.5 %copy-start.9 = (bf16[73728]{0:T(1024)(128)(2,1)S(1)}, bf16[73728]{0:T(1024)(128)(2,1)}, u32[]{:S(2)}) copy-start(bf16[73728]{0:T(1024)(128)(2,1)} %param.17) | copy-start | bytes 442372
  7.2 100.5 %all-gather.2.cloned.1.call-start = ((), (), s32[]{:S(2)}) async-start(), calls=%async_computation | async-start | bytes 9732096 | tf_op jit(solution)/shard_map/all_gather | solution.py:995
  9.2 2.4 copy-start.10
  9.4 2.5 copy-start.22
  9.4 2.5 copy-start.23
  9.4 8.3 %copy-start.11 = (bf16[18432]{0:T(1024)(128)(2,1)S(1)}, bf16[18432]{0:T(1024)(128)(2,1)}, u32[]{:S(2)}) copy-start(bf16[18432]{0:T(1024)(128)(2,1)} %param.15) | copy-start | bytes 110596
  12.0 8.0 %collective-permute-start = (bf16[1,1,1,1,1,24,1280]{6,5,4,3,2,1,0:T(8,128)(2,1)S(1)}, bf16[1,1,1,1,1,24,1280]{6,5,4,3,2,1,0:T(8,128)(2,1)S(1)}, u32[]{:S(2)}, u32[]{:S(2)}) collective-permute-start(bf16[1,1,1,1,1,24,1280]{6,5,4,3,2,1,0:T(8,128)(2,1)S(1)} %fusion.8), channel_id=1, source_target_pairs={{0,2},{1,3},{2,0},{3,1},{4,6},{5,7},{6,4},{7,5},{8,10},{9,11},{10,... | collective-permute-start | bytes 184328 | tf_op jit(solution)/shard_map/ppermute | solution.py:83
  15.1 9.8 %collective-permute-start.1 = (bf16[1,1,1,1,1,24,1280]{6,5,4,3,2,1,0:T(8,128)(2,1)S(1)}, bf16[1,1,1,1,1,24,1280]{6,5,4,3,2,1,0:T(8,128)(2,1)S(1)}, u32[]{:S(2)}, u32[]{:S(2)}) collective-permute-start(bf16[1,1,1,1,1,24,1280]{6,5,4,3,2,1,0:T(8,128)(2,1)S(1)} %fusion.8), channel_id=1, source_target_pairs={{0,4},{1,5},{2,6},{3,7},{4,0},{5,1},{6,2},{7,3},{8,12},{9,13},{10,... | collective-permute-start | bytes 184328 | tf_op jit(solution)/shard_map/ppermute | solution.py:83
  17.6 7.2 %collective-permute-start.2 = (bf16[1,1,1,1,1,24,1280]{6,5,4,3,2,1,0:T(8,128)(2,1)S(1)}, bf16[1,1,1,1,1,24,1280]{6,5,4,3,2,1,0:T(8,128)(2,1)S(1)}, u32[]{:S(2)}, u32[]{:S(2)}) collective-permute-start(bf16[1,1,1,1,1,24,1280]{6,5,4,3,2,1,0:T(8,128)(2,1)S(1)} %fusion.8), channel_id=1, source_target_pairs={{0,6},{1,7},{2,4},{3,5},{4,2},{5,3},{6,0},{7,1},{8,14},{9,15},{10,... | collective-permute-start | bytes 184328 | tf_op jit(solution)/shard_map/ppermute | solution.py:83
  17.8 11.0 %collective-permute-start.3 = (bf16[1,1,1,1,1,24,1920]{6,5,4,3,2,1,0:T(8,128)(2,1)S(1)}, bf16[1,1,1,1,1,24,1920]{6,5,4,3,2,1,0:T(8,128)(2,1)S(1)}, u32[]{:S(2)}, u32[]{:S(2)}) collective-permute-start(bf16[1,1,1,1,1,24,1920]{6,5,4,3,2,1,0:T(8,128)(2,1)S(1)} %maximum_bitcast_fusion.1), channel_id=1, source_target_pairs={{0,4},{1,5},{2,6},{3,7},{4,0},{5,1},{6,2},{7,3},{8,12},{9,13},{10,... | collective-permute-start | bytes 276488 | tf_op jit(solution)/shard_map/ppermute | solution.py:83
  19.8 21.4 %copy-start.20 = (s32[3]{0:T(128)S(1)}, s32[3]{0:T(128)}, u32[]{:S(2)}) copy-start(s32[3]{0:T(128)} %param.13) | copy-start | bytes 40
  19.9 21.4 %copy-start.21 = (s32[3]{0:T(128)S(1)}, s32[3]{0:T(128)}, u32[]{:S(2)}) copy-start(s32[3]{0:T(128)} %param.12) | copy-start | bytes 40
  28.9 9.9 %collective-permute-start.4 = (bf16[1,1,2,2,1,24,1280]{6,5,4,3,2,1,0:T(8,128)(2,1)S(1)}, bf16[1,1,2,2,1,24,1280]{6,5,4,3,2,1,0:T(8,128)(2,1)S(1)}, u32[]{:S(2)}, u32[]{:S(2)}) collective-permute-start(bf16[1,1,2,2,1,24,1280]{6,5,4,3,2,1,0:T(8,128)(2,1)S(1)} %constant_dynamic-update-slice_fusion.16), channel_id=1, source_target_pairs={{0,8},{1,9},{2,10},{3,11},{4,12},{5,13},{6,14},{7,15},{8,0},{9,1},... | collective-permute-start | bytes 737288 | tf_op jit(solution)/shard_map/ppermute | solution.py:83
  30.5 10.5 %collective-permute-start.5 = (bf16[1,1,2,2,1,24,1280]{6,5,4,3,2,1,0:T(8,128)(2,1)S(1)}, bf16[1,1,2,2,1,24,1280]{6,5,4,3,2,1,0:T(8,128)(2,1)S(1)}, u32[]{:S(2)}, u32[]{:S(2)}) collective-permute-start(bf16[1,1,2,2,1,24,1280]{6,5,4,3,2,1,0:T(8,128)(2,1)S(1)} %constant_dynamic-update-slice_fusion.16), channel_id=1, source_target_pairs={{0,16},{1,17},{2,18},{3,19},{4,20},{5,21},{6,22},{7,23},{8,24},{9,... | collective-permute-start | bytes 737288 | tf_op jit(solution)/shard_map/ppermute | solution.py:83
  32.1 9.0 %collective-permute-start.6 = (bf16[1,1,2,2,1,24,1280]{6,5,4,3,2,1,0:T(8,128)(2,1)S(1)}, bf16[1,1,2,2,1,24,1280]{6,5,4,3,2,1,0:T(8,128)(2,1)S(1)}, u32[]{:S(2)}, u32[]{:S(2)}) collective-permute-start(bf16[1,1,2,2,1,24,1280]{6,5,4,3,2,1,0:T(8,128)(2,1)S(1)} %constant_dynamic-update-slice_fusion.16), channel_id=1, source_target_pairs={{0,24},{1,25},{2,26},{3,27},{4,28},{5,29},{6,30},{7,31},{8,16},{9,... | collective-permute-start | bytes 737288 | tf_op jit(solution)/shard_map/ppermute | solution.py:83
  32.5 6.3 %collective-permute-start.7 = (bf16[1,1,2,1,1,24,1920]{6,5,4,3,2,1,0:T(8,128)(2,1)S(1)}, bf16[1,1,2,1,1,24,1920]{6,5,4,3,2,1,0:T(8,128)(2,1)S(1)}, u32[]{:S(2)}, u32[]{:S(2)}) collective-permute-start(bf16[1,1,2,1,1,24,1920]{6,5,4,3,2,1,0:T(8,128)(2,1)S(1)} %constant_dynamic-update-slice_fusion.13), channel_id=1, source_target_pairs={{0,2},{1,3},{2,0},{3,1},{4,6},{5,7},{6,4},{7,5},{8,10},{9,11},{10,... | collective-permute-start | bytes 552968 | tf_op jit(solution)/shard_map/ppermute | solution.py:83
  41.2 6.7 %collective-permute-start.8 = (bf16[2,2,2,2,1,24,1280]{6,5,4,3,2,1,0:T(8,128)(2,1)S(1)}, bf16[2,2,2,2,1,24,1280]{6,5,4,3,2,1,0:T(8,128)(2,1)S(1)}, u32[]{:S(2)}, u32[]{:S(2)}) collective-permute-start(bf16[2,2,2,2,1,24,1280]{6,5,4,3,2,1,0:T(8,128)(2,1)S(1)} %constant_dynamic-update-slice_fusion.10), channel_id=1, source_target_pairs={{0,1},{1,0},{2,3},{3,2},{4,5},{5,4},{6,7},{7,6},{8,9},{9,8},{10,11... | collective-permute-start | bytes 2949128 | tf_op jit(solution)/shard_map/ppermute | solution.py:83
  42.0 29.2 %collective-permute-start.10 = (bf16[1,1,2,2,1,24,1920]{6,5,4,3,2,1,0:T(8,128)(2,1)S(1)}, bf16[1,1,2,2,1,24,1920]{6,5,4,3,2,1,0:T(8,128)(2,1)}, u32[]{:S(2)}, u32[]{:S(2)}) collective-permute-start(bf16[1,1,2,2,1,24,1920]{6,5,4,3,2,1,0:T(8,128)(2,1)S(1)} %constant_dynamic-update-slice_fusion.6), channel_id=1, source_target_pairs={{0,16},{1,17},{2,18},{3,19},{4,20},{5,21},{6,22},{7,23},{8,24},{9,... | collective-permute-start | bytes 1105928 | tf_op jit(solution)/shard_map/ppermute | solution.py:83
  43.6 27.6 %collective-permute-start.11 = (bf16[1,1,2,2,1,24,1920]{6,5,4,3,2,1,0:T(8,128)(2,1)S(1)}, bf16[1,1,2,2,1,24,1920]{6,5,4,3,2,1,0:T(8,128)(2,1)S(1)}, u32[]{:S(2)}, u32[]{:S(2)}) collective-permute-start(bf16[1,1,2,2,1,24,1920]{6,5,4,3,2,1,0:T(8,128)(2,1)S(1)} %constant_dynamic-update-slice_fusion.6), channel_id=1, source_target_pairs={{0,24},{1,25},{2,26},{3,27},{4,28},{5,29},{6,30},{7,31},{8,16},{9,... | collective-permute-start | bytes 1105928 | tf_op jit(solution)/shard_map/ppermute | solution.py:83
  44.8 26.5 %collective-permute-start.9 = (bf16[1,1,2,2,1,24,1920]{6,5,4,3,2,1,0:T(8,128)(2,1)S(1)}, bf16[1,1,2,2,1,24,1920]{6,5,4,3,2,1,0:T(8,128)(2,1)}, u32[]{:S(2)}, u32[]{:S(2)}) collective-permute-start(bf16[1,1,2,2,1,24,1920]{6,5,4,3,2,1,0:T(8,128)(2,1)S(1)} %constant_dynamic-update-slice_fusion.6), channel_id=1, source_target_pairs={{0,8},{1,9},{2,10},{3,11},{4,12},{5,13},{6,14},{7,15},{8,0},{9,1},... | collective-permute-start | bytes 1105928 | tf_op jit(solution)/shard_map/ppermute | solution.py:83
  48.0 1.3 copy-start
  75.5 6.0 %collective-permute-start.12 = (bf16[2,2,2,2,1,24,1920]{6,5,4,3,2,1,0:T(8,128)(2,1)}, bf16[2,2,2,2,1,24,1920]{6,5,4,3,2,1,0:T(8,128)(2,1)S(1)}, u32[]{:S(2)}, u32[]{:S(2)}) collective-permute-start(bf16[2,2,2,2,1,24,1920]{6,5,4,3,2,1,0:T(8,128)(2,1)} %constant_dynamic-update-slice_fusion.2), channel_id=1, source_target_pairs={{0,1},{1,0},{2,3},{3,2},{4,5},{5,4},{6,7},{7,6},{8,9},{9,8},{10,11... | collective-permute-start | bytes 4423688 | tf_op jit(solution)/shard_map/ppermute | solution.py:83
  160.1 21.3 %collective-permute-start.13 = (bf16[768,3072]{1,0:T(8,128)(2,1)}, bf16[768,3072]{1,0:T(8,128)(2,1)}, u32[]{:S(2)}, u32[]{:S(2)}) collective-permute-start(bf16[768,3072]{1,0:T(8,128)(2,1)} %get-tuple-element.170), channel_id=1, source_target_pairs={{0,1},{1,0},{2,3},{3,2},{4,5},{5,4},{6,7},{7,6},{8,9},{9,8},{10,11... | collective-permute-start | bytes 14155784 | tf_op jit(solution)/shard_map/ppermute | solution.py:83
  185.8 34.1 %collective-permute-start.14 = (bf16[2,4,48,1536]{3,2,1,0:T(8,128)(2,1)}, bf16[2,4,48,1536]{3,2,1,0:T(8,128)(2,1)}, u32[]{:S(2)}, u32[]{:S(2)}) collective-permute-start(bf16[2,4,48,1536]{3,2,1,0:T(8,128)(2,1)} %get-tuple-element.187), channel_id=1, source_target_pairs={{0,16},{1,17},{2,18},{3,19},{4,20},{5,21},{6,22},{7,23},{8,24},{9,... | collective-permute-start | bytes 3538952 | tf_op jit(solution)/shard_map/ppermute | solution.py:83
  187.3 32.6 %collective-permute-start.15 = (bf16[2,4,48,1536]{3,2,1,0:T(8,128)(2,1)}, bf16[2,4,48,1536]{3,2,1,0:T(8,128)(2,1)}, u32[]{:S(2)}, u32[]{:S(2)}) collective-permute-start(bf16[2,4,48,1536]{3,2,1,0:T(8,128)(2,1)} %get-tuple-element.188), channel_id=1, source_target_pairs={{0,8},{1,9},{2,10},{3,11},{4,12},{5,13},{6,14},{7,15},{8,0},{9,1},... | collective-permute-start | bytes 3538952 | tf_op jit(solution)/shard_map/ppermute | solution.py:83
  220.0 6.2 %copy-start.12 = (f32[1,3072]{1,0:T(1,128)S(1)}, f32[1,3072]{1,0:T(1,128)}, u32[]{:S(2)}) copy-start(f32[1,3072]{1,0:T(1,128)} %get-tuple-element.224) | copy-start | bytes 36868
  223.6 30.9 %collective-permute-start.18 = (bf16[16,24,1920]{2,1,0:T(8,128)(2,1)}, bf16[16,24,1920]{2,1,0:T(8,128)(2,1)}, u32[]{:S(2)}, u32[]{:S(2)}) collective-permute-start(bf16[16,24,1920]{2,1,0:T(8,128)(2,1)} %get-tuple-element.206), channel_id=1, source_target_pairs={{0,1},{1,0},{2,3},{3,2},{4,5},{5,4},{6,7},{7,6},{8,9},{9,8},{10,11... | collective-permute-start | bytes 4423688 | tf_op jit(solution)/shard_map/ppermute | solution.py:83
  223.7 30.9 %collective-permute-start.16 = (bf16[4,48,1536]{2,1,0:T(8,128)(2,1)}, bf16[4,48,1536]{2,1,0:T(8,128)(2,1)S(1)}, u32[]{:S(2)}, u32[]{:S(2)}) collective-permute-start(bf16[4,48,1536]{2,1,0:T(8,128)(2,1)} %get-tuple-element.204), channel_id=1, source_target_pairs={{0,8},{1,9},{2,10},{3,11},{4,12},{5,13},{6,14},{7,15},{8,0},{9,1},... | collective-permute-start | bytes 1769480 | tf_op jit(solution)/shard_map/ppermute | solution.py:83
  225.2 29.4 %collective-permute-start.17 = (bf16[4,48,1536]{2,1,0:T(8,128)(2,1)}, bf16[4,48,1536]{2,1,0:T(8,128)(2,1)}, u32[]{:S(2)}, u32[]{:S(2)}) collective-permute-start(bf16[4,48,1536]{2,1,0:T(8,128)(2,1)} %get-tuple-element.205), channel_id=1, source_target_pairs={{0,16},{1,17},{2,18},{3,19},{4,20},{5,21},{6,22},{7,23},{8,24},{9,... | collective-permute-start | bytes 1769480 | tf_op jit(solution)/shard_map/ppermute | solution.py:83
  227.2 27.3 %copy-start.13 = (f32[1,1152]{1,0:T(1,128)S(1)}, f32[1,1152]{1,0:T(1,128)}, u32[]{:S(2)}) copy-start(f32[1,1152]{1,0:T(1,128)} %get-tuple-element.219) | copy-start | bytes 13828
  227.2 28.2 %copy-start.16 = (f32[1,768]{1,0:T(1,128)S(1)}, f32[1,768]{1,0:T(1,128)}, u32[]{:S(2)}) copy-start(f32[1,768]{1,0:T(1,128)} %get-tuple-element.221) | copy-start | bytes 9220
  227.2 28.3 %copy-start.18 = (f32[1,768]{1,0:T(1,128)S(1)}, f32[1,768]{1,0:T(1,128)}, u32[]{:S(2)}) copy-start(f32[1,768]{1,0:T(1,128)} %get-tuple-element.214) | copy-start | bytes 9220
  227.2 28.3 %copy-start.19 = (f32[1,768]{1,0:T(1,128)S(1)}, f32[1,768]{1,0:T(1,128)}, u32[]{:S(2)}) copy-start(f32[1,768]{1,0:T(1,128)} %get-tuple-element.216) | copy-start | bytes 9220
  227.2 29.5 %copy-start.17 = (f32[1,768]{1,0:T(1,128)S(1)}, f32[1,768]{1,0:T(1,128)}, u32[]{:S(2)}) copy-start(f32[1,768]{1,0:T(1,128)} %get-tuple-element.218) | copy-start | bytes 9220
  227.2 29.6 %copy-start.15 = (f32[1,768]{1,0:T(1,128)S(1)}, f32[1,768]{1,0:T(1,128)}, u32[]{:S(2)}) copy-start(f32[1,768]{1,0:T(1,128)} %get-tuple-element.222) | copy-start | bytes 9220
  227.2 29.6 %copy-start.14 = (f32[1,768]{1,0:T(1,128)S(1)}, f32[1,768]{1,0:T(1,128)}, u32[]{:S(2)}) copy-start(f32[1,768]{1,0:T(1,128)} %get-tuple-element.223) | copy-start | bytes 9220
  254.6 2.7 copy-start.5
  266.4 23.0 %collective-permute-start.20 = (bf16[16,24,1280]{2,1,0:T(8,128)(2,1)}, bf16[16,24,1280]{2,1,0:T(8,128)(2,1)}, u32[]{:S(2)}, u32[]{:S(2)}) collective-permute-start(bf16[16,24,1280]{2,1,0:T(8,128)(2,1)} %dynamic_update_slice.86), channel_id=1, source_target_pairs={{0,1},{1,0},{2,3},{3,2},{4,5},{5,4},{6,7},{7,6},{8,9},{9,8},{10,11... | collective-permute-start | bytes 2949128 | tf_op jit(solution)/shard_map/ppermute | solution.py:83
  266.4 22.9 %collective-permute-start.19 = (bf16[2,48,3072]{2,1,0:T(8,128)(2,1)}, bf16[2,48,3072]{2,1,0:T(8,128)(2,1)}, u32[]{:S(2)}, u32[]{:S(2)}) collective-permute-start(bf16[2,48,3072]{2,1,0:T(8,128)(2,1)} %get-tuple-element.228), channel_id=1, source_target_pairs={{0,2},{1,3},{2,0},{3,1},{4,6},{5,7},{6,4},{7,5},{8,10},{9,11},{10,... | collective-permute-start | bytes 1769480 | tf_op jit(solution)/shard_map/ppermute | solution.py:83
  267.0 22.3 %collective-permute-start.21 = (bf16[4,24,1920]{2,1,0:T(8,128)(2,1)}, bf16[4,24,1920]{2,1,0:T(8,128)(2,1)}, u32[]{:S(2)}, u32[]{:S(2)}) collective-permute-start(bf16[4,24,1920]{2,1,0:T(8,128)(2,1)} %get-tuple-element.230), channel_id=1, source_target_pairs={{0,8},{1,9},{2,10},{3,11},{4,12},{5,13},{6,14},{7,15},{8,0},{9,1},... | collective-permute-start | bytes 1105928 | tf_op jit(solution)/shard_map/ppermute | solution.py:83
  268.4 20.9 %collective-permute-start.22 = (bf16[4,24,1920]{2,1,0:T(8,128)(2,1)}, bf16[4,24,1920]{2,1,0:T(8,128)(2,1)}, u32[]{:S(2)}, u32[]{:S(2)}) collective-permute-start(bf16[4,24,1920]{2,1,0:T(8,128)(2,1)} %get-tuple-element.231), channel_id=1, source_target_pairs={{0,16},{1,17},{2,18},{3,19},{4,20},{5,21},{6,22},{7,23},{8,24},{9,... | collective-permute-start | bytes 1105928 | tf_op jit(solution)/shard_map/ppermute | solution.py:83
  269.0 20.3 %collective-permute-start.23 = (bf16[4,24,1920]{2,1,0:T(8,128)(2,1)}, bf16[4,24,1920]{2,1,0:T(8,128)(2,1)}, u32[]{:S(2)}, u32[]{:S(2)}) collective-permute-start(bf16[4,24,1920]{2,1,0:T(8,128)(2,1)} %get-tuple-element.232), channel_id=1, source_target_pairs={{0,24},{1,25},{2,26},{3,27},{4,28},{5,29},{6,30},{7,31},{8,16},{9,... | collective-permute-start | bytes 1105928 | tf_op jit(solution)/shard_map/ppermute | solution.py:83
  285.9 5.9 %copy-start.6 = (bf16[2,48,3072]{2,1,0:T(8,128)(2,1)S(1)}, bf16[2,48,3072]{2,1,0:T(8,128)(2,1)}, u32[]{:S(2)}) copy-start(bf16[2,48,3072]{2,1,0:T(8,128)(2,1)} %get-tuple-element.209) | copy-start | bytes 1769476
  289.3 38.4 %copy-start.1 = (bf16[4,24,1920]{2,1,0:T(8,128)(2,1)}, bf16[4,24,1920]{2,1,0:T(8,128)(2,1)S(1)}, u32[]{:S(2)}) copy-start(bf16[4,24,1920]{2,1,0:T(8,128)(2,1)S(1)} %dynamic-slice_bitcast_fusion) | copy-start | bytes 1105924
  295.5 24.5 %collective-permute-start.24 = (bf16[1,48,3072]{2,1,0:T(8,128)(2,1)}, bf16[1,48,3072]{2,1,0:T(8,128)(2,1)}, u32[]{:S(2)}, u32[]{:S(2)}) collective-permute-start(bf16[1,48,3072]{2,1,0:T(8,128)(2,1)} %add_convert_fusion.3), channel_id=1, source_target_pairs={{0,4},{1,5},{2,6},{3,7},{4,0},{5,1},{6,2},{7,3},{8,12},{9,13},{10,... | collective-permute-start | bytes 884744 | tf_op jit(solution)/shard_map/ppermute | solution.py:83
  298.5 21.5 %collective-permute-start.25 = (bf16[4,24,1280]{2,1,0:T(8,128)(2,1)}, bf16[4,24,1280]{2,1,0:T(8,128)(2,1)}, u32[]{:S(2)}, u32[]{:S(2)}) collective-permute-start(bf16[4,24,1280]{2,1,0:T(8,128)(2,1)} %get-tuple-element.246), channel_id=1, source_target_pairs={{0,8},{1,9},{2,10},{3,11},{4,12},{5,13},{6,14},{7,15},{8,0},{9,1},... | collective-permute-start | bytes 737288 | tf_op jit(solution)/shard_map/ppermute | solution.py:83
  299.8 20.2 %collective-permute-start.26 = (bf16[4,24,1280]{2,1,0:T(8,128)(2,1)}, bf16[4,24,1280]{2,1,0:T(8,128)(2,1)}, u32[]{:S(2)}, u32[]{:S(2)}) collective-permute-start(bf16[4,24,1280]{2,1,0:T(8,128)(2,1)} %get-tuple-element.247), channel_id=1, source_target_pairs={{0,16},{1,17},{2,18},{3,19},{4,20},{5,21},{6,22},{7,23},{8,24},{9,... | collective-permute-start | bytes 737288 | tf_op jit(solution)/shard_map/ppermute | solution.py:83
  300.6 19.4 %collective-permute-start.27 = (bf16[4,24,1280]{2,1,0:T(8,128)(2,1)}, bf16[4,24,1280]{2,1,0:T(8,128)(2,1)}, u32[]{:S(2)}, u32[]{:S(2)}) collective-permute-start(bf16[4,24,1280]{2,1,0:T(8,128)(2,1)} %get-tuple-element.248), channel_id=1, source_target_pairs={{0,24},{1,25},{2,26},{3,27},{4,28},{5,29},{6,30},{7,31},{8,16},{9,... | collective-permute-start | bytes 737288 | tf_op jit(solution)/shard_map/ppermute | solution.py:83
  303.6 16.3 %collective-permute-start.28 = (bf16[2,1,24,1920]{3,2,1,0:T(8,128)(2,1)}, bf16[2,1,24,1920]{3,2,1,0:T(8,128)(2,1)S(1)}, u32[]{:S(2)}, u32[]{:S(2)}) collective-permute-start(bf16[2,1,24,1920]{3,2,1,0:T(8,128)(2,1)} %add_convert_fusion.7), channel_id=1, source_target_pairs={{0,2},{1,3},{2,0},{3,1},{4,6},{5,7},{6,4},{7,5},{8,10},{9,11},{10,... | collective-permute-start | bytes 552968 | tf_op jit(solution)/shard_map/ppermute | solution.py:83
  318.9 2.5 copy-start.3
  319.9 10.7 %copy-start.4 = (bf16[4,24,1280]{2,1,0:T(8,128)(2,1)}, bf16[4,24,1280]{2,1,0:T(8,128)(2,1)S(1)}, u32[]{:S(2)}) copy-start(bf16[4,24,1280]{2,1,0:T(8,128)(2,1)S(1)} %dynamic-slice_bitcast_fusion.2) | copy-start | bytes 737284
  319.9 10.7 %copy-start.7 = (bf16[2,1,24,1920]{3,2,1,0:T(8,128)(2,1)}, bf16[2,1,24,1920]{3,2,1,0:T(8,128)(2,1)S(1)}, u32[]{:S(2)}) copy-start(bf16[2,1,24,1920]{3,2,1,0:T(8,128)(2,1)S(1)} %collective-permute-done.28) | copy-start | bytes 552964
  321.4 8.5 %collective-permute-start.33 = (f32[1,24,3072]{2,1,0:T(8,128)S(1)}, f32[1,24,3072]{2,1,0:T(8,128)S(1)}, u32[]{:S(2)}, u32[]{:S(2)}) collective-permute-start(f32[1,24,3072]{2,1,0:T(8,128)S(1)} %constant_dynamic-slice_fusion), channel_id=1, source_target_pairs={{0,1},{1,0},{2,3},{3,2},{4,5},{5,4},{6,7},{7,6},{8,9},{9,8},{10,11... | collective-permute-start | bytes 884744 | tf_op jit(solution)/shard_map/ppermute | solution.py:83
  323.3 13.2 %collective-permute-start.30 = (bf16[24,1280]{1,0:T(8,128)(2,1)}, bf16[24,1280]{1,0:T(8,128)(2,1)}, u32[]{:S(2)}, u32[]{:S(2)}) collective-permute-start(bf16[24,1280]{1,0:T(8,128)(2,1)} %get-tuple-element.278), channel_id=1, source_target_pairs={{0,2},{1,3},{2,0},{3,1},{4,6},{5,7},{6,4},{7,5},{8,10},{9,11},{10,... | collective-permute-start | bytes 184328 | tf_op jit(solution)/shard_map/ppermute | solution.py:83
  325.2 11.3 %collective-permute-start.31 = (bf16[24,1280]{1,0:T(8,128)(2,1)}, bf16[24,1280]{1,0:T(8,128)(2,1)}, u32[]{:S(2)}, u32[]{:S(2)}) collective-permute-start(bf16[24,1280]{1,0:T(8,128)(2,1)} %get-tuple-element.277), channel_id=1, source_target_pairs={{0,4},{1,5},{2,6},{3,7},{4,0},{5,1},{6,2},{7,3},{8,12},{9,13},{10,... | collective-permute-start | bytes 184328 | tf_op jit(solution)/shard_map/ppermute | solution.py:83
  325.2 11.3 %collective-permute-start.32 = (bf16[24,1280]{1,0:T(8,128)(2,1)}, bf16[24,1280]{1,0:T(8,128)(2,1)}, u32[]{:S(2)}, u32[]{:S(2)}) collective-permute-start(bf16[24,1280]{1,0:T(8,128)(2,1)} %get-tuple-element.276), channel_id=1, source_target_pairs={{0,6},{1,7},{2,4},{3,5},{4,2},{5,3},{6,0},{7,1},{8,14},{9,15},{10,... | collective-permute-start | bytes 184328 | tf_op jit(solution)/shard_map/ppermute | solution.py:83
  329.4 8.8 %collective-permute-start.29 = (bf16[1,1,24,1920]{3,2,1,0:T(8,128)(2,1)}, bf16[1,1,24,1920]{3,2,1,0:T(8,128)(2,1)}, u32[]{:S(2)}, u32[]{:S(2)}) collective-permute-start(bf16[1,1,24,1920]{3,2,1,0:T(8,128)(2,1)} %add_convert_fusion.8), channel_id=1, source_target_pairs={{0,4},{1,5},{2,6},{3,7},{4,0},{5,1},{6,2},{7,3},{8,12},{9,13},{10,... | collective-permute-start | bytes 276488 | tf_op jit(solution)/shard_map/ppermute | solution.py:83
  333.0 2.6 copy-start.2
  333.0 5.1 %copy-start.8 = (bf16[2,1,24,1920]{3,2,1,0:T(8,128)(2,1)S(1)}, bf16[2,1,24,1920]{3,2,1,0:T(8,128)(2,1)}, u32[]{:S(2)}) copy-start(bf16[2,1,24,1920]{3,2,1,0:T(8,128)(2,1)} %copy-done.7) | copy-start | bytes 552964
Sparse Core Ops, SparseCore 0:
  11.7 95.2 all-gather.1
